TPU v7x, 512 devices: a whole 4x4x16 slice. The times are simulated.
512 devices in a mesh: dom: 64 (over z, y), rep: 8 (over x, core).
Axes of the slice: x: 4, y: 4, z: 16, core: 2. Of those that a mesh axis runs over, the one named last changes fastest.
Arguments:
- feats: bfloat16 [49152, 512], P('dom'), may hold values from -6 to 6
- halo_index: int32 [64, 64, 8], P('dom'), may hold values from 8 to 767
- seed_ids: int32 [262144], P(('dom', 'rep')), may hold values from 0 to 767, as said below
- tiles: bfloat16 [7168, 128, 128], P(('dom', 'rep')), may hold values from -1.25 to 1.25
- tile_dst: int32 [512, 14], P(('dom', 'rep')), may hold values from 0 to 3, as said below
- tile_src: int32 [512, 14], P(('dom', 'rep')), may hold values from 0 to 13
- tile_count: int32 [512], P(('dom', 'rep')), may hold values from 2 to 14, as said below
- w_self: bfloat16 [512, 512], replicated, may hold values from -0.25 to 0.25
- w_neigh: bfloat16 [512, 512], replicated, may hold values from -0.25 to 0.25
- bias: bfloat16 [512], replicated, may hold values from -3 to 3
- cotangent: bfloat16 [262144, 512], P(('dom', 'rep')), may hold values from -6 to 6
Outputs:
- out: bfloat16 [262144, 512], P(('dom', 'rep'))
- input_grad: float32 [49152, 512], P(('dom', 'rep'))
- grad_self: bfloat16 [512, 512], replicated
- grad_neigh: bfloat16 [512, 512], replicated
- grad_bias: float32 [512], replicated
Inputs may be any that keep to these rules, and one draw needn't show every extreme that they name: `halo_index`: halo lists never name a hub row, that is a row under 8. `seed_ids`: the 512 ids of one device are distinct. `tile_dst`: the 14 slots of one device name distinct (seed block, source block) pairs. `tile_count`: some device uses all 14 slots in every draw.
All inputs are finite; a program needn't handle non-finite values.
Results may differ from a plain program's by a relative error of at most 0.007.
Values may be sent and summed in bfloat16 or wider, within the bound.
No kernel may reach another device: no remote copies, remote signals or barrier semaphores. Data moves between devices by JAX's collectives and lax.ppermute only.
A program may use at most 64 MiB of HBM per device.

v0:
```python
import jax
import jax.numpy as jnp
from jax import lax
from jax.sharding import PartitionSpec as P

BLK = 128
SLOTS = 8
HUB_DEV = 8


def body(
    feats,
    halo_index,
    seed_ids,
    tiles,
    tile_dst,
    tile_src,
    tile_count,
    w_self,
    w_neigh,
    bias,
    cotangent,
):
    part_total = lax.axis_size("dom")
    rep_total = lax.axis_size("rep")
    local_rows, feat_width = feats.shape
    seed_rows = cotangent.shape[0]
    dst_total = seed_rows // BLK
    halo_lists = halo_index[0]
    highest = lax.Precision.HIGHEST
    hub_table = lax.all_gather(feats[:HUB_DEV][None], "dom", axis=0, tiled=True)
    halo_table = lax.all_to_all(feats[halo_lists], "dom", split_axis=0, concat_axis=0, tiled=True)
    source = jnp.concatenate(
        [feats, halo_table.reshape(-1, feat_width), hub_table.reshape(-1, feat_width)], 0
    )
    blocks = source.reshape(-1, BLK, feat_width)
    src_total = blocks.shape[0]
    live_count = tile_count[0]
    dst_block = tile_dst[0]
    src_block = tile_src[0]
    slot_ids = jnp.arange(tiles.shape[0], dtype=jnp.int32)
    live_mask = (slot_ids < live_count).astype(jnp.float32)
    dst_onehot = (dst_block[None, :] == jnp.arange(dst_total, dtype=jnp.int32)[:, None]).astype(
        jnp.float32
    ) * live_mask[None, :]
    products = jnp.einsum(
        "tij,tjh->tih", tiles, blocks[src_block], preferred_element_type=jnp.float32
    )
    aggregate = jnp.einsum("bt,tih->bih", dst_onehot, products, precision=highest)
    aggregate = aggregate.reshape(seed_rows, feat_width).astype(jnp.bfloat16)
    chosen = feats[seed_ids]
    preact = jnp.dot(chosen, w_self, preferred_element_type=jnp.float32)
    preact = preact + jnp.dot(aggregate, w_neigh, preferred_element_type=jnp.float32)
    preact = preact + bias.astype(jnp.float32)
    sigmoid_v = jax.nn.sigmoid(preact)
    output = (preact * sigmoid_v).astype(jnp.bfloat16)
    d_pre = (cotangent.astype(jnp.float32) * sigmoid_v * (1.0 + preact * (1.0 - sigmoid_v))).astype(
        jnp.bfloat16
    )
    part_self = jnp.dot(chosen.T, d_pre, preferred_element_type=jnp.float32)
    part_neigh = jnp.dot(aggregate.T, d_pre, preferred_element_type=jnp.float32)
    part_bias = jnp.sum(d_pre.astype(jnp.float32), 0)
    summed = lax.psum((part_self, part_neigh, part_bias), ("dom", "rep"))
    d_seed = jnp.dot(d_pre, w_self.T, preferred_element_type=jnp.float32)
    d_agg = jnp.dot(d_pre, w_neigh.T, preferred_element_type=jnp.float32).astype(jnp.bfloat16)
    d_blocks = d_agg.reshape(dst_total, BLK, feat_width)
    src_onehot = (src_block[None, :] == jnp.arange(src_total, dtype=jnp.int32)[:, None]).astype(
        jnp.float32
    ) * live_mask[None, :]
    back = jnp.einsum(
        "tij,tih->tjh", tiles, d_blocks[dst_block], preferred_element_type=jnp.float32
    )
    d_source = jnp.einsum("st,tjh->sjh", src_onehot, back, precision=highest)
    d_source = d_source.reshape(-1, feat_width)
    row_grad = d_source[:local_rows].at[seed_ids].add(d_seed)
    halo_start = local_rows + part_total * SLOTS
    halo_grad = d_source[local_rows:halo_start].reshape(part_total, SLOTS, feat_width)
    hub_grad = d_source[halo_start:].reshape(part_total, HUB_DEV, feat_width)
    back_halo, back_hub = (
        lax.all_to_all(
            halo_grad.astype(jnp.bfloat16), "dom", split_axis=0, concat_axis=0, tiled=True
        ).astype(halo_grad.dtype),
        lax.all_to_all(
            hub_grad.astype(jnp.bfloat16), "dom", split_axis=0, concat_axis=0, tiled=True
        ).astype(hub_grad.dtype),
    )
    row_grad = row_grad.at[halo_lists].add(back_halo)
    row_grad = row_grad.at[:HUB_DEV].add(jnp.sum(back_hub, 0))
    input_grad = lax.psum_scatter(row_grad, "rep", scatter_dimension=0, tiled=True)
    grad_scale = float(seed_rows * part_total * rep_total) ** (-0.5)
    grad_self = (summed[0] * grad_scale).astype(jnp.bfloat16)
    grad_neigh = (summed[1] * grad_scale).astype(jnp.bfloat16)
    grad_bias = summed[2] * grad_scale
    return (output, input_grad, grad_self, grad_neigh, grad_bias)


def solution(mesh):
    placed = (
        P("dom", None),
        P("dom", None, None),
        P(("dom", "rep")),
        P(("dom", "rep"), None, None),
        P(("dom", "rep"), None),
        P(("dom", "rep"), None),
        P(("dom", "rep")),
        P(),
        P(),
        P(),
        P(("dom", "rep"), None),
    )
    return jax.shard_map(
        body,
        mesh=mesh,
        in_specs=placed,
        out_specs=(P(("dom", "rep"), None), P(("dom", "rep"), None), P(), P(), P()),
        check_vma=False,
    )
```

profile of v0, /device:TPU:1, one launch (start us, length us, event | category | flops | bytes accessed | tf_op | source)
XLA Modules:
  0.0 747.7 jit_solution(13152586454608055532)
XLA Ops:
  8.0 0.0 copy-start
  8.0 0.7 compare_select_fusion
  8.8 0.1 copy.16
  8.8 0.1 reshape.164
  9.0 4.0 gather_fusion.1
  12.9 19.3 %all-to-all-start = ((bf16[64,8,512]{2,1,0:T(8,128)(2,1)}), bf16[64,8,512]{2,1,0:T(8,128)(2,1)S(1)}, u32[]{:S(2)}, u32[]{:S(2)}) async-start(bf16[64,8,512]{2,1,0:T(8,128)(2,1)} %bitcast.4), calls=%async_computation | async-start | bytes 1048576 | tf_op jit(solution)/shard_map/all_to_all | solution.py:32
  33.0 0.0 slice-start
  33.0 2.0 gather_fusion
  35.1 99.0 %all-gather = bf16[512,512]{1,0:T(8,128)(2,1)} all-gather(bf16[8,512]{1,0:T(8,128)(2,1)S(1)} %slice-done), channel_id=2, replica_groups=mesh['dom'=64,'rep'=8] {'dom'}, dimensions={0}, use_global_device_ids=true | all-gather | bytes 532480 | tf_op jit(solution)/shard_map/all_gather | solution.py:31
  134.1 1.5 fusion.28
  135.6 0.8 copy-done.5
  136.4 1.3 pad_maximum_fusion
  137.7 2.0 gather_fusion.2
  139.7 4.0 fusion.29
  143.7 5.3 copy.21
  149.0 4.4 fusion.5
  153.4 0.1 copy.17
  153.6 1.7 convert_reduce_fusion
  155.2 0.5 convolution_convert_fusion
  155.7 2.0 gather_fusion.3
  157.7 4.0 fusion.30
  161.7 5.4 copy.22
  167.0 7.8 %fusion.27 = (bf16[14,128,512]{2,0,1:T(8,128)(2,1)S(1)}, f32[14,128,512]{2,0,1:T(8,128)}) fusion(f32[14,512,128]{1,0,2:T(8,128)} %copy.22, f32[14]{0:T(128)S(1)} %compare_convert_fusion, s32[14]{0:T(128)S(1)} %bitcast.71), kind=kOutput, calls=%fused_computation.54 | convolution fusion | flops 155058560 | bytes 9175152 | tf_op jit(solution)/shard_map/st,tjh->sjh/dot_general | solution.py:73
  174.8 0.5 fusion.26
  175.4 0.9 copy.19
  176.3 10.5 %all-to-all-start.1 = ((bf16[64,8,512]{2,1,0:T(8,128)(2,1)}), bf16[64,8,512]{2,1,0:T(8,128)(2,1)S(1)}, u32[]{:S(2)}, u32[]{:S(2)}) async-start(bf16[64,8,512]{2,1,0:T(8,128)(2,1)} %bitcast.18), calls=%async_computation.1 | async-start | bytes 1048576 | tf_op jit(solution)/shard_map/all_to_all | solution.py:80
  186.8 0.9 copy.20
  187.7 21.0 %all-to-all-done.1 = bf16[64,8,512]{2,1,0:T(8,128)(2,1)S(1)} async-done(((bf16[64,8,512]{2,1,0:T(8,128)(2,1)}), bf16[64,8,512]{2,1,0:T(8,128)(2,1)S(1)}, u32[]{:S(2)}, u32[]{:S(2)}) %all-to-all-start.1) | async-done | bytes 524320 | tf_op jit(solution)/shard_map/all_to_all | solution.py:80
  208.7 5.6 all-to-all-start.2
  214.2 0.0 all-reduce.3.cloned.1.call-start
  214.3 1.4 fusion.33
  215.7 1.5 fusion.32
  217.2 0.0 all-reduce.3.cloned.1.call-update
  217.2 0.0 reduce-scatter.2.cloned.1.call-start
  217.3 1.8 slice.52
  219.1 0.9 copy.18
  220.0 0.1 copy-done.9
  220.1 1.5 fusion.31
  221.6 4.8 scatter_fusion
  226.4 4.2 scatter_custom_fusion.1
  230.7 14.9 %all-to-all-done.2 = bf16[64,8,512]{2,1,0:T(8,128)(2,1)S(1)} async-done(((bf16[64,8,512]{2,1,0:T(8,128)(2,1)}), bf16[64,8,512]{2,1,0:T(8,128)(2,1)S(1)}, u32[]{:S(2)}, u32[]{:S(2)}) %all-to-all-start.2) | async-done | bytes 524320 | tf_op jit(solution)/shard_map/all_to_all | solution.py:83
  245.6 0.1 convert_reduce_fusion.1
  245.7 1.2 copy-done.2
  246.9 0.0 reduce-scatter.2.cloned.1.call-update
  246.9 130.9 %psum.23 = f32[512]{0:T(512)S(1)} all-reduce(f32[512]{0:T(512)S(1)} %get-tuple-element.19), channel_id=1, replica_groups=mesh['dom'=64,'rep'=8] {'dom','rep'}, use_global_device_ids=true, to_apply=%region_7.0 | all-reduce | flops 512 | bytes 4096 | tf_op jit(solution)/shard_map/psum | solution.py:63
  377.9 0.6 broadcast_multiply_fusion
  378.4 359.1 %all-reduce.3.cloned.1.call-done = (f32[512,512]{1,0:T(8,128)}, f32[512,512]{1,0:T(8,128)}) async-done(((f32[512,512]{1,0:T(8,128)}, f32[512,512]{1,0:T(8,128)}), (f32[512,512]{1,0:T(8,128)}, f32[512,512]{1,0:T(8,128)})) %all-reduce.3.cloned.1.call-update) | async-done | bytes 2097168 | tf_op jit(solution)/shard_map/psum | solution.py:63
  737.5 2.8 multiply_convert_fusion
  (45 shorter events, 0.1 us)
Async XLA Ops:
  8.0 145.5 %copy-start = (bf16[512,512]{1,0:T(8,128)(2,1)S(1)}, bf16[512,512]{1,0:T(8,128)(2,1)}, u32[]{:S(2)}) copy-start(bf16[512,512]{1,0:T(8,128)(2,1)} %param.21) | copy-start | bytes 1572868
  9.0 23.9 %copy-start.13 = (s32[512]{0:T(512)S(1)}, s32[512]{0:T(512)}, u32[]{:S(2)}) copy-start(s32[512]{0:T(512)} %param.15) | copy-start | bytes 6148
  9.0 23.9 %copy-start.1 = (bf16[768,512]{1,0:T(8,128)(2,1)S(1)}, bf16[768,512]{1,0:T(8,128)(2,1)}, u32[]{:S(2)}) copy-start(bf16[768,512]{1,0:T(8,128)(2,1)} %param.13) | copy-start | bytes 2359300
  12.9 122.7 %all-to-all-start = ((bf16[64,8,512]{2,1,0:T(8,128)(2,1)}), bf16[64,8,512]{2,1,0:T(8,128)(2,1)S(1)}, u32[]{:S(2)}, u32[]{:S(2)}) async-start(bf16[64,8,512]{2,1,0:T(8,128)(2,1)} %bitcast.4), calls=%async_computation | async-start | bytes 1048576 | tf_op jit(solution)/shard_map/all_to_all | solution.py:32
  32.9 2.0 copy-start.14
  32.9 2.1 copy-start.16
  32.9 2.1 copy-start.15
  33.0 2.1 slice-start
  33.0 101.2 %copy-start.8 = (bf16[512,512]{1,0:T(8,128)(2,1)S(1)}, bf16[512,512]{1,0:T(8,128)(2,1)}, u32[]{:S(2)}) copy-start(bf16[512,512]{1,0:T(8,128)(2,1)} %param.20) | copy-start | bytes 1572868
  35.0 100.6 %copy-start.3 = (bf16[512,512]{1,0:T(8,128)(2,1)}, bf16[512,512]{1,0:T(8,128)(2,1)S(1)}, u32[]{:S(2)}) copy-start(bf16[512,512]{1,0:T(8,128)(2,1)S(1)} %gather_fusion) | copy-start | bytes 1572868
  135.6 0.8 copy-start.5
  137.7 2.0 copy-start.10
  149.0 4.5 copy-start.12
  149.0 4.5 copy-start.17
  155.7 2.0 copy-start.11
  176.3 32.4 %all-to-all-start.1 = ((bf16[64,8,512]{2,1,0:T(8,128)(2,1)}), bf16[64,8,512]{2,1,0:T(8,128)(2,1)S(1)}, u32[]{:S(2)}, u32[]{:S(2)}) async-start(bf16[64,8,512]{2,1,0:T(8,128)(2,1)} %bitcast.18), calls=%async_computation.1 | async-start | bytes 1048576 | tf_op jit(solution)/shard_map/all_to_all | solution.py:80
  187.7 28.0 %copy-start.4 = (bf16[512,512]{1,0:T(8,128)(2,1)S(1)}, bf16[512,512]{1,0:T(8,128)(2,1)}, u32[]{:S(2)}) copy-start(bf16[512,512]{1,0:T(8,128)(2,1)} %copy-done.3) | copy-start | bytes 1572868
  208.7 8.6 %copy-start.6 = (bf16[64,8,512]{2,1,0:T(8,128)(2,1)}, bf16[64,8,512]{2,1,0:T(8,128)(2,1)S(1)}, u32[]{:S(2)}) copy-start(bf16[64,8,512]{2,1,0:T(8,128)(2,1)S(1)} %all-to-all-done.1) | copy-start | bytes 1572868
  208.7 36.9 %all-to-all-start.2 = ((bf16[64,8,512]{2,1,0:T(8,128)(2,1)}), bf16[64,8,512]{2,1,0:T(8,128)(2,1)S(1)}, u32[]{:S(2)}, u32[]{:S(2)}) async-start(bf16[64,8,512]{2,1,0:T(8,128)(2,1)} %bitcast.20), calls=%async_computation.2 | async-start | bytes 1048576 | tf_op jit(solution)/shard_map/all_to_all | solution.py:83
  214.2 523.3 %all-reduce.3.cloned.1.call-start = ((), (), s32[]{:S(2)}) async-start(), calls=%async_computation.5 | async-start | bytes 4194304 | tf_op jit(solution)/shard_map/psum | solution.py:63
  217.2 523.0 %reduce-scatter.2.cloned.1.call-start = ((), (), s32[]{:S(2)}) async-start(), calls=%async_computation.4 | async-start | bytes 1769472 | tf_op jit(solution)/shard_map/reduce_scatter | solution.py:89
  219.1 1.0 copy-start.9
  221.6 4.9 copy-start.7
  245.7 1.2 copy-start.2
Sparse Core Ops, SparseCore 0:
  220.5 516.9 all-reduce.2
Sparse Core Ops, SparseCore 1:
  247.0 63.9 reduce-scatter.1
where the time goes:
time: 749 us; the launch traced here: 748 us
  waiting for transfers between devices  395 us (53%)
  blocking collectives  230 us (31%)
  starting transfers between devices  35.5 us (5%)
  matrix products  28.1 us (4%)
  local copies, waits for them, and re-layouts  28 us (4%)
  between operations  16.5 us (2%)
  other arithmetic  14.7 us (2%)
    psum x1, waiting for transfers between devices, body(): summed = lax.psum((part_self, part_neigh, part_bias), ('dom', 'rep'))  359 us
    psum x1, blocking collectives, body(): summed = lax.psum((part_self, part_neigh, part_bias), ('dom', 'rep'))  131 us
    all_gather x1, blocking collectives, body(): hub_table = lax.all_gather(feats[:HUB_DEV][None], 'dom', axis=0, tiled=True)  99 us
    all_to_all x1, waiting for transfers between devices, body(): lax.all_to_all(halo_grad.astype(jnp.bfloat16), 'dom', split_axis=0, conca...  21 us
    all_to_all x1, starting transfers between devices, body(): lax.all_to_all(feats[halo_lists], 'dom', split_axis=0, concat_axis=0, til...  19.3 us
  transfers between devices with their start and end apart: 5, of which 3 were waited for; matrix products, arithmetic and copies ran while one was open for 3% of the time, Pallas kernels for 0%

commit v1 on v0

v1 whole, which is shorter than its diff:
```python
import functools

import jax
import jax.numpy as jnp
from jax import lax
from jax.experimental import pallas as pl
from jax.experimental.pallas import tpu as pltpu
from jax.sharding import PartitionSpec as P

BLK = 128
SLOTS = 8
HUB_DEV = 8
BF16 = jnp.bfloat16
F32 = jnp.float32
VMEM_BYTES = 48 * 1024 * 1024


def dot(a, b, contract_a=1, contract_b=0):
    return lax.dot_general(
        a, b, (((contract_a,), (contract_b,)), ((), ())), preferred_element_type=F32
    )


def iota(shape, dim):
    return lax.broadcasted_iota(jnp.int32, shape, dim)


def vmem(count):
    return [pl.BlockSpec(memory_space=pltpu.VMEM)] * count


def smem(count):
    return [pl.BlockSpec(memory_space=pltpu.SMEM)] * count


def params():
    return pltpu.CompilerParams(vmem_limit_bytes=VMEM_BYTES)


def cost(flops, size):
    return pl.CostEstimate(flops=flops, bytes_accessed=size, transcendentals=0)


def place_tiles(dst_ref, src_ref, count_ref, tiles_ref, adj_ref, first, last):
    adj_ref[...] = jnp.zeros_like(adj_ref)

    def step(slot, carry):
        block = src_ref[0, slot]

        @pl.when(jnp.logical_and(block >= first, block < last))
        def _():
            row = pl.multiple_of(dst_ref[0, slot] * BLK, BLK)
            col = pl.multiple_of((block - first) * BLK, BLK)
            adj_ref[pl.ds(row, BLK), pl.ds(col, BLK)] = tiles_ref[slot]

        return carry

    lax.fori_loop(0, count_ref[0], step, 0)


def send_kernel(rep_ref, lists_ref, feats_ref, send_ref):
    parts, slots = lists_ref.shape
    rows = feats_ref.shape[0]
    rep = rep_ref[0]
    lists = lists_ref[...].astype(F32)
    wanted = jnp.sum(
        jnp.where(iota((parts, slots), 1) == rep, lists, 0.0), axis=1, keepdims=True
    ).astype(jnp.int32)
    place = iota((parts, rows), 1)
    halo = dot((place == wanted).astype(BF16), feats_ref[...]).astype(BF16)
    hub = dot((place == rep).astype(BF16), feats_ref[...]).astype(BF16)
    both = jnp.concatenate([halo, hub], 0)
    shape = (2 * parts, 2 * parts)
    out, into = iota(shape, 0), iota(shape, 1)
    spread = (into == (out % 2) * parts + out // 2).astype(BF16)
    send_ref[...] = dot(spread, both).astype(BF16)


def own_kernel(
    dst_ref, src_ref, count_ref, tiles_ref, feats_ref, seeds_ref, w_self_ref, bias_ref,
    chosen_ref, preact_ref, part_ref, adj_ref,
):
    rows = feats_ref.shape[0]
    seeds = seeds_ref.shape[1]
    place_tiles(dst_ref, src_ref, count_ref, tiles_ref, adj_ref, 0, rows // BLK)
    picks = (iota((rows, seeds), 0) == seeds_ref[...]).astype(BF16)
    chosen = dot(picks, feats_ref[...], 0, 0).astype(BF16)
    chosen_ref[...] = chosen
    preact_ref[...] = dot(chosen, w_self_ref[...]) + bias_ref[...].astype(F32)
    part_ref[...] = dot(adj_ref[...], feats_ref[...])


def forward_kernel(
    own_blocks, dst_ref, src_ref, count_ref, tiles_ref, table_ref, chosen_ref, preact_ref, part_ref,
    w_neigh_ref, cot_ref, out_ref, grad_ref, bias_ref, d_pre_ref, d_agg_ref, adj_ref, source_ref,
):
    reps, both, width = table_ref.shape
    parts = both // 2
    owners = BLK // reps
    blocks = parts * reps // BLK
    place_tiles(
        dst_ref, src_ref, count_ref, tiles_ref, adj_ref, own_blocks, own_blocks + 2 * blocks
    )
    shape = (2 * BLK, 2 * BLK)
    out, into = iota(shape, 0), iota(shape, 1)
    line = out % BLK
    order = (into == (line % reps) * (2 * owners) + (line // reps) * 2 + out // BLK).astype(BF16)
    for block in range(blocks):
        arrived = table_ref[:, 2 * owners * block : 2 * owners * (block + 1), :]
        sorted_rows = dot(order, arrived.reshape(2 * BLK, width)).astype(BF16)
        source_ref[block * BLK : (block + 1) * BLK] = sorted_rows[:BLK]
        source_ref[(blocks + block) * BLK : (blocks + block + 1) * BLK] = sorted_rows[BLK:]
    aggregate = (part_ref[...] + dot(adj_ref[...], source_ref[...])).astype(BF16)
    preact = preact_ref[...] + dot(aggregate, w_neigh_ref[...])
    gate = jax.nn.sigmoid(preact)
    out_ref[...] = (preact * gate).astype(BF16)
    d_pre = (cot_ref[...].astype(F32) * gate * (1.0 + preact * (1.0 - gate))).astype(BF16)
    d_pre_ref[...] = d_pre
    half = chosen_ref.shape[1]
    grad_ref[:half] = dot(chosen_ref[...], d_pre, 0, 0).astype(BF16)
    grad_ref[half:] = dot(aggregate, d_pre, 0, 0).astype(BF16)
    bias_ref[...] = jnp.sum(d_pre.astype(F32), 0, keepdims=True)
    d_agg_ref[...] = dot(d_pre, w_neigh_ref[...], 1, 1).astype(BF16)


def split_rows(wide, rows):
    high = wide.astype(BF16)
    low = (wide - high.astype(F32)).astype(BF16)
    row = iota((rows, wide.shape[1]), 0)
    zero = jnp.zeros((), F32)
    return jnp.where(row == 0, high.astype(F32), jnp.where(row == 1, low.astype(F32), zero)).astype(
        BF16
    )


def backward_kernel(
    dst_ref, src_ref, count_ref, tiles_ref, seeds_ref, d_pre_ref, d_agg_ref, w_self_ref, bias_ref,
    own_ref, send_ref, adj_ref,
):
    reps, lines, width = send_ref.shape
    rows = own_ref.shape[0]
    own_blocks = rows // BLK
    blocks = (adj_ref.shape[1] // BLK - own_blocks) // 2
    parts = blocks * BLK // reps
    owners = BLK // reps
    place_tiles(
        dst_ref, src_ref, count_ref, tiles_ref, adj_ref, 0, own_blocks + 2 * blocks
    )
    d_agg = d_agg_ref[...]
    out, into = iota((BLK, BLK), 0), iota((BLK, BLK), 1)
    order = (into == (out % owners) * reps + out // owners).astype(BF16)
    for kind in range(2):
        for block in range(blocks):
            start = (own_blocks + kind * blocks + block) * BLK
            grad = dot(adj_ref[:, start : start + BLK], d_agg, 0, 0).astype(BF16)
            grad = dot(order, grad).astype(BF16).reshape(reps, owners, width)
            first = kind * parts + block * owners
            send_ref[:, first : first + owners, :] = grad
    bias_rows = split_rows(bias_ref[...], lines - 2 * parts)
    for rep in range(reps):
        send_ref[rep, 2 * parts :, :] = bias_rows
    picks = (iota((rows, d_agg.shape[0]), 0) == seeds_ref[...]).astype(BF16)
    seeded = dot(picks, d_pre_ref[...]).astype(BF16)
    own_ref[...] = dot(seeded, w_self_ref[...], 1, 1) + dot(
        adj_ref[:, :rows], d_agg, 0, 0
    )


def scatter_kernel(rep_ref, lists_ref, back_ref, own_ref, row_ref):
    parts, slots = lists_ref.shape
    rows = own_ref.shape[0]
    rep = rep_ref[0]
    lists = lists_ref[...].astype(F32)
    wanted = jnp.sum(
        jnp.where(iota((parts, slots), 1) == rep, lists, 0.0), axis=1, keepdims=True
    ).astype(jnp.int32)
    place = iota((parts, rows), 1)
    halo_place = (place == wanted).astype(BF16)
    hub_place = (place == rep).astype(BF16)
    picks = jnp.concatenate([halo_place, hub_place], 0)
    row_ref[...] = (own_ref[...] + dot(picks, back_ref[...], 0, 0)).astype(BF16)


def body(
    feats,
    halo_index,
    seed_ids,
    tiles,
    tile_dst,
    tile_src,
    tile_count,
    w_self,
    w_neigh,
    bias,
    cotangent,
):
    parts = lax.axis_size("dom")
    reps = lax.axis_size("rep")
    rows, width = feats.shape
    seeds = cotangent.shape[0]
    rep = lax.axis_index("rep").astype(jnp.int32).reshape(1)
    lists = halo_index[0]
    seed_row = seed_ids.reshape(1, seeds)
    halo_rows = parts * SLOTS
    tile_args = (tile_dst, tile_src, tile_count, tiles)

    def swap(values, axis):
        return lax.all_to_all(values, axis, split_axis=0, concat_axis=0, tiled=True)

    def spread(values, axis, total):
        return swap(jnp.broadcast_to(values[None], (total,) + values.shape), axis)

    send = pl.pallas_call(
        send_kernel,
        out_shape=jax.ShapeDtypeStruct((2 * parts, width), BF16),
        in_specs=smem(1) + vmem(2),
        out_specs=vmem(1)[0],
        compiler_params=params(),
        cost_estimate=cost(4 * parts * rows * width, 2**20),
        name="pick_boundary",
    )(rep, lists, feats)
    arrived = swap(send.reshape(parts, 2, width), "dom")
    table = spread(arrived.reshape(2 * parts, width), "rep", reps)

    chosen, preact, part = pl.pallas_call(
        own_kernel,
        out_shape=(
            jax.ShapeDtypeStruct((seeds, width), BF16),
            jax.ShapeDtypeStruct((seeds, width), F32),
            jax.ShapeDtypeStruct((seeds, width), F32),
        ),
        in_specs=smem(3) + vmem(5),
        out_specs=tuple(vmem(3)),
        scratch_shapes=[pltpu.VMEM((seeds, rows), BF16)],
        compiler_params=params(),
        cost_estimate=cost(2 * seeds * width * (2 * rows + width), 5 * 2**20),
        name="own_rows",
    )(*tile_args, feats, seed_row, w_self, bias.reshape(1, width))

    out, grads, bias_part, d_pre, d_agg = pl.pallas_call(
        functools.partial(forward_kernel, rows // BLK),
        out_shape=(
            jax.ShapeDtypeStruct((seeds, width), BF16),
            jax.ShapeDtypeStruct((2 * width, width), BF16),
            jax.ShapeDtypeStruct((1, width), F32),
            jax.ShapeDtypeStruct((seeds, width), BF16),
            jax.ShapeDtypeStruct((seeds, width), BF16),
        ),
        in_specs=smem(3) + vmem(7),
        out_specs=tuple(vmem(5)),
        scratch_shapes=[
            pltpu.VMEM((seeds, 2 * halo_rows), BF16),
            pltpu.VMEM((2 * halo_rows, width), BF16),
        ],
        compiler_params=params(),
        cost_estimate=cost(2 * seeds * width * (2 * halo_rows + 4 * width), 6 * 2**20),
        name="forward",
    )(*tile_args, table, chosen, preact, part, w_neigh, cotangent)

    weight_parts = swap(grads.reshape(reps, -1, width), "rep")

    own, back_send = pl.pallas_call(
        backward_kernel,
        out_shape=(
            jax.ShapeDtypeStruct((rows, width), F32),
            jax.ShapeDtypeStruct((reps, 2 * parts + 16, width), BF16),
        ),
        in_specs=smem(3) + vmem(6),
        out_specs=tuple(vmem(2)),
        scratch_shapes=[pltpu.VMEM((seeds, rows + 2 * halo_rows), BF16)],
        compiler_params=params(),
        cost_estimate=cost(2 * seeds * width * (3 * rows + 2 * halo_rows), 5 * 2**20),
        name="backward",
    )(*tile_args, seed_row, d_pre, d_agg, w_self, bias_part)

    back_parts = swap(back_send, "rep")

    weight_sum = jnp.sum(weight_parts.astype(F32), 0).astype(BF16)
    weight_rows = weight_sum.reshape(parts, -1, width)
    weight_dom = swap(weight_rows, "dom")

    back_sum = jnp.sum(back_parts.astype(F32), 0)
    bias_sum = back_sum[2 * parts] + back_sum[2 * parts + 1]
    bias_high = bias_sum.astype(BF16)
    bias_low = (bias_sum - bias_high.astype(F32)).astype(BF16)
    back_rows = jnp.stack(
        [
            back_sum[:parts].astype(BF16),
            back_sum[parts : 2 * parts].astype(BF16),
            jnp.broadcast_to(bias_high[None], (parts, width)),
            jnp.broadcast_to(bias_low[None], (parts, width)),
        ],
        1,
    )
    back_dom = swap(back_rows, "dom")

    grad_scale = float(seeds * parts * reps) ** (-0.5)
    weight_done = (jnp.sum(weight_dom.astype(F32), 0) * grad_scale).astype(BF16)
    weight_table = spread(weight_done, "dom", parts).reshape(-1, width)
    weight_all = spread(weight_table, "rep", reps).reshape(2 * width, width)

    grad_bias = jnp.sum(back_dom[:, 2:].astype(F32), (0, 1)) * grad_scale
    back = jnp.swapaxes(back_dom[:, :2], 0, 1).reshape(2 * parts, width)
    row_part = pl.pallas_call(
        scatter_kernel,
        out_shape=jax.ShapeDtypeStruct((rows, width), BF16),
        in_specs=smem(1) + vmem(3),
        out_specs=vmem(1)[0],
        compiler_params=params(),
        cost_estimate=cost(4 * parts * rows * width, 3 * 2**20),
        name="return_rows",
    )(rep, lists, back, own)
    row_parts = swap(row_part.reshape(reps, -1, width), "rep")
    input_grad = jnp.sum(row_parts.astype(F32), 0)
    return (out, input_grad, weight_all[:width], weight_all[width:], grad_bias)


def solution(mesh):
    placed = (
        P("dom", None),
        P("dom", None, None),
        P(("dom", "rep")),
        P(("dom", "rep"), None, None),
        P(("dom", "rep"), None),
        P(("dom", "rep"), None),
        P(("dom", "rep")),
        P(),
        P(),
        P(),
        P(("dom", "rep"), None),
    )
    return jax.shard_map(
        body,
        mesh=mesh,
        in_specs=placed,
        out_specs=(P(("dom", "rep"), None), P(("dom", "rep"), None), P(), P(), P()),
        check_vma=False,
    )
```

time: 749 us -> 220 us (0.29)
  waiting for transfers between devices: 395 us -> 104 us
  blocking collectives: 230 us -> 34 us
  matrix products: 28.1 us -> 0 us
  between operations: 16.5 us -> 1.58 us
  Pallas kernels: 0 us -> 13.9 us
  local copies, waits for them, and re-layouts: 28 us -> 15.5 us
  starting transfers between devices: 35.5 us -> 47.3 us
  other arithmetic: 14.7 us -> 3.21 us
    psum x1 -> x0, waiting for transfers between devices: 359 us -> none  [body(): summed = lax.psum((part_self, part_neigh, part_bias), ('dom', 'rep'))]
    psum x1 -> x0, blocking collectives: 131 us -> none  [body(): summed = lax.psum((part_self, part_neigh, part_bias), ('dom', 'rep'))]
    all_gather x1 -> x0, blocking collectives: 99 us -> none  [body(): hub_table = lax.all_gather(feats[:HUB_DEV][None], 'dom', axis=0, tiled=True)]
    all_to_all x3 -> x8, waiting for transfers between devices: 35.9 us -> 104 us  [swap(): return lax.all_to_all(values, axis, split_axis=0, concat_axis=0, tiled=True)]
    all_to_all x0 -> x1, blocking collectives: none -> 34 us  [swap(): return lax.all_to_all(values, axis, split_axis=0, concat_axis=0, tiled=True)]
    dot_general x10 -> x0, matrix products: 28.1 us -> none  [the longest x1 7.78 us: body(): d_source = jnp.einsum('st,tjh->sjh', src_onehot, back, precision=highest)]
    pallas_call x0 -> x5, Pallas kernels: none -> 13.9 us  [the longest x1 5.12 us: body(): pl.pallas_call(backward_kernel, out_shape=(jax.ShapeDtypeStruct((rows, wi...]
    all_to_all x3 -> x8, starting transfers between devices: 35.4 us -> 47.3 us  [swap(): return lax.all_to_all(values, axis, split_axis=0, concat_axis=0, tiled=True)]
  transfers between devices with their start and end apart: 5 -> 8, of which waited for: 3 -> 8; matrix products, arithmetic and copies ran while one was open for 3% -> 2% of each run, Pallas kernels for 0% -> 4%
where the time goes in v1:
time: 220 us; the launch traced here: 219 us
  waiting for transfers between devices  104 us (47%)
  starting transfers between devices  47.3 us (22%)
  blocking collectives  34 us (15%)
  local copies, waits for them, and re-layouts  15.5 us (7%)
  Pallas kernels  13.9 us (6%)
  other arithmetic  3.21 us (1%)
    all_to_all x8, waiting for transfers between devices, swap(): return lax.all_to_all(values, axis, split_axis=0, concat_axis=0, tiled=True)  104 us
    all_to_all x8, starting transfers between devices, swap(): return lax.all_to_all(values, axis, split_axis=0, concat_axis=0, tiled=True)  47.3 us
    all_to_all x1, blocking collectives, swap(): return lax.all_to_all(values, axis, split_axis=0, concat_axis=0, tiled=True)  34 us
    unnamed x41, local copies, waits for them, and re-layouts  9.65 us
    pallas_call x1, Pallas kernels, body(): pl.pallas_call(backward_kernel, out_shape=(jax.ShapeDtypeStruct((rows, wi...  5.12 us
    pallas_call x1, Pallas kernels, body(): pl.pallas_call(functools.partial(forward_kernel, rows // BLK), out_shape=...  4.85 us
  transfers between devices with their start and end apart: 8, of which 8 were waited for; matrix products, arithmetic and copies ran while one was open for 2% of the time, Pallas kernels for 4%

profile of v1, /device:TPU:1, one launch (start us, length us, event | category | flops | bytes accessed | tf_op | source)
XLA Modules:
  0.0 219.0 jit_solution(11309954156607711936)
XLA Ops:
  0.6 0.8 copy.34
  1.4 1.1 copy-done
  2.5 0.6 pick_boundary.1
  3.1 0.1 reshape.45
  3.2 34.0 %all_to_all.45 = bf16[64,2,512]{2,1,0:T(2,128)(2,1)S(1)} all-to-all(bf16[64,2,512]{2,1,0:T(2,128)(2,1)S(1)} %reshape.45), channel_id=1, replica_groups=mesh['dom'=64,'rep'=8] {'dom'}, dimensions={0} | all-to-all | bytes 262144 | tf_op jit(solution)/shard_map/all_to_all | solution.py:208
  37.2 0.1 broadcast_in_dim.10
  37.2 0.0 copy-start.19
  37.3 1.0 broadcast_in_dim.11
  38.4 8.0 %all-to-all-start.1 = ((bf16[8,128,512]{2,1,0:T(8,128)(2,1)}), bf16[8,128,512]{2,1,0:T(8,128)(2,1)S(1)}, u32[]{:S(2)}, u32[]{:S(2)}) async-start(bf16[8,128,512]{2,1,0:T(8,128)(2,1)} %broadcast_in_dim.11), calls=%async_computation.1 | async-start | bytes 2097152 | tf_op jit(solution)/shard_map/all_to_all | solution.py:208
  47.1 1.0 copy-done.5
  48.1 2.0 own_rows.1
  50.1 1.0 copy-done.11
  51.1 1.0 copy-done.12
  52.1 0.8 copy-done.17
  52.9 8.6 %all-to-all-done.1.table_ref = bf16[8,128,512]{2,1,0:T(8,128)(2,1)S(1)} async-done(((bf16[8,128,512]{2,1,0:T(8,128)(2,1)}), bf16[8,128,512]{2,1,0:T(8,128)(2,1)S(1)}, u32[]{:S(2)}, u32[]{:S(2)}) %all-to-all-start.1) | async-done | bytes 1048608 | tf_op jit(solution)/shard_map/all_to_all | solution.py:208
  61.5 1.0 copy-done.6
  62.5 1.0 copy-done.18
  63.6 4.8 %forward.1 = (bf16[512,512]{1,0:T(8,128)(2,1)}, bf16[1024,512]{1,0:T(8,128)(2,1)}, f32[1,512]{1,0:T(1,128)S(1)}, bf16[512,512]{1,0:T(8,128)(2,1)S(1)}, bf16[512,512]{1,0:T(8,128)(2,1)S(1)}) custom-call(s32[1,14]{1,0:T(1,128)S(1)} %copy-done.9, s32[1,14]{1,0:T(1,128)S(1)} %copy-done.10, s32[1]{0:T(128)S(6)} %copy.39.count_ref, ...), custom_call_target="tpu_custom_call" | custom-call | flops 1610612736 | bytes 6291456 | tf_op jit(solution)/shard_map/forward/pallas_call | solution.py:240
  68.4 0.8 copy-done.13
  69.2 5.0 %all-to-all-start.5 = ((bf16[8,128,512]{2,1,0:T(8,128)(2,1)}), bf16[8,128,512]{2,1,0:T(8,128)(2,1)}, u32[]{:S(2)}, u32[]{:S(2)}) async-start(bf16[8,128,512]{2,1,0:T(8,128)(2,1)} %bitcast.9), calls=%async_computation.5 | async-start | bytes 2097152 | tf_op jit(solution)/shard_map/all_to_all | solution.py:208
  74.3 1.0 copy-done.16
  75.3 5.1 %backward.1 = (f32[768,512]{1,0:T(8,128)S(1)}, bf16[8,144,512]{2,1,0:T(8,128)(2,1)}) custom-call(s32[1,14]{1,0:T(1,128)S(1)} %copy-done.9, s32[1,14]{1,0:T(1,128)S(1)} %copy-done.10, s32[1]{0:T(128)S(6)} %copy.39.count_ref, bf16[14,128,128]{2,1,0:T(8,128)(2,1)S(1)} %copy-done.7, s32[1,512]{1,0:T(1,128)S(1)} %bitcast.19, bf16[512,512]{1,0:T(8,128)(2,1)S(1)} %copy-done.14, ...), custom_call_target="tpu_custom_call" | custom-call | flops 1744830464 | bytes 5242880 | tf_op jit(solution)/shard_map/backward/pallas_call | solution.py:262
  80.4 9.0 %all-to-all-done.5 = bf16[8,128,512]{2,1,0:T(8,128)(2,1)} async-done(((bf16[8,128,512]{2,1,0:T(8,128)(2,1)}), bf16[8,128,512]{2,1,0:T(8,128)(2,1)}, u32[]{:S(2)}, u32[]{:S(2)}) %all-to-all-start.5) | async-done | bytes 1048608 | tf_op jit(solution)/shard_map/all_to_all | solution.py:208
  89.5 4.3 %all-to-all-start.2 = ((bf16[8,144,512]{2,1,0:T(8,128)(2,1)}), bf16[8,144,512]{2,1,0:T(8,128)(2,1)S(1)}, u32[]{:S(2)}, u32[]{:S(2)}) async-start(bf16[8,144,512]{2,1,0:T(8,128)(2,1)} %get-tuple-element.22), calls=%async_computation.2 | async-start | bytes 2359296 | tf_op jit(solution)/shard_map/all_to_all | solution.py:208
  93.8 1.4 reduce_sum.50
  95.2 0.7 reshape.51
  95.9 14.4 %all-to-all-done.2 = bf16[8,144,512]{2,1,0:T(8,128)(2,1)S(1)} async-done(((bf16[8,144,512]{2,1,0:T(8,128)(2,1)}), bf16[8,144,512]{2,1,0:T(8,128)(2,1)S(1)}, u32[]{:S(2)}, u32[]{:S(2)}) %all-to-all-start.2) | async-done | bytes 1179680 | tf_op jit(solution)/shard_map/all_to_all | solution.py:208
  110.3 4.6 %all-to-all-start.6 = ((bf16[64,2,512]{2,1,0:T(2,128)(2,1)}), bf16[64,2,512]{2,1,0:T(2,128)(2,1)S(1)}, u32[]{:S(2)}, u32[]{:S(2)}) async-start(bf16[64,2,512]{2,1,0:T(2,128)(2,1)} %reshape.51), calls=%async_computation.6 | async-start | bytes 262144 | tf_op jit(solution)/shard_map/all_to_all | solution.py:208
  115.0 0.2 convert_reduce_fusion
  115.3 0.9 copy.35
  116.2 14.0 %all-to-all-done.6 = bf16[64,2,512]{2,1,0:T(2,128)(2,1)S(1)} async-done(((bf16[64,2,512]{2,1,0:T(2,128)(2,1)}), bf16[64,2,512]{2,1,0:T(2,128)(2,1)S(1)}, u32[]{:S(2)}, u32[]{:S(2)}) %all-to-all-start.6) | async-done | bytes 131104 | tf_op jit(solution)/shard_map/all_to_all | solution.py:208
  130.1 6.1 %all-to-all-start.3 = ((bf16[64,4,512]{2,1,0:T(4,128)(2,1)}), bf16[64,4,512]{2,1,0:T(4,128)(2,1)S(1)}, u32[]{:S(2)}, u32[]{:S(2)}) async-start(bf16[64,4,512]{2,1,0:T(4,128)(2,1)} %copy.35), calls=%async_computation.3 | async-start | bytes 524288 | tf_op jit(solution)/shard_map/all_to_all | solution.py:208
  136.3 18.2 %all-to-all-done.3 = bf16[64,4,512]{2,1,0:T(4,128)(2,1)S(1)} async-done(((bf16[64,4,512]{2,1,0:T(4,128)(2,1)}), bf16[64,4,512]{2,1,0:T(4,128)(2,1)S(1)}, u32[]{:S(2)}, u32[]{:S(2)}) %all-to-all-start.3) | async-done | bytes 262176 | tf_op jit(solution)/shard_map/all_to_all | solution.py:208
  154.5 0.7 broadcast_in_dim.24
  155.2 7.4 %all-to-all-start.7 = ((bf16[64,2,512]{2,1,0:T(2,128)(2,1)}), bf16[64,2,512]{2,1,0:T(2,128)(2,1)S(1)}, u32[]{:S(2)}, u32[]{:S(2)}) async-start(bf16[64,2,512]{2,1,0:T(2,128)(2,1)} %broadcast_in_dim.24), calls=%async_computation.7 | async-start | bytes 262144 | tf_op jit(solution)/shard_map/all_to_all | solution.py:208
  162.7 0.1 slice_bitcast_fusion
  162.8 1.4 return_rows.1
  164.1 13.5 %all-to-all-done.7 = bf16[64,2,512]{2,1,0:T(2,128)(2,1)S(1)} async-done(((bf16[64,2,512]{2,1,0:T(2,128)(2,1)}), bf16[64,2,512]{2,1,0:T(2,128)(2,1)S(1)}, u32[]{:S(2)}, u32[]{:S(2)}) %all-to-all-start.7) | async-done | bytes 131104 | tf_op jit(solution)/shard_map/all_to_all | solution.py:208
  177.6 7.4 %all-to-all-start.4 = ((bf16[8,96,512]{2,1,0:T(8,128)(2,1)}), bf16[8,96,512]{2,1,0:T(8,128)(2,1)S(1)}, u32[]{:S(2)}, u32[]{:S(2)}) async-start(bf16[8,96,512]{2,1,0:T(8,128)(2,1)} %bitcast.8), calls=%async_computation.4 | async-start | bytes 1572864 | tf_op jit(solution)/shard_map/all_to_all | solution.py:208
  185.1 0.1 broadcast_in_dim.25
  185.1 12.2 %all-to-all-done.4 = bf16[8,96,512]{2,1,0:T(8,128)(2,1)S(1)} async-done(((bf16[8,96,512]{2,1,0:T(8,128)(2,1)}), bf16[8,96,512]{2,1,0:T(8,128)(2,1)S(1)}, u32[]{:S(2)}, u32[]{:S(2)}) %all-to-all-start.4) | async-done | bytes 786464 | tf_op jit(solution)/shard_map/all_to_all | solution.py:208
  197.4 1.1 broadcast_in_dim.26
  198.5 4.3 %all-to-all-start.8 = ((bf16[8,128,512]{2,1,0:T(8,128)(2,1)}), bf16[8,128,512]{2,1,0:T(8,128)(2,1)S(1)}, u32[]{:S(2)}, u32[]{:S(2)}) async-start(bf16[8,128,512]{2,1,0:T(8,128)(2,1)} %broadcast_in_dim.26), calls=%async_computation.8 | async-start | bytes 2097152 | tf_op jit(solution)/shard_map/all_to_all | solution.py:208
  202.8 0.2 convert_reduce_fusion.2
  203.0 0.6 broadcast_multiply_fusion
  203.6 0.8 convert_reduce_fusion.1
  204.4 13.6 %all-to-all-done.8 = bf16[8,128,512]{2,1,0:T(8,128)(2,1)S(1)} async-done(((bf16[8,128,512]{2,1,0:T(8,128)(2,1)}), bf16[8,128,512]{2,1,0:T(8,128)(2,1)S(1)}, u32[]{:S(2)}, u32[]{:S(2)}) %all-to-all-start.8) | async-done | bytes 1048608 | tf_op jit(solution)/shard_map/all_to_all | solution.py:208
  217.9 1.1 fusion
  (41 shorter events, 0.2 us)
Async XLA Ops:
  1.4 1.1 copy-start
  37.2 9.8 %copy-start.19 = (bf16[512]{0:T(512)(128)(2,1)S(1)}, bf16[512]{0:T(512)(128)(2,1)}, u32[]{:S(2)}) copy-start(bf16[512]{0:T(512)(128)(2,1)} %param.20) | copy-start | bytes 3076
  37.3 9.8 %copy-start.1 = (bf16[768,512]{1,0:T(8,128)(2,1)S(1)}, bf16[768,512]{1,0:T(8,128)(2,1)}, u32[]{:S(2)}) copy-start(bf16[768,512]{1,0:T(8,128)(2,1)} %feats_ref.3) | copy-start | bytes 2359300
  37.3 9.8 %copy-start.4 = (bf16[512,512]{1,0:T(8,128)(2,1)S(1)}, bf16[512,512]{1,0:T(8,128)(2,1)}, u32[]{:S(2)}) copy-start(bf16[512,512]{1,0:T(8,128)(2,1)} %w_self_ref.3) | copy-start | bytes 1572868
  37.3 9.8 %copy-start.8 = (s32[512]{0:T(512)S(1)}, s32[512]{0:T(512)}, u32[]{:S(2)}) copy-start(s32[512]{0:T(512)} %param.13) | copy-start | bytes 6148
  37.3 9.8 %copy-start.9 = (s32[1,14]{1,0:T(1,128)S(1)}, s32[1,14]{1,0:T(1,128)}, u32[]{:S(2)}) copy-start(s32[1,14]{1,0:T(1,128)} %dst_ref.5) | copy-start | bytes 172
  37.3 9.8 %copy-start.10 = (s32[1,14]{1,0:T(1,128)S(1)}, s32[1,14]{1,0:T(1,128)}, u32[]{:S(2)}) copy-start(s32[1,14]{1,0:T(1,128)} %src_ref.5) | copy-start | bytes 172
  38.4 23.1 %all-to-all-start.1 = ((bf16[8,128,512]{2,1,0:T(8,128)(2,1)}), bf16[8,128,512]{2,1,0:T(8,128)(2,1)S(1)}, u32[]{:S(2)}, u32[]{:S(2)}) async-start(bf16[8,128,512]{2,1,0:T(8,128)(2,1)} %broadcast_in_dim.11), calls=%async_computation.1 | async-start | bytes 2097152 | tf_op jit(solution)/shard_map/all_to_all | solution.py:208
  47.1 1.0 copy-start.5
  48.1 13.4 %copy-start.2 = (bf16[512,512]{1,0:T(8,128)(2,1)S(1)}, bf16[512,512]{1,0:T(8,128)(2,1)}, u32[]{:S(2)}) copy-start(bf16[512,512]{1,0:T(8,128)(2,1)} %w_neigh_ref.1) | copy-start | bytes 1572868
  48.1 13.4 %copy-start.3 = (bf16[512,512]{1,0:T(8,128)(2,1)S(1)}, bf16[512,512]{1,0:T(8,128)(2,1)}, u32[]{:S(2)}) copy-start(bf16[512,512]{1,0:T(8,128)(2,1)} %cot_ref.1) | copy-start | bytes 1572868
  50.1 1.0 copy-start.11
  51.1 1.0 copy-start.12
  52.1 0.8 copy-start.17
  61.5 1.0 copy-start.6
  62.5 1.0 copy-start.18
  68.4 0.8 copy-start.13
  69.2 5.1 %copy-start.15 = (bf16[512,512]{1,0:T(8,128)(2,1)}, bf16[512,512]{1,0:T(8,128)(2,1)S(1)}, u32[]{:S(2)}) copy-start(bf16[512,512]{1,0:T(8,128)(2,1)S(1)} %get-tuple-element.20.d_agg_ref) | copy-start | bytes 1572868
  69.2 5.1 %copy-start.7 = (bf16[14,128,128]{2,1,0:T(8,128)(2,1)S(1)}, bf16[14,128,128]{2,1,0:T(8,128)(2,1)}, u32[]{:S(2)}) copy-start(bf16[14,128,128]{2,1,0:T(8,128)(2,1)} %tiles_ref.5) | copy-start | bytes 1376260
  69.2 5.1 %copy-start.14 = (bf16[512,512]{1,0:T(8,128)(2,1)S(1)}, bf16[512,512]{1,0:T(8,128)(2,1)}, u32[]{:S(2)}) copy-start(bf16[512,512]{1,0:T(8,128)(2,1)} %copy-done.13) | copy-start | bytes 1572868
  69.2 20.3 %all-to-all-start.5 = ((bf16[8,128,512]{2,1,0:T(8,128)(2,1)}), bf16[8,128,512]{2,1,0:T(8,128)(2,1)}, u32[]{:S(2)}, u32[]{:S(2)}) async-start(bf16[8,128,512]{2,1,0:T(8,128)(2,1)} %bitcast.9), calls=%async_computation.5 | async-start | bytes 2097152 | tf_op jit(solution)/shard_map/all_to_all | solution.py:208
  74.3 1.0 copy-start.16
  89.5 20.9 %all-to-all-start.2 = ((bf16[8,144,512]{2,1,0:T(8,128)(2,1)}), bf16[8,144,512]{2,1,0:T(8,128)(2,1)S(1)}, u32[]{:S(2)}, u32[]{:S(2)}) async-start(bf16[8,144,512]{2,1,0:T(8,128)(2,1)} %get-tuple-element.22), calls=%async_computation.2 | async-start | bytes 2359296 | tf_op jit(solution)/shard_map/all_to_all | solution.py:208
  110.3 19.8 %all-to-all-start.6 = ((bf16[64,2,512]{2,1,0:T(2,128)(2,1)}), bf16[64,2,512]{2,1,0:T(2,128)(2,1)S(1)}, u32[]{:S(2)}, u32[]{:S(2)}) async-start(bf16[64,2,512]{2,1,0:T(2,128)(2,1)} %reshape.51), calls=%async_computation.6 | async-start | bytes 262144 | tf_op jit(solution)/shard_map/all_to_all | solution.py:208
  130.1 24.4 %all-to-all-start.3 = ((bf16[64,4,512]{2,1,0:T(4,128)(2,1)}), bf16[64,4,512]{2,1,0:T(4,128)(2,1)S(1)}, u32[]{:S(2)}, u32[]{:S(2)}) async-start(bf16[64,4,512]{2,1,0:T(4,128)(2,1)} %copy.35), calls=%async_computation.3 | async-start | bytes 524288 | tf_op jit(solution)/shard_map/all_to_all | solution.py:208
  155.2 22.4 %all-to-all-start.7 = ((bf16[64,2,512]{2,1,0:T(2,128)(2,1)}), bf16[64,2,512]{2,1,0:T(2,128)(2,1)S(1)}, u32[]{:S(2)}, u32[]{:S(2)}) async-start(bf16[64,2,512]{2,1,0:T(2,128)(2,1)} %broadcast_in_dim.24), calls=%async_computation.7 | async-start | bytes 262144 | tf_op jit(solution)/shard_map/all_to_all | solution.py:208
  177.6 19.7 %all-to-all-start.4 = ((bf16[8,96,512]{2,1,0:T(8,128)(2,1)}), bf16[8,96,512]{2,1,0:T(8,128)(2,1)S(1)}, u32[]{:S(2)}, u32[]{:S(2)}) async-start(bf16[8,96,512]{2,1,0:T(8,128)(2,1)} %bitcast.8), calls=%async_computation.4 | async-start | bytes 1572864 | tf_op jit(solution)/shard_map/all_to_all | solution.py:208
  198.5 19.4 %all-to-all-start.8 = ((bf16[8,128,512]{2,1,0:T(8,128)(2,1)}), bf16[8,128,512]{2,1,0:T(8,128)(2,1)S(1)}, u32[]{:S(2)}, u32[]{:S(2)}) async-start(bf16[8,128,512]{2,1,0:T(8,128)(2,1)} %broadcast_in_dim.26), calls=%async_computation.8 | async-start | bytes 2097152 | tf_op jit(solution)/shard_map/all_to_all | solution.py:208

commit v2 on v0

v2 whole, which is shorter than its diff:
```python
import functools

import jax
import jax.numpy as jnp
from jax import lax
from jax.experimental import pallas as pl
from jax.experimental.pallas import tpu as pltpu
from jax.sharding import Mesh
from jax.sharding import PartitionSpec as P

BLK = 128
LANES = 128
SLOTS = 8
X_SIZE = 4
CORES = 2
Y_SIZE = 4
PLANE = Y_SIZE * X_SIZE
BF16 = jnp.bfloat16
F32 = jnp.float32
VMEM_BYTES = 24 * 1024 * 1024


def dot(a, b, contract_a=1, contract_b=0):
    return lax.dot_general(
        a, b, (((contract_a,), (contract_b,)), ((), ())), preferred_element_type=F32
    )


def move(matrix, rows):
    return dot(matrix.astype(BF16), rows).astype(BF16)


def iota(shape, dim):
    return lax.broadcasted_iota(jnp.int32, shape, dim)


def split(wide):
    high = wide.astype(BF16)
    return high, (wide - high.astype(F32)).astype(BF16)


def call(kernel, name, outs, scalars, arrays, scratch=(), flops=0):
    shapes = tuple(jax.ShapeDtypeStruct(shape, dtype) for shape, dtype in outs)
    size = sum(a.size * a.dtype.itemsize for a in (*arrays, *shapes))
    return pl.pallas_call(
        kernel,
        out_shape=shapes,
        in_specs=[pl.BlockSpec(memory_space=pltpu.SMEM)] * len(scalars)
        + [pl.BlockSpec(memory_space=pltpu.VMEM)] * len(arrays),
        out_specs=tuple(pl.BlockSpec(memory_space=pltpu.VMEM) for _ in outs),
        scratch_shapes=list(scratch),
        compiler_params=pltpu.CompilerParams(vmem_limit_bytes=VMEM_BYTES),
        cost_estimate=pl.CostEstimate(flops=flops, bytes_accessed=size, transcendentals=0),
        name=name,
    )(*scalars, *arrays)


def place_tiles(dst_ref, src_ref, count_ref, tiles_ref, adj_ref, first, last):
    adj_ref[...] = jnp.zeros_like(adj_ref)

    def step(slot, carry):
        block = src_ref[0, slot]

        @pl.when(jnp.logical_and(block >= first, block < last))
        def _():
            row = pl.multiple_of(dst_ref[0, slot] * BLK, BLK)
            col = pl.multiple_of((block - first) * BLK, BLK)
            adj_ref[pl.ds(row, BLK), pl.ds(col, BLK)] = tiles_ref[slot]

        return carry

    lax.fori_loop(0, count_ref[0], step, 0)


def boundary_places(rep, lists_ref, rows):
    parts, slots = lists_ref.shape
    lists = lists_ref[...].astype(F32)
    wanted = jnp.sum(
        jnp.where(iota((parts, slots), 1) == rep, lists, 0.0), axis=1, keepdims=True
    ).astype(jnp.int32)
    place = iota((parts, rows), 1)
    return jnp.concatenate(
        [(place == wanted).astype(BF16), (place == rep).astype(BF16)], 0
    )


def by_z(parts):
    shape = (2 * parts, 2 * parts)
    out, into = iota(shape, 0), iota(shape, 1)
    y, kind, z = out % Y_SIZE, out // Y_SIZE % 2, out // (2 * Y_SIZE)
    return into == kind * parts + z * Y_SIZE + y


def send_kernel(rep_ref, lists_ref, feats_ref, send_ref):
    parts = lists_ref.shape[0]
    places = boundary_places(rep_ref[0], lists_ref, feats_ref.shape[0])
    places = move(by_z(parts), places)
    send_ref[...] = move(places, feats_ref[...])


def plane_kernel(arrived_ref, send_ref):
    chunk = send_ref.shape[1]
    depth = chunk // 2
    total = arrived_ref.shape[0]
    shape = (total, total)
    out, into = iota(shape, 0), iota(shape, 1)
    z, kind, y = out % depth, out // depth % 2, out // chunk
    moved = move(into == z * (2 * Y_SIZE) + kind * Y_SIZE + y, arrived_ref[...])
    for y_to in range(Y_SIZE):
        for x_to in range(X_SIZE):
            send_ref[y_to * X_SIZE + x_to] = moved[y_to * chunk : (y_to + 1) * chunk]


def own_kernel(
    core_ref, dst_ref, src_ref, count_ref, tiles_ref, feats_ref, seeds_ref, w_self_ref, bias_ref,
    chosen_t_ref, preact_ref, part_ref, near_ref, near_t_ref, far_ref, far_t_ref,
    own_adj_ref, adj_ref,
):
    rows = feats_ref.shape[0]
    seeds = seeds_ref.shape[1]
    own_blocks = rows // BLK
    table = adj_ref.shape[1]
    place_tiles(dst_ref, src_ref, count_ref, tiles_ref, own_adj_ref, 0, own_blocks)
    place_tiles(
        dst_ref, src_ref, count_ref, tiles_ref, adj_ref, own_blocks, own_blocks + table // BLK
    )
    picks = (iota((rows, seeds), 0) == seeds_ref[...]).astype(BF16)
    feats = feats_ref[...]
    chosen_t_ref[...] = dot(feats, picks, 0, 0).astype(BF16)
    chosen = dot(picks, feats, 0, 0).astype(BF16)
    preact_ref[...] = dot(chosen, w_self_ref[...]) + bias_ref[...].astype(F32)
    part_ref[...] = dot(own_adj_ref[...], feats)
    adj = adj_ref[...]
    half = table // 2
    depth = half // PLANE // 2
    shape = (half, table)
    line, source = iota(shape, 0), iota(shape, 1)
    z, kind = line % depth, line // depth % 2
    x, y = line // (2 * depth) % X_SIZE, line // (2 * depth * X_SIZE)
    start = kind * half + (z * Y_SIZE + y) * SLOTS + x * CORES
    for core, to_ref, to_t_ref in (
        (core_ref[0], near_ref, near_t_ref),
        (1 - core_ref[0], far_ref, far_t_ref),
    ):
        order = (source == start + core).astype(BF16)
        to_ref[...] = dot(adj, order, 1, 1).astype(BF16)
        to_t_ref[...] = dot(order, adj, 1, 1).astype(BF16)


def middle_kernel(
    core_ref, near_ref, far_ref, near_adj_ref, near_adj_t_ref, far_adj_ref, far_adj_t_ref,
    chosen_t_ref, preact_ref, part_ref, w_neigh_ref, cot_ref,
    out_ref, d_pre_ref, d_agg_ref, keep_ref, send_ref,
):
    width = w_neigh_ref.shape[0]
    half = near_ref.shape[0]
    aggregate = (
        part_ref[...]
        + dot(near_adj_ref[...], near_ref[...])
        + dot(far_adj_ref[...], far_ref[...])
    ).astype(BF16)
    preact = preact_ref[...] + dot(aggregate, w_neigh_ref[...])
    gate = jax.nn.sigmoid(preact)
    out_ref[...] = (preact * gate).astype(BF16)
    d_pre = (cot_ref[...].astype(F32) * gate * (1.0 + preact * (1.0 - gate))).astype(BF16)
    d_pre_ref[...] = d_pre
    d_agg = dot(d_pre, w_neigh_ref[...], 1, 1).astype(BF16)
    d_agg_ref[...] = d_agg
    first = dot(chosen_t_ref[...], d_pre).astype(BF16)
    second = dot(aggregate, d_pre, 0, 0).astype(BF16)
    is_first = core_ref[0] == 0
    keep_ref[:width] = jnp.where(is_first, first, second)
    send_ref[:width] = jnp.where(is_first, second, first)
    keep_ref[width : width + half] = dot(near_adj_t_ref[...], d_agg).astype(BF16)
    send_ref[width : width + half] = dot(far_adj_t_ref[...], d_agg).astype(BF16)
    high, low = split(jnp.sum(d_pre.astype(F32), 0, keepdims=True))
    row = iota((keep_ref.shape[0] - width - half, width), 0)
    pair = jnp.where(
        row == 0, high.astype(F32), jnp.where(row == 1, low.astype(F32), 0.0)
    ).astype(BF16)
    keep_ref[width + half :] = pair
    send_ref[width + half :] = pair


def pair_sum_kernel(keep_ref, other_ref, send_ref):
    chunks, lines, width = send_ref.shape
    total = keep_ref[...].astype(F32) + other_ref[...].astype(F32)
    weight, table = width // chunks, (lines - 8 - width // chunks)
    tail = width + chunks * table
    high, low = split(total[tail : tail + 1] + total[tail + 1 : tail + 2])
    row = iota((8, width), 0)
    pair = jnp.where(row == 0, high.astype(F32), jnp.where(row == 1, low.astype(F32), 0.0))
    for chunk in range(chunks):
        send_ref[chunk] = jnp.concatenate(
            [
                total[chunk * weight : (chunk + 1) * weight],
                total[width + chunk * table : width + (chunk + 1) * table],
                pair,
            ],
            0,
        ).astype(BF16)


def plane_sum_kernel(arrived_ref, send_ref):
    chunks, lines, width = arrived_ref.shape
    depth = send_ref.shape[0]
    block = send_ref.shape[1]
    weight = width // chunks
    table = lines - 8 - weight
    groups = width // LANES
    each = weight // depth
    by_y = []
    rest = None
    for y in range(Y_SIZE):
        some = arrived_ref[y * X_SIZE].astype(F32)
        for x in range(1, X_SIZE):
            some = some + arrived_ref[y * X_SIZE + x].astype(F32)
        by_y.append(some[weight : weight + table].astype(BF16))
        rest = some if rest is None else rest + some
    back = jnp.concatenate(by_y, 0)
    shape = (depth * block, Y_SIZE * table)
    out, into = iota(shape, 0), iota(shape, 1)
    y, kind, z = out % Y_SIZE, out // Y_SIZE % 2, out // block
    moved = move(into == y * table + kind * depth + z, back)
    send_ref[:, :, :width] = moved.reshape(depth, block, width)

    weights = rest[:weight].astype(BF16)
    high, low = split(rest[weight + table : weight + table + 1] + rest[weight + table + 1 : weight + table + 2])
    pair_row = iota((16, width), 0)
    pair = jnp.where(
        pair_row == 0, high.astype(F32), jnp.where(pair_row == 1, low.astype(F32), 0.0)
    ).astype(BF16)
    shape = (depth * block, weight)
    out, into = iota(shape, 0), iota(shape, 1)
    line, z = out % block, out // block
    pair_shape = (depth * block, 16)
    pair_line, pair_into = iota(pair_shape, 0) % block, iota(pair_shape, 1)
    weight_block = jnp.zeros((depth * block, LANES), F32)
    bias_block = jnp.zeros((depth * block, LANES), F32)
    for group in range(groups):
        lanes = slice(group * LANES, (group + 1) * LANES)
        here = jnp.logical_and(line // each == group, into == z * each + line % each)
        weight_block += dot(here.astype(BF16), weights[:, lanes])
        here = jnp.logical_and(pair_line // 2 == group, pair_into == pair_line % 2)
        bias_block += dot(here.astype(BF16), pair[:, lanes])
    send_ref[:, :, width : width + LANES] = weight_block.astype(BF16).reshape(depth, block, LANES)
    send_ref[:, :, width + LANES :] = bias_block.astype(BF16).reshape(depth, block, LANES)


def weight_kernel(scale, arrived_ref, send_ref, bias_ref):
    depth, block, _ = arrived_ref.shape
    width = arrived_ref.shape[2] - 2 * LANES
    total = jnp.sum(arrived_ref[:, :, width:].astype(F32), 0) * scale
    done = total[:, :LANES].astype(BF16)
    for z in range(depth):
        send_ref[z] = done
    bias_ref[...] = total[:, LANES:]


def gather_kernel(arrived_ref, send_ref):
    chunks, weight, width = send_ref.shape
    depth, block, _ = arrived_ref.shape
    groups = width // LANES
    each = weight // depth
    arrived = arrived_ref[...].reshape(depth * block, LANES)
    shape = (weight, depth * block)
    out, into = iota(shape, 0), iota(shape, 1)
    z, line = out // each, out % each
    parts = [
        move(into == z * block + group * each + line, arrived) for group in range(groups)
    ]
    whole = jnp.concatenate(parts, 1)
    for chunk in range(chunks):
        send_ref[chunk] = whole


def own_back_kernel(
    dst_ref, src_ref, count_ref, tiles_ref, seeds_ref, d_pre_ref, d_agg_ref, w_self_ref,
    own_ref, adj_ref,
):
    rows = own_ref.shape[0]
    seeds = seeds_ref.shape[1]
    place_tiles(dst_ref, src_ref, count_ref, tiles_ref, adj_ref, 0, rows // BLK)
    picks = (iota((rows, seeds), 0) == seeds_ref[...]).astype(BF16)
    seeded = dot(picks, d_pre_ref[...]).astype(BF16)
    own_ref[...] = dot(seeded, w_self_ref[...], 1, 1) + dot(adj_ref[...], d_agg_ref[...], 0, 0)


def scatter_kernel(rep_ref, core_ref, lists_ref, arrived_ref, own_ref, keep_ref, send_ref):
    parts = lists_ref.shape[0]
    rows, width = own_ref.shape
    places = move(by_z(parts), boundary_places(rep_ref[0], lists_ref, rows))
    back = arrived_ref[:, :, :width].reshape(2 * parts, width)
    total = (own_ref[...] + dot(places, back, 0, 0)).astype(BF16)
    share = rows // (X_SIZE * CORES)
    first = core_ref[0] == 0
    for x in range(X_SIZE):
        low = total[2 * x * share : (2 * x + 1) * share]
        high = total[(2 * x + 1) * share : (2 * x + 2) * share]
        keep_ref[x] = jnp.where(first, low, high)
        send_ref[x] = jnp.where(first, high, low)


def body(
    feats,
    halo_index,
    seed_ids,
    tiles,
    tile_dst,
    tile_src,
    tile_count,
    w_self,
    w_neigh,
    bias,
    cotangent,
):
    depth = lax.axis_size("z")
    parts = depth * Y_SIZE
    reps = X_SIZE * CORES
    rows, width = feats.shape
    seeds = cotangent.shape[0]
    half = parts * SLOTS
    core_id = lax.axis_index("core").astype(jnp.int32)
    x_id = lax.axis_index("x").astype(jnp.int32)
    core = core_id.reshape(1)
    rep = (x_id * CORES + core_id).reshape(1)
    lists = halo_index[0]
    seed_row = seed_ids.reshape(1, seeds)
    tile_scalars = (tile_dst, tile_src, tile_count)
    scale = float(seeds * parts * reps) ** (-0.5)

    def swap(values, axis):
        return lax.all_to_all(values, axis, split_axis=0, concat_axis=0, tiled=True)

    def pair(values):
        return lax.ppermute(values, "core", [(0, 1), (1, 0)])

    (send,) = call(
        send_kernel, "pick_boundary", [((2 * parts, width), BF16)], [rep], [lists, feats],
        flops=4 * parts * rows * width,
    )
    by_depth = swap(send.reshape(depth, 2 * Y_SIZE, width), "z").reshape(2 * parts, width)
    (plane,) = call(
        plane_kernel, "spread_plane", [((PLANE, 2 * depth, width), BF16)], [], [by_depth],
        flops=8 * parts * parts * width,
    )
    near = swap(plane, ("y", "x")).reshape(half, width)
    far = pair(near)

    chosen_t, preact, part, near_adj, near_adj_t, far_adj, far_adj_t = call(
        own_kernel, "own_rows",
        [
            ((width, seeds), BF16),
            ((seeds, width), F32),
            ((seeds, width), F32),
            ((seeds, half), BF16),
            ((half, seeds), BF16),
            ((seeds, half), BF16),
            ((half, seeds), BF16),
        ],
        [core, *tile_scalars],
        [tiles, feats, seed_row, w_self, bias.reshape(1, width)],
        scratch=[pltpu.VMEM((seeds, rows), BF16), pltpu.VMEM((seeds, 2 * half), BF16)],
        flops=2 * seeds * (3 * rows * width + width * width + 8 * half * half),
    )

    out, d_pre, d_agg, keep, pair_send = call(
        middle_kernel, "forward_backward",
        [
            ((seeds, width), BF16),
            ((seeds, width), BF16),
            ((seeds, width), BF16),
            ((width + half + 16, width), BF16),
            ((width + half + 16, width), BF16),
        ],
        [core],
        [
            near, far, near_adj, near_adj_t, far_adj, far_adj_t,
            chosen_t, preact, part, w_neigh, cotangent,
        ],
        flops=2 * seeds * width * (4 * half + 4 * width),
    )

    pair_arrived = pair(pair_send)
    (plane_send,) = call(
        pair_sum_kernel, "sum_pair",
        [((PLANE, width // PLANE + 2 * depth + 8, width), BF16)],
        [], [keep, pair_arrived],
    )
    plane_arrived = swap(plane_send, ("y", "x"))
    (depth_send,) = call(
        plane_sum_kernel, "sum_plane",
        [((depth, 2 * Y_SIZE, width + 2 * LANES), BF16)],
        [], [plane_arrived],
    )
    depth_arrived = swap(depth_send, "z")
    weight_send, bias_rows = call(
        functools.partial(weight_kernel, scale), "sum_weights",
        [((depth, 2 * Y_SIZE, LANES), BF16), ((2 * Y_SIZE, LANES), F32)],
        [], [depth_arrived],
    )
    weight_depth = swap(weight_send, "z")
    (weight_plane,) = call(
        gather_kernel, "gather_weights",
        [((PLANE, width // PLANE, width), BF16)],
        [], [weight_depth],
    )
    weight_near = swap(weight_plane, ("y", "x")).reshape(width, width)
    weight_far = pair(weight_near)
    grad_self = jnp.where(core_id == 0, weight_near, weight_far)
    grad_neigh = jnp.where(core_id == 0, weight_far, weight_near)
    groups = width // LANES
    grad_bias = bias_rows[: 2 * groups].reshape(groups, 2, LANES).sum(1).reshape(width)

    (own,) = call(
        own_back_kernel, "own_rows_back", [((rows, width), F32)],
        [*tile_scalars], [tiles, seed_row, d_pre, d_agg, w_self],
        scratch=[pltpu.VMEM((seeds, rows), BF16)],
        flops=2 * seeds * width * 3 * rows,
    )
    share = rows // reps
    row_keep, row_send = call(
        scatter_kernel, "return_rows",
        [((X_SIZE, share, width), BF16), ((X_SIZE, share, width), BF16)],
        [rep, core], [lists, depth_arrived, own],
        flops=4 * parts * rows * width,
    )
    row_pair = row_keep.astype(F32) + pair(row_send).astype(F32)
    rows_out = row_pair.astype(BF16)
    input_grad = lax.dynamic_index_in_dim(row_pair, x_id, 0, keepdims=False)
    for shift in range(1, X_SIZE):
        chunk = lax.dynamic_index_in_dim(rows_out, (x_id + shift) % X_SIZE, 0, keepdims=False)
        chunk = lax.ppermute(chunk, "x", [(x, (x + shift) % X_SIZE) for x in range(X_SIZE)])
        input_grad = input_grad + chunk.astype(F32)
    return (out, input_grad, grad_self, grad_neigh, grad_bias)


def solution(mesh):
    parts = mesh.shape["dom"]
    physical = Mesh(
        mesh.devices.reshape(parts // Y_SIZE, Y_SIZE, X_SIZE, CORES), ("z", "y", "x", "core")
    )
    dom = ("z", "y")
    every = ("z", "y", "x", "core")
    placed = (
        P(dom, None),
        P(dom, None, None),
        P(every),
        P(every, None, None),
        P(every, None),
        P(every, None),
        P(every),
        P(),
        P(),
        P(),
        P(every, None),
    )
    return jax.shard_map(
        body,
        mesh=physical,
        in_specs=placed,
        out_specs=(P(every, None), P(every, None), P(), P(), P()),
        check_vma=False,
    )
```

time: 749 us -> 158 us (0.21)
  waiting for transfers between devices: 395 us -> 7.48 us
  blocking collectives: 230 us -> 101 us
  matrix products: 28.1 us -> 0 us
  local copies, waits for them, and re-layouts: 28 us -> 2 us
  between operations: 16.5 us -> 1.64 us
  Pallas kernels: 0 us -> 12.3 us
  other arithmetic: 14.7 us -> 2.52 us
    psum x1 -> x0, waiting for transfers between devices: 359 us -> none  [body(): summed = lax.psum((part_self, part_neigh, part_bias), ('dom', 'rep'))]
    psum x1 -> x0, blocking collectives: 131 us -> none  [body(): summed = lax.psum((part_self, part_neigh, part_bias), ('dom', 'rep'))]
    all_to_all x0 -> x5, blocking collectives: none -> 101 us  [swap(): return lax.all_to_all(values, axis, split_axis=0, concat_axis=0, tiled=True)]
    all_gather x1 -> x0, blocking collectives: 99 us -> none  [body(): hub_table = lax.all_gather(feats[:HUB_DEV][None], 'dom', axis=0, tiled=True)]
    all_to_all x3 -> x1, waiting for transfers between devices: 35.9 us -> 1.95 us  [swap(): return lax.all_to_all(values, axis, split_axis=0, concat_axis=0, tiled=True)]
    all_to_all x3 -> x1, starting transfers between devices: 35.4 us -> 3.57 us  [swap(): return lax.all_to_all(values, axis, split_axis=0, concat_axis=0, tiled=True)]
    dot_general x10 -> x0, matrix products: 28.1 us -> none  [the longest x1 7.78 us: body(): d_source = jnp.einsum('st,tjh->sjh', src_onehot, back, precision=highest)]
    ppermute x0 -> x7, starting transfers between devices: none -> 27.1 us  [the longest x4 18.6 us: pair(): return lax.ppermute(values, 'core', [(0, 1), (1, 0)])]
  transfers between devices with their start and end apart: 5 -> 8, of which waited for: 3 -> 4; matrix products, arithmetic and copies ran while one was open for 3% -> 1% of each run, Pallas kernels for 0% -> 5%
where the time goes in v2:
time: 158 us; the launch traced here: 157 us
  blocking collectives  101 us (64%)
  starting transfers between devices  30.6 us (19%)
  Pallas kernels  12.3 us (8%)
  waiting for transfers between devices  7.48 us (5%)
  other arithmetic  2.52 us (2%)
  local copies, waits for them, and re-layouts  2 us (1%)
  between operations  1.64 us (1%)
    all_to_all x5, blocking collectives, swap(): return lax.all_to_all(values, axis, split_axis=0, concat_axis=0, tiled=True)  101 us
    ppermute x4, starting transfers between devices, pair(): return lax.ppermute(values, 'core', [(0, 1), (1, 0)])  18.6 us
    pallas_call x10, Pallas kernels, call(): pl.pallas_call(kernel, out_shape=shapes, in_specs=[pl.BlockSpec(memory_sp...  12.3 us
    ppermute x3, starting transfers between devices, body(): lax.ppermute(chunk, 'x', [(x, (x + shift) % X_SIZE) for x in range(X_SIZE)])  8.42 us
    all_to_all x1, starting transfers between devices, swap(): return lax.all_to_all(values, axis, split_axis=0, concat_axis=0, tiled=True)  3.57 us
  transfers between devices with their start and end apart: 8, of which 4 were waited for; matrix products, arithmetic and copies ran while one was open for 1% of the time, Pallas kernels for 5%

profile of v2, /device:TPU:1, one launch (start us, length us, event | category | flops | bytes accessed | tf_op | source)
XLA Modules:
  0.0 157.3 jit_solution(15175572269536467074)
XLA Ops:
  0.6 0.8 copy.16
  1.4 1.1 copy-done
  2.5 0.5 pick_boundary.1
  3.0 0.0 copy-start.9
  3.0 0.0 copy-start.1
  3.0 0.0 copy-start.4
  3.0 0.0 copy-start.5
  3.0 0.0 copy-start.6
  3.1 0.0 copy-start.7
  3.1 0.0 copy-start.8
  3.1 27.7 %all_to_all.30 = bf16[16,8,512]{2,1,0:T(8,128)(2,1)S(1)} all-to-all(bf16[16,8,512]{2,1,0:T(8,128)(2,1)S(1)} %bitcast.25), channel_id=1, replica_groups=mesh['z'=16,'y'=4,'x'=4,'core'=2] {'z'}, dimensions={0} | all-to-all | bytes 262144 | tf_op jit(solution)/shard_map/all_to_all | solution.py:333
  30.8 0.2 spread_plane.1
  30.9 15.8 %all_to_all.31 = bf16[16,32,512]{2,1,0:T(8,128)(2,1)S(1)} all-to-all(bf16[16,32,512]{2,1,0:T(8,128)(2,1)S(1)} %spread_plane.1), channel_id=1, replica_groups=mesh['z'=16,'y'=4,'x'=4,'core'=2] {'y','x'}, dimensions={0} | all-to-all | bytes 1048576 | tf_op jit(solution)/shard_map/all_to_all | solution.py:333
  46.7 6.8 %collective-permute-start = (bf16[512,512]{1,0:T(8,128)(2,1)S(1)}, bf16[512,512]{1,0:T(8,128)(2,1)S(1)}, u32[]{:S(2)}, u32[]{:S(2)}) collective-permute-start(bf16[512,512]{1,0:T(8,128)(2,1)S(1)} %bitcast.26), channel_id=1, source_target_pairs={{0,1},{1,0},{2,3},{3,2},{4,5},{5,4},{6,7},{7,6},{8,9},{9,8},{10,11... | collective-permute-start | bytes 1572872 | tf_op jit(solution)/shard_map/ppermute | solution.py:336
  54.1 0.0 copy-done.9
  54.1 0.0 copy-done.1
  54.2 0.0 copy-done.4
  54.2 0.0 copy-start.2
  54.2 0.0 copy-start.3
  54.2 4.7 %own_rows.1 = (bf16[512,512]{1,0:T(8,128)(2,1)S(1)}, f32[512,512]{1,0:T(8,128)S(1)}, f32[512,512]{1,0:T(8,128)S(1)}, bf16[512,512]{1,0:T(8,128)(2,1)S(1)}, bf16[...) custom-call(s32[1]{0:T(128)} %bitcast.core_ref, s32[1,14]{1,0:T(1,128)S(1)} %copy-done.7, ...), custom_call_target="tpu_custom_call" | custom-call | flops 3623878656 | bytes 6491136 | tf_op jit(solution)/shard_map/own_rows/pallas_call | solution.py:45
  58.9 0.0 collective-permute-done.far_ref
  59.0 2.7 %forward_backward.1 = (bf16[512,512]{1,0:T(8,128)(2,1)}, bf16[512,512]{1,0:T(8,128)(2,1)S(1)}, bf16[512,512]{1,0:T(8,128)(2,1)S(1)}, bf16[1040,512]{1,0:T(8,128)(2,1)S(1)}, bf16[1040,512]{1,0:T(8,128)(2,1)S(1)}) custom-call(s32[1]{0:T(128)} %bitcast.core_ref, bf16[512,512]{1,0:T(8,128)(2,1)S(1)} %bitcast.27, ...), custom_call_target="tpu_custom_call" | custom-call | flops 2147483648 | bytes 10518528 | tf_op jit(solution)/shard_map/forward_backward/pallas_call | solution.py:45
  61.7 2.0 %collective-permute-start.1 = (bf16[1040,512]{1,0:T(8,128)(2,1)S(1)}, bf16[1040,512]{1,0:T(8,128)(2,1)S(1)}, u32[]{:S(2)}, u32[]{:S(2)}) collective-permute-start(bf16[1040,512]{1,0:T(8,128)(2,1)S(1)} %get-tuple-element.30), channel_id=1, source_target_pairs={{0,1},{1,0},{2,3},{3,2},{4,5},{5,4},{6,7},{7,6},{8,9},{9,8},{10,11... | collective-permute-start | bytes 3194888 | tf_op jit(solution)/shard_map/ppermute | solution.py:336
  63.7 2.6 %collective-permute-done.1.other_ref = bf16[1040,512]{1,0:T(8,128)(2,1)S(1)} collective-permute-done((bf16[1040,512]{1,0:T(8,128)(2,1)S(1)}, bf16[1040,512]{1,0:T(8,128)(2,1)S(1)}, u32[]{:S(2)}, u32[]{:S(2)}) %collective-permute-start.1) | collective-permute-done | bytes 1064992 | tf_op jit(solution)/shard_map/ppermute | solution.py:336
  66.3 0.2 sum_pair.1
  66.5 21.0 %all_to_all.32.arrived_ref = bf16[16,72,512]{2,1,0:T(8,128)(2,1)S(1)} all-to-all(bf16[16,72,512]{2,1,0:T(8,128)(2,1)S(1)} %sum_pair.1), channel_id=1, replica_groups=mesh['z'=16,'y'=4,'x'=4,'core'=2] {'y','x'}, dimensions={0} | all-to-all | bytes 2359296 | tf_op jit(solution)/shard_map/all_to_all | solution.py:333
  87.5 0.4 sum_plane.1
  87.9 16.5 %all_to_all.33.arrived_ref = bf16[16,8,768]{2,1,0:T(8,128)(2,1)S(1)} all-to-all(bf16[16,8,768]{2,1,0:T(8,128)(2,1)S(1)} %sum_plane.1), channel_id=1, replica_groups=mesh['z'=16,'y'=4,'x'=4,'core'=2] {'z'}, dimensions={0} | all-to-all | bytes 393216 | tf_op jit(solution)/shard_map/all_to_all | solution.py:333
  104.4 19.8 %all_to_all.34.arrived_ref = bf16[16,8,128]{2,1,0:T(8,128)(2,1)S(1)} all-to-all(bf16[16,8,128]{2,1,0:T(8,128)(2,1)S(1)} %get-tuple-element.35), channel_id=1, replica_groups=mesh['z'=16,'y'=4,'x'=4,'core'=2] {'z'}, dimensions={0} | all-to-all | bytes 65536 | tf_op jit(solution)/shard_map/all_to_all | solution.py:333
  124.2 1.0 gather_weights.1
  125.2 3.6 %all-to-all-start.5 = ((bf16[16,32,512]{2,1,0:T(8,128)(2,1)}), bf16[16,32,512]{2,1,0:T(8,128)(2,1)S(1)}, u32[]{:S(2)}, u32[]{:S(2)}) async-start(bf16[16,32,512]{2,1,0:T(8,128)(2,1)} %gather_weights.1), calls=%async_computation.5 | async-start | bytes 1048576 | tf_op jit(solution)/shard_map/all_to_all | solution.py:333
  128.8 2.0 %own_rows_back.1.own_ref = f32[768,512]{1,0:T(8,128)S(1)} custom-call(s32[1,14]{1,0:T(1,128)S(1)} %copy-done.7, s32[1,14]{1,0:T(1,128)S(1)} %copy-done.8, s32[1]{0:T(128)S(6)} %copy.17.count_ref, bf16[14,128,128]{2,1,0:T(8,128)(2,1)S(1)} %copy-done.5, s32[1,512]{1,0:T(1,128)S(1)} %bitcast.32, bf16[512,512]{1,0:T(8,128)(2,1)S(1)} %get-tuple-element.31.d_pre_ref, ...), custom_call_target="tpu_custom_call" | custom-call | flops 1207959552 | bytes 3606528 | tf_op jit(solution)/shard_map/own_rows_back/pallas_call | solution.py:45
  130.8 0.6 return_rows.1
  131.4 4.5 %collective-permute-start.2 = (bf16[4,96,512]{2,1,0:T(8,128)(2,1)S(1)}, bf16[4,96,512]{2,1,0:T(8,128)(2,1)S(1)}, u32[]{:S(2)}, u32[]{:S(2)}) collective-permute-start(bf16[4,96,512]{2,1,0:T(8,128)(2,1)S(1)} %get-tuple-element.34), channel_id=1, source_target_pairs={{0,1},{1,0},{2,3},{3,2},{4,5},{5,4},{6,7},{7,6},{8,9},{9,8},{10,11... | collective-permute-start | bytes 1179656 | tf_op jit(solution)/shard_map/ppermute | solution.py:336
  136.0 1.9 %all-to-all-done.5 = bf16[16,32,512]{2,1,0:T(8,128)(2,1)S(1)} async-done(((bf16[16,32,512]{2,1,0:T(8,128)(2,1)}), bf16[16,32,512]{2,1,0:T(8,128)(2,1)S(1)}, u32[]{:S(2)}, u32[]{:S(2)}) %all-to-all-start.5) | async-done | bytes 524320 | tf_op jit(solution)/shard_map/all_to_all | solution.py:333
  138.0 5.4 %collective-permute-start.6 = (bf16[512,512]{1,0:T(8,128)(2,1)S(1)}, bf16[512,512]{1,0:T(8,128)(2,1)S(1)}, u32[]{:S(2)}, u32[]{:S(2)}) collective-permute-start(bf16[512,512]{1,0:T(8,128)(2,1)S(1)} %bitcast.33), channel_id=1, source_target_pairs={{0,1},{1,0},{2,3},{3,2},{4,5},{5,4},{6,7},{7,6},{8,9},{9,8},{10,11... | collective-permute-start | bytes 1572872 | tf_op jit(solution)/shard_map/ppermute | solution.py:336
  143.3 0.0 collective-permute-done.2
  143.3 0.1 convert_add_fusion
  143.5 2.2 %collective-permute-start.3 = (bf16[96,512]{1,0:T(8,128)(2,1)S(1)}, bf16[96,512]{1,0:T(8,128)(2,1)S(1)}, u32[]{:S(2)}, u32[]{:S(2)}) collective-permute-start(bf16[96,512]{1,0:T(8,128)(2,1)S(1)} %get-tuple-element.41), channel_id=1, source_target_pairs={{0,2},{2,4},{4,6},{6,0},{1,3},{3,5},{5,7},{7,1},{8,10},{10,12},{12... | collective-permute-start | bytes 294920 | tf_op jit(solution)/shard_map/ppermute | solution.py:433
  145.7 3.1 %collective-permute-start.4 = (bf16[96,512]{1,0:T(8,128)(2,1)S(1)}, bf16[96,512]{1,0:T(8,128)(2,1)S(1)}, u32[]{:S(2)}, u32[]{:S(2)}) collective-permute-start(bf16[96,512]{1,0:T(8,128)(2,1)S(1)} %get-tuple-element.43), channel_id=1, source_target_pairs={{0,4},{2,6},{4,0},{6,2},{1,5},{3,7},{5,1},{7,3},{8,12},{10,14},{12... | collective-permute-start | bytes 294920 | tf_op jit(solution)/shard_map/ppermute | solution.py:433
  148.9 3.1 %collective-permute-start.5 = (bf16[96,512]{1,0:T(8,128)(2,1)S(1)}, bf16[96,512]{1,0:T(8,128)(2,1)S(1)}, u32[]{:S(2)}, u32[]{:S(2)}) collective-permute-start(bf16[96,512]{1,0:T(8,128)(2,1)S(1)} %get-tuple-element.42), channel_id=1, source_target_pairs={{0,6},{2,0},{4,2},{6,4},{1,7},{3,1},{5,3},{7,5},{8,14},{10,8},{12,... | collective-permute-start | bytes 294920 | tf_op jit(solution)/shard_map/ppermute | solution.py:433
  152.0 0.6 reduce_sum.9
  152.6 0.0 collective-permute-done.3
  152.6 0.7 collective-permute-done.4
  153.2 2.3 %collective-permute-done.5 = bf16[96,512]{1,0:T(8,128)(2,1)S(1)} collective-permute-done((bf16[96,512]{1,0:T(8,128)(2,1)S(1)}, bf16[96,512]{1,0:T(8,128)(2,1)S(1)}, u32[]{:S(2)}, u32[]{:S(2)}) %collective-permute-start.5) | collective-permute-done | bytes 98336 | tf_op jit(solution)/shard_map/ppermute | solution.py:433
  155.5 0.7 fusion.1
  156.2 0.0 collective-permute-done.6
  156.2 1.1 broadcast_select_fusion
  (10 shorter events, 0.1 us)
Async XLA Ops:
  1.4 1.1 copy-start
  3.0 51.1 %copy-start.9 = (bf16[512]{0:T(512)(128)(2,1)S(1)}, bf16[512]{0:T(512)(128)(2,1)}, u32[]{:S(2)}) copy-start(bf16[512]{0:T(512)(128)(2,1)} %param.20) | copy-start | bytes 3076
  3.0 51.1 %copy-start.1 = (bf16[768,512]{1,0:T(8,128)(2,1)S(1)}, bf16[768,512]{1,0:T(8,128)(2,1)}, u32[]{:S(2)}) copy-start(bf16[768,512]{1,0:T(8,128)(2,1)} %feats_ref.3) | copy-start | bytes 2359300
  3.0 51.1 %copy-start.4 = (bf16[512,512]{1,0:T(8,128)(2,1)S(1)}, bf16[512,512]{1,0:T(8,128)(2,1)}, u32[]{:S(2)}) copy-start(bf16[512,512]{1,0:T(8,128)(2,1)} %w_self_ref.3) | copy-start | bytes 1572868
  3.0 51.1 %copy-start.5 = (bf16[14,128,128]{2,1,0:T(8,128)(2,1)S(1)}, bf16[14,128,128]{2,1,0:T(8,128)(2,1)}, u32[]{:S(2)}) copy-start(bf16[14,128,128]{2,1,0:T(8,128)(2,1)} %tiles_ref.3) | copy-start | bytes 1376260
  3.0 51.1 %copy-start.6 = (s32[512]{0:T(512)S(1)}, s32[512]{0:T(512)}, u32[]{:S(2)}) copy-start(s32[512]{0:T(512)} %param.13) | copy-start | bytes 6148
  3.1 51.1 %copy-start.7 = (s32[1,14]{1,0:T(1,128)S(1)}, s32[1,14]{1,0:T(1,128)}, u32[]{:S(2)}) copy-start(s32[1,14]{1,0:T(1,128)} %dst_ref.3) | copy-start | bytes 172
  3.1 51.1 %copy-start.8 = (s32[1,14]{1,0:T(1,128)S(1)}, s32[1,14]{1,0:T(1,128)}, u32[]{:S(2)}) copy-start(s32[1,14]{1,0:T(1,128)} %src_ref.3) | copy-start | bytes 172
  46.7 12.3 %collective-permute-start = (bf16[512,512]{1,0:T(8,128)(2,1)S(1)}, bf16[512,512]{1,0:T(8,128)(2,1)S(1)}, u32[]{:S(2)}, u32[]{:S(2)}) collective-permute-start(bf16[512,512]{1,0:T(8,128)(2,1)S(1)} %bitcast.26), channel_id=1, source_target_pairs={{0,1},{1,0},{2,3},{3,2},{4,5},{5,4},{6,7},{7,6},{8,9},{9,8},{10,11... | collective-permute-start | bytes 1572872 | tf_op jit(solution)/shard_map/ppermute | solution.py:336
  54.2 4.8 %copy-start.2 = (bf16[512,512]{1,0:T(8,128)(2,1)S(1)}, bf16[512,512]{1,0:T(8,128)(2,1)}, u32[]{:S(2)}) copy-start(bf16[512,512]{1,0:T(8,128)(2,1)} %w_neigh_ref.1) | copy-start | bytes 1572868
  54.2 4.8 %copy-start.3 = (bf16[512,512]{1,0:T(8,128)(2,1)S(1)}, bf16[512,512]{1,0:T(8,128)(2,1)}, u32[]{:S(2)}) copy-start(bf16[512,512]{1,0:T(8,128)(2,1)} %cot_ref.1) | copy-start | bytes 1572868
  61.7 4.6 %collective-permute-start.1 = (bf16[1040,512]{1,0:T(8,128)(2,1)S(1)}, bf16[1040,512]{1,0:T(8,128)(2,1)S(1)}, u32[]{:S(2)}, u32[]{:S(2)}) collective-permute-start(bf16[1040,512]{1,0:T(8,128)(2,1)S(1)} %get-tuple-element.30), channel_id=1, source_target_pairs={{0,1},{1,0},{2,3},{3,2},{4,5},{5,4},{6,7},{7,6},{8,9},{9,8},{10,11... | collective-permute-start | bytes 3194888 | tf_op jit(solution)/shard_map/ppermute | solution.py:336
  125.2 12.8 %all-to-all-start.5 = ((bf16[16,32,512]{2,1,0:T(8,128)(2,1)}), bf16[16,32,512]{2,1,0:T(8,128)(2,1)S(1)}, u32[]{:S(2)}, u32[]{:S(2)}) async-start(bf16[16,32,512]{2,1,0:T(8,128)(2,1)} %gather_weights.1), calls=%async_computation.5 | async-start | bytes 1048576 | tf_op jit(solution)/shard_map/all_to_all | solution.py:333
  131.4 11.9 %collective-permute-start.2 = (bf16[4,96,512]{2,1,0:T(8,128)(2,1)S(1)}, bf16[4,96,512]{2,1,0:T(8,128)(2,1)S(1)}, u32[]{:S(2)}, u32[]{:S(2)}) collective-permute-start(bf16[4,96,512]{2,1,0:T(8,128)(2,1)S(1)} %get-tuple-element.34), channel_id=1, source_target_pairs={{0,1},{1,0},{2,3},{3,2},{4,5},{5,4},{6,7},{7,6},{8,9},{9,8},{10,11... | collective-permute-start | bytes 1179656 | tf_op jit(solution)/shard_map/ppermute | solution.py:336
  138.0 18.3 %collective-permute-start.6 = (bf16[512,512]{1,0:T(8,128)(2,1)S(1)}, bf16[512,512]{1,0:T(8,128)(2,1)S(1)}, u32[]{:S(2)}, u32[]{:S(2)}) collective-permute-start(bf16[512,512]{1,0:T(8,128)(2,1)S(1)} %bitcast.33), channel_id=1, source_target_pairs={{0,1},{1,0},{2,3},{3,2},{4,5},{5,4},{6,7},{7,6},{8,9},{9,8},{10,11... | collective-permute-start | bytes 1572872 | tf_op jit(solution)/shard_map/ppermute | solution.py:336
  143.5 9.0 %collective-permute-start.3 = (bf16[96,512]{1,0:T(8,128)(2,1)S(1)}, bf16[96,512]{1,0:T(8,128)(2,1)S(1)}, u32[]{:S(2)}, u32[]{:S(2)}) collective-permute-start(bf16[96,512]{1,0:T(8,128)(2,1)S(1)} %get-tuple-element.41), channel_id=1, source_target_pairs={{0,2},{2,4},{4,6},{6,0},{1,3},{3,5},{5,7},{7,1},{8,10},{10,12},{12... | collective-permute-start | bytes 294920 | tf_op jit(solution)/shard_map/ppermute | solution.py:433
  145.7 7.5 %collective-permute-start.4 = (bf16[96,512]{1,0:T(8,128)(2,1)S(1)}, bf16[96,512]{1,0:T(8,128)(2,1)S(1)}, u32[]{:S(2)}, u32[]{:S(2)}) collective-permute-start(bf16[96,512]{1,0:T(8,128)(2,1)S(1)} %get-tuple-element.43), channel_id=1, source_target_pairs={{0,4},{2,6},{4,0},{6,2},{1,5},{3,7},{5,1},{7,3},{8,12},{10,14},{12... | collective-permute-start | bytes 294920 | tf_op jit(solution)/shard_map/ppermute | solution.py:433
  148.9 6.6 %collective-permute-start.5 = (bf16[96,512]{1,0:T(8,128)(2,1)S(1)}, bf16[96,512]{1,0:T(8,128)(2,1)S(1)}, u32[]{:S(2)}, u32[]{:S(2)}) collective-permute-start(bf16[96,512]{1,0:T(8,128)(2,1)S(1)} %get-tuple-element.42), channel_id=1, source_target_pairs={{0,6},{2,0},{4,2},{6,4},{1,7},{3,1},{5,3},{7,5},{8,14},{10,8},{12,... | collective-permute-start | bytes 294920 | tf_op jit(solution)/shard_map/ppermute | solution.py:433

commit v3 on v2

--- a/solution.py
+++ b/solution.py
@@ -39,20 +39,24 @@
     return high, (wide - high.astype(F32)).astype(BF16)
 
 
-def call(kernel, name, outs, scalars, arrays, scratch=(), flops=0):
+def call(kernel, name, outs, scalars, arrays, scratch=(), flops=0, after=(), space=pltpu.VMEM):
+    if after:
+        inner, at = kernel, len(scalars) + len(arrays)
+        kernel = lambda *refs: inner(*refs[:at], *refs[at + len(after) :])
     shapes = tuple(jax.ShapeDtypeStruct(shape, dtype) for shape, dtype in outs)
     size = sum(a.size * a.dtype.itemsize for a in (*arrays, *shapes))
     return pl.pallas_call(
         kernel,
         out_shape=shapes,
         in_specs=[pl.BlockSpec(memory_space=pltpu.SMEM)] * len(scalars)
-        + [pl.BlockSpec(memory_space=pltpu.VMEM)] * len(arrays),
+        + [pl.BlockSpec(memory_space=space)] * len(arrays)
+        + [pl.BlockSpec(memory_space=pl.ANY)] * len(after),
         out_specs=tuple(pl.BlockSpec(memory_space=pltpu.VMEM) for _ in outs),
         scratch_shapes=list(scratch),
         compiler_params=pltpu.CompilerParams(vmem_limit_bytes=VMEM_BYTES),
         cost_estimate=pl.CostEstimate(flops=flops, bytes_accessed=size, transcendentals=0),
         name=name,
-    )(*scalars, *arrays)
+    )(*scalars, *arrays, *after)
 
 
 def place_tiles(dst_ref, src_ref, count_ref, tiles_ref, adj_ref, first, last):
@@ -73,15 +77,14 @@
 
 
 def boundary_places(rep, lists_ref, rows):
-    parts, slots = lists_ref.shape
+    slots, parts = lists_ref.shape
     lists = lists_ref[...].astype(F32)
     wanted = jnp.sum(
-        jnp.where(iota((parts, slots), 1) == rep, lists, 0.0), axis=1, keepdims=True
+        jnp.where(iota((slots, parts), 0) == rep, lists, 0.0), axis=0, keepdims=True
     ).astype(jnp.int32)
-    place = iota((parts, rows), 1)
-    return jnp.concatenate(
-        [(place == wanted).astype(BF16), (place == rep).astype(BF16)], 0
-    )
+    place = iota((rows, parts), 0)
+    places = jnp.concatenate([(place == wanted).astype(BF16), (place == rep).astype(BF16)], 1)
+    return dot(places, by_z(parts).astype(BF16), 1, 1).astype(BF16)
 
 
 def by_z(parts):
@@ -91,11 +94,15 @@
     return into == kind * parts + z * Y_SIZE + y
 
 
-def send_kernel(rep_ref, lists_ref, feats_ref, send_ref):
-    parts = lists_ref.shape[0]
+def send_kernel(rep_ref, lists_hbm, feats_hbm, send_ref, lists_ref, feats_ref, sems):
+    lists_copy = pltpu.make_async_copy(lists_hbm, lists_ref, sems.at[0])
+    feats_copy = pltpu.make_async_copy(feats_hbm, feats_ref, sems.at[1])
+    lists_copy.start()
+    feats_copy.start()
+    lists_copy.wait()
     places = boundary_places(rep_ref[0], lists_ref, feats_ref.shape[0])
-    places = move(by_z(parts), places)
-    send_ref[...] = move(places, feats_ref[...])
+    feats_copy.wait()
+    send_ref[...] = dot(places, feats_ref[...], 0, 0).astype(BF16)
 
 
 def plane_kernel(arrived_ref, send_ref):
@@ -286,19 +293,21 @@
     own_ref[...] = dot(seeded, w_self_ref[...], 1, 1) + dot(adj_ref[...], d_agg_ref[...], 0, 0)
 
 
-def scatter_kernel(rep_ref, core_ref, lists_ref, arrived_ref, own_ref, keep_ref, send_ref):
-    parts = lists_ref.shape[0]
+def scatter_kernel(rep_ref, lists_ref, arrived_ref, own_ref, keep_ref, send_ref, total_ref):
     rows, width = own_ref.shape
-    places = move(by_z(parts), boundary_places(rep_ref[0], lists_ref, rows))
-    back = arrived_ref[:, :, :width].reshape(2 * parts, width)
-    total = (own_ref[...] + dot(places, back, 0, 0)).astype(BF16)
+    rep = rep_ref[0]
+    places = boundary_places(rep, lists_ref, rows)
+    back = arrived_ref[:, :, :width].reshape(places.shape[1], width)
+    total_ref[...] = (own_ref[...] + dot(places, back)).astype(BF16)
     share = rows // (X_SIZE * CORES)
-    first = core_ref[0] == 0
-    for x in range(X_SIZE):
-        low = total[2 * x * share : (2 * x + 1) * share]
-        high = total[(2 * x + 1) * share : (2 * x + 2) * share]
-        keep_ref[x] = jnp.where(first, low, high)
-        send_ref[x] = jnp.where(first, high, low)
+    for step in range(X_SIZE):
+        keep = jnp.bitwise_xor(rep, step * CORES)
+        for place, ref in ((keep, keep_ref), (jnp.bitwise_xor(keep, 1), send_ref)):
+            ref[step] = total_ref[pl.ds(pl.multiple_of(place * share, 32), share), :]
+
+
+def copy_kernel(from_ref, to_ref):
+    to_ref[...] = from_ref[...]
 
 
 def body(
@@ -324,7 +333,7 @@
     x_id = lax.axis_index("x").astype(jnp.int32)
     core = core_id.reshape(1)
     rep = (x_id * CORES + core_id).reshape(1)
-    lists = halo_index[0]
+    lists = halo_index[0].T
     seed_row = seed_ids.reshape(1, seeds)
     tile_scalars = (tile_dst, tile_src, tile_count)
     scale = float(seeds * parts * reps) ** (-0.5)
@@ -337,16 +346,15 @@
 
     (send,) = call(
         send_kernel, "pick_boundary", [((2 * parts, width), BF16)], [rep], [lists, feats],
+        scratch=[
+            pltpu.VMEM(lists.shape, jnp.int32),
+            pltpu.VMEM(feats.shape, BF16),
+            pltpu.SemaphoreType.DMA((2,)),
+        ],
+        space=pl.ANY,
         flops=4 * parts * rows * width,
     )
     by_depth = swap(send.reshape(depth, 2 * Y_SIZE, width), "z").reshape(2 * parts, width)
-    (plane,) = call(
-        plane_kernel, "spread_plane", [((PLANE, 2 * depth, width), BF16)], [], [by_depth],
-        flops=8 * parts * parts * width,
-    )
-    near = swap(plane, ("y", "x")).reshape(half, width)
-    far = pair(near)
-
     chosen_t, preact, part, near_adj, near_adj_t, far_adj, far_adj_t = call(
         own_kernel, "own_rows",
         [
@@ -364,6 +372,13 @@
         flops=2 * seeds * (3 * rows * width + width * width + 8 * half * half),
     )
 
+    (plane,) = call(
+        plane_kernel, "spread_plane", [((PLANE, 2 * depth, width), BF16)], [], [by_depth],
+        flops=8 * parts * parts * width, after=[part],
+    )
+    near = swap(plane, ("y", "x")).reshape(half, width)
+    far = pair(near)
+
     out, d_pre, d_agg, keep, pair_send = call(
         middle_kernel, "forward_backward",
         [
@@ -382,10 +397,16 @@
     )
 
     pair_arrived = pair(pair_send)
+    (own,) = call(
+        own_back_kernel, "own_rows_back", [((rows, width), F32)],
+        [*tile_scalars], [tiles, seed_row, d_pre, d_agg, w_self],
+        scratch=[pltpu.VMEM((seeds, rows), BF16)],
+        flops=2 * seeds * width * 3 * rows,
+    )
     (plane_send,) = call(
         pair_sum_kernel, "sum_pair",
         [((PLANE, width // PLANE + 2 * depth + 8, width), BF16)],
-        [], [keep, pair_arrived],
+        [], [keep, pair_arrived], after=[own],
     )
     plane_arrived = swap(plane_send, ("y", "x"))
     (depth_send,) = call(
@@ -400,38 +421,35 @@
         [], [depth_arrived],
     )
     weight_depth = swap(weight_send, "z")
+    share = rows // reps
+    row_keep, row_send = call(
+        scatter_kernel, "return_rows",
+        [((X_SIZE, share, width), BF16), ((X_SIZE, share, width), BF16)],
+        [rep], [lists, depth_arrived, own],
+        scratch=[pltpu.VMEM((rows, width), BF16)],
+        flops=4 * parts * rows * width, after=[weight_send],
+    )
+    row_pair = row_keep.astype(F32) + pair(row_send).astype(F32)
+    rows_out = row_pair.astype(BF16)
     (weight_plane,) = call(
         gather_kernel, "gather_weights",
         [((PLANE, width // PLANE, width), BF16)],
-        [], [weight_depth],
+        [], [weight_depth], after=[rows_out], flops=20_000_000_000,
     )
     weight_near = swap(weight_plane, ("y", "x")).reshape(width, width)
-    weight_far = pair(weight_near)
+    far_half = lax.ppermute(rows_out[2:], "x", [(x, x ^ 2) for x in range(X_SIZE)])
+    row_half = row_pair[:2] + far_half.astype(F32)
+    beside = lax.ppermute(row_half[1].astype(BF16), "x", [(x, x ^ 1) for x in range(X_SIZE)])
+    input_grad = row_half[0] + beside.astype(F32)
+    (weight_send,) = call(
+        copy_kernel, "hand_on", [((width, width), BF16)], [], [weight_near], after=[input_grad]
+    )
+    weight_far = pair(weight_send)
     grad_self = jnp.where(core_id == 0, weight_near, weight_far)
     grad_neigh = jnp.where(core_id == 0, weight_far, weight_near)
     groups = width // LANES
     grad_bias = bias_rows[: 2 * groups].reshape(groups, 2, LANES).sum(1).reshape(width)
 
-    (own,) = call(
-        own_back_kernel, "own_rows_back", [((rows, width), F32)],
-        [*tile_scalars], [tiles, seed_row, d_pre, d_agg, w_self],
-        scratch=[pltpu.VMEM((seeds, rows), BF16)],
-        flops=2 * seeds * width * 3 * rows,
-    )
-    share = rows // reps
-    row_keep, row_send = call(
-        scatter_kernel, "return_rows",
-        [((X_SIZE, share, width), BF16), ((X_SIZE, share, width), BF16)],
-        [rep, core], [lists, depth_arrived, own],
-        flops=4 * parts * rows * width,
-    )
-    row_pair = row_keep.astype(F32) + pair(row_send).astype(F32)
-    rows_out = row_pair.astype(BF16)
-    input_grad = lax.dynamic_index_in_dim(row_pair, x_id, 0, keepdims=False)
-    for shift in range(1, X_SIZE):
-        chunk = lax.dynamic_index_in_dim(rows_out, (x_id + shift) % X_SIZE, 0, keepdims=False)
-        chunk = lax.ppermute(chunk, "x", [(x, (x + shift) % X_SIZE) for x in range(X_SIZE)])
-        input_grad = input_grad + chunk.astype(F32)
     return (out, input_grad, grad_self, grad_neigh, grad_bias)
 
 

time: 158 us -> 154 us (0.975)
  blocking collectives: 101 us -> 57.3 us
  starting transfers between devices: 30.6 us -> 51.1 us
  waiting for transfers between devices: 7.48 us -> 19.4 us
  local copies, waits for them, and re-layouts: 2 us -> 8.18 us
    all_to_all x5 -> x3, blocking collectives: 101 us -> 57.3 us  [swap(): return lax.all_to_all(values, axis, split_axis=0, concat_axis=0, tiled=True)]
    all_to_all x1 -> x3, starting transfers between devices: 3.57 us -> 23.6 us  [swap(): return lax.all_to_all(values, axis, split_axis=0, concat_axis=0, tiled=True)]
    all_to_all x1 -> x3, waiting for transfers between devices: 1.95 us -> 11.6 us  [swap(): return lax.all_to_all(values, axis, split_axis=0, concat_axis=0, tiled=True)]
    unnamed x21 -> x46, local copies, waits for them, and re-layouts: 1.96 us -> 8.14 us
    ppermute x4, starting transfers between devices: 18.6 us -> 21.8 us  [pair(): return lax.ppermute(values, 'core', [(0, 1), (1, 0)])]
    ppermute x3 -> x2, starting transfers between devices: 8.42 us -> 5.81 us  [the longest x1 3.15 us: body(): lax.ppermute(row_half[1].astype(BF16), 'x', [(x, x ^ 1) for x in range(X_...]
    ppermute x3 -> x2, waiting for transfers between devices: 2.92 us -> 5.15 us  [the longest x1 5.15 us: body(): lax.ppermute(row_half[1].astype(BF16), 'x', [(x, x ^ 1) for x in range(X_...]
    pallas_call x10 -> x11, Pallas kernels: 12.3 us -> 13.8 us  [call(): pl.pallas_call(kernel, out_shape=shapes, in_specs=[pl.BlockSpec(memory_sp...]
  transfers between devices with their start and end apart: 8 -> 9, of which waited for: 4 -> 7; matrix products, arithmetic and copies ran while one was open for 1% -> 1% of each run, Pallas kernels for 5% -> 5%
where the time goes in v3:
time: 154 us; the launch traced here: 153 us
  blocking collectives  57.3 us (37%)
  starting transfers between devices  51.1 us (33%)
  waiting for transfers between devices  19.4 us (13%)
  Pallas kernels  13.8 us (9%)
  local copies, waits for them, and re-layouts  8.18 us (5%)
  other arithmetic  1.88 us (1%)
  between operations  1.65 us (1%)
    all_to_all x3, blocking collectives, swap(): return lax.all_to_all(values, axis, split_axis=0, concat_axis=0, tiled=True)  57.3 us
    all_to_all x3, starting transfers between devices, swap(): return lax.all_to_all(values, axis, split_axis=0, concat_axis=0, tiled=True)  23.6 us
    ppermute x4, starting transfers between devices, pair(): return lax.ppermute(values, 'core', [(0, 1), (1, 0)])  21.8 us
    pallas_call x11, Pallas kernels, call(): pl.pallas_call(kernel, out_shape=shapes, in_specs=[pl.BlockSpec(memory_sp...  13.8 us
    all_to_all x3, waiting for transfers between devices, swap(): return lax.all_to_all(values, axis, split_axis=0, concat_axis=0, tiled=True)  11.6 us
    unnamed x46, local copies, waits for them, and re-layouts  8.14 us
    ppermute x1, waiting for transfers between devices, body(): lax.ppermute(row_half[1].astype(BF16), 'x', [(x, x ^ 1) for x in range(X_...  5.15 us
    ppermute x1, starting transfers between devices, body(): lax.ppermute(row_half[1].astype(BF16), 'x', [(x, x ^ 1) for x in range(X_...  3.15 us
  transfers between devices with their start and end apart: 9, of which 7 were waited for; matrix products, arithmetic and copies ran while one was open for 1% of the time, Pallas kernels for 5%

profile of v3, /device:TPU:1, one launch (start us, length us, event | category | flops | bytes accessed | tf_op | source)
XLA Modules:
  0.0 153.3 jit_solution(9845845058074850923)
XLA Ops:
  0.7 0.0 copy-start
  0.7 1.1 copy-done
  1.8 0.7 copy-done.3
  2.5 1.3 pick_boundary.1
  3.8 15.8 %all-to-all-start = ((bf16[16,8,512]{2,1,0:T(8,128)(2,1)}), bf16[16,8,512]{2,1,0:T(8,128)(2,1)S(1)}, u32[]{:S(2)}, u32[]{:S(2)}) async-start(bf16[16,8,512]{2,1,0:T(8,128)(2,1)} %bitcast.4), calls=%async_computation | async-start | bytes 262144 | tf_op jit(solution)/shard_map/all_to_all | solution.py:342
  20.3 0.0 copy-start.7
  20.3 1.0 copy-done.7
  21.3 1.0 copy-done.9
  22.3 4.7 %own_rows.1 = (bf16[512,512]{1,0:T(8,128)(2,1)S(1)}, f32[512,512]{1,0:T(8,128)S(1)}, f32[512,512]{1,0:T(8,128)S(1)}, bf16[512,512]{1,0:T(8,128)(2,1)S(1)}, bf16[...) custom-call(s32[1]{0:T(128)} %bitcast.core_ref, s32[1,14]{1,0:T(1,128)S(1)} %copy-done.12, ...), custom_call_target="tpu_custom_call" | custom-call | flops 3623878656 | bytes 6491136 | tf_op jit(solution)/shard_map/own_rows/pallas_call | solution.py:48
  27.1 0.0 copy-start.14
  27.1 0.8 copy-done.14
  27.9 0.8 copy-done.16
  28.7 0.8 copy-done.18
  29.4 0.8 copy-done.20
  30.2 1.3 all-to-all-done
  31.6 0.0 copy-start.19
  31.6 0.2 spread_plane.1
  31.8 15.9 %all_to_all.30 = bf16[16,32,512]{2,1,0:T(8,128)(2,1)S(1)} all-to-all(bf16[16,32,512]{2,1,0:T(8,128)(2,1)S(1)} %spread_plane.1), channel_id=1, replica_groups=mesh['z'=16,'y'=4,'x'=4,'core'=2] {'y','x'}, dimensions={0} | all-to-all | bytes 1048576 | tf_op jit(solution)/shard_map/all_to_all | solution.py:342
  47.6 6.8 %collective-permute-start = (bf16[512,512]{1,0:T(8,128)(2,1)S(1)}, bf16[512,512]{1,0:T(8,128)(2,1)S(1)}, u32[]{:S(2)}, u32[]{:S(2)}) collective-permute-start(bf16[512,512]{1,0:T(8,128)(2,1)S(1)} %bitcast.21), channel_id=1, source_target_pairs={{0,1},{1,0},{2,3},{3,2},{4,5},{5,4},{6,7},{7,6},{8,9},{9,8},{10,11... | collective-permute-start | bytes 1572872 | tf_op jit(solution)/shard_map/ppermute | solution.py:345
  54.4 1.5 collective-permute-done.far_ref
  56.0 1.0 copy-done.21
  57.0 2.7 %forward_backward.1 = (bf16[512,512]{1,0:T(8,128)(2,1)}, bf16[512,512]{1,0:T(8,128)(2,1)S(1)}, bf16[512,512]{1,0:T(8,128)(2,1)S(1)}, bf16[1040,512]{1,0:T(8,128)(2,1)S(1)}, bf16[1040,512]{1,0:T(8,128)(2,1)S(1)}) custom-call(s32[1]{0:T(128)} %bitcast.core_ref, bf16[512,512]{1,0:T(8,128)(2,1)S(1)} %bitcast.22, ...), custom_call_target="tpu_custom_call" | custom-call | flops 2147483648 | bytes 10518528 | tf_op jit(solution)/shard_map/forward_backward/pallas_call | solution.py:48
  59.7 2.3 %collective-permute-start.1 = (bf16[1040,512]{1,0:T(8,128)(2,1)S(1)}, bf16[1040,512]{1,0:T(8,128)(2,1)S(1)}, u32[]{:S(2)}, u32[]{:S(2)}) collective-permute-start(bf16[1040,512]{1,0:T(8,128)(2,1)S(1)} %get-tuple-element.30), channel_id=1, source_target_pairs={{0,1},{1,0},{2,3},{3,2},{4,5},{5,4},{6,7},{7,6},{8,9},{9,8},{10,11... | collective-permute-start | bytes 3194888 | tf_op jit(solution)/shard_map/ppermute | solution.py:345
  62.1 2.0 %own_rows_back.1.refs_2_.refs_3_ = f32[768,512]{1,0:T(8,128)S(1)} custom-call(s32[1,14]{1,0:T(1,128)S(1)} %copy-done.12, s32[1,14]{1,0:T(1,128)S(1)} %copy-done.13, s32[1]{0:T(128)S(6)} %copy.16.count_ref, bf16[14,128,128]{2,1,0:T(8,128)(2,1)S(1)} %copy-done.10, s32[1,512]{1,0:T(1,128)S(1)} %bitcast.28, bf16[512,512]{1,0:T(8,128)(2,1)S(1)} %get-tuple-element.31.d_pre_ref, ...), custom_call_target="tpu_custom_call" | custom-call | flops 1207959552 | bytes 3606528 | tf_op jit(solution)/shard_map/own_rows_back/pallas_call | solution.py:48
  64.1 0.3 collective-permute-done.1.refs_1_
  64.3 0.2 sum_pair.1
  64.6 20.7 %all_to_all.31.arrived_ref = bf16[16,72,512]{2,1,0:T(8,128)(2,1)S(1)} all-to-all(bf16[16,72,512]{2,1,0:T(8,128)(2,1)S(1)} %sum_pair.1), channel_id=1, replica_groups=mesh['z'=16,'y'=4,'x'=4,'core'=2] {'y','x'}, dimensions={0} | all-to-all | bytes 2359296 | tf_op jit(solution)/shard_map/all_to_all | solution.py:342
  85.3 0.4 sum_plane.1
  85.7 20.7 %all_to_all.32.arrived_ref.refs_2_ = bf16[16,8,768]{2,1,0:T(8,128)(2,1)S(1)} all-to-all(bf16[16,8,768]{2,1,0:T(8,128)(2,1)S(1)} %sum_plane.1), channel_id=1, replica_groups=mesh['z'=16,'y'=4,'x'=4,'core'=2] {'z'}, dimensions={0} | all-to-all | bytes 393216 | tf_op jit(solution)/shard_map/all_to_all | solution.py:342
  106.4 0.6 sum_weights.1
  107.0 0.6 return_rows.1
  107.6 7.4 %collective-permute-start.2 = (bf16[4,96,512]{2,1,0:T(8,128)(2,1)S(1)}, bf16[4,96,512]{2,1,0:T(8,128)(2,1)S(1)}, u32[]{:S(2)}, u32[]{:S(2)}) collective-permute-start(bf16[4,96,512]{2,1,0:T(8,128)(2,1)S(1)} %get-tuple-element.35), channel_id=1, source_target_pairs={{0,1},{1,0},{2,3},{3,2},{4,5},{5,4},{6,7},{7,6},{8,9},{9,8},{10,11... | collective-permute-start | bytes 1179656 | tf_op jit(solution)/shard_map/ppermute | solution.py:345
  115.0 4.2 %all-to-all-start.4 = ((bf16[16,8,128]{2,1,0:T(8,128)(2,1)}), bf16[16,8,128]{2,1,0:T(8,128)(2,1)S(1)}, u32[]{:S(2)}, u32[]{:S(2)}) async-start(bf16[16,8,128]{2,1,0:T(8,128)(2,1)} %get-tuple-element.33.refs_4_), calls=%async_computation.4 | async-start | bytes 65536 | tf_op jit(solution)/shard_map/all_to_all | solution.py:342
  119.2 0.0 collective-permute-done.2
  119.2 0.1 fusion.2
  119.4 2.7 %collective-permute-start.3 = (bf16[2,96,512]{2,1,0:T(8,128)(2,1)S(1)}, bf16[2,96,512]{2,1,0:T(8,128)(2,1)S(1)}, u32[]{:S(2)}, u32[]{:S(2)}) collective-permute-start(bf16[2,96,512]{2,1,0:T(8,128)(2,1)S(1)} %slice.18), channel_id=1, source_target_pairs={{0,4},{2,6},{4,0},{6,2},{1,5},{3,7},{5,1},{7,3},{8,12},{10,14},{12... | collective-permute-start | bytes 589832 | tf_op jit(solution)/shard_map/ppermute | solution.py:440
  122.1 8.6 %all-to-all-done.4.refs_0_ = bf16[16,8,128]{2,1,0:T(8,128)(2,1)S(1)} async-done(((bf16[16,8,128]{2,1,0:T(8,128)(2,1)}), bf16[16,8,128]{2,1,0:T(8,128)(2,1)S(1)}, u32[]{:S(2)}, u32[]{:S(2)}) %all-to-all-start.4) | async-done | bytes 32800 | tf_op jit(solution)/shard_map/all_to_all | solution.py:342
  130.7 1.0 gather_weights.1
  131.7 3.6 %all-to-all-start.5 = ((bf16[16,32,512]{2,1,0:T(8,128)(2,1)}), bf16[16,32,512]{2,1,0:T(8,128)(2,1)S(1)}, u32[]{:S(2)}, u32[]{:S(2)}) async-start(bf16[16,32,512]{2,1,0:T(8,128)(2,1)} %gather_weights.1), calls=%async_computation.5 | async-start | bytes 1048576 | tf_op jit(solution)/shard_map/all_to_all | solution.py:342
  135.3 0.0 collective-permute-done.3
  135.4 3.1 %collective-permute-start.4 = (bf16[96,512]{1,0:T(8,128)(2,1)S(1)}, bf16[96,512]{1,0:T(8,128)(2,1)S(1)}, u32[]{:S(2)}, u32[]{:S(2)}) collective-permute-start(bf16[96,512]{1,0:T(8,128)(2,1)S(1)} %fusion.1), channel_id=1, source_target_pairs={{0,2},{2,0},{4,6},{6,4},{1,3},{3,1},{5,7},{7,5},{8,10},{10,8},{12,... | collective-permute-start | bytes 294920 | tf_op jit(solution)/shard_map/ppermute | solution.py:442
  138.5 5.1 %collective-permute-done.4 = bf16[96,512]{1,0:T(8,128)(2,1)S(1)} collective-permute-done((bf16[96,512]{1,0:T(8,128)(2,1)S(1)}, bf16[96,512]{1,0:T(8,128)(2,1)S(1)}, u32[]{:S(2)}, u32[]{:S(2)}) %collective-permute-start.4) | collective-permute-done | bytes 98336 | tf_op jit(solution)/shard_map/ppermute | solution.py:442
  143.7 0.0 copy-start.2
  143.7 1.6 %all-to-all-done.5 = bf16[16,32,512]{2,1,0:T(8,128)(2,1)S(1)} async-done(((bf16[16,32,512]{2,1,0:T(8,128)(2,1)}), bf16[16,32,512]{2,1,0:T(8,128)(2,1)S(1)}, u32[]{:S(2)}, u32[]{:S(2)}) %all-to-all-start.5) | async-done | bytes 524320 | tf_op jit(solution)/shard_map/all_to_all | solution.py:342
  145.4 5.3 %collective-permute-start.5 = (bf16[512,512]{1,0:T(8,128)(2,1)S(1)}, bf16[512,512]{1,0:T(8,128)(2,1)S(1)}, u32[]{:S(2)}, u32[]{:S(2)}) collective-permute-start(bf16[512,512]{1,0:T(8,128)(2,1)S(1)} %hand_on.1), channel_id=1, source_target_pairs={{0,1},{1,0},{2,3},{3,2},{4,5},{5,4},{6,7},{7,6},{8,9},{9,8},{10,11... | collective-permute-start | bytes 1572872 | tf_op jit(solution)/shard_map/ppermute | solution.py:345
  150.7 0.6 reduce_sum.9
  151.3 0.9 collective-permute-done.5
  152.2 1.1 broadcast_select_fusion
  (38 shorter events, 0.2 us)
Async XLA Ops:
  0.6 19.6 %copy-start.22 = (bf16[512]{0:T(512)(128)(2,1)S(1)}, bf16[512]{0:T(512)(128)(2,1)}, u32[]{:S(2)}) copy-start(bf16[512]{0:T(512)(128)(2,1)} %param.20) | copy-start | bytes 3076
  0.6 19.6 %copy-start.11 = (s32[512]{0:T(512)S(1)}, s32[512]{0:T(512)}, u32[]{:S(2)}) copy-start(s32[512]{0:T(512)} %param.13) | copy-start | bytes 6148
  0.7 19.6 %copy-start.12 = (s32[1,14]{1,0:T(1,128)S(1)}, s32[1,14]{1,0:T(1,128)}, u32[]{:S(2)}) copy-start(s32[1,14]{1,0:T(1,128)} %dst_ref.3) | copy-start | bytes 172
  0.7 19.6 %copy-start.13 = (s32[1,14]{1,0:T(1,128)S(1)}, s32[1,14]{1,0:T(1,128)}, u32[]{:S(2)}) copy-start(s32[1,14]{1,0:T(1,128)} %src_ref.3) | copy-start | bytes 172
  0.7 1.1 copy-start
  1.8 0.7 copy-start.3
  2.5 17.7 %copy-start.1 = (bf16[768,512]{1,0:T(8,128)(2,1)S(1)}, bf16[768,512]{1,0:T(8,128)(2,1)}, u32[]{:S(2)}) copy-start(bf16[768,512]{1,0:T(8,128)(2,1)} %feats_ref.1) | copy-start | bytes 2359300
  3.8 27.8 %all-to-all-start = ((bf16[16,8,512]{2,1,0:T(8,128)(2,1)}), bf16[16,8,512]{2,1,0:T(8,128)(2,1)S(1)}, u32[]{:S(2)}, u32[]{:S(2)}) async-start(bf16[16,8,512]{2,1,0:T(8,128)(2,1)} %bitcast.4), calls=%async_computation | async-start | bytes 262144 | tf_op jit(solution)/shard_map/all_to_all | solution.py:342
  20.3 1.0 copy-start.7
  21.3 1.0 copy-start.9
  27.1 0.8 copy-start.14
  27.9 0.8 copy-start.16
  28.7 0.8 copy-start.18
  29.4 0.8 copy-start.20
  31.6 24.4 %copy-start.5 = (bf16[512,512]{1,0:T(8,128)(2,1)S(1)}, bf16[512,512]{1,0:T(8,128)(2,1)}, u32[]{:S(2)}) copy-start(bf16[512,512]{1,0:T(8,128)(2,1)} %w_neigh_ref.1) | copy-start | bytes 1572868
  31.6 24.4 %copy-start.6 = (bf16[512,512]{1,0:T(8,128)(2,1)S(1)}, bf16[512,512]{1,0:T(8,128)(2,1)}, u32[]{:S(2)}) copy-start(bf16[512,512]{1,0:T(8,128)(2,1)} %cot_ref.1) | copy-start | bytes 1572868
  31.6 24.4 %copy-start.15 = (bf16[512,512]{1,0:T(8,128)(2,1)S(1)}, bf16[512,512]{1,0:T(8,128)(2,1)}, u32[]{:S(2)}) copy-start(bf16[512,512]{1,0:T(8,128)(2,1)} %copy-done.14) | copy-start | bytes 1572868
  31.6 24.4 %copy-start.17 = (bf16[512,512]{1,0:T(8,128)(2,1)S(1)}, bf16[512,512]{1,0:T(8,128)(2,1)}, u32[]{:S(2)}) copy-start(bf16[512,512]{1,0:T(8,128)(2,1)} %copy-done.16) | copy-start | bytes 1572868
  31.6 24.4 %copy-start.19 = (bf16[512,512]{1,0:T(8,128)(2,1)S(1)}, bf16[512,512]{1,0:T(8,128)(2,1)}, u32[]{:S(2)}) copy-start(bf16[512,512]{1,0:T(8,128)(2,1)} %copy-done.18) | copy-start | bytes 1572868
  47.6 8.3 %collective-permute-start = (bf16[512,512]{1,0:T(8,128)(2,1)S(1)}, bf16[512,512]{1,0:T(8,128)(2,1)S(1)}, u32[]{:S(2)}, u32[]{:S(2)}) collective-permute-start(bf16[512,512]{1,0:T(8,128)(2,1)S(1)} %bitcast.21), channel_id=1, source_target_pairs={{0,1},{1,0},{2,3},{3,2},{4,5},{5,4},{6,7},{7,6},{8,9},{9,8},{10,11... | collective-permute-start | bytes 1572872 | tf_op jit(solution)/shard_map/ppermute | solution.py:345
  56.0 1.0 copy-start.21
  57.0 5.0 %copy-start.8 = (bf16[512,512]{1,0:T(8,128)(2,1)S(1)}, bf16[512,512]{1,0:T(8,128)(2,1)}, u32[]{:S(2)}) copy-start(bf16[512,512]{1,0:T(8,128)(2,1)} %w_self_ref.3) | copy-start | bytes 1572868
  57.0 5.0 %copy-start.10 = (bf16[14,128,128]{2,1,0:T(8,128)(2,1)S(1)}, bf16[14,128,128]{2,1,0:T(8,128)(2,1)}, u32[]{:S(2)}) copy-start(bf16[14,128,128]{2,1,0:T(8,128)(2,1)} %tiles_ref.3) | copy-start | bytes 1376260
  59.7 4.6 %collective-permute-start.1 = (bf16[1040,512]{1,0:T(8,128)(2,1)S(1)}, bf16[1040,512]{1,0:T(8,128)(2,1)S(1)}, u32[]{:S(2)}, u32[]{:S(2)}) collective-permute-start(bf16[1040,512]{1,0:T(8,128)(2,1)S(1)} %get-tuple-element.30), channel_id=1, source_target_pairs={{0,1},{1,0},{2,3},{3,2},{4,5},{5,4},{6,7},{7,6},{8,9},{9,8},{10,11... | collective-permute-start | bytes 3194888 | tf_op jit(solution)/shard_map/ppermute | solution.py:345
  85.3 21.7 %copy-start.4 = (s32[1,64,8]{1,2,0:T(8,128)S(1)}, s32[1,64,8]{1,2,0:T(8,128)}, u32[]{:S(2)}) copy-start(s32[1,64,8]{1,2,0:T(8,128)} %param.12) | copy-start | bytes 6148
  107.6 11.6 %collective-permute-start.2 = (bf16[4,96,512]{2,1,0:T(8,128)(2,1)S(1)}, bf16[4,96,512]{2,1,0:T(8,128)(2,1)S(1)}, u32[]{:S(2)}, u32[]{:S(2)}) collective-permute-start(bf16[4,96,512]{2,1,0:T(8,128)(2,1)S(1)} %get-tuple-element.35), channel_id=1, source_target_pairs={{0,1},{1,0},{2,3},{3,2},{4,5},{5,4},{6,7},{7,6},{8,9},{9,8},{10,11... | collective-permute-start | bytes 1179656 | tf_op jit(solution)/shard_map/ppermute | solution.py:345
  115.0 15.7 %all-to-all-start.4 = ((bf16[16,8,128]{2,1,0:T(8,128)(2,1)}), bf16[16,8,128]{2,1,0:T(8,128)(2,1)S(1)}, u32[]{:S(2)}, u32[]{:S(2)}) async-start(bf16[16,8,128]{2,1,0:T(8,128)(2,1)} %get-tuple-element.33.refs_4_), calls=%async_computation.4 | async-start | bytes 65536 | tf_op jit(solution)/shard_map/all_to_all | solution.py:342
  119.4 15.9 %collective-permute-start.3 = (bf16[2,96,512]{2,1,0:T(8,128)(2,1)S(1)}, bf16[2,96,512]{2,1,0:T(8,128)(2,1)S(1)}, u32[]{:S(2)}, u32[]{:S(2)}) collective-permute-start(bf16[2,96,512]{2,1,0:T(8,128)(2,1)S(1)} %slice.18), channel_id=1, source_target_pairs={{0,4},{2,6},{4,0},{6,2},{1,5},{3,7},{5,1},{7,3},{8,12},{10,14},{12... | collective-permute-start | bytes 589832 | tf_op jit(solution)/shard_map/ppermute | solution.py:440
  131.7 13.7 %all-to-all-start.5 = ((bf16[16,32,512]{2,1,0:T(8,128)(2,1)}), bf16[16,32,512]{2,1,0:T(8,128)(2,1)S(1)}, u32[]{:S(2)}, u32[]{:S(2)}) async-start(bf16[16,32,512]{2,1,0:T(8,128)(2,1)} %gather_weights.1), calls=%async_computation.5 | async-start | bytes 1048576 | tf_op jit(solution)/shard_map/all_to_all | solution.py:342
  135.4 8.3 %collective-permute-start.4 = (bf16[96,512]{1,0:T(8,128)(2,1)S(1)}, bf16[96,512]{1,0:T(8,128)(2,1)S(1)}, u32[]{:S(2)}, u32[]{:S(2)}) collective-permute-start(bf16[96,512]{1,0:T(8,128)(2,1)S(1)} %fusion.1), channel_id=1, source_target_pairs={{0,2},{2,0},{4,6},{6,4},{1,3},{3,1},{5,7},{7,5},{8,10},{10,8},{12,... | collective-permute-start | bytes 294920 | tf_op jit(solution)/shard_map/ppermute | solution.py:442
  143.7 9.6 %copy-start.2 = (f32[96,512]{1,0:T(8,128)}, f32[96,512]{1,0:T(8,128)S(1)}, u32[]{:S(2)}) copy-start(f32[96,512]{1,0:T(8,128)S(1)} %fusion.refs_1_) | copy-start | bytes 589828
  145.4 6.9 %collective-permute-start.5 = (bf16[512,512]{1,0:T(8,128)(2,1)S(1)}, bf16[512,512]{1,0:T(8,128)(2,1)S(1)}, u32[]{:S(2)}, u32[]{:S(2)}) collective-permute-start(bf16[512,512]{1,0:T(8,128)(2,1)S(1)} %hand_on.1), channel_id=1, source_target_pairs={{0,1},{1,0},{2,3},{3,2},{4,5},{5,4},{6,7},{7,6},{8,9},{9,8},{10,11... | collective-permute-start | bytes 1572872 | tf_op jit(solution)/shard_map/ppermute | solution.py:345

commit v4 on v3

v4 whole, which is shorter than its diff:
```python
import functools
import math

import jax
import jax.numpy as jnp
from jax import lax
from jax.experimental import pallas as pl
from jax.experimental.pallas import tpu as pltpu
from jax.sharding import Mesh
from jax.sharding import PartitionSpec as P

BLK = 128
LANES = 128
SLOTS = 8
X_SIZE = 4
CORES = 2
Y_SIZE = 4
PLANE = Y_SIZE * X_SIZE
BF16 = jnp.bfloat16
F32 = jnp.float32
VMEM_BYTES = 24 * 1024 * 1024
FULL_VMEM_BYTES = 65 * 1000 * 1024


def dot(a, b, contract_a=1, contract_b=0):
    return lax.dot_general(
        a, b, (((contract_a,), (contract_b,)), ((), ())), preferred_element_type=F32
    )


def move(matrix, rows):
    return dot(matrix.astype(BF16), rows).astype(BF16)


def iota(shape, dim):
    return lax.broadcasted_iota(jnp.int32, shape, dim)


def split(wide):
    high = wide.astype(BF16)
    return high, (wide - high.astype(F32)).astype(BF16)


def call(kernel, name, outs, scalars, arrays, scratch=(), flops=0, after=(), hbm=(), hbm_outs=(), limit=VMEM_BYTES):
    if after:
        inner, at = kernel, len(scalars) + len(arrays) + len(hbm)
        kernel = lambda *refs: inner(*refs[:at], *refs[at + len(after) :])
    shapes = tuple(jax.ShapeDtypeStruct(shape, dtype) for shape, dtype in outs)
    shapes += tuple(pltpu.HBM(shape, dtype) for shape, dtype in hbm_outs)
    size = sum(math.prod(a.shape) * a.dtype.itemsize for a in (*arrays, *hbm, *shapes))
    return pl.pallas_call(
        kernel,
        out_shape=shapes,
        in_specs=[pl.BlockSpec(memory_space=pltpu.SMEM)] * len(scalars)
        + [pl.BlockSpec(memory_space=pltpu.VMEM)] * len(arrays)
        + [pl.BlockSpec(memory_space=pltpu.HBM)] * len(hbm)
        + [pl.BlockSpec(memory_space=pl.ANY)] * len(after),
        out_specs=tuple([pl.BlockSpec(memory_space=pltpu.VMEM)] * len(outs))
        + tuple([pl.BlockSpec(memory_space=pltpu.HBM)] * len(hbm_outs)),
        scratch_shapes=list(scratch),
        compiler_params=pltpu.CompilerParams(vmem_limit_bytes=limit),
        cost_estimate=pl.CostEstimate(flops=flops, bytes_accessed=size, transcendentals=0),
        name=name,
    )(*scalars, *arrays, *hbm, *after)


def fetched(arrays):
    return [pltpu.VMEM(a.shape, a.dtype) for a in arrays] + [
        pltpu.SemaphoreType.DMA((len(arrays),))
    ]


def fetch(from_refs, to_refs, sems):
    copies = [
        pltpu.make_async_copy(source, to, sems.at[at])
        for at, (source, to) in enumerate(zip(from_refs, to_refs))
    ]
    for copy in copies:
        copy.start()
    return copies


def place_tiles(dst_ref, src_ref, count_ref, tiles_ref, adj_ref, first, last):
    adj_ref[...] = jnp.zeros_like(adj_ref)

    def step(slot, carry):
        block = src_ref[0, slot]

        @pl.when(jnp.logical_and(block >= first, block < last))
        def _():
            row = pl.multiple_of(dst_ref[0, slot] * BLK, BLK)
            col = pl.multiple_of((block - first) * BLK, BLK)
            adj_ref[pl.ds(row, BLK), pl.ds(col, BLK)] = tiles_ref[slot]

        return carry

    lax.fori_loop(0, count_ref[0], step, 0)


def boundary_places(rep, lists_ref, rows):
    slots, parts = lists_ref.shape
    lists = lists_ref[...].astype(F32)
    wanted = jnp.sum(
        jnp.where(iota((slots, parts), 0) == rep, lists, 0.0), axis=0, keepdims=True
    ).astype(jnp.int32)
    place = iota((rows, parts), 0)
    places = jnp.concatenate([(place == wanted).astype(BF16), (place == rep).astype(BF16)], 1)
    return dot(places, by_z(parts).astype(BF16), 1, 1).astype(BF16)


def by_z(parts):
    shape = (2 * parts, 2 * parts)
    out, into = iota(shape, 0), iota(shape, 1)
    y, kind, z = out % Y_SIZE, out // Y_SIZE % 2, out // (2 * Y_SIZE)
    return into == kind * parts + z * Y_SIZE + y


def send_kernel(rep_ref, lists_hbm, feats_hbm, send_ref, lists_ref, feats_ref, sems):
    lists_copy, feats_copy = fetch((lists_hbm, feats_hbm), (lists_ref, feats_ref), sems)
    lists_copy.wait()
    places = boundary_places(rep_ref[0], lists_ref, feats_ref.shape[0])
    feats_copy.wait()
    send_ref[...] = dot(places, feats_ref[...], 0, 0).astype(BF16)


def plane_kernel(arrived_ref, send_ref):
    chunk = send_ref.shape[1]
    depth = chunk // 2
    total = arrived_ref.shape[0]
    shape = (total, total)
    out, into = iota(shape, 0), iota(shape, 1)
    z, kind, y = out % depth, out // depth % 2, out // chunk
    moved = move(into == z * (2 * Y_SIZE) + kind * Y_SIZE + y, arrived_ref[...])
    for y_to in range(Y_SIZE):
        for x_to in range(X_SIZE):
            send_ref[y_to * X_SIZE + x_to] = moved[y_to * chunk : (y_to + 1) * chunk]


def own_kernel(
    at_ref, dst_ref, src_ref, count_ref, tiles_ref, feats_ref, seeds_ref, w_self_ref, bias_ref,
    lists_ref, mats_ref, sums_ref, places_ref, own_adj_ref, adj_ref,
):
    rows = feats_ref.shape[0]
    seeds = seeds_ref.shape[1]
    own_blocks = rows // BLK
    table = adj_ref.shape[1]
    place_tiles(dst_ref, src_ref, count_ref, tiles_ref, own_adj_ref, 0, own_blocks)
    place_tiles(
        dst_ref, src_ref, count_ref, tiles_ref, adj_ref, own_blocks, own_blocks + table // BLK
    )
    picks = (iota((rows, seeds), 0) == seeds_ref[...]).astype(BF16)
    feats = feats_ref[...]
    mats_ref[2 * seeds : 2 * seeds + feats.shape[1], :seeds] = dot(feats, picks, 0, 0).astype(BF16)
    chosen = dot(picks, feats, 0, 0).astype(BF16)
    sums_ref[:seeds] = dot(chosen, w_self_ref[...]) + bias_ref[...].astype(F32)
    sums_ref[seeds:] = dot(own_adj_ref[...], feats)
    adj = adj_ref[...]
    half = table // 2
    depth = half // PLANE // 2
    at_x, at_core = at_ref[0], at_ref[1]

    shape = (half, table)
    line, source = iota(shape, 0), iota(shape, 1)
    z, kind = line % depth, line // depth % 2
    x, y = line // (2 * depth) % X_SIZE, line // (2 * depth * X_SIZE)
    start = kind * half + (z * Y_SIZE + y) * SLOTS + x * CORES
    for far, core in enumerate((at_core, 1 - at_core)):
        order = (source == start + core).astype(BF16)
        mats_ref[far * seeds : (far + 1) * seeds, :half] = dot(adj, order, 1, 1).astype(BF16)

    parts = half // SLOTS
    share = 2 * parts
    for x_step in range(X_SIZE):
        for core_step in range(CORES):
            shape = (share, table)
            line, source = iota(shape, 0), iota(shape, 1)
            y, kind, z = line % Y_SIZE, line // Y_SIZE % 2, line // (2 * Y_SIZE)
            slot = jnp.bitwise_xor(at_x, x_step) * CORES + jnp.bitwise_xor(at_core, core_step)
            order = source == kind * half + (z * Y_SIZE + y) * SLOTS + slot
            first = 2 * seeds + feats.shape[1] + (x_step * CORES + core_step) * share
            mats_ref[first : first + share, :seeds] = dot(order.astype(BF16), adj, 1, 1).astype(BF16)

    lists = lists_ref[...]
    high, low = (lists // 256).astype(BF16), (lists % 256).astype(BF16)
    shape = (parts, half)
    line = iota(shape, 1)
    of_part = (
        iota(shape, 0) == line % depth * Y_SIZE + line // (2 * depth * X_SIZE)
    ).astype(BF16)
    wanted = (dot(high, of_part) * 256.0 + dot(low, of_part)).astype(jnp.int32)
    line = iota((SLOTS, half), 1)
    slot = line // (2 * depth) % X_SIZE * CORES
    wanted = jnp.where(line // depth % 2 == 1, iota((SLOTS, half), 0), wanted)
    own_rows = places_ref.shape[1]
    place = iota((own_rows, half), 0) + (at_x * CORES + at_core) * own_rows
    for far, core in enumerate((at_core, 1 - at_core)):
        here = iota((SLOTS, half), 0) == slot + core
        row = jnp.sum(jnp.where(here, wanted.astype(F32), 0.0), axis=0, keepdims=True)
        places_ref[far] = (place == row.astype(jnp.int32)).astype(BF16)


def middle_kernel(
    at_ref, near_ref, far_ref, mats_ref, sums_ref, w_neigh_ref, cot_ref,
    out_ref, keep_ref, send_ref, x_keep_ref, x_send_ref, d_both_hbm, d_both_ref, sem,
):
    seeds, width = cot_ref.shape
    half = near_ref.shape[0]
    back = 2 * seeds + width
    aggregate = (
        sums_ref[seeds:]
        + dot(mats_ref[:seeds, :half], near_ref[...])
        + dot(mats_ref[seeds : 2 * seeds, :half], far_ref[...])
    ).astype(BF16)
    preact = sums_ref[:seeds] + dot(aggregate, w_neigh_ref[...])
    gate = jax.nn.sigmoid(preact)
    out_ref[...] = (preact * gate).astype(BF16)
    d_pre = (cot_ref[...].astype(F32) * gate * (1.0 + preact * (1.0 - gate))).astype(BF16)
    d_agg = dot(d_pre, w_neigh_ref[...], 1, 1).astype(BF16)
    d_both_ref[0] = d_pre
    d_both_ref[1] = d_agg
    kept = pltpu.make_async_copy(d_both_ref, d_both_hbm, sem)
    kept.start()
    first = dot(mats_ref[2 * seeds : back, :seeds], d_pre).astype(BF16)
    second = dot(aggregate, d_pre, 0, 0).astype(BF16)
    is_first = at_ref[1] == 0
    keep_ref[:width] = jnp.where(is_first, first, second)
    send_ref[:width] = jnp.where(is_first, second, first)
    high, low = split(jnp.sum(d_pre.astype(F32), 0, keepdims=True))
    pair = two_rows(high, low, keep_ref.shape[0] - width)
    keep_ref[width:] = pair
    send_ref[width:] = pair
    x_keep_ref[...] = dot(mats_ref[back : back + half, :seeds], d_agg)
    x_send_ref[...] = dot(mats_ref[back + half :, :seeds], d_agg).astype(BF16)
    kept.wait()


def two_rows(high, low, rows):
    row = iota((rows, high.shape[1]), 0)
    high, low = high.astype(F32), low.astype(F32)
    return jnp.where(row == 0, high, jnp.where(row == 1, low, 0.0)).astype(BF16)


def halve_kernel(keep_ref, other_ref, next_keep_ref, next_send_ref):
    half = next_keep_ref.shape[0]
    next_keep_ref[...] = keep_ref[:half] + other_ref[:half].astype(F32)
    next_send_ref[...] = (keep_ref[half:] + other_ref[half:].astype(F32)).astype(BF16)


def pair_sum_kernel(keep_ref, other_ref, send_ref):
    chunks, lines, width = send_ref.shape
    total = keep_ref[...].astype(F32) + other_ref[...].astype(F32)
    weight = width // chunks
    high, low = split(total[width : width + 1] + total[width + 1 : width + 2])
    pair = two_rows(high, low, lines - weight).astype(F32)
    for chunk in range(chunks):
        send_ref[chunk] = jnp.concatenate(
            [total[chunk * weight : (chunk + 1) * weight], pair], 0
        ).astype(BF16)


def plane_sum_kernel(arrived_ref, send_ref):
    chunks, lines, width = arrived_ref.shape
    depth, block, _ = send_ref.shape
    weight = width // chunks
    groups = width // LANES
    each = weight // depth
    total = arrived_ref[0].astype(F32)
    for chunk in range(1, chunks):
        total = total + arrived_ref[chunk].astype(F32)
    weights = total[:weight].astype(BF16)
    high, low = split(total[weight : weight + 1] + total[weight + 1 : weight + 2])
    pair = two_rows(high, low, 16)
    shape = (depth * block, weight)
    out, into = iota(shape, 0), iota(shape, 1)
    line, z = out % block, out // block
    pair_shape = (depth * block, 16)
    pair_line, pair_into = iota(pair_shape, 0) % block, iota(pair_shape, 1)
    weight_block = jnp.zeros((depth * block, LANES), F32)
    bias_block = jnp.zeros((depth * block, LANES), F32)
    for group in range(groups):
        lanes = slice(group * LANES, (group + 1) * LANES)
        here = jnp.logical_and(line // each == group, into == z * each + line % each)
        weight_block += dot(here.astype(BF16), weights[:, lanes])
        here = jnp.logical_and(pair_line // 2 == group, pair_into == pair_line % 2)
        bias_block += dot(here.astype(BF16), pair[:, lanes])
    send_ref[:, :, :LANES] = weight_block.astype(BF16).reshape(depth, block, LANES)
    send_ref[:, :, LANES:] = bias_block.astype(BF16).reshape(depth, block, LANES)


def weight_kernel(scale, arrived_ref, done_ref, bias_ref):
    total = jnp.sum(arrived_ref[...].astype(F32), 0) * scale
    done_ref[...] = total[:, :LANES]
    bias_ref[...] = total[:, LANES:]


def pack_kernel(done_ref, keep_ref, other_ref, send_ref):
    depth, block, lanes = send_ref.shape
    width = lanes - LANES
    back = (keep_ref[...] + other_ref[...].astype(F32)).astype(BF16)
    send_ref[:, :, :width] = back.reshape(depth, block, width)
    done = done_ref[...].astype(BF16)
    for z in range(depth):
        send_ref[z, :, width:] = done


def gather_kernel(arrived_ref, send_ref):
    chunks, lines, width = send_ref.shape
    depth, block, _ = arrived_ref.shape
    groups = width // LANES
    weight = width // chunks
    each = weight // depth
    total = depth * block
    arrived = arrived_ref[:, :, width:].reshape(total, LANES)
    shape = (weight, total)
    out, into = iota(shape, 0), iota(shape, 1)
    z, line = out // each, out % each
    whole = jnp.concatenate(
        [move(into == z * block + group * each + line, arrived) for group in range(groups)], 1
    )
    back = arrived_ref[:, :, :width].reshape(total, width)
    shape = (total, total)
    out, into = iota(shape, 0), iota(shape, 1)
    z, kind, y = out % depth, out // depth % 2, out // (2 * depth)
    moved = move(into == z * block + kind * Y_SIZE + y, back)
    for y_to in range(Y_SIZE):
        for x_to in range(X_SIZE):
            chunk = y_to * X_SIZE + x_to
            send_ref[chunk, :weight] = whole
            send_ref[chunk, weight:] = moved[y_to * 2 * depth : (y_to + 1) * 2 * depth]


def own_back_kernel(
    at_ref, dst_ref, src_ref, count_ref, tiles_ref, seeds_ref, d_both_ref, w_self_ref,
    keep_ref, send_ref, adj_ref, own_ref,
):
    rows = own_ref.shape[0]
    seeds = seeds_ref.shape[1]
    place_tiles(dst_ref, src_ref, count_ref, tiles_ref, adj_ref, 0, rows // BLK)
    picks = (iota((rows, seeds), 0) == seeds_ref[...]).astype(BF16)
    seeded = dot(picks, d_both_ref[0]).astype(BF16)
    own_ref[...] = dot(seeded, w_self_ref[...], 1, 1) + dot(adj_ref[...], d_both_ref[1], 0, 0)
    share = rows // (X_SIZE * CORES)
    for step in range(X_SIZE):
        keep = jnp.bitwise_xor(at_ref[0], step) * CORES + at_ref[1]
        send = jnp.bitwise_xor(keep, 1)
        keep_ref[step] = own_ref[pl.ds(pl.multiple_of(keep * share, 32), share), :]
        send_ref[step] = own_ref[pl.ds(pl.multiple_of(send * share, 32), share), :].astype(BF16)


def copy_kernel(from_ref, to_ref):
    to_ref[...] = from_ref[...]


def finish_kernel(
    at_ref, near_ref, far_ref, places_ref, own_ref, rows_ref, first_ref, second_ref,
):
    chunks, lines, width = near_ref.shape
    weight = width // chunks
    near, far = near_ref[:, :weight].reshape(width, width), far_ref[:, :weight].reshape(width, width)
    is_first = at_ref[1] == 0
    first_ref[...] = jnp.where(is_first, near, far)
    second_ref[...] = jnp.where(is_first, far, near)
    total = chunks * (lines - weight)
    rows_ref[...] = (
        own_ref[...]
        + dot(places_ref[0], near_ref[:, weight:].reshape(total, width))
        + dot(places_ref[1], far_ref[:, weight:].reshape(total, width))
    )


def body(
    feats,
    halo_index,
    seed_ids,
    tiles,
    tile_dst,
    tile_src,
    tile_count,
    w_self,
    w_neigh,
    bias,
    cotangent,
):
    depth = lax.axis_size("z")
    parts = depth * Y_SIZE
    reps = X_SIZE * CORES
    rows, width = feats.shape
    seeds = cotangent.shape[0]
    half = parts * SLOTS
    core_id = lax.axis_index("core").astype(jnp.int32)
    x_id = lax.axis_index("x").astype(jnp.int32)
    at = jnp.stack([x_id, core_id])
    rep = (x_id * CORES + core_id).reshape(1)
    lists = halo_index[0].T
    seed_row = seed_ids.reshape(1, seeds)
    tile_scalars = (tile_dst, tile_src, tile_count)
    scale = float(seeds * parts * reps) ** (-0.5)
    weight = width // PLANE
    share = rows // reps
    window = 20_000_000_000

    def swap(values, axis):
        return lax.all_to_all(values, axis, split_axis=0, concat_axis=0, tiled=True)

    def pair(values):
        return lax.ppermute(values, "core", [(0, 1), (1, 0)])

    def cross(values, step):
        return lax.ppermute(values, "x", [(x, x ^ step) for x in range(X_SIZE)])

    (send,) = call(
        send_kernel, "pick_boundary", [((2 * parts, width), BF16)], [rep], [], hbm=[lists, feats],
        scratch=fetched([lists, feats]), flops=4 * parts * rows * width, limit=FULL_VMEM_BYTES,
    )
    by_depth = swap(send.reshape(depth, 2 * Y_SIZE, width), "z").reshape(2 * parts, width)
    mats, sums, places = call(
        own_kernel, "own_rows",
        [
            ((2 * seeds + width + 2 * half, max(seeds, half)), BF16),
            ((2 * seeds, width), F32),
            ((CORES, share, half), BF16),
        ],
        [at, *tile_scalars],
        [tiles, feats, seed_row, w_self, bias.reshape(1, width), lists],
        scratch=[pltpu.VMEM((seeds, rows), BF16), pltpu.VMEM((seeds, 2 * half), BF16)],
        flops=2 * seeds * (3 * rows * width + width * width + 8 * half * half),
    )
    (plane,) = call(
        plane_kernel, "spread_plane", [((PLANE, 2 * depth, width), BF16)], [], [by_depth],
        flops=8 * parts * parts * width, after=[sums],
    )
    near = swap(plane, ("y", "x")).reshape(half, width)
    far = pair(near)

    out, keep, pair_send, x_keep, x_send, d_both = call(
        middle_kernel, "forward_backward",
        [
            ((seeds, width), BF16),
            ((width + 16, width), BF16),
            ((width + 16, width), BF16),
            ((half, width), F32),
            ((half, width), BF16),
        ],
        [at],
        [near, far, mats, sums, w_neigh, cotangent],
        hbm_outs=[((2, seeds, width), BF16)],
        scratch=[pltpu.VMEM((2, seeds, width), BF16), pltpu.SemaphoreType.DMA],
        flops=2 * seeds * width * (4 * half + 4 * width),
    )

    (plane_send,) = call(
        pair_sum_kernel, "sum_pair", [((PLANE, weight + 8, width), BF16)],
        [], [keep, pair(pair_send)],
    )
    plane_arrived = swap(plane_send, ("y", "x"))
    x_keep, x_send = call(
        halve_kernel, "halve_x", [((half // 2, width), F32), ((half // 2, width), BF16)],
        [], [x_keep, cross(x_send, 2)],
    )
    row_keep, row_send = call(
        own_back_kernel, "own_rows_back",
        [((X_SIZE, share, width), F32), ((X_SIZE, share, width), BF16)],
        [at, *tile_scalars], [tiles, seed_row, d_both, w_self],
        scratch=[pltpu.VMEM((seeds, rows), BF16), pltpu.VMEM((rows, width), F32)],
        flops=2 * seeds * width * 3 * rows,
    )
    (depth_send,) = call(
        plane_sum_kernel, "sum_plane", [((depth, 2 * Y_SIZE, 2 * LANES), BF16)],
        [], [plane_arrived], after=[x_send, row_send], flops=window,
    )
    depth_arrived = swap(depth_send, "z")
    core_keep, core_send = call(
        halve_kernel, "halve_core", [((half // 4, width), F32), ((half // 4, width), BF16)],
        [], [x_keep, cross(x_send, 1)],
    )
    weight_done, bias_rows = call(
        functools.partial(weight_kernel, scale), "sum_weights",
        [((2 * Y_SIZE, LANES), F32), ((2 * Y_SIZE, LANES), F32)],
        [], [depth_arrived], after=[core_send], flops=window,
    )

    (depth_send,) = call(
        pack_kernel, "pack_depth", [((depth, 2 * Y_SIZE, width + LANES), BF16)],
        [], [weight_done, core_keep, pair(core_send)],
    )
    depth_arrived = swap(depth_send, "z")
    row_pair = row_keep + pair(row_send).astype(F32)
    rows_out = row_pair[2:].astype(BF16)
    (plane_send,) = call(
        gather_kernel, "gather_depth", [((PLANE, weight + 2 * depth, width), BF16)],
        [], [depth_arrived], after=[rows_out], flops=window,
    )
    near = swap(plane_send, ("y", "x"))
    row_half = row_pair[:2] + cross(rows_out, 2).astype(F32)
    own = row_half[0] + cross(row_half[1].astype(BF16), 1).astype(F32)
    (near_send,) = call(
        copy_kernel, "hand_on", [(near.shape, BF16)], [], [near], after=[own]
    )
    input_grad, grad_self, grad_neigh = call(
        finish_kernel, "finish",
        [((share, width), F32), ((width, width), BF16), ((width, width), BF16)],
        [at], [near, pair(near_send), places, own],
        flops=4 * share * half * width,
    )
    groups = width // LANES
    grad_bias = bias_rows[: 2 * groups].reshape(groups, 2, LANES).sum(1).reshape(width)
    return (out, input_grad, grad_self, grad_neigh, grad_bias)


def solution(mesh):
    parts = mesh.shape["dom"]
    physical = Mesh(
        mesh.devices.reshape(parts // Y_SIZE, Y_SIZE, X_SIZE, CORES), ("z", "y", "x", "core")
    )
    dom = ("z", "y")
    every = ("z", "y", "x", "core")
    placed = (
        P(dom, None),
        P(dom, None, None),
        P(every),
        P(every, None, None),
        P(every, None),
        P(every, None),
        P(every),
        P(),
        P(),
        P(),
        P(every, None),
    )
    return jax.shard_map(
        body,
        mesh=physical,
        in_specs=placed,
        out_specs=(P(every, None), P(every, None), P(), P(), P()),
        check_vma=False,
    )
```

time: 154 us -> 176 us (1.14)
  blocking collectives: 57.3 us -> 17 us
  starting transfers between devices: 51.1 us -> 76.3 us
  waiting for transfers between devices: 19.4 us -> 41.2 us
  Pallas kernels: 13.8 us -> 22.6 us
  local copies, waits for them, and re-layouts: 8.18 us -> 13.9 us
    all_to_all x3 -> x1, blocking collectives: 57.3 us -> 17 us  [swap(): return lax.all_to_all(values, axis, split_axis=0, concat_axis=0, tiled=True)]
    all_to_all x3 -> x5, starting transfers between devices: 23.6 us -> 43.6 us  [swap(): return lax.all_to_all(values, axis, split_axis=0, concat_axis=0, tiled=True)]
    ppermute x2 -> x4, waiting for transfers between devices: 5.15 us -> 20.5 us  [cross(): return lax.ppermute(values, 'x', [(x, x ^ step) for x in range(X_SIZE)])]
    pallas_call x11 -> x14, Pallas kernels: 13.8 us -> 22.6 us  [call(): pl.pallas_call(kernel, out_shape=shapes, in_specs=[pl.BlockSpec(memory_sp...]
    ppermute x2 -> x4, starting transfers between devices: 5.81 us -> 13.8 us  [cross(): return lax.ppermute(values, 'x', [(x, x ^ step) for x in range(X_SIZE)])]
    unnamed x46 -> x44, local copies, waits for them, and re-layouts: 8.14 us -> 13.2 us
    all_to_all x3 -> x5, waiting for transfers between devices: 11.6 us -> 15.9 us  [swap(): return lax.all_to_all(values, axis, split_axis=0, concat_axis=0, tiled=True)]
    ppermute x4 -> x5, starting transfers between devices: 21.8 us -> 18.9 us  [pair(): return lax.ppermute(values, 'core', [(0, 1), (1, 0)])]
  transfers between devices with their start and end apart: 9 -> 14, of which waited for: 7 -> 8; matrix products, arithmetic and copies ran while one was open for 1% -> 1% of each run, Pallas kernels for 5% -> 7%
where the time goes in v4:
time: 176 us; the launch traced here: 174 us
  starting transfers between devices  76.3 us (43%)
  waiting for transfers between devices  41.2 us (23%)
  Pallas kernels  22.6 us (13%)
  blocking collectives  17 us (10%)
  local copies, waits for them, and re-layouts  13.9 us (8%)
    all_to_all x5, starting transfers between devices, swap(): return lax.all_to_all(values, axis, split_axis=0, concat_axis=0, tiled=True)  43.6 us
    pallas_call x14, Pallas kernels, call(): pl.pallas_call(kernel, out_shape=shapes, in_specs=[pl.BlockSpec(memory_sp...  22.6 us
    ppermute x4, waiting for transfers between devices, cross(): return lax.ppermute(values, 'x', [(x, x ^ step) for x in range(X_SIZE)])  20.5 us
    ppermute x5, starting transfers between devices, pair(): return lax.ppermute(values, 'core', [(0, 1), (1, 0)])  18.9 us
    all_to_all x1, blocking collectives, swap(): return lax.all_to_all(values, axis, split_axis=0, concat_axis=0, tiled=True)  17 us
    all_to_all x5, waiting for transfers between devices, swap(): return lax.all_to_all(values, axis, split_axis=0, concat_axis=0, tiled=True)  15.9 us
    ppermute x4, starting transfers between devices, cross(): return lax.ppermute(values, 'x', [(x, x ^ step) for x in range(X_SIZE)])  13.8 us
    unnamed x44, local copies, waits for them, and re-layouts  13.2 us
  transfers between devices with their start and end apart: 14, of which 8 were waited for; matrix products, arithmetic and copies ran while one was open for 1% of the time, Pallas kernels for 7%

profile of v4, /device:TPU:1, one launch (start us, length us, event | category | flops | bytes accessed | tf_op | source)
XLA Modules:
  0.0 173.6 jit_solution(2716080702109701603)
XLA Ops:
  0.6 2.1 %pick_boundary.1 = bf16[128,512]{1,0:T(8,128)(2,1)} custom-call(s32[1]{0:T(128)} %bitcast.2.rep_ref, s32[8,64]{1,0:T(8,128)} %bitcast.21, bf16[768,512]{1,0:T(8,128)(2,1)} %feats_ref.1), custom_call_target="tpu_custom_call" | custom-call | flops 100663296 | bytes 919552 | tf_op jit(solution)/shard_map/pick_boundary/pallas_call | solution.py:51
  2.8 15.8 %all-to-all-start = ((bf16[16,8,512]{2,1,0:T(8,128)(2,1)}), bf16[16,8,512]{2,1,0:T(8,128)(2,1)S(1)}, u32[]{:S(2)}, u32[]{:S(2)}) async-start(bf16[16,8,512]{2,1,0:T(8,128)(2,1)} %bitcast.26), calls=%async_computation | async-start | bytes 262144 | tf_op jit(solution)/shard_map/all_to_all | solution.py:403
  19.2 0.7 reshape.39.bias_ref
  19.9 1.1 copy-done
  21.1 0.7 copy-done.3
  21.8 1.0 copy-done.6
  22.8 1.0 copy-done.8
  23.8 0.7 copy-done.13
  24.5 0.7 copy-done.15
  25.2 0.7 copy-done.17
  25.8 6.5 %own_rows.1 = (bf16[2560,512]{1,0:T(8,128)(2,1)S(1)}, f32[1024,512]{1,0:T(8,128)S(1)}, bf16[2,96,512]{2,1,0:T(8,128)(2,1)S(1)}) custom-call(s32[2]{0:T(128)S(1)} %pad_add_fusion.at_ref, s32[1,14]{1,0:T(1,128)S(1)} %copy-done.15, s32[1,14]{1,0:T(1,128)S(1)} %copy-done.17, s32[1]{0:T(128)S(6)} %copy.16.count_ref, bf16[14,128,128]{2,1,0:T(8,128)(2,1)S(1)} %copy-done.8, ...), custom_call_target="tpu_custom_call" | custom-call | flops 3623878656 | bytes 6689792 | tf_op jit(solution)/shard_map/own_rows/pallas_call | solution.py:51
  32.3 1.5 copy-done.19
  34.0 17.0 %all_to_all.30 = bf16[16,32,512]{2,1,0:T(8,128)(2,1)S(1)} all-to-all(bf16[16,32,512]{2,1,0:T(8,128)(2,1)S(1)} %spread_plane.1), channel_id=1, replica_groups=mesh['z'=16,'y'=4,'x'=4,'core'=2] {'y','x'}, dimensions={0} | all-to-all | bytes 1048576 | tf_op jit(solution)/shard_map/all_to_all | solution.py:403
  51.0 4.1 %collective-permute-start = (bf16[512,512]{1,0:T(8,128)(2,1)S(1)}, bf16[512,512]{1,0:T(8,128)(2,1)S(1)}, u32[]{:S(2)}, u32[]{:S(2)}) collective-permute-start(bf16[512,512]{1,0:T(8,128)(2,1)S(1)} %bitcast.18), channel_id=1, source_target_pairs={{0,1},{1,0},{2,3},{3,2},{4,5},{5,4},{6,7},{7,6},{8,9},{9,8},{10,11... | collective-permute-start | bytes 1572872 | tf_op jit(solution)/shard_map/ppermute | solution.py:406
  55.1 1.5 collective-permute-done.far_ref
  56.6 5.1 %forward_backward.1 = (bf16[512,512]{1,0:T(8,128)(2,1)}, bf16[528,512]{1,0:T(8,128)(2,1)S(1)}, bf16[528,512]{1,0:T(8,128)(2,1)S(1)}, f32[512,512]{1,0:T(8,128)S(...) custom-call(s32[2]{0:T(128)S(1)} %pad_add_fusion.at_ref, bf16[512,512]{1,0:T(8,128)(2,1)S(1)} %bitcast.19, ...), custom_call_target="tpu_custom_call" | custom-call | flops 2147483648 | bytes 11042816 | tf_op jit(solution)/shard_map/forward_backward/pallas_call | solution.py:51
  61.8 2.4 %collective-permute-start.1 = (bf16[528,512]{1,0:T(8,128)(2,1)S(1)}, bf16[528,512]{1,0:T(8,128)(2,1)S(1)}, u32[]{:S(2)}, u32[]{:S(2)}) collective-permute-start(bf16[528,512]{1,0:T(8,128)(2,1)S(1)} %get-tuple-element.29), channel_id=1, source_target_pairs={{0,1},{1,0},{2,3},{3,2},{4,5},{5,4},{6,7},{7,6},{8,9},{9,8},{10,11... | collective-permute-start | bytes 1622024 | tf_op jit(solution)/shard_map/ppermute | solution.py:406
  64.2 1.5 collective-permute-done.1.other_ref
  65.7 1.0 sum_pair.1
  66.7 3.6 %all-to-all-start.2 = ((bf16[16,40,512]{2,1,0:T(8,128)(2,1)}), bf16[16,40,512]{2,1,0:T(8,128)(2,1)S(1)}, u32[]{:S(2)}, u32[]{:S(2)}) async-start(bf16[16,40,512]{2,1,0:T(8,128)(2,1)} %sum_pair.1), calls=%async_computation.2 | async-start | bytes 1310720 | tf_op jit(solution)/shard_map/all_to_all | solution.py:403
  70.3 4.7 %collective-permute-start.2 = (bf16[512,512]{1,0:T(8,128)(2,1)}, bf16[512,512]{1,0:T(8,128)(2,1)S(1)}, u32[]{:S(2)}, u32[]{:S(2)}) collective-permute-start(bf16[512,512]{1,0:T(8,128)(2,1)} %get-tuple-element.31), channel_id=1, source_target_pairs={{0,4},{2,6},{4,0},{6,2},{1,5},{3,7},{5,1},{7,3},{8,12},{10,14},{12... | collective-permute-start | bytes 1572872 | tf_op jit(solution)/shard_map/ppermute | solution.py:409
  75.0 1.0 copy-done.7
  76.0 1.0 copy-done.9
  77.1 1.2 copy-done.21
  78.3 2.2 %own_rows_back.1 = (f32[4,96,512]{2,1,0:T(8,128)S(1)}, bf16[4,96,512]{2,1,0:T(8,128)(2,1)S(1)}) custom-call(s32[2]{0:T(128)S(1)} %pad_add_fusion.at_ref, s32[1,14]{1,0:T(1,128)S(1)} %copy-done.16, s32[1,14]{1,0:T(1,128)S(1)} %copy-done.18, s32[1]{0:T(128)S(6)} %copy.16.count_ref, bf16[14,128,128]{2,1,0:T(8,128)(2,1)S(1)} %copy-done.9, ...), custom_call_target="tpu_custom_call" | custom-call | flops 1207959552 | bytes 3213312 | tf_op jit(solution)/shard_map/own_rows_back/pallas_call | solution.py:51
  80.5 0.7 copy-done.10
  81.2 10.8 %collective-permute-done.2.other_ref = bf16[512,512]{1,0:T(8,128)(2,1)S(1)} collective-permute-done((bf16[512,512]{1,0:T(8,128)(2,1)}, bf16[512,512]{1,0:T(8,128)(2,1)S(1)}, u32[]{:S(2)}, u32[]{:S(2)}) %collective-permute-start.2) | collective-permute-done | bytes 524320 | tf_op jit(solution)/shard_map/ppermute | solution.py:409
  92.0 0.8 halve_x.1
  92.8 0.8 copy-done.1
  93.6 2.2 %collective-permute-start.3 = (bf16[256,512]{1,0:T(8,128)(2,1)}, bf16[256,512]{1,0:T(8,128)(2,1)S(1)}, u32[]{:S(2)}, u32[]{:S(2)}) collective-permute-start(bf16[256,512]{1,0:T(8,128)(2,1)} %get-tuple-element.32.refs_1_), channel_id=1, source_target_pairs={{0,2},{2,0},{4,6},{6,4},{1,3},{3,1},{5,7},{7,5},{8,10},{10,8},{12,... | collective-permute-start | bytes 786440 | tf_op jit(solution)/shard_map/ppermute | solution.py:409
  95.8 1.0 copy-done.11
  96.8 0.9 sum_plane.1
  97.7 11.5 %all-to-all-start.3 = ((bf16[16,8,256]{2,1,0:T(8,128)(2,1)}), bf16[16,8,256]{2,1,0:T(8,128)(2,1)S(1)}, u32[]{:S(2)}, u32[]{:S(2)}) async-start(bf16[16,8,256]{2,1,0:T(8,128)(2,1)} %sum_plane.1), calls=%async_computation.3 | async-start | bytes 131072 | tf_op jit(solution)/shard_map/all_to_all | solution.py:403
  109.3 3.7 %collective-permute-start.5 = (bf16[4,96,512]{2,1,0:T(8,128)(2,1)S(1)}, bf16[4,96,512]{2,1,0:T(8,128)(2,1)S(1)}, u32[]{:S(2)}, u32[]{:S(2)}) collective-permute-start(bf16[4,96,512]{2,1,0:T(8,128)(2,1)S(1)} %copy-done.12), channel_id=1, source_target_pairs={{0,1},{1,0},{2,3},{3,2},{4,5},{5,4},{6,7},{7,6},{8,9},{9,8},{10,11... | collective-permute-start | bytes 1179656 | tf_op jit(solution)/shard_map/ppermute | solution.py:406
  113.0 1.9 %collective-permute-start.4 = (bf16[128,512]{1,0:T(8,128)(2,1)S(1)}, bf16[128,512]{1,0:T(8,128)(2,1)S(1)}, u32[]{:S(2)}, u32[]{:S(2)}) collective-permute-start(bf16[128,512]{1,0:T(8,128)(2,1)S(1)} %get-tuple-element.36.refs_1_), channel_id=1, source_target_pairs={{0,1},{1,0},{2,3},{3,2},{4,5},{5,4},{6,7},{7,6},{8,9},{9,8},{10,11... | collective-permute-start | bytes 393224 | tf_op jit(solution)/shard_map/ppermute | solution.py:406
  115.0 5.9 %all-to-all-done.3.refs_0_ = bf16[16,8,256]{2,1,0:T(8,128)(2,1)S(1)} async-done(((bf16[16,8,256]{2,1,0:T(8,128)(2,1)}), bf16[16,8,256]{2,1,0:T(8,128)(2,1)S(1)}, u32[]{:S(2)}, u32[]{:S(2)}) %all-to-all-start.3) | async-done | bytes 65568 | tf_op jit(solution)/shard_map/all_to_all | solution.py:403
  120.9 0.7 pack_depth.1
  121.6 7.1 %all-to-all-start.4 = ((bf16[16,8,640]{2,1,0:T(8,128)(2,1)}), bf16[16,8,640]{2,1,0:T(8,128)(2,1)S(1)}, u32[]{:S(2)}, u32[]{:S(2)}) async-start(bf16[16,8,640]{2,1,0:T(8,128)(2,1)} %pack_depth.1), calls=%async_computation.4 | async-start | bytes 327680 | tf_op jit(solution)/shard_map/all_to_all | solution.py:403
  128.9 3.7 %collective-permute-start.6 = (bf16[2,96,512]{2,1,0:T(8,128)(2,1)S(1)}, bf16[2,96,512]{2,1,0:T(8,128)(2,1)S(1)}, u32[]{:S(2)}, u32[]{:S(2)}) collective-permute-start(bf16[2,96,512]{2,1,0:T(8,128)(2,1)S(1)} %slice.30.refs_1_), channel_id=1, source_target_pairs={{0,4},{2,6},{4,0},{6,2},{1,5},{3,7},{5,1},{7,3},{8,12},{10,14},{12... | collective-permute-start | bytes 589832 | tf_op jit(solution)/shard_map/ppermute | solution.py:409
  132.6 8.8 %all-to-all-done.4.refs_0_ = bf16[16,8,640]{2,1,0:T(8,128)(2,1)S(1)} async-done(((bf16[16,8,640]{2,1,0:T(8,128)(2,1)}), bf16[16,8,640]{2,1,0:T(8,128)(2,1)S(1)}, u32[]{:S(2)}, u32[]{:S(2)}) %all-to-all-start.4) | async-done | bytes 163872 | tf_op jit(solution)/shard_map/all_to_all | solution.py:403
  141.4 1.2 gather_depth.1
  142.6 5.6 %all-to-all-start.5 = ((bf16[16,64,512]{2,1,0:T(8,128)(2,1)}), bf16[16,64,512]{2,1,0:T(8,128)(2,1)S(1)}, u32[]{:S(2)}, u32[]{:S(2)}) async-start(bf16[16,64,512]{2,1,0:T(8,128)(2,1)} %gather_depth.1), calls=%async_computation.5 | async-start | bytes 2097152 | tf_op jit(solution)/shard_map/all_to_all | solution.py:403
  148.4 3.3 %collective-permute-start.7 = (bf16[96,512]{1,0:T(8,128)(2,1)S(1)}, bf16[96,512]{1,0:T(8,128)(2,1)S(1)}, u32[]{:S(2)}, u32[]{:S(2)}) collective-permute-start(bf16[96,512]{1,0:T(8,128)(2,1)S(1)} %fusion.1), channel_id=1, source_target_pairs={{0,2},{2,0},{4,6},{6,4},{1,3},{3,1},{5,7},{7,5},{8,10},{10,8},{12,... | collective-permute-start | bytes 294920 | tf_op jit(solution)/shard_map/ppermute | solution.py:409
  151.6 9.7 %collective-permute-done.7 = bf16[96,512]{1,0:T(8,128)(2,1)S(1)} collective-permute-done((bf16[96,512]{1,0:T(8,128)(2,1)S(1)}, bf16[96,512]{1,0:T(8,128)(2,1)S(1)}, u32[]{:S(2)}, u32[]{:S(2)}) %collective-permute-start.7) | collective-permute-done | bytes 98336 | tf_op jit(solution)/shard_map/ppermute | solution.py:409
  161.4 1.2 all-to-all-done.5.refs_0_.near_ref
  162.6 6.8 %collective-permute-start.8 = (bf16[16,64,512]{2,1,0:T(8,128)(2,1)S(1)}, bf16[16,64,512]{2,1,0:T(8,128)(2,1)S(1)}, u32[]{:S(2)}, u32[]{:S(2)}) collective-permute-start(bf16[16,64,512]{2,1,0:T(8,128)(2,1)S(1)} %hand_on.1), channel_id=1, source_target_pairs={{0,1},{1,0},{2,3},{3,2},{4,5},{5,4},{6,7},{7,6},{8,9},{9,8},{10,11... | collective-permute-start | bytes 3145736 | tf_op jit(solution)/shard_map/ppermute | solution.py:406
  170.1 1.7 collective-permute-done.8.far_ref
  171.7 1.8 %finish.1 = (f32[96,512]{1,0:T(8,128)}, bf16[512,512]{1,0:T(8,128)(2,1)}, bf16[512,512]{1,0:T(8,128)(2,1)}) custom-call(s32[2]{0:T(128)S(1)} %pad_add_fusion.at_ref, bf16[16,64,512]{2,1,0:T(8,128)(2,1)S(1)} %all-to-all-done.5.refs_0_.near_ref, bf16[16,64,512]{2,1,0:T(8,128)(2,1)S(1)} %collective-permute-done.8.far_ref, ...), custom_call_target="tpu_custom_call" | custom-call | flops 100663296 | bytes 3735552 | tf_op jit(solution)/shard_map/finish/pallas_call | solution.py:51
  (47 shorter events, 1.3 us)
Async XLA Ops:
  2.8 31.0 %all-to-all-start = ((bf16[16,8,512]{2,1,0:T(8,128)(2,1)}), bf16[16,8,512]{2,1,0:T(8,128)(2,1)S(1)}, u32[]{:S(2)}, u32[]{:S(2)}) async-start(bf16[16,8,512]{2,1,0:T(8,128)(2,1)} %bitcast.26), calls=%async_computation | async-start | bytes 262144 | tf_op jit(solution)/shard_map/all_to_all | solution.py:403
  19.9 1.1 copy-start
  21.1 0.7 copy-start.3
  21.8 1.0 copy-start.6
  22.8 1.0 copy-start.8
  23.8 0.7 copy-start.13
  24.5 0.7 copy-start.15
  25.2 0.7 copy-start.17
  32.3 1.5 copy-start.19
  33.8 22.8 %copy-start.4 = (bf16[512,512]{1,0:T(8,128)(2,1)S(1)}, bf16[512,512]{1,0:T(8,128)(2,1)}, u32[]{:S(2)}) copy-start(bf16[512,512]{1,0:T(8,128)(2,1)} %w_neigh_ref.1) | copy-start | bytes 1572868
  33.8 22.8 %copy-start.5 = (bf16[512,512]{1,0:T(8,128)(2,1)S(1)}, bf16[512,512]{1,0:T(8,128)(2,1)}, u32[]{:S(2)}) copy-start(bf16[512,512]{1,0:T(8,128)(2,1)} %cot_ref.1) | copy-start | bytes 1572868
  33.8 22.8 %copy-start.20 = (bf16[2560,512]{1,0:T(8,128)(2,1)S(1)}, bf16[2560,512]{1,0:T(8,128)(2,1)}, u32[]{:S(2)}) copy-start(bf16[2560,512]{1,0:T(8,128)(2,1)} %copy-done.19) | copy-start | bytes 7864324
  51.0 5.6 %collective-permute-start = (bf16[512,512]{1,0:T(8,128)(2,1)S(1)}, bf16[512,512]{1,0:T(8,128)(2,1)S(1)}, u32[]{:S(2)}, u32[]{:S(2)}) collective-permute-start(bf16[512,512]{1,0:T(8,128)(2,1)S(1)} %bitcast.18), channel_id=1, source_target_pairs={{0,1},{1,0},{2,3},{3,2},{4,5},{5,4},{6,7},{7,6},{8,9},{9,8},{10,11... | collective-permute-start | bytes 1572872 | tf_op jit(solution)/shard_map/ppermute | solution.py:406
  61.7 13.3 %copy-start.14 = (s32[512]{0:T(512)S(1)}, s32[512]{0:T(512)}, u32[]{:S(2)}) copy-start(s32[512]{0:T(512)} %param.13) | copy-start | bytes 6148
  61.7 13.2 %copy-start.16 = (s32[1,14]{1,0:T(1,128)S(1)}, s32[1,14]{1,0:T(1,128)}, u32[]{:S(2)}) copy-start(s32[1,14]{1,0:T(1,128)} %dst_ref.3) | copy-start | bytes 172
  61.7 13.2 %copy-start.18 = (s32[1,14]{1,0:T(1,128)S(1)}, s32[1,14]{1,0:T(1,128)}, u32[]{:S(2)}) copy-start(s32[1,14]{1,0:T(1,128)} %src_ref.3) | copy-start | bytes 172
  61.8 4.0 %collective-permute-start.1 = (bf16[528,512]{1,0:T(8,128)(2,1)S(1)}, bf16[528,512]{1,0:T(8,128)(2,1)S(1)}, u32[]{:S(2)}, u32[]{:S(2)}) collective-permute-start(bf16[528,512]{1,0:T(8,128)(2,1)S(1)} %get-tuple-element.29), channel_id=1, source_target_pairs={{0,1},{1,0},{2,3},{3,2},{4,5},{5,4},{6,7},{7,6},{8,9},{9,8},{10,11... | collective-permute-start | bytes 1622024 | tf_op jit(solution)/shard_map/ppermute | solution.py:406
  66.7 29.1 %all-to-all-start.2 = ((bf16[16,40,512]{2,1,0:T(8,128)(2,1)}), bf16[16,40,512]{2,1,0:T(8,128)(2,1)S(1)}, u32[]{:S(2)}, u32[]{:S(2)}) async-start(bf16[16,40,512]{2,1,0:T(8,128)(2,1)} %sum_pair.1), calls=%async_computation.2 | async-start | bytes 1310720 | tf_op jit(solution)/shard_map/all_to_all | solution.py:403
  70.3 21.7 %collective-permute-start.2 = (bf16[512,512]{1,0:T(8,128)(2,1)}, bf16[512,512]{1,0:T(8,128)(2,1)S(1)}, u32[]{:S(2)}, u32[]{:S(2)}) collective-permute-start(bf16[512,512]{1,0:T(8,128)(2,1)} %get-tuple-element.31), channel_id=1, source_target_pairs={{0,4},{2,6},{4,0},{6,2},{1,5},{3,7},{5,1},{7,3},{8,12},{10,14},{12... | collective-permute-start | bytes 1572872 | tf_op jit(solution)/shard_map/ppermute | solution.py:409
  75.0 1.0 copy-start.7
  76.0 1.0 copy-start.9
  77.1 1.2 copy-start.21
  80.5 0.7 copy-start.10
  92.8 0.8 copy-start.1
  93.6 19.4 %collective-permute-start.3 = (bf16[256,512]{1,0:T(8,128)(2,1)}, bf16[256,512]{1,0:T(8,128)(2,1)S(1)}, u32[]{:S(2)}, u32[]{:S(2)}) collective-permute-start(bf16[256,512]{1,0:T(8,128)(2,1)} %get-tuple-element.32.refs_1_), channel_id=1, source_target_pairs={{0,2},{2,0},{4,6},{6,4},{1,3},{3,1},{5,7},{7,5},{8,10},{10,8},{12,... | collective-permute-start | bytes 786440 | tf_op jit(solution)/shard_map/ppermute | solution.py:409
  95.8 1.0 copy-start.11
  96.8 12.5 %copy-start.12 = (bf16[4,96,512]{2,1,0:T(8,128)(2,1)S(1)}, bf16[4,96,512]{2,1,0:T(8,128)(2,1)}, u32[]{:S(2)}) copy-start(bf16[4,96,512]{2,1,0:T(8,128)(2,1)} %copy-done.10) | copy-start | bytes 1179652
  96.8 16.2 %copy-start.2 = (f32[256,512]{1,0:T(8,128)S(1)}, f32[256,512]{1,0:T(8,128)}, u32[]{:S(2)}) copy-start(f32[256,512]{1,0:T(8,128)} %copy-done.1) | copy-start | bytes 1572868
  97.7 23.1 %all-to-all-start.3 = ((bf16[16,8,256]{2,1,0:T(8,128)(2,1)}), bf16[16,8,256]{2,1,0:T(8,128)(2,1)S(1)}, u32[]{:S(2)}, u32[]{:S(2)}) async-start(bf16[16,8,256]{2,1,0:T(8,128)(2,1)} %sum_plane.1), calls=%async_computation.3 | async-start | bytes 131072 | tf_op jit(solution)/shard_map/all_to_all | solution.py:403
  109.3 19.4 %collective-permute-start.5 = (bf16[4,96,512]{2,1,0:T(8,128)(2,1)S(1)}, bf16[4,96,512]{2,1,0:T(8,128)(2,1)S(1)}, u32[]{:S(2)}, u32[]{:S(2)}) collective-permute-start(bf16[4,96,512]{2,1,0:T(8,128)(2,1)S(1)} %copy-done.12), channel_id=1, source_target_pairs={{0,1},{1,0},{2,3},{3,2},{4,5},{5,4},{6,7},{7,6},{8,9},{9,8},{10,11... | collective-permute-start | bytes 1179656 | tf_op jit(solution)/shard_map/ppermute | solution.py:406
  113.0 7.8 %collective-permute-start.4 = (bf16[128,512]{1,0:T(8,128)(2,1)S(1)}, bf16[128,512]{1,0:T(8,128)(2,1)S(1)}, u32[]{:S(2)}, u32[]{:S(2)}) collective-permute-start(bf16[128,512]{1,0:T(8,128)(2,1)S(1)} %get-tuple-element.36.refs_1_), channel_id=1, source_target_pairs={{0,1},{1,0},{2,3},{3,2},{4,5},{5,4},{6,7},{7,6},{8,9},{9,8},{10,11... | collective-permute-start | bytes 393224 | tf_op jit(solution)/shard_map/ppermute | solution.py:406
  121.6 19.8 %all-to-all-start.4 = ((bf16[16,8,640]{2,1,0:T(8,128)(2,1)}), bf16[16,8,640]{2,1,0:T(8,128)(2,1)S(1)}, u32[]{:S(2)}, u32[]{:S(2)}) async-start(bf16[16,8,640]{2,1,0:T(8,128)(2,1)} %pack_depth.1), calls=%async_computation.4 | async-start | bytes 327680 | tf_op jit(solution)/shard_map/all_to_all | solution.py:403
  128.9 19.4 %collective-permute-start.6 = (bf16[2,96,512]{2,1,0:T(8,128)(2,1)S(1)}, bf16[2,96,512]{2,1,0:T(8,128)(2,1)S(1)}, u32[]{:S(2)}, u32[]{:S(2)}) collective-permute-start(bf16[2,96,512]{2,1,0:T(8,128)(2,1)S(1)} %slice.30.refs_1_), channel_id=1, source_target_pairs={{0,4},{2,6},{4,0},{6,2},{1,5},{3,7},{5,1},{7,3},{8,12},{10,14},{12... | collective-permute-start | bytes 589832 | tf_op jit(solution)/shard_map/ppermute | solution.py:409
  142.6 19.9 %all-to-all-start.5 = ((bf16[16,64,512]{2,1,0:T(8,128)(2,1)}), bf16[16,64,512]{2,1,0:T(8,128)(2,1)S(1)}, u32[]{:S(2)}, u32[]{:S(2)}) async-start(bf16[16,64,512]{2,1,0:T(8,128)(2,1)} %gather_depth.1), calls=%async_computation.5 | async-start | bytes 2097152 | tf_op jit(solution)/shard_map/all_to_all | solution.py:403
  148.4 13.0 %collective-permute-start.7 = (bf16[96,512]{1,0:T(8,128)(2,1)S(1)}, bf16[96,512]{1,0:T(8,128)(2,1)S(1)}, u32[]{:S(2)}, u32[]{:S(2)}) collective-permute-start(bf16[96,512]{1,0:T(8,128)(2,1)S(1)} %fusion.1), channel_id=1, source_target_pairs={{0,2},{2,0},{4,6},{6,4},{1,3},{3,1},{5,7},{7,5},{8,10},{10,8},{12,... | collective-permute-start | bytes 294920 | tf_op jit(solution)/shard_map/ppermute | solution.py:409
  162.6 9.1 %collective-permute-start.8 = (bf16[16,64,512]{2,1,0:T(8,128)(2,1)S(1)}, bf16[16,64,512]{2,1,0:T(8,128)(2,1)S(1)}, u32[]{:S(2)}, u32[]{:S(2)}) collective-permute-start(bf16[16,64,512]{2,1,0:T(8,128)(2,1)S(1)} %hand_on.1), channel_id=1, source_target_pairs={{0,1},{1,0},{2,3},{3,2},{4,5},{5,4},{6,7},{7,6},{8,9},{9,8},{10,11... | collective-permute-start | bytes 3145736 | tf_op jit(solution)/shard_map/ppermute | solution.py:406

commit v5 on v3

--- a/solution.py
+++ b/solution.py
@@ -1,4 +1,5 @@
 import functools
+import math
 
 import jax
 import jax.numpy as jnp
@@ -18,6 +19,7 @@
 BF16 = jnp.bfloat16
 F32 = jnp.float32
 VMEM_BYTES = 24 * 1024 * 1024
+FULL_VMEM_BYTES = 65 * 1000 * 1024
 
 
 def dot(a, b, contract_a=1, contract_b=0):
@@ -39,24 +41,43 @@
     return high, (wide - high.astype(F32)).astype(BF16)
 
 
-def call(kernel, name, outs, scalars, arrays, scratch=(), flops=0, after=(), space=pltpu.VMEM):
+def call(kernel, name, outs, scalars, arrays, scratch=(), flops=0, after=(), hbm=(), hbm_outs=(), limit=VMEM_BYTES):
     if after:
-        inner, at = kernel, len(scalars) + len(arrays)
+        inner, at = kernel, len(scalars) + len(arrays) + len(hbm)
         kernel = lambda *refs: inner(*refs[:at], *refs[at + len(after) :])
     shapes = tuple(jax.ShapeDtypeStruct(shape, dtype) for shape, dtype in outs)
-    size = sum(a.size * a.dtype.itemsize for a in (*arrays, *shapes))
+    shapes += tuple(pltpu.HBM(shape, dtype) for shape, dtype in hbm_outs)
+    size = sum(math.prod(a.shape) * a.dtype.itemsize for a in (*arrays, *hbm, *shapes))
     return pl.pallas_call(
         kernel,
         out_shape=shapes,
         in_specs=[pl.BlockSpec(memory_space=pltpu.SMEM)] * len(scalars)
-        + [pl.BlockSpec(memory_space=space)] * len(arrays)
+        + [pl.BlockSpec(memory_space=pltpu.VMEM)] * len(arrays)
+        + [pl.BlockSpec(memory_space=pltpu.HBM)] * len(hbm)
         + [pl.BlockSpec(memory_space=pl.ANY)] * len(after),
-        out_specs=tuple(pl.BlockSpec(memory_space=pltpu.VMEM) for _ in outs),
+        out_specs=tuple([pl.BlockSpec(memory_space=pltpu.VMEM)] * len(outs))
+        + tuple([pl.BlockSpec(memory_space=pltpu.HBM)] * len(hbm_outs)),
         scratch_shapes=list(scratch),
-        compiler_params=pltpu.CompilerParams(vmem_limit_bytes=VMEM_BYTES),
+        compiler_params=pltpu.CompilerParams(vmem_limit_bytes=limit),
         cost_estimate=pl.CostEstimate(flops=flops, bytes_accessed=size, transcendentals=0),
         name=name,
-    )(*scalars, *arrays, *after)
+    )(*scalars, *arrays, *hbm, *after)
+
+
+def fetched(arrays):
+    return [pltpu.VMEM(a.shape, a.dtype) for a in arrays] + [
+        pltpu.SemaphoreType.DMA((len(arrays),))
+    ]
+
+
+def fetch(from_refs, to_refs, sems):
+    copies = [
+        pltpu.make_async_copy(source, to, sems.at[at])
+        for at, (source, to) in enumerate(zip(from_refs, to_refs))
+    ]
+    for copy in copies:
+        copy.start()
+    return copies
 
 
 def place_tiles(dst_ref, src_ref, count_ref, tiles_ref, adj_ref, first, last):
@@ -76,7 +97,7 @@
     lax.fori_loop(0, count_ref[0], step, 0)
 
 
-def boundary_places(rep, lists_ref, rows):
+def boundary_places(rep, lists_ref, rows, order):
     slots, parts = lists_ref.shape
     lists = lists_ref[...].astype(F32)
     wanted = jnp.sum(
@@ -84,7 +105,7 @@
     ).astype(jnp.int32)
     place = iota((rows, parts), 0)
     places = jnp.concatenate([(place == wanted).astype(BF16), (place == rep).astype(BF16)], 1)
-    return dot(places, by_z(parts).astype(BF16), 1, 1).astype(BF16)
+    return dot(places, order.astype(BF16), 1, 1).astype(BF16)
 
 
 def by_z(parts):
@@ -94,13 +115,20 @@
     return into == kind * parts + z * Y_SIZE + y
 
 
+def summed_by_z(parts):
+    shape = (2 * parts, 2 * parts)
+    out, into = iota(shape, 0), iota(shape, 1)
+    line, z = out % (2 * Y_SIZE), out // (2 * Y_SIZE)
+    halo = jnp.logical_and(line < Y_SIZE, into == z * Y_SIZE + line)
+    hub = jnp.logical_and(line == Y_SIZE, into == parts)
+    return jnp.logical_or(halo, hub)
+
+
 def send_kernel(rep_ref, lists_hbm, feats_hbm, send_ref, lists_ref, feats_ref, sems):
-    lists_copy = pltpu.make_async_copy(lists_hbm, lists_ref, sems.at[0])
-    feats_copy = pltpu.make_async_copy(feats_hbm, feats_ref, sems.at[1])
-    lists_copy.start()
-    feats_copy.start()
+    lists_copy, feats_copy = fetch((lists_hbm, feats_hbm), (lists_ref, feats_ref), sems)
     lists_copy.wait()
-    places = boundary_places(rep_ref[0], lists_ref, feats_ref.shape[0])
+    parts = lists_ref.shape[1]
+    places = boundary_places(rep_ref[0], lists_ref, feats_ref.shape[0], by_z(parts))
     feats_copy.wait()
     send_ref[...] = dot(places, feats_ref[...], 0, 0).astype(BF16)
 
@@ -120,8 +148,7 @@
 
 def own_kernel(
     core_ref, dst_ref, src_ref, count_ref, tiles_ref, feats_ref, seeds_ref, w_self_ref, bias_ref,
-    chosen_t_ref, preact_ref, part_ref, near_ref, near_t_ref, far_ref, far_t_ref,
-    own_adj_ref, adj_ref,
+    mats_ref, sums_ref, own_adj_ref, adj_ref,
 ):
     rows = feats_ref.shape[0]
     seeds = seeds_ref.shape[1]
@@ -133,10 +160,10 @@
     )
     picks = (iota((rows, seeds), 0) == seeds_ref[...]).astype(BF16)
     feats = feats_ref[...]
-    chosen_t_ref[...] = dot(feats, picks, 0, 0).astype(BF16)
+    mats_ref[2 * seeds + adj_ref.shape[1] :, :seeds] = dot(feats, picks, 0, 0).astype(BF16)
     chosen = dot(picks, feats, 0, 0).astype(BF16)
-    preact_ref[...] = dot(chosen, w_self_ref[...]) + bias_ref[...].astype(F32)
-    part_ref[...] = dot(own_adj_ref[...], feats)
+    sums_ref[:seeds] = dot(chosen, w_self_ref[...]) + bias_ref[...].astype(F32)
+    sums_ref[seeds:] = dot(own_adj_ref[...], feats)
     adj = adj_ref[...]
     half = table // 2
     depth = half // PLANE // 2
@@ -145,41 +172,40 @@
     z, kind = line % depth, line // depth % 2
     x, y = line // (2 * depth) % X_SIZE, line // (2 * depth * X_SIZE)
     start = kind * half + (z * Y_SIZE + y) * SLOTS + x * CORES
-    for core, to_ref, to_t_ref in (
-        (core_ref[0], near_ref, near_t_ref),
-        (1 - core_ref[0], far_ref, far_t_ref),
-    ):
+    for far, core in enumerate((core_ref[0], 1 - core_ref[0])):
         order = (source == start + core).astype(BF16)
-        to_ref[...] = dot(adj, order, 1, 1).astype(BF16)
-        to_t_ref[...] = dot(order, adj, 1, 1).astype(BF16)
+        mats_ref[far * seeds : (far + 1) * seeds, :half] = dot(adj, order, 1, 1).astype(BF16)
+        first = 2 * seeds + far * half
+        mats_ref[first : first + half, :seeds] = dot(order, adj, 1, 1).astype(BF16)
 
 
 def middle_kernel(
-    core_ref, near_ref, far_ref, near_adj_ref, near_adj_t_ref, far_adj_ref, far_adj_t_ref,
-    chosen_t_ref, preact_ref, part_ref, w_neigh_ref, cot_ref,
+    core_ref, near_ref, far_ref, mats_ref, sums_ref, w_neigh_ref, cot_ref,
     out_ref, d_pre_ref, d_agg_ref, keep_ref, send_ref,
 ):
     width = w_neigh_ref.shape[0]
     half = near_ref.shape[0]
+    seeds = cot_ref.shape[0]
+    near_back, far_back, chosen_t = (2 * seeds + step * half for step in range(3))
     aggregate = (
-        part_ref[...]
-        + dot(near_adj_ref[...], near_ref[...])
-        + dot(far_adj_ref[...], far_ref[...])
+        sums_ref[seeds:]
+        + dot(mats_ref[:seeds, :half], near_ref[...])
+        + dot(mats_ref[seeds : 2 * seeds, :half], far_ref[...])
     ).astype(BF16)
-    preact = preact_ref[...] + dot(aggregate, w_neigh_ref[...])
+    preact = sums_ref[:seeds] + dot(aggregate, w_neigh_ref[...])
     gate = jax.nn.sigmoid(preact)
     out_ref[...] = (preact * gate).astype(BF16)
     d_pre = (cot_ref[...].astype(F32) * gate * (1.0 + preact * (1.0 - gate))).astype(BF16)
     d_pre_ref[...] = d_pre
     d_agg = dot(d_pre, w_neigh_ref[...], 1, 1).astype(BF16)
     d_agg_ref[...] = d_agg
-    first = dot(chosen_t_ref[...], d_pre).astype(BF16)
+    first = dot(mats_ref[chosen_t:, :seeds], d_pre).astype(BF16)
     second = dot(aggregate, d_pre, 0, 0).astype(BF16)
     is_first = core_ref[0] == 0
     keep_ref[:width] = jnp.where(is_first, first, second)
     send_ref[:width] = jnp.where(is_first, second, first)
-    keep_ref[width : width + half] = dot(near_adj_t_ref[...], d_agg).astype(BF16)
-    send_ref[width : width + half] = dot(far_adj_t_ref[...], d_agg).astype(BF16)
+    keep_ref[width : width + half] = dot(mats_ref[near_back:far_back, :seeds], d_agg).astype(BF16)
+    send_ref[width : width + half] = dot(mats_ref[far_back:chosen_t, :seeds], d_agg).astype(BF16)
     high, low = split(jnp.sum(d_pre.astype(F32), 0, keepdims=True))
     row = iota((keep_ref.shape[0] - width - half, width), 0)
     pair = jnp.where(
@@ -210,58 +236,48 @@
 
 def plane_sum_kernel(arrived_ref, send_ref):
     chunks, lines, width = arrived_ref.shape
-    depth = send_ref.shape[0]
-    block = send_ref.shape[1]
+    depth, block, _ = send_ref.shape
     weight = width // chunks
-    table = lines - 8 - weight
-    groups = width // LANES
     each = weight // depth
-    by_y = []
+    tail = weight + 2 * depth
+    rows = []
     rest = None
     for y in range(Y_SIZE):
         some = arrived_ref[y * X_SIZE].astype(F32)
         for x in range(1, X_SIZE):
             some = some + arrived_ref[y * X_SIZE + x].astype(F32)
-        by_y.append(some[weight : weight + table].astype(BF16))
+        rows.append(some[weight : weight + depth])
         rest = some if rest is None else rest + some
-    back = jnp.concatenate(by_y, 0)
-    shape = (depth * block, Y_SIZE * table)
-    out, into = iota(shape, 0), iota(shape, 1)
-    y, kind, z = out % Y_SIZE, out // Y_SIZE % 2, out // block
-    moved = move(into == y * table + kind * depth + z, back)
-    send_ref[:, :, :width] = moved.reshape(depth, block, width)
-
-    weights = rest[:weight].astype(BF16)
-    high, low = split(rest[weight + table : weight + table + 1] + rest[weight + table + 1 : weight + table + 2])
-    pair_row = iota((16, width), 0)
-    pair = jnp.where(
-        pair_row == 0, high.astype(F32), jnp.where(pair_row == 1, low.astype(F32), 0.0)
-    ).astype(BF16)
-    shape = (depth * block, weight)
+    bias = jnp.zeros((depth, width), F32) + jnp.sum(rest[tail:], 0, keepdims=True)
+    rows += [rest[weight + depth : tail], rest[:weight], bias]
+    rows = jnp.concatenate(rows, 0).astype(BF16)
+    shape = (depth * block, rows.shape[0])
     out, into = iota(shape, 0), iota(shape, 1)
     line, z = out % block, out // block
-    pair_shape = (depth * block, 16)
-    pair_line, pair_into = iota(pair_shape, 0) % block, iota(pair_shape, 1)
-    weight_block = jnp.zeros((depth * block, LANES), F32)
-    bias_block = jnp.zeros((depth * block, LANES), F32)
-    for group in range(groups):
-        lanes = slice(group * LANES, (group + 1) * LANES)
-        here = jnp.logical_and(line // each == group, into == z * each + line % each)
-        weight_block += dot(here.astype(BF16), weights[:, lanes])
-        here = jnp.logical_and(pair_line // 2 == group, pair_into == pair_line % 2)
-        bias_block += dot(here.astype(BF16), pair[:, lanes])
-    send_ref[:, :, width : width + LANES] = weight_block.astype(BF16).reshape(depth, block, LANES)
-    send_ref[:, :, width + LANES :] = bias_block.astype(BF16).reshape(depth, block, LANES)
+    first = (Y_SIZE + 1) * depth
+    of_weight = jnp.logical_and(line > Y_SIZE, line <= Y_SIZE + each)
+    wanted = jnp.where(
+        of_weight,
+        first + z * each + line - Y_SIZE - 1,
+        jnp.where(line <= Y_SIZE, line * depth, first + weight) + z,
+    )
+    send_ref[...] = move(into == wanted, rows).reshape(depth, block, width)
 
 
 def weight_kernel(scale, arrived_ref, send_ref, bias_ref):
-    depth, block, _ = arrived_ref.shape
-    width = arrived_ref.shape[2] - 2 * LANES
-    total = jnp.sum(arrived_ref[:, :, width:].astype(F32), 0) * scale
-    done = total[:, :LANES].astype(BF16)
+    depth, block, width = arrived_ref.shape
+    total = jnp.sum(arrived_ref[...].astype(F32), 0) * scale
+    each = block - Y_SIZE - 2
+    row = iota((block, LANES), 0)
+    done = jnp.zeros((block, LANES), F32)
+    for group in range(width // LANES):
+        for line in range(each):
+            some = total[Y_SIZE + 1 + line : Y_SIZE + 2 + line, group * LANES : (group + 1) * LANES]
+            done = jnp.where(row == group * each + line, some, done)
+    done = done.astype(BF16)
     for z in range(depth):
         send_ref[z] = done
-    bias_ref[...] = total[:, LANES:]
+    bias_ref[...] = total[block - 1 :]
 
 
 def gather_kernel(arrived_ref, send_ref):
@@ -296,8 +312,8 @@
 def scatter_kernel(rep_ref, lists_ref, arrived_ref, own_ref, keep_ref, send_ref, total_ref):
     rows, width = own_ref.shape
     rep = rep_ref[0]
-    places = boundary_places(rep, lists_ref, rows)
-    back = arrived_ref[:, :, :width].reshape(places.shape[1], width)
+    places = boundary_places(rep, lists_ref, rows, summed_by_z(lists_ref.shape[1]))
+    back = arrived_ref[...].reshape(places.shape[1], width)
     total_ref[...] = (own_ref[...] + dot(places, back)).astype(BF16)
     share = rows // (X_SIZE * CORES)
     for step in range(X_SIZE):
@@ -345,26 +361,15 @@
         return lax.ppermute(values, "core", [(0, 1), (1, 0)])
 
     (send,) = call(
-        send_kernel, "pick_boundary", [((2 * parts, width), BF16)], [rep], [lists, feats],
-        scratch=[
-            pltpu.VMEM(lists.shape, jnp.int32),
-            pltpu.VMEM(feats.shape, BF16),
-            pltpu.SemaphoreType.DMA((2,)),
-        ],
-        space=pl.ANY,
-        flops=4 * parts * rows * width,
+        send_kernel, "pick_boundary", [((2 * parts, width), BF16)], [rep], [], hbm=[lists, feats],
+        scratch=fetched([lists, feats]), flops=4 * parts * rows * width, limit=FULL_VMEM_BYTES,
     )
     by_depth = swap(send.reshape(depth, 2 * Y_SIZE, width), "z").reshape(2 * parts, width)
-    chosen_t, preact, part, near_adj, near_adj_t, far_adj, far_adj_t = call(
+    mats, sums = call(
         own_kernel, "own_rows",
         [
-            ((width, seeds), BF16),
-            ((seeds, width), F32),
-            ((seeds, width), F32),
-            ((seeds, half), BF16),
-            ((half, seeds), BF16),
-            ((seeds, half), BF16),
-            ((half, seeds), BF16),
+            ((2 * (seeds + half) + width, max(seeds, half)), BF16),
+            ((2 * seeds, width), F32),
         ],
         [core, *tile_scalars],
         [tiles, feats, seed_row, w_self, bias.reshape(1, width)],
@@ -374,7 +379,7 @@
 
     (plane,) = call(
         plane_kernel, "spread_plane", [((PLANE, 2 * depth, width), BF16)], [], [by_depth],
-        flops=8 * parts * parts * width, after=[part],
+        flops=8 * parts * parts * width, after=[sums],
     )
     near = swap(plane, ("y", "x")).reshape(half, width)
     far = pair(near)
@@ -390,8 +395,7 @@
         ],
         [core],
         [
-            near, far, near_adj, near_adj_t, far_adj, far_adj_t,
-            chosen_t, preact, part, w_neigh, cotangent,
+            near, far, mats, sums, w_neigh, cotangent,
         ],
         flops=2 * seeds * width * (4 * half + 4 * width),
     )
@@ -411,13 +415,13 @@
     plane_arrived = swap(plane_send, ("y", "x"))
     (depth_send,) = call(
         plane_sum_kernel, "sum_plane",
-        [((depth, 2 * Y_SIZE, width + 2 * LANES), BF16)],
+        [((depth, 2 * Y_SIZE, width), BF16)],
         [], [plane_arrived],
     )
     depth_arrived = swap(depth_send, "z")
-    weight_send, bias_rows = call(
+    weight_send, bias_row = call(
         functools.partial(weight_kernel, scale), "sum_weights",
-        [((depth, 2 * Y_SIZE, LANES), BF16), ((2 * Y_SIZE, LANES), F32)],
+        [((depth, 2 * Y_SIZE, LANES), BF16), ((1, width), F32)],
         [], [depth_arrived],
     )
     weight_depth = swap(weight_send, "z")
@@ -434,22 +438,20 @@
     (weight_plane,) = call(
         gather_kernel, "gather_weights",
         [((PLANE, width // PLANE, width), BF16)],
-        [], [weight_depth], after=[rows_out], flops=20_000_000_000,
+        [], [weight_depth], flops=20_000_000_000,
     )
     weight_near = swap(weight_plane, ("y", "x")).reshape(width, width)
-    far_half = lax.ppermute(rows_out[2:], "x", [(x, x ^ 2) for x in range(X_SIZE)])
-    row_half = row_pair[:2] + far_half.astype(F32)
-    beside = lax.ppermute(row_half[1].astype(BF16), "x", [(x, x ^ 1) for x in range(X_SIZE)])
-    input_grad = row_half[0] + beside.astype(F32)
+    input_grad = row_pair[0]
+    for step in range(1, X_SIZE):
+        beside = lax.ppermute(rows_out[step], "x", [(x, x ^ step) for x in range(X_SIZE)])
+        input_grad = input_grad + beside.astype(F32)
     (weight_send,) = call(
         copy_kernel, "hand_on", [((width, width), BF16)], [], [weight_near], after=[input_grad]
     )
     weight_far = pair(weight_send)
     grad_self = jnp.where(core_id == 0, weight_near, weight_far)
     grad_neigh = jnp.where(core_id == 0, weight_far, weight_near)
-    groups = width // LANES
-    grad_bias = bias_rows[: 2 * groups].reshape(groups, 2, LANES).sum(1).reshape(width)
-
+    grad_bias = bias_row.reshape(width)
     return (out, input_grad, grad_self, grad_neigh, grad_bias)
 
 

time: 154 us -> 150 us (0.974)
  local copies, waits for them, and re-layouts: 8.18 us -> 3.73 us
  starting transfers between devices: 51.1 us -> 53.7 us
  blocking collectives: 57.3 us -> 55.6 us
    unnamed x46 -> x28, local copies, waits for them, and re-layouts: 8.14 us -> 3.71 us
    ppermute x2 -> x3, starting transfers between devices: 5.81 us -> 9.58 us  [body(): lax.ppermute(rows_out[step], 'x', [(x, x ^ step) for x in range(X_SIZE)])]
    ppermute x4, starting transfers between devices: 21.8 us -> 19.3 us  [pair(): return lax.ppermute(values, 'core', [(0, 1), (1, 0)])]
    all_to_all x3, waiting for transfers between devices: 11.6 us -> 9.47 us  [swap(): return lax.all_to_all(values, axis, split_axis=0, concat_axis=0, tiled=True)]
    all_to_all x3, blocking collectives: 57.3 us -> 55.6 us  [swap(): return lax.all_to_all(values, axis, split_axis=0, concat_axis=0, tiled=True)]
    ppermute x2 -> x3, waiting for transfers between devices: 5.15 us -> 5.6 us  [body(): lax.ppermute(rows_out[step], 'x', [(x, x ^ step) for x in range(X_SIZE)])]
  transfers between devices with their start and end apart: 9 -> 10, of which waited for: 7 -> 7; matrix products, arithmetic and copies ran while one was open for 1% -> 0% of each run, Pallas kernels for 5% -> 6%
where the time goes in v5:
time: 150 us; the launch traced here: 149 us
  blocking collectives  55.6 us (37%)
  starting transfers between devices  53.7 us (36%)
  waiting for transfers between devices  18.3 us (12%)
  Pallas kernels  14.8 us (10%)
  local copies, waits for them, and re-layouts  3.73 us (2%)
  between operations  1.62 us (1%)
    all_to_all x3, blocking collectives, swap(): return lax.all_to_all(values, axis, split_axis=0, concat_axis=0, tiled=True)  55.6 us
    all_to_all x3, starting transfers between devices, swap(): return lax.all_to_all(values, axis, split_axis=0, concat_axis=0, tiled=True)  24.8 us
    ppermute x4, starting transfers between devices, pair(): return lax.ppermute(values, 'core', [(0, 1), (1, 0)])  19.3 us
    pallas_call x11, Pallas kernels, call(): pl.pallas_call(kernel, out_shape=shapes, in_specs=[pl.BlockSpec(memory_sp...  14.8 us
    ppermute x3, starting transfers between devices, body(): lax.ppermute(rows_out[step], 'x', [(x, x ^ step) for x in range(X_SIZE)])  9.58 us
    all_to_all x3, waiting for transfers between devices, swap(): return lax.all_to_all(values, axis, split_axis=0, concat_axis=0, tiled=True)  9.47 us
    ppermute x3, waiting for transfers between devices, body(): lax.ppermute(rows_out[step], 'x', [(x, x ^ step) for x in range(X_SIZE)])  5.6 us
    unnamed x28, local copies, waits for them, and re-layouts  3.71 us
  transfers between devices with their start and end apart: 10, of which 7 were waited for; matrix products, arithmetic and copies ran while one was open for 0% of the time, Pallas kernels for 6%

profile of v5, /device:TPU:1, one launch (start us, length us, event | category | flops | bytes accessed | tf_op | source)
XLA Modules:
  0.0 149.0 jit_solution(9160631599338696350)
XLA Ops:
  0.6 0.0 copy-start.13
  0.6 0.0 copy-start.8
  0.7 0.0 copy-start.7
  0.7 0.0 copy-start.9
  0.7 0.0 copy-start.10
  0.7 2.2 %pick_boundary.1 = bf16[128,512]{1,0:T(8,128)(2,1)} custom-call(s32[1]{0:T(128)} %bitcast.1.rep_ref.refs_0_, s32[8,64]{1,0:T(8,128)} %bitcast.31, bf16[768,512]{1,0:T(8,128)(2,1)} %feats_ref.1), custom_call_target="tpu_custom_call" | custom-call | flops 100663296 | bytes 919552 | tf_op jit(solution)/shard_map/pick_boundary/pallas_call | solution.py:51
  2.9 15.8 %all-to-all-start = ((bf16[16,8,512]{2,1,0:T(8,128)(2,1)}), bf16[16,8,512]{2,1,0:T(8,128)(2,1)S(1)}, u32[]{:S(2)}, u32[]{:S(2)}) async-start(bf16[16,8,512]{2,1,0:T(8,128)(2,1)} %bitcast.35), calls=%async_computation | async-start | bytes 262144 | tf_op jit(solution)/shard_map/all_to_all | solution.py:358
  19.3 0.0 copy-start
  19.3 1.1 copy-done
  20.5 1.0 copy-done.5
  21.5 4.9 %own_rows.1 = (bf16[2560,512]{1,0:T(8,128)(2,1)S(1)}, f32[1024,512]{1,0:T(8,128)S(1)}) custom-call(s32[1]{0:T(128)} %bitcast.core_ref, s32[1,14]{1,0:T(1,128)S(1)} %copy-done.9, s32[1,14]{1,0:T(1,128)S(1)} %copy-done.10, s32[1]{0:T(128)S(6)} %copy.16.count_ref, bf16[14,128,128]{2,1,0:T(8,128)(2,1)S(1)} %copy-done.7, bf16[768,512]{1,0:T(8,128)(2,1)S(1)} %copy-done, ...), custom_call_target="tpu_custom_call" | custom-call | flops 3623878656 | bytes 6491136 | tf_op jit(solution)/shard_map/own_rows/pallas_call | solution.py:51
  26.4 1.5 %copy-done.11 = bf16[2560,512]{1,0:T(8,128)(2,1)} copy-done((bf16[2560,512]{1,0:T(8,128)(2,1)}, bf16[2560,512]{1,0:T(8,128)(2,1)S(1)}, u32[]{:S(2)}) %copy-start.11) | copy-done | bytes 2621464
  27.9 2.7 %all-to-all-done = bf16[16,8,512]{2,1,0:T(8,128)(2,1)S(1)} async-done(((bf16[16,8,512]{2,1,0:T(8,128)(2,1)}), bf16[16,8,512]{2,1,0:T(8,128)(2,1)S(1)}, u32[]{:S(2)}, u32[]{:S(2)}) %all-to-all-start) | async-done | bytes 131104 | tf_op jit(solution)/shard_map/all_to_all | solution.py:358
  30.6 0.2 spread_plane.1
  30.8 16.0 %all_to_all.30 = bf16[16,32,512]{2,1,0:T(8,128)(2,1)S(1)} all-to-all(bf16[16,32,512]{2,1,0:T(8,128)(2,1)S(1)} %spread_plane.1), channel_id=1, replica_groups=mesh['z'=16,'y'=4,'x'=4,'core'=2] {'y','x'}, dimensions={0} | all-to-all | bytes 1048576 | tf_op jit(solution)/shard_map/all_to_all | solution.py:358
  46.8 6.8 %collective-permute-start = (bf16[512,512]{1,0:T(8,128)(2,1)S(1)}, bf16[512,512]{1,0:T(8,128)(2,1)S(1)}, u32[]{:S(2)}, u32[]{:S(2)}) collective-permute-start(bf16[512,512]{1,0:T(8,128)(2,1)S(1)} %bitcast.28), channel_id=1, source_target_pairs={{0,1},{1,0},{2,3},{3,2},{4,5},{5,4},{6,7},{7,6},{8,9},{9,8},{10,11... | collective-permute-start | bytes 1572872 | tf_op jit(solution)/shard_map/ppermute | solution.py:361
  53.6 1.5 %collective-permute-done.far_ref = bf16[512,512]{1,0:T(8,128)(2,1)S(1)} collective-permute-done((bf16[512,512]{1,0:T(8,128)(2,1)S(1)}, bf16[512,512]{1,0:T(8,128)(2,1)S(1)}, u32[]{:S(2)}, u32[]{:S(2)}) %collective-permute-start) | collective-permute-done | bytes 524320 | tf_op jit(solution)/shard_map/ppermute | solution.py:361
  55.1 0.0 copy-done.3
  55.1 2.7 %forward_backward.1 = (bf16[512,512]{1,0:T(8,128)(2,1)}, bf16[512,512]{1,0:T(8,128)(2,1)S(1)}, bf16[512,512]{1,0:T(8,128)(2,1)S(1)}, bf16[1040,512]{1,0:T(8,128)(2,1)S(1)}, bf16[1040,512]{1,0:T(8,128)(2,1)S(1)}) custom-call(s32[1]{0:T(128)} %bitcast.core_ref, bf16[512,512]{1,0:T(8,128)(2,1)S(1)} %bitcast.29, ...), custom_call_target="tpu_custom_call" | custom-call | flops 2147483648 | bytes 10518528 | tf_op jit(solution)/shard_map/forward_backward/pallas_call | solution.py:51
  57.8 2.3 %collective-permute-start.1 = (bf16[1040,512]{1,0:T(8,128)(2,1)S(1)}, bf16[1040,512]{1,0:T(8,128)(2,1)S(1)}, u32[]{:S(2)}, u32[]{:S(2)}) collective-permute-start(bf16[1040,512]{1,0:T(8,128)(2,1)S(1)} %get-tuple-element.20), channel_id=1, source_target_pairs={{0,1},{1,0},{2,3},{3,2},{4,5},{5,4},{6,7},{7,6},{8,9},{9,8},{10,11... | collective-permute-start | bytes 3194888 | tf_op jit(solution)/shard_map/ppermute | solution.py:361
  60.1 0.0 copy-done.6
  60.1 2.1 %own_rows_back.1.refs_2_.refs_3_ = f32[768,512]{1,0:T(8,128)S(1)} custom-call(s32[1,14]{1,0:T(1,128)S(1)} %copy-done.9, s32[1,14]{1,0:T(1,128)S(1)} %copy-done.10, s32[1]{0:T(128)S(6)} %copy.16.count_ref, bf16[14,128,128]{2,1,0:T(8,128)(2,1)S(1)} %copy-done.7, s32[1,512]{1,0:T(1,128)S(1)} %bitcast.34, bf16[512,512]{1,0:T(8,128)(2,1)S(1)} %get-tuple-element.21.d_pre_ref, ...), custom_call_target="tpu_custom_call" | custom-call | flops 1207959552 | bytes 3606528 | tf_op jit(solution)/shard_map/own_rows_back/pallas_call | solution.py:51
  62.2 0.2 collective-permute-done.1.refs_1_
  62.4 0.2 sum_pair.1
  62.7 20.7 %all_to_all.31.arrived_ref = bf16[16,72,512]{2,1,0:T(8,128)(2,1)S(1)} all-to-all(bf16[16,72,512]{2,1,0:T(8,128)(2,1)S(1)} %sum_pair.1), channel_id=1, replica_groups=mesh['z'=16,'y'=4,'x'=4,'core'=2] {'y','x'}, dimensions={0} | all-to-all | bytes 2359296 | tf_op jit(solution)/shard_map/all_to_all | solution.py:358
  83.4 0.3 sum_plane.1
  83.7 18.9 %all_to_all.32.arrived_ref.refs_2_ = bf16[16,8,512]{2,1,0:T(8,128)(2,1)S(1)} all-to-all(bf16[16,8,512]{2,1,0:T(8,128)(2,1)S(1)} %sum_plane.1), channel_id=1, replica_groups=mesh['z'=16,'y'=4,'x'=4,'core'=2] {'z'}, dimensions={0} | all-to-all | bytes 262144 | tf_op jit(solution)/shard_map/all_to_all | solution.py:358
  102.6 0.6 sum_weights.1
  103.2 5.3 %all-to-all-start.4 = ((bf16[16,8,128]{2,1,0:T(8,128)(2,1)}), bf16[16,8,128]{2,1,0:T(8,128)(2,1)S(1)}, u32[]{:S(2)}, u32[]{:S(2)}) async-start(bf16[16,8,128]{2,1,0:T(8,128)(2,1)} %get-tuple-element.23.refs_4_), calls=%async_computation.4 | async-start | bytes 65536 | tf_op jit(solution)/shard_map/all_to_all | solution.py:358
  108.5 0.6 return_rows.1
  109.2 4.1 %collective-permute-start.2 = (bf16[4,96,512]{2,1,0:T(8,128)(2,1)S(1)}, bf16[4,96,512]{2,1,0:T(8,128)(2,1)S(1)}, u32[]{:S(2)}, u32[]{:S(2)}) collective-permute-start(bf16[4,96,512]{2,1,0:T(8,128)(2,1)S(1)} %get-tuple-element.25), channel_id=1, source_target_pairs={{0,1},{1,0},{2,3},{3,2},{4,5},{5,4},{6,7},{7,6},{8,9},{9,8},{10,11... | collective-permute-start | bytes 1179656 | tf_op jit(solution)/shard_map/ppermute | solution.py:361
  113.3 6.7 %all-to-all-done.4.arrived_ref = bf16[16,8,128]{2,1,0:T(8,128)(2,1)S(1)} async-done(((bf16[16,8,128]{2,1,0:T(8,128)(2,1)}), bf16[16,8,128]{2,1,0:T(8,128)(2,1)S(1)}, u32[]{:S(2)}, u32[]{:S(2)}) %all-to-all-start.4) | async-done | bytes 32800 | tf_op jit(solution)/shard_map/all_to_all | solution.py:358
  120.0 1.0 gather_weights.1
  121.0 3.7 %all-to-all-start.5 = ((bf16[16,32,512]{2,1,0:T(8,128)(2,1)}), bf16[16,32,512]{2,1,0:T(8,128)(2,1)S(1)}, u32[]{:S(2)}, u32[]{:S(2)}) async-start(bf16[16,32,512]{2,1,0:T(8,128)(2,1)} %gather_weights.1), calls=%async_computation.5 | async-start | bytes 1048576 | tf_op jit(solution)/shard_map/all_to_all | solution.py:358
  124.8 0.0 collective-permute-done.2
  124.8 0.1 fusion.3
  124.9 3.3 %collective-permute-start.3 = (bf16[96,512]{1,0:T(8,128)(2,1)S(1)}, bf16[96,512]{1,0:T(8,128)(2,1)S(1)}, u32[]{:S(2)}, u32[]{:S(2)}) collective-permute-start(bf16[96,512]{1,0:T(8,128)(2,1)S(1)} %get-tuple-element.31), channel_id=1, source_target_pairs={{0,2},{2,0},{4,6},{6,4},{1,3},{3,1},{5,7},{7,5},{8,10},{10,8},{12,... | collective-permute-start | bytes 294920 | tf_op jit(solution)/shard_map/ppermute | solution.py:446
  128.2 4.3 %collective-permute-start.4 = (bf16[96,512]{1,0:T(8,128)(2,1)S(1)}, bf16[96,512]{1,0:T(8,128)(2,1)S(1)}, u32[]{:S(2)}, u32[]{:S(2)}) collective-permute-start(bf16[96,512]{1,0:T(8,128)(2,1)S(1)} %get-tuple-element.33), channel_id=1, source_target_pairs={{0,4},{2,6},{4,0},{6,2},{1,5},{3,7},{5,1},{7,3},{8,12},{10,14},{12... | collective-permute-start | bytes 294920 | tf_op jit(solution)/shard_map/ppermute | solution.py:446
  132.5 2.0 %collective-permute-start.5 = (bf16[96,512]{1,0:T(8,128)(2,1)S(1)}, bf16[96,512]{1,0:T(8,128)(2,1)S(1)}, u32[]{:S(2)}, u32[]{:S(2)}) collective-permute-start(bf16[96,512]{1,0:T(8,128)(2,1)S(1)} %get-tuple-element.32), channel_id=1, source_target_pairs={{0,6},{2,4},{4,2},{6,0},{1,7},{3,5},{5,3},{7,1},{8,14},{10,12},{12... | collective-permute-start | bytes 294920 | tf_op jit(solution)/shard_map/ppermute | solution.py:446
  134.6 0.0 collective-permute-done.3
  134.6 1.9 %collective-permute-done.4 = bf16[96,512]{1,0:T(8,128)(2,1)S(1)} collective-permute-done((bf16[96,512]{1,0:T(8,128)(2,1)S(1)}, bf16[96,512]{1,0:T(8,128)(2,1)S(1)}, u32[]{:S(2)}, u32[]{:S(2)}) %collective-permute-start.4) | collective-permute-done | bytes 98336 | tf_op jit(solution)/shard_map/ppermute | solution.py:446
  136.5 3.7 %collective-permute-done.5 = bf16[96,512]{1,0:T(8,128)(2,1)S(1)} collective-permute-done((bf16[96,512]{1,0:T(8,128)(2,1)S(1)}, bf16[96,512]{1,0:T(8,128)(2,1)S(1)}, u32[]{:S(2)}, u32[]{:S(2)}) %collective-permute-start.5) | collective-permute-done | bytes 98336 | tf_op jit(solution)/shard_map/ppermute | solution.py:446
  140.2 0.1 fusion.2.refs_1_
  140.2 0.0 copy-start.1
  140.2 0.0 all-to-all-done.5
  140.3 6.1 %collective-permute-start.6 = (bf16[512,512]{1,0:T(8,128)(2,1)S(1)}, bf16[512,512]{1,0:T(8,128)(2,1)S(1)}, u32[]{:S(2)}, u32[]{:S(2)}) collective-permute-start(bf16[512,512]{1,0:T(8,128)(2,1)S(1)} %hand_on.1), channel_id=1, source_target_pairs={{0,1},{1,0},{2,3},{3,2},{4,5},{5,4},{6,7},{7,6},{8,9},{9,8},{10,11... | collective-permute-start | bytes 1572872 | tf_op jit(solution)/shard_map/ppermute | solution.py:361
  146.4 1.5 %collective-permute-done.6 = bf16[512,512]{1,0:T(8,128)(2,1)S(1)} collective-permute-done((bf16[512,512]{1,0:T(8,128)(2,1)S(1)}, bf16[512,512]{1,0:T(8,128)(2,1)S(1)}, u32[]{:S(2)}, u32[]{:S(2)}) %collective-permute-start.6) | collective-permute-done | bytes 524320 | tf_op jit(solution)/shard_map/ppermute | solution.py:361
  147.9 1.1 broadcast_select_fusion
  (19 shorter events, 0.1 us)
Async XLA Ops:
  0.6 18.6 %copy-start.13 = (bf16[512]{0:T(512)(128)(2,1)S(1)}, bf16[512]{0:T(512)(128)(2,1)}, u32[]{:S(2)}) copy-start(bf16[512]{0:T(512)(128)(2,1)} %param.20) | copy-start | bytes 3076
  0.6 18.7 %copy-start.8 = (s32[512]{0:T(512)S(1)}, s32[512]{0:T(512)}, u32[]{:S(2)}) copy-start(s32[512]{0:T(512)} %param.13) | copy-start | bytes 6148
  0.7 18.7 %copy-start.7 = (bf16[14,128,128]{2,1,0:T(8,128)(2,1)S(1)}, bf16[14,128,128]{2,1,0:T(8,128)(2,1)}, u32[]{:S(2)}) copy-start(bf16[14,128,128]{2,1,0:T(8,128)(2,1)} %tiles_ref.3) | copy-start | bytes 1376260
  0.7 18.7 %copy-start.9 = (s32[1,14]{1,0:T(1,128)S(1)}, s32[1,14]{1,0:T(1,128)}, u32[]{:S(2)}) copy-start(s32[1,14]{1,0:T(1,128)} %dst_ref.3) | copy-start | bytes 172
  0.7 18.7 %copy-start.10 = (s32[1,14]{1,0:T(1,128)S(1)}, s32[1,14]{1,0:T(1,128)}, u32[]{:S(2)}) copy-start(s32[1,14]{1,0:T(1,128)} %src_ref.3) | copy-start | bytes 172
  2.9 27.8 %all-to-all-start = ((bf16[16,8,512]{2,1,0:T(8,128)(2,1)}), bf16[16,8,512]{2,1,0:T(8,128)(2,1)S(1)}, u32[]{:S(2)}, u32[]{:S(2)}) async-start(bf16[16,8,512]{2,1,0:T(8,128)(2,1)} %bitcast.35), calls=%async_computation | async-start | bytes 262144 | tf_op jit(solution)/shard_map/all_to_all | solution.py:358
  19.3 1.1 copy-start
  20.5 1.0 copy-start.5
  26.4 1.5 %copy-start.11 = (bf16[2560,512]{1,0:T(8,128)(2,1)}, bf16[2560,512]{1,0:T(8,128)(2,1)S(1)}, u32[]{:S(2)}) copy-start(bf16[2560,512]{1,0:T(8,128)(2,1)S(1)} %get-tuple-element.17.mats_ref) | copy-start | bytes 7864324
  30.6 24.5 %copy-start.3 = (bf16[512,512]{1,0:T(8,128)(2,1)S(1)}, bf16[512,512]{1,0:T(8,128)(2,1)}, u32[]{:S(2)}) copy-start(bf16[512,512]{1,0:T(8,128)(2,1)} %w_neigh_ref.1) | copy-start | bytes 1572868
  30.6 24.5 %copy-start.4 = (bf16[512,512]{1,0:T(8,128)(2,1)S(1)}, bf16[512,512]{1,0:T(8,128)(2,1)}, u32[]{:S(2)}) copy-start(bf16[512,512]{1,0:T(8,128)(2,1)} %cot_ref.1) | copy-start | bytes 1572868
  30.6 24.5 %copy-start.12 = (bf16[2560,512]{1,0:T(8,128)(2,1)S(1)}, bf16[2560,512]{1,0:T(8,128)(2,1)}, u32[]{:S(2)}) copy-start(bf16[2560,512]{1,0:T(8,128)(2,1)} %copy-done.11) | copy-start | bytes 7864324
  46.8 8.3 %collective-permute-start = (bf16[512,512]{1,0:T(8,128)(2,1)S(1)}, bf16[512,512]{1,0:T(8,128)(2,1)S(1)}, u32[]{:S(2)}, u32[]{:S(2)}) collective-permute-start(bf16[512,512]{1,0:T(8,128)(2,1)S(1)} %bitcast.28), channel_id=1, source_target_pairs={{0,1},{1,0},{2,3},{3,2},{4,5},{5,4},{6,7},{7,6},{8,9},{9,8},{10,11... | collective-permute-start | bytes 1572872 | tf_op jit(solution)/shard_map/ppermute | solution.py:361
  55.1 5.0 %copy-start.6 = (bf16[512,512]{1,0:T(8,128)(2,1)S(1)}, bf16[512,512]{1,0:T(8,128)(2,1)}, u32[]{:S(2)}) copy-start(bf16[512,512]{1,0:T(8,128)(2,1)} %w_self_ref.3) | copy-start | bytes 1572868
  57.8 4.6 %collective-permute-start.1 = (bf16[1040,512]{1,0:T(8,128)(2,1)S(1)}, bf16[1040,512]{1,0:T(8,128)(2,1)S(1)}, u32[]{:S(2)}, u32[]{:S(2)}) collective-permute-start(bf16[1040,512]{1,0:T(8,128)(2,1)S(1)} %get-tuple-element.20), channel_id=1, source_target_pairs={{0,1},{1,0},{2,3},{3,2},{4,5},{5,4},{6,7},{7,6},{8,9},{9,8},{10,11... | collective-permute-start | bytes 3194888 | tf_op jit(solution)/shard_map/ppermute | solution.py:361
  83.4 25.2 %copy-start.2 = (s32[1,64,8]{1,2,0:T(8,128)S(1)}, s32[1,64,8]{1,2,0:T(8,128)}, u32[]{:S(2)}) copy-start(s32[1,64,8]{1,2,0:T(8,128)} %param.12) | copy-start | bytes 6148
  103.2 16.8 %all-to-all-start.4 = ((bf16[16,8,128]{2,1,0:T(8,128)(2,1)}), bf16[16,8,128]{2,1,0:T(8,128)(2,1)S(1)}, u32[]{:S(2)}, u32[]{:S(2)}) async-start(bf16[16,8,128]{2,1,0:T(8,128)(2,1)} %get-tuple-element.23.refs_4_), calls=%async_computation.4 | async-start | bytes 65536 | tf_op jit(solution)/shard_map/all_to_all | solution.py:358
  109.2 15.6 %collective-permute-start.2 = (bf16[4,96,512]{2,1,0:T(8,128)(2,1)S(1)}, bf16[4,96,512]{2,1,0:T(8,128)(2,1)S(1)}, u32[]{:S(2)}, u32[]{:S(2)}) collective-permute-start(bf16[4,96,512]{2,1,0:T(8,128)(2,1)S(1)} %get-tuple-element.25), channel_id=1, source_target_pairs={{0,1},{1,0},{2,3},{3,2},{4,5},{5,4},{6,7},{7,6},{8,9},{9,8},{10,11... | collective-permute-start | bytes 1179656 | tf_op jit(solution)/shard_map/ppermute | solution.py:361
  121.0 19.2 %all-to-all-start.5 = ((bf16[16,32,512]{2,1,0:T(8,128)(2,1)}), bf16[16,32,512]{2,1,0:T(8,128)(2,1)S(1)}, u32[]{:S(2)}, u32[]{:S(2)}) async-start(bf16[16,32,512]{2,1,0:T(8,128)(2,1)} %gather_weights.1), calls=%async_computation.5 | async-start | bytes 1048576 | tf_op jit(solution)/shard_map/all_to_all | solution.py:358
  124.9 9.6 %collective-permute-start.3 = (bf16[96,512]{1,0:T(8,128)(2,1)S(1)}, bf16[96,512]{1,0:T(8,128)(2,1)S(1)}, u32[]{:S(2)}, u32[]{:S(2)}) collective-permute-start(bf16[96,512]{1,0:T(8,128)(2,1)S(1)} %get-tuple-element.31), channel_id=1, source_target_pairs={{0,2},{2,0},{4,6},{6,4},{1,3},{3,1},{5,7},{7,5},{8,10},{10,8},{12,... | collective-permute-start | bytes 294920 | tf_op jit(solution)/shard_map/ppermute | solution.py:446
  128.2 8.3 %collective-permute-start.4 = (bf16[96,512]{1,0:T(8,128)(2,1)S(1)}, bf16[96,512]{1,0:T(8,128)(2,1)S(1)}, u32[]{:S(2)}, u32[]{:S(2)}) collective-permute-start(bf16[96,512]{1,0:T(8,128)(2,1)S(1)} %get-tuple-element.33), channel_id=1, source_target_pairs={{0,4},{2,6},{4,0},{6,2},{1,5},{3,7},{5,1},{7,3},{8,12},{10,14},{12... | collective-permute-start | bytes 294920 | tf_op jit(solution)/shard_map/ppermute | solution.py:446
  132.5 7.6 %collective-permute-start.5 = (bf16[96,512]{1,0:T(8,128)(2,1)S(1)}, bf16[96,512]{1,0:T(8,128)(2,1)S(1)}, u32[]{:S(2)}, u32[]{:S(2)}) collective-permute-start(bf16[96,512]{1,0:T(8,128)(2,1)S(1)} %get-tuple-element.32), channel_id=1, source_target_pairs={{0,6},{2,4},{4,2},{6,0},{1,7},{3,5},{5,3},{7,1},{8,14},{10,12},{12... | collective-permute-start | bytes 294920 | tf_op jit(solution)/shard_map/ppermute | solution.py:446
  140.2 8.8 %copy-start.1 = (f32[96,512]{1,0:T(8,128)}, f32[96,512]{1,0:T(8,128)S(1)}, u32[]{:S(2)}) copy-start(f32[96,512]{1,0:T(8,128)S(1)} %fusion.2.refs_1_) | copy-start | bytes 589828
  140.3 7.6 %collective-permute-start.6 = (bf16[512,512]{1,0:T(8,128)(2,1)S(1)}, bf16[512,512]{1,0:T(8,128)(2,1)S(1)}, u32[]{:S(2)}, u32[]{:S(2)}) collective-permute-start(bf16[512,512]{1,0:T(8,128)(2,1)S(1)} %hand_on.1), channel_id=1, source_target_pairs={{0,1},{1,0},{2,3},{3,2},{4,5},{5,4},{6,7},{7,6},{8,9},{9,8},{10,11... | collective-permute-start | bytes 1572872 | tf_op jit(solution)/shard_map/ppermute | solution.py:361

commit v6 on v5

--- a/solution.py
+++ b/solution.py
@@ -280,8 +280,8 @@
     bias_ref[...] = total[block - 1 :]
 
 
-def gather_kernel(arrived_ref, send_ref):
-    chunks, weight, width = send_ref.shape
+def gather_kernel(arrived_ref, whole_ref):
+    weight, width = whole_ref.shape
     depth, block, _ = arrived_ref.shape
     groups = width // LANES
     each = weight // depth
@@ -289,12 +289,14 @@
     shape = (weight, depth * block)
     out, into = iota(shape, 0), iota(shape, 1)
     z, line = out // each, out % each
-    parts = [
-        move(into == z * block + group * each + line, arrived) for group in range(groups)
-    ]
-    whole = jnp.concatenate(parts, 1)
-    for chunk in range(chunks):
-        send_ref[chunk] = whole
+    for group in range(groups):
+        rows = move(into == z * block + group * each + line, arrived)
+        whole_ref[:, group * LANES : (group + 1) * LANES] = rows
+
+
+def spread_kernel(whole_ref, send_ref):
+    for chunk in range(send_ref.shape[0]):
+        send_ref[chunk] = whole_ref[...]
 
 
 def own_back_kernel(
@@ -309,21 +311,44 @@
     own_ref[...] = dot(seeded, w_self_ref[...], 1, 1) + dot(adj_ref[...], d_agg_ref[...], 0, 0)
 
 
-def scatter_kernel(rep_ref, lists_ref, arrived_ref, own_ref, keep_ref, send_ref, total_ref):
+def scatter_kernel(rep_ref, lists_ref, arrived_ref, own_ref, keep_ref, *send_refs_and_total):
+    *send_refs, total_ref = send_refs_and_total
     rows, width = own_ref.shape
     rep = rep_ref[0]
     places = boundary_places(rep, lists_ref, rows, summed_by_z(lists_ref.shape[1]))
     back = arrived_ref[...].reshape(places.shape[1], width)
-    total_ref[...] = (own_ref[...] + dot(places, back)).astype(BF16)
+    total_ref[...] = own_ref[...] + dot(places, back)
     share = rows // (X_SIZE * CORES)
-    for step in range(X_SIZE):
-        keep = jnp.bitwise_xor(rep, step * CORES)
-        for place, ref in ((keep, keep_ref), (jnp.bitwise_xor(keep, 1), send_ref)):
-            ref[step] = total_ref[pl.ds(pl.multiple_of(place * share, 32), share), :]
-
-
-def copy_kernel(from_ref, to_ref):
-    to_ref[...] = from_ref[...]
+    for step, ref in enumerate([keep_ref, *send_refs]):
+        for core in range(CORES):
+            place = jnp.bitwise_xor(rep, step * CORES + core)
+            some = total_ref[pl.ds(pl.multiple_of(place * share, 32), share), :]
+            ref[core * share : (core + 1) * share] = some.astype(ref.dtype)
+
+
+def row_sum_kernel(keep_ref, *refs):
+    *arrived_refs, own_ref, send_ref = refs
+    share = own_ref.shape[0]
+    total = keep_ref[...]
+    for ref in arrived_refs:
+        total = total + ref[...].astype(F32)
+    own_ref[...] = total[:share]
+    send_ref[...] = total[share:].astype(BF16)
+
+
+def join_kernel(weights_ref, rows_ref, send_ref):
+    width = weights_ref.shape[0]
+    send_ref[:width] = weights_ref[...]
+    send_ref[width:] = rows_ref[...]
+
+
+def finish_kernel(core_ref, near_ref, own_ref, far_ref, first_ref, second_ref, rows_ref):
+    width = near_ref.shape[0]
+    near, far = near_ref[...], far_ref[:width]
+    is_first = core_ref[0] == 0
+    first_ref[...] = jnp.where(is_first, near, far)
+    second_ref[...] = jnp.where(is_first, far, near)
+    rows_ref[...] = own_ref[...] + far_ref[width:].astype(F32)
 
 
 def body(
@@ -426,31 +451,38 @@
     )
     weight_depth = swap(weight_send, "z")
     share = rows // reps
-    row_keep, row_send = call(
+    row_keep, *row_sends = call(
         scatter_kernel, "return_rows",
-        [((X_SIZE, share, width), BF16), ((X_SIZE, share, width), BF16)],
+        [((CORES * share, width), F32)] + [((CORES * share, width), BF16)] * (X_SIZE - 1),
         [rep], [lists, depth_arrived, own],
-        scratch=[pltpu.VMEM((rows, width), BF16)],
+        scratch=[pltpu.VMEM((rows, width), F32)],
         flops=4 * parts * rows * width, after=[weight_send],
     )
-    row_pair = row_keep.astype(F32) + pair(row_send).astype(F32)
-    rows_out = row_pair.astype(BF16)
+    row_arrived = [
+        lax.ppermute(some, "x", [(x, x ^ step) for x in range(X_SIZE)])
+        for step, some in enumerate(row_sends, 1)
+    ]
+    (weight_rows,) = call(
+        gather_kernel, "gather_weights", [((width // PLANE, width), BF16)],
+        [], [weight_depth], flops=20_000_000_000,
+    )
+    row_own, row_send = call(
+        row_sum_kernel, "sum_rows", [((share, width), F32), ((share, width), BF16)],
+        [], [row_keep, *row_arrived],
+    )
     (weight_plane,) = call(
-        gather_kernel, "gather_weights",
-        [((PLANE, width // PLANE, width), BF16)],
-        [], [weight_depth], flops=20_000_000_000,
+        spread_kernel, "spread_weights", [((PLANE, width // PLANE, width), BF16)],
+        [], [weight_rows], after=[row_send],
     )
     weight_near = swap(weight_plane, ("y", "x")).reshape(width, width)
-    input_grad = row_pair[0]
-    for step in range(1, X_SIZE):
-        beside = lax.ppermute(rows_out[step], "x", [(x, x ^ step) for x in range(X_SIZE)])
-        input_grad = input_grad + beside.astype(F32)
-    (weight_send,) = call(
-        copy_kernel, "hand_on", [((width, width), BF16)], [], [weight_near], after=[input_grad]
-    )
-    weight_far = pair(weight_send)
-    grad_self = jnp.where(core_id == 0, weight_near, weight_far)
-    grad_neigh = jnp.where(core_id == 0, weight_far, weight_near)
+    (last_send,) = call(
+        join_kernel, "join", [((width + share, width), BF16)], [], [weight_near, row_send]
+    )
+    grad_self, grad_neigh, input_grad = call(
+        finish_kernel, "finish",
+        [((width, width), BF16), ((width, width), BF16), ((share, width), F32)],
+        [core], [weight_near, row_own, pair(last_send)],
+    )
     grad_bias = bias_row.reshape(width)
     return (out, input_grad, grad_self, grad_neigh, grad_bias)
 

time: 150 us -> 148 us (0.987)
  blocking collectives: 55.6 us -> 69.4 us
  starting transfers between devices: 53.7 us -> 43.9 us
  waiting for transfers between devices: 18.3 us -> 13.8 us
    all_to_all x3 -> x4, blocking collectives: 55.6 us -> 69.4 us  [swap(): return lax.all_to_all(values, axis, split_axis=0, concat_axis=0, tiled=True)]
    ppermute x4 -> x3, starting transfers between devices: 19.3 us -> 13.3 us  [pair(): return lax.ppermute(values, 'core', [(0, 1), (1, 0)])]
    all_to_all x3 -> x2, waiting for transfers between devices: 9.47 us -> 4.15 us  [swap(): return lax.all_to_all(values, axis, split_axis=0, concat_axis=0, tiled=True)]
    all_to_all x3 -> x2, starting transfers between devices: 24.8 us -> 21 us  [swap(): return lax.all_to_all(values, axis, split_axis=0, concat_axis=0, tiled=True)]
    ppermute x4 -> x3, waiting for transfers between devices: 3.21 us -> 3.44 us  [pair(): return lax.ppermute(values, 'core', [(0, 1), (1, 0)])]
    pallas_call x11 -> x14, Pallas kernels: 14.8 us -> 15 us  [call(): pl.pallas_call(kernel, out_shape=shapes, in_specs=[pl.BlockSpec(memory_sp...]
    unnamed x28 -> x26, local copies, waits for them, and re-layouts: 3.71 us -> 3.71 us
  transfers between devices with their start and end apart: 10 -> 8, of which waited for: 7 -> 7; matrix products, arithmetic and copies ran while one was open for 0% -> 0% of each run, Pallas kernels for 6% -> 5%
where the time goes in v6:
time: 148 us; the launch traced here: 147 us
  blocking collectives  69.4 us (47%)
  starting transfers between devices  43.9 us (30%)
  Pallas kernels  15 us (10%)
  waiting for transfers between devices  13.8 us (9%)
  local copies, waits for them, and re-layouts  3.71 us (3%)
  between operations  1.56 us (1%)
    all_to_all x4, blocking collectives, swap(): return lax.all_to_all(values, axis, split_axis=0, concat_axis=0, tiled=True)  69.4 us
    all_to_all x2, starting transfers between devices, swap(): return lax.all_to_all(values, axis, split_axis=0, concat_axis=0, tiled=True)  21 us
    pallas_call x14, Pallas kernels, call(): pl.pallas_call(kernel, out_shape=shapes, in_specs=[pl.BlockSpec(memory_sp...  15 us
    ppermute x3, starting transfers between devices, pair(): return lax.ppermute(values, 'core', [(0, 1), (1, 0)])  13.3 us
    ppermute x3, starting transfers between devices, body(): lax.ppermute(some, 'x', [(x, x ^ step) for x in range(X_SIZE)])  9.58 us
    ppermute x3, waiting for transfers between devices, body(): lax.ppermute(some, 'x', [(x, x ^ step) for x in range(X_SIZE)])  6.18 us
    all_to_all x2, waiting for transfers between devices, swap(): return lax.all_to_all(values, axis, split_axis=0, concat_axis=0, tiled=True)  4.15 us
    unnamed x26, local copies, waits for them, and re-layouts  3.71 us
  transfers between devices with their start and end apart: 8, of which 7 were waited for; matrix products, arithmetic and copies ran while one was open for 0% of the time, Pallas kernels for 5%

profile of v6, /device:TPU:1, one launch (start us, length us, event | category | flops | bytes accessed | tf_op | source)
XLA Modules:
  0.0 147.3 jit_solution(6339830011360967594)
XLA Ops:
  0.6 0.0 copy-start.12
  0.6 0.0 copy-start.9
  0.7 0.0 copy-start.8
  0.7 0.0 copy-start.6
  0.7 0.0 copy-start.7
  0.7 2.2 %pick_boundary.1 = bf16[128,512]{1,0:T(8,128)(2,1)} custom-call(s32[1]{0:T(128)} %bitcast.1.rep_ref.refs_0_, s32[8,64]{1,0:T(8,128)} %bitcast.16, bf16[768,512]{1,0:T(8,128)(2,1)} %feats_ref.1), custom_call_target="tpu_custom_call" | custom-call | flops 100663296 | bytes 919552 | tf_op jit(solution)/shard_map/pick_boundary/pallas_call | solution.py:51
  2.9 15.8 %all-to-all-start = ((bf16[16,8,512]{2,1,0:T(8,128)(2,1)}), bf16[16,8,512]{2,1,0:T(8,128)(2,1)S(1)}, u32[]{:S(2)}, u32[]{:S(2)}) async-start(bf16[16,8,512]{2,1,0:T(8,128)(2,1)} %bitcast.20), calls=%async_computation | async-start | bytes 262144 | tf_op jit(solution)/shard_map/all_to_all | solution.py:383
  19.3 0.0 copy-done.12
  19.3 0.0 copy-done.9
  19.3 0.0 copy-done.8
  19.3 0.0 copy-done.6
  19.3 0.0 copy-done.7
  19.3 0.0 copy-start
  19.4 1.1 copy-done
  20.5 1.0 copy-done.4
  21.5 4.7 %own_rows.1 = (bf16[2560,512]{1,0:T(8,128)(2,1)S(1)}, f32[1024,512]{1,0:T(8,128)S(1)}) custom-call(s32[1]{0:T(128)} %bitcast.core_ref, s32[1,14]{1,0:T(1,128)S(1)} %copy-done.8, s32[1,14]{1,0:T(1,128)S(1)} %copy-done.9, s32[1]{0:T(128)S(6)} %copy.16.count_ref, bf16[14,128,128]{2,1,0:T(8,128)(2,1)S(1)} %copy-done.6, bf16[768,512]{1,0:T(8,128)(2,1)S(1)} %copy-done, ...), custom_call_target="tpu_custom_call" | custom-call | flops 3623878656 | bytes 6491136 | tf_op jit(solution)/shard_map/own_rows/pallas_call | solution.py:51
  26.2 0.0 copy-start.10
  26.2 1.5 %copy-done.10 = bf16[2560,512]{1,0:T(8,128)(2,1)} copy-done((bf16[2560,512]{1,0:T(8,128)(2,1)}, bf16[2560,512]{1,0:T(8,128)(2,1)S(1)}, u32[]{:S(2)}) %copy-start.10) | copy-done | bytes 2621464
  27.7 2.9 %all-to-all-done = bf16[16,8,512]{2,1,0:T(8,128)(2,1)S(1)} async-done(((bf16[16,8,512]{2,1,0:T(8,128)(2,1)}), bf16[16,8,512]{2,1,0:T(8,128)(2,1)S(1)}, u32[]{:S(2)}, u32[]{:S(2)}) %all-to-all-start) | async-done | bytes 131104 | tf_op jit(solution)/shard_map/all_to_all | solution.py:383
  30.6 0.2 spread_plane.1
  30.8 16.0 %all_to_all.30 = bf16[16,32,512]{2,1,0:T(8,128)(2,1)S(1)} all-to-all(bf16[16,32,512]{2,1,0:T(8,128)(2,1)S(1)} %spread_plane.1), channel_id=1, replica_groups=mesh['z'=16,'y'=4,'x'=4,'core'=2] {'y','x'}, dimensions={0} | all-to-all | bytes 1048576 | tf_op jit(solution)/shard_map/all_to_all | solution.py:383
  46.8 6.8 %collective-permute-start = (bf16[512,512]{1,0:T(8,128)(2,1)S(1)}, bf16[512,512]{1,0:T(8,128)(2,1)S(1)}, u32[]{:S(2)}, u32[]{:S(2)}) collective-permute-start(bf16[512,512]{1,0:T(8,128)(2,1)S(1)} %bitcast.13), channel_id=1, source_target_pairs={{0,1},{1,0},{2,3},{3,2},{4,5},{5,4},{6,7},{7,6},{8,9},{9,8},{10,11... | collective-permute-start | bytes 1572872 | tf_op jit(solution)/shard_map/ppermute | solution.py:386
  53.6 1.5 %collective-permute-done.far_ref = bf16[512,512]{1,0:T(8,128)(2,1)S(1)} collective-permute-done((bf16[512,512]{1,0:T(8,128)(2,1)S(1)}, bf16[512,512]{1,0:T(8,128)(2,1)S(1)}, u32[]{:S(2)}, u32[]{:S(2)}) %collective-permute-start) | collective-permute-done | bytes 524320 | tf_op jit(solution)/shard_map/ppermute | solution.py:386
  55.1 0.0 copy-done.2
  55.1 2.7 %forward_backward.1 = (bf16[512,512]{1,0:T(8,128)(2,1)}, bf16[512,512]{1,0:T(8,128)(2,1)S(1)}, bf16[512,512]{1,0:T(8,128)(2,1)S(1)}, bf16[1040,512]{1,0:T(8,128)(2,1)S(1)}, bf16[1040,512]{1,0:T(8,128)(2,1)S(1)}) custom-call(s32[1]{0:T(128)} %bitcast.core_ref, bf16[512,512]{1,0:T(8,128)(2,1)S(1)} %bitcast.14, ...), custom_call_target="tpu_custom_call" | custom-call | flops 2147483648 | bytes 10518528 | tf_op jit(solution)/shard_map/forward_backward/pallas_call | solution.py:51
  57.8 2.3 %collective-permute-start.1 = (bf16[1040,512]{1,0:T(8,128)(2,1)S(1)}, bf16[1040,512]{1,0:T(8,128)(2,1)S(1)}, u32[]{:S(2)}, u32[]{:S(2)}) collective-permute-start(bf16[1040,512]{1,0:T(8,128)(2,1)S(1)} %get-tuple-element.27), channel_id=1, source_target_pairs={{0,1},{1,0},{2,3},{3,2},{4,5},{5,4},{6,7},{7,6},{8,9},{9,8},{10,11... | collective-permute-start | bytes 3194888 | tf_op jit(solution)/shard_map/ppermute | solution.py:386
  60.1 2.0 %own_rows_back.1.refs_2_.refs_3_ = f32[768,512]{1,0:T(8,128)S(1)} custom-call(s32[1,14]{1,0:T(1,128)S(1)} %copy-done.8, s32[1,14]{1,0:T(1,128)S(1)} %copy-done.9, s32[1]{0:T(128)S(6)} %copy.16.count_ref, bf16[14,128,128]{2,1,0:T(8,128)(2,1)S(1)} %copy-done.6, s32[1,512]{1,0:T(1,128)S(1)} %bitcast.19, bf16[512,512]{1,0:T(8,128)(2,1)S(1)} %get-tuple-element.28.d_pre_ref, ...), custom_call_target="tpu_custom_call" | custom-call | flops 1207959552 | bytes 3606528 | tf_op jit(solution)/shard_map/own_rows_back/pallas_call | solution.py:51
  62.2 0.3 collective-permute-done.1.refs_1_
  62.4 0.2 sum_pair.1
  62.7 20.7 %all_to_all.31.arrived_ref = bf16[16,72,512]{2,1,0:T(8,128)(2,1)S(1)} all-to-all(bf16[16,72,512]{2,1,0:T(8,128)(2,1)S(1)} %sum_pair.1), channel_id=1, replica_groups=mesh['z'=16,'y'=4,'x'=4,'core'=2] {'y','x'}, dimensions={0} | all-to-all | bytes 2359296 | tf_op jit(solution)/shard_map/all_to_all | solution.py:383
  83.4 0.3 sum_plane.1
  83.7 18.8 %all_to_all.32.arrived_ref.refs_2_ = bf16[16,8,512]{2,1,0:T(8,128)(2,1)S(1)} all-to-all(bf16[16,8,512]{2,1,0:T(8,128)(2,1)S(1)} %sum_plane.1), channel_id=1, replica_groups=mesh['z'=16,'y'=4,'x'=4,'core'=2] {'z'}, dimensions={0} | all-to-all | bytes 262144 | tf_op jit(solution)/shard_map/all_to_all | solution.py:383
  102.5 0.6 sum_weights.1
  103.2 5.3 %all-to-all-start.4 = ((bf16[16,8,128]{2,1,0:T(8,128)(2,1)}), bf16[16,8,128]{2,1,0:T(8,128)(2,1)S(1)}, u32[]{:S(2)}, u32[]{:S(2)}) async-start(bf16[16,8,128]{2,1,0:T(8,128)(2,1)} %get-tuple-element.30.refs_4_), calls=%async_computation.4 | async-start | bytes 65536 | tf_op jit(solution)/shard_map/all_to_all | solution.py:383
  108.5 0.6 return_rows.1
  109.1 1.9 %collective-permute-start.2 = (bf16[192,512]{1,0:T(8,128)(2,1)S(1)}, bf16[192,512]{1,0:T(8,128)(2,1)S(1)}, u32[]{:S(2)}, u32[]{:S(2)}) collective-permute-start(bf16[192,512]{1,0:T(8,128)(2,1)S(1)} %get-tuple-element.32), channel_id=1, source_target_pairs={{0,2},{2,0},{4,6},{6,4},{1,3},{3,1},{5,7},{7,5},{8,10},{10,8},{12,... | collective-permute-start | bytes 589832 | tf_op jit(solution)/shard_map/ppermute | solution.py:462
  111.1 3.5 %collective-permute-start.3 = (bf16[192,512]{1,0:T(8,128)(2,1)S(1)}, bf16[192,512]{1,0:T(8,128)(2,1)S(1)}, u32[]{:S(2)}, u32[]{:S(2)}) collective-permute-start(bf16[192,512]{1,0:T(8,128)(2,1)S(1)} %get-tuple-element.33), channel_id=1, source_target_pairs={{0,4},{2,6},{4,0},{6,2},{1,5},{3,7},{5,1},{7,3},{8,12},{10,14},{12... | collective-permute-start | bytes 589832 | tf_op jit(solution)/shard_map/ppermute | solution.py:462
  114.6 4.2 %collective-permute-start.4 = (bf16[192,512]{1,0:T(8,128)(2,1)S(1)}, bf16[192,512]{1,0:T(8,128)(2,1)S(1)}, u32[]{:S(2)}, u32[]{:S(2)}) collective-permute-start(bf16[192,512]{1,0:T(8,128)(2,1)S(1)} %get-tuple-element.34), channel_id=1, source_target_pairs={{0,6},{2,4},{4,2},{6,0},{1,7},{3,5},{5,3},{7,1},{8,14},{10,12},{12... | collective-permute-start | bytes 589832 | tf_op jit(solution)/shard_map/ppermute | solution.py:462
  118.7 1.3 all-to-all-done.4.arrived_ref
  120.0 0.1 gather_weights.1.refs_0_
  120.1 0.0 collective-permute-done.2.refs_0_
  120.1 1.2 collective-permute-done.3.refs_1_
  121.3 5.0 %collective-permute-done.4.refs_2_ = bf16[192,512]{1,0:T(8,128)(2,1)S(1)} collective-permute-done((bf16[192,512]{1,0:T(8,128)(2,1)S(1)}, bf16[192,512]{1,0:T(8,128)(2,1)S(1)}, u32[]{:S(2)}, u32[]{:S(2)}) %collective-permute-start.4) | collective-permute-done | bytes 196640 | tf_op jit(solution)/shard_map/ppermute | solution.py:462
  126.3 0.1 sum_rows.1
  126.4 13.8 %all_to_all.33 = bf16[16,32,512]{2,1,0:T(8,128)(2,1)S(1)} all-to-all(bf16[16,32,512]{2,1,0:T(8,128)(2,1)S(1)} %spread_weights.1), channel_id=1, replica_groups=mesh['z'=16,'y'=4,'x'=4,'core'=2] {'y','x'}, dimensions={0} | all-to-all | bytes 1048576 | tf_op jit(solution)/shard_map/all_to_all | solution.py:383
  140.3 4.3 %collective-permute-start.5 = (bf16[608,512]{1,0:T(8,128)(2,1)S(1)}, bf16[608,512]{1,0:T(8,128)(2,1)S(1)}, u32[]{:S(2)}, u32[]{:S(2)}) collective-permute-start(bf16[608,512]{1,0:T(8,128)(2,1)S(1)} %join.1), channel_id=1, source_target_pairs={{0,1},{1,0},{2,3},{3,2},{4,5},{5,4},{6,7},{7,6},{8,9},{9,8},{10,11... | collective-permute-start | bytes 1867784 | tf_op jit(solution)/shard_map/ppermute | solution.py:386
  144.6 1.7 %collective-permute-done.5.far_ref = bf16[608,512]{1,0:T(8,128)(2,1)S(1)} collective-permute-done((bf16[608,512]{1,0:T(8,128)(2,1)S(1)}, bf16[608,512]{1,0:T(8,128)(2,1)S(1)}, u32[]{:S(2)}, u32[]{:S(2)}) %collective-permute-start.5) | collective-permute-done | bytes 622624 | tf_op jit(solution)/shard_map/ppermute | solution.py:386
  146.2 1.1 finish.1
  (13 shorter events, 0.1 us)
Async XLA Ops:
  0.6 18.6 %copy-start.12 = (bf16[512]{0:T(512)(128)(2,1)S(1)}, bf16[512]{0:T(512)(128)(2,1)}, u32[]{:S(2)}) copy-start(bf16[512]{0:T(512)(128)(2,1)} %param.20) | copy-start | bytes 3076
  0.6 18.7 %copy-start.9 = (s32[1,14]{1,0:T(1,128)S(1)}, s32[1,14]{1,0:T(1,128)}, u32[]{:S(2)}) copy-start(s32[1,14]{1,0:T(1,128)} %src_ref.3) | copy-start | bytes 172
  0.7 18.7 %copy-start.8 = (s32[1,14]{1,0:T(1,128)S(1)}, s32[1,14]{1,0:T(1,128)}, u32[]{:S(2)}) copy-start(s32[1,14]{1,0:T(1,128)} %dst_ref.3) | copy-start | bytes 172
  0.7 18.7 %copy-start.6 = (bf16[14,128,128]{2,1,0:T(8,128)(2,1)S(1)}, bf16[14,128,128]{2,1,0:T(8,128)(2,1)}, u32[]{:S(2)}) copy-start(bf16[14,128,128]{2,1,0:T(8,128)(2,1)} %tiles_ref.3) | copy-start | bytes 1376260
  0.7 18.7 %copy-start.7 = (s32[512]{0:T(512)S(1)}, s32[512]{0:T(512)}, u32[]{:S(2)}) copy-start(s32[512]{0:T(512)} %param.13) | copy-start | bytes 6148
  2.9 27.8 %all-to-all-start = ((bf16[16,8,512]{2,1,0:T(8,128)(2,1)}), bf16[16,8,512]{2,1,0:T(8,128)(2,1)S(1)}, u32[]{:S(2)}, u32[]{:S(2)}) async-start(bf16[16,8,512]{2,1,0:T(8,128)(2,1)} %bitcast.20), calls=%async_computation | async-start | bytes 262144 | tf_op jit(solution)/shard_map/all_to_all | solution.py:383
  19.3 1.1 copy-start
  20.5 1.0 copy-start.4
  26.2 1.5 %copy-start.10 = (bf16[2560,512]{1,0:T(8,128)(2,1)}, bf16[2560,512]{1,0:T(8,128)(2,1)S(1)}, u32[]{:S(2)}) copy-start(bf16[2560,512]{1,0:T(8,128)(2,1)S(1)} %get-tuple-element.24.mats_ref) | copy-start | bytes 7864324
  30.6 24.5 %copy-start.2 = (bf16[512,512]{1,0:T(8,128)(2,1)S(1)}, bf16[512,512]{1,0:T(8,128)(2,1)}, u32[]{:S(2)}) copy-start(bf16[512,512]{1,0:T(8,128)(2,1)} %w_neigh_ref.1) | copy-start | bytes 1572868
  30.6 24.5 %copy-start.3 = (bf16[512,512]{1,0:T(8,128)(2,1)S(1)}, bf16[512,512]{1,0:T(8,128)(2,1)}, u32[]{:S(2)}) copy-start(bf16[512,512]{1,0:T(8,128)(2,1)} %cot_ref.1) | copy-start | bytes 1572868
  30.6 24.5 %copy-start.11 = (bf16[2560,512]{1,0:T(8,128)(2,1)S(1)}, bf16[2560,512]{1,0:T(8,128)(2,1)}, u32[]{:S(2)}) copy-start(bf16[2560,512]{1,0:T(8,128)(2,1)} %copy-done.10) | copy-start | bytes 7864324
  46.8 8.3 %collective-permute-start = (bf16[512,512]{1,0:T(8,128)(2,1)S(1)}, bf16[512,512]{1,0:T(8,128)(2,1)S(1)}, u32[]{:S(2)}, u32[]{:S(2)}) collective-permute-start(bf16[512,512]{1,0:T(8,128)(2,1)S(1)} %bitcast.13), channel_id=1, source_target_pairs={{0,1},{1,0},{2,3},{3,2},{4,5},{5,4},{6,7},{7,6},{8,9},{9,8},{10,11... | collective-permute-start | bytes 1572872 | tf_op jit(solution)/shard_map/ppermute | solution.py:386
  55.1 5.0 %copy-start.5 = (bf16[512,512]{1,0:T(8,128)(2,1)S(1)}, bf16[512,512]{1,0:T(8,128)(2,1)}, u32[]{:S(2)}) copy-start(bf16[512,512]{1,0:T(8,128)(2,1)} %w_self_ref.3) | copy-start | bytes 1572868
  57.8 4.6 %collective-permute-start.1 = (bf16[1040,512]{1,0:T(8,128)(2,1)S(1)}, bf16[1040,512]{1,0:T(8,128)(2,1)S(1)}, u32[]{:S(2)}, u32[]{:S(2)}) collective-permute-start(bf16[1040,512]{1,0:T(8,128)(2,1)S(1)} %get-tuple-element.27), channel_id=1, source_target_pairs={{0,1},{1,0},{2,3},{3,2},{4,5},{5,4},{6,7},{7,6},{8,9},{9,8},{10,11... | collective-permute-start | bytes 3194888 | tf_op jit(solution)/shard_map/ppermute | solution.py:386
  83.4 25.1 %copy-start.1 = (s32[1,64,8]{1,2,0:T(8,128)S(1)}, s32[1,64,8]{1,2,0:T(8,128)}, u32[]{:S(2)}) copy-start(s32[1,64,8]{1,2,0:T(8,128)} %param.12) | copy-start | bytes 6148
  103.2 16.8 %all-to-all-start.4 = ((bf16[16,8,128]{2,1,0:T(8,128)(2,1)}), bf16[16,8,128]{2,1,0:T(8,128)(2,1)S(1)}, u32[]{:S(2)}, u32[]{:S(2)}) async-start(bf16[16,8,128]{2,1,0:T(8,128)(2,1)} %get-tuple-element.30.refs_4_), calls=%async_computation.4 | async-start | bytes 65536 | tf_op jit(solution)/shard_map/all_to_all | solution.py:383
  109.1 11.0 %collective-permute-start.2 = (bf16[192,512]{1,0:T(8,128)(2,1)S(1)}, bf16[192,512]{1,0:T(8,128)(2,1)S(1)}, u32[]{:S(2)}, u32[]{:S(2)}) collective-permute-start(bf16[192,512]{1,0:T(8,128)(2,1)S(1)} %get-tuple-element.32), channel_id=1, source_target_pairs={{0,2},{2,0},{4,6},{6,4},{1,3},{3,1},{5,7},{7,5},{8,10},{10,8},{12,... | collective-permute-start | bytes 589832 | tf_op jit(solution)/shard_map/ppermute | solution.py:462
  111.1 10.2 %collective-permute-start.3 = (bf16[192,512]{1,0:T(8,128)(2,1)S(1)}, bf16[192,512]{1,0:T(8,128)(2,1)S(1)}, u32[]{:S(2)}, u32[]{:S(2)}) collective-permute-start(bf16[192,512]{1,0:T(8,128)(2,1)S(1)} %get-tuple-element.33), channel_id=1, source_target_pairs={{0,4},{2,6},{4,0},{6,2},{1,5},{3,7},{5,1},{7,3},{8,12},{10,14},{12... | collective-permute-start | bytes 589832 | tf_op jit(solution)/shard_map/ppermute | solution.py:462
  114.6 11.8 %collective-permute-start.4 = (bf16[192,512]{1,0:T(8,128)(2,1)S(1)}, bf16[192,512]{1,0:T(8,128)(2,1)S(1)}, u32[]{:S(2)}, u32[]{:S(2)}) collective-permute-start(bf16[192,512]{1,0:T(8,128)(2,1)S(1)} %get-tuple-element.34), channel_id=1, source_target_pairs={{0,6},{2,4},{4,2},{6,0},{1,7},{3,5},{5,3},{7,1},{8,14},{10,12},{12... | collective-permute-start | bytes 589832 | tf_op jit(solution)/shard_map/ppermute | solution.py:462
  140.3 5.9 %collective-permute-start.5 = (bf16[608,512]{1,0:T(8,128)(2,1)S(1)}, bf16[608,512]{1,0:T(8,128)(2,1)S(1)}, u32[]{:S(2)}, u32[]{:S(2)}) collective-permute-start(bf16[608,512]{1,0:T(8,128)(2,1)S(1)} %join.1), channel_id=1, source_target_pairs={{0,1},{1,0},{2,3},{3,2},{4,5},{5,4},{6,7},{7,6},{8,9},{9,8},{10,11... | collective-permute-start | bytes 1867784 | tf_op jit(solution)/shard_map/ppermute | solution.py:386

commit v7 on v6

--- a/solution.py
+++ b/solution.py
@@ -379,6 +379,8 @@
     tile_scalars = (tile_dst, tile_src, tile_count)
     scale = float(seeds * parts * reps) ** (-0.5)
 
+    window = 20_000_000_000
+
     def swap(values, axis):
         return lax.all_to_all(values, axis, split_axis=0, concat_axis=0, tiled=True)
 
@@ -459,20 +461,20 @@
         flops=4 * parts * rows * width, after=[weight_send],
     )
     row_arrived = [
-        lax.ppermute(some, "x", [(x, x ^ step) for x in range(X_SIZE)])
-        for step, some in enumerate(row_sends, 1)
+        lax.ppermute(row_sends[step - 1], "x", [(x, x ^ step) for x in range(X_SIZE)])
+        for step in (2, 1, 3)
     ]
     (weight_rows,) = call(
         gather_kernel, "gather_weights", [((width // PLANE, width), BF16)],
-        [], [weight_depth], flops=20_000_000_000,
+        [], [weight_depth], flops=window, after=[row_keep],
     )
     row_own, row_send = call(
         row_sum_kernel, "sum_rows", [((share, width), F32), ((share, width), BF16)],
-        [], [row_keep, *row_arrived],
+        [], [row_keep, *row_arrived], flops=window,
     )
     (weight_plane,) = call(
         spread_kernel, "spread_weights", [((PLANE, width // PLANE, width), BF16)],
-        [], [weight_rows], after=[row_send],
+        [], [weight_rows],
     )
     weight_near = swap(weight_plane, ("y", "x")).reshape(width, width)
     (last_send,) = call(

time: 148 us -> 144 us (0.973)
  blocking collectives: 69.4 us -> 55.6 us
  starting transfers between devices: 43.9 us -> 49.1 us
  waiting for transfers between devices: 13.8 us -> 17 us
    all_to_all x4 -> x3, blocking collectives: 69.4 us -> 55.6 us  [swap(): return lax.all_to_all(values, axis, split_axis=0, concat_axis=0, tiled=True)]
    all_to_all x2 -> x3, waiting for transfers between devices: 4.15 us -> 13.6 us  [swap(): return lax.all_to_all(values, axis, split_axis=0, concat_axis=0, tiled=True)]
    ppermute x3, waiting for transfers between devices: 6.18 us -> 0.01 us  [body(): lax.ppermute(row_sends[step - 1], 'x', [(x, x ^ step) for x in range(X_SI...]
    all_to_all x2 -> x3, starting transfers between devices: 21 us -> 24.7 us  [swap(): return lax.all_to_all(values, axis, split_axis=0, concat_axis=0, tiled=True)]
    ppermute x3, starting transfers between devices: 13.3 us -> 15.4 us  [pair(): return lax.ppermute(values, 'core', [(0, 1), (1, 0)])]
  transfers between devices with their start and end apart: 8 -> 9, of which waited for: 7 -> 6; matrix products, arithmetic and copies ran while one was open for 0% -> 0% of each run, Pallas kernels for 5% -> 6%
where the time goes in v7:
time: 144 us; the launch traced here: 143 us
  blocking collectives  55.6 us (39%)
  starting transfers between devices  49.1 us (34%)
  waiting for transfers between devices  17 us (12%)
  Pallas kernels  15.9 us (11%)
  local copies, waits for them, and re-layouts  3.72 us (3%)
  between operations  1.58 us (1%)
    all_to_all x3, blocking collectives, swap(): return lax.all_to_all(values, axis, split_axis=0, concat_axis=0, tiled=True)  55.6 us
    all_to_all x3, starting transfers between devices, swap(): return lax.all_to_all(values, axis, split_axis=0, concat_axis=0, tiled=True)  24.7 us
    pallas_call x14, Pallas kernels, call(): pl.pallas_call(kernel, out_shape=shapes, in_specs=[pl.BlockSpec(memory_sp...  15.9 us
    ppermute x3, starting transfers between devices, pair(): return lax.ppermute(values, 'core', [(0, 1), (1, 0)])  15.4 us
    all_to_all x3, waiting for transfers between devices, swap(): return lax.all_to_all(values, axis, split_axis=0, concat_axis=0, tiled=True)  13.6 us
    ppermute x3, starting transfers between devices, body(): lax.ppermute(row_sends[step - 1], 'x', [(x, x ^ step) for x in range(X_SI...  8.98 us
    unnamed x26, local copies, waits for them, and re-layouts  3.72 us
    ppermute x3, waiting for transfers between devices, pair(): return lax.ppermute(values, 'core', [(0, 1), (1, 0)])  3.43 us
  transfers between devices with their start and end apart: 9, of which 6 were waited for; matrix products, arithmetic and copies ran while one was open for 0% of the time, Pallas kernels for 6%

profile of v7, /device:TPU:1, one launch (start us, length us, event | category | flops | bytes accessed | tf_op | source)
XLA Modules:
  0.0 143.0 jit_solution(18129553838428032808)
XLA Ops:
  0.6 0.0 copy-start.12
  0.6 0.0 copy-start.9
  0.7 0.0 copy-start.8
  0.7 0.0 copy-start.6
  0.7 0.0 copy-start.7
  0.7 2.2 %pick_boundary.1 = bf16[128,512]{1,0:T(8,128)(2,1)} custom-call(s32[1]{0:T(128)} %bitcast.1.rep_ref.refs_0_, s32[8,64]{1,0:T(8,128)} %bitcast.16, bf16[768,512]{1,0:T(8,128)(2,1)} %feats_ref.1), custom_call_target="tpu_custom_call" | custom-call | flops 100663296 | bytes 919552 | tf_op jit(solution)/shard_map/pick_boundary/pallas_call | solution.py:51
  2.9 15.8 %all-to-all-start = ((bf16[16,8,512]{2,1,0:T(8,128)(2,1)}), bf16[16,8,512]{2,1,0:T(8,128)(2,1)S(1)}, u32[]{:S(2)}, u32[]{:S(2)}) async-start(bf16[16,8,512]{2,1,0:T(8,128)(2,1)} %bitcast.20), calls=%async_computation | async-start | bytes 262144 | tf_op jit(solution)/shard_map/all_to_all | solution.py:385
  19.3 0.0 copy-done.12
  19.3 0.0 copy-done.9
  19.3 0.0 copy-done.8
  19.3 0.0 copy-done.6
  19.3 0.0 copy-done.7
  19.3 0.0 copy-start
  19.4 1.1 copy-done
  20.5 1.0 copy-done.4
  21.5 4.7 %own_rows.1 = (bf16[2560,512]{1,0:T(8,128)(2,1)S(1)}, f32[1024,512]{1,0:T(8,128)S(1)}) custom-call(s32[1]{0:T(128)} %bitcast.core_ref, s32[1,14]{1,0:T(1,128)S(1)} %copy-done.8, s32[1,14]{1,0:T(1,128)S(1)} %copy-done.9, s32[1]{0:T(128)S(6)} %copy.16.count_ref, bf16[14,128,128]{2,1,0:T(8,128)(2,1)S(1)} %copy-done.6, bf16[768,512]{1,0:T(8,128)(2,1)S(1)} %copy-done, ...), custom_call_target="tpu_custom_call" | custom-call | flops 3623878656 | bytes 6491136 | tf_op jit(solution)/shard_map/own_rows/pallas_call | solution.py:51
  26.2 1.5 %copy-done.10 = bf16[2560,512]{1,0:T(8,128)(2,1)} copy-done((bf16[2560,512]{1,0:T(8,128)(2,1)}, bf16[2560,512]{1,0:T(8,128)(2,1)S(1)}, u32[]{:S(2)}) %copy-start.10) | copy-done | bytes 2621464
  27.7 2.9 %all-to-all-done = bf16[16,8,512]{2,1,0:T(8,128)(2,1)S(1)} async-done(((bf16[16,8,512]{2,1,0:T(8,128)(2,1)}), bf16[16,8,512]{2,1,0:T(8,128)(2,1)S(1)}, u32[]{:S(2)}, u32[]{:S(2)}) %all-to-all-start) | async-done | bytes 131104 | tf_op jit(solution)/shard_map/all_to_all | solution.py:385
  30.6 0.2 spread_plane.1
  30.8 16.0 %all_to_all.30 = bf16[16,32,512]{2,1,0:T(8,128)(2,1)S(1)} all-to-all(bf16[16,32,512]{2,1,0:T(8,128)(2,1)S(1)} %spread_plane.1), channel_id=1, replica_groups=mesh['z'=16,'y'=4,'x'=4,'core'=2] {'y','x'}, dimensions={0} | all-to-all | bytes 1048576 | tf_op jit(solution)/shard_map/all_to_all | solution.py:385
  46.8 6.8 %collective-permute-start = (bf16[512,512]{1,0:T(8,128)(2,1)S(1)}, bf16[512,512]{1,0:T(8,128)(2,1)S(1)}, u32[]{:S(2)}, u32[]{:S(2)}) collective-permute-start(bf16[512,512]{1,0:T(8,128)(2,1)S(1)} %bitcast.13), channel_id=1, source_target_pairs={{0,1},{1,0},{2,3},{3,2},{4,5},{5,4},{6,7},{7,6},{8,9},{9,8},{10,11... | collective-permute-start | bytes 1572872 | tf_op jit(solution)/shard_map/ppermute | solution.py:388
  53.6 1.5 %collective-permute-done.far_ref = bf16[512,512]{1,0:T(8,128)(2,1)S(1)} collective-permute-done((bf16[512,512]{1,0:T(8,128)(2,1)S(1)}, bf16[512,512]{1,0:T(8,128)(2,1)S(1)}, u32[]{:S(2)}, u32[]{:S(2)}) %collective-permute-start) | collective-permute-done | bytes 524320 | tf_op jit(solution)/shard_map/ppermute | solution.py:388
  55.1 2.7 %forward_backward.1 = (bf16[512,512]{1,0:T(8,128)(2,1)}, bf16[512,512]{1,0:T(8,128)(2,1)S(1)}, bf16[512,512]{1,0:T(8,128)(2,1)S(1)}, bf16[1040,512]{1,0:T(8,128)(2,1)S(1)}, bf16[1040,512]{1,0:T(8,128)(2,1)S(1)}) custom-call(s32[1]{0:T(128)} %bitcast.core_ref, bf16[512,512]{1,0:T(8,128)(2,1)S(1)} %bitcast.14, ...), custom_call_target="tpu_custom_call" | custom-call | flops 2147483648 | bytes 10518528 | tf_op jit(solution)/shard_map/forward_backward/pallas_call | solution.py:51
  57.9 2.3 %collective-permute-start.1 = (bf16[1040,512]{1,0:T(8,128)(2,1)S(1)}, bf16[1040,512]{1,0:T(8,128)(2,1)S(1)}, u32[]{:S(2)}, u32[]{:S(2)}) collective-permute-start(bf16[1040,512]{1,0:T(8,128)(2,1)S(1)} %get-tuple-element.27), channel_id=1, source_target_pairs={{0,1},{1,0},{2,3},{3,2},{4,5},{5,4},{6,7},{7,6},{8,9},{9,8},{10,11... | collective-permute-start | bytes 3194888 | tf_op jit(solution)/shard_map/ppermute | solution.py:388
  60.2 2.0 %own_rows_back.1.refs_2_.refs_3_ = f32[768,512]{1,0:T(8,128)S(1)} custom-call(s32[1,14]{1,0:T(1,128)S(1)} %copy-done.8, s32[1,14]{1,0:T(1,128)S(1)} %copy-done.9, s32[1]{0:T(128)S(6)} %copy.16.count_ref, bf16[14,128,128]{2,1,0:T(8,128)(2,1)S(1)} %copy-done.6, s32[1,512]{1,0:T(1,128)S(1)} %bitcast.19, bf16[512,512]{1,0:T(8,128)(2,1)S(1)} %get-tuple-element.28.d_pre_ref, ...), custom_call_target="tpu_custom_call" | custom-call | flops 1207959552 | bytes 3606528 | tf_op jit(solution)/shard_map/own_rows_back/pallas_call | solution.py:51
  62.2 0.3 collective-permute-done.1.refs_1_
  62.5 0.2 sum_pair.1
  62.7 20.7 %all_to_all.31.arrived_ref = bf16[16,72,512]{2,1,0:T(8,128)(2,1)S(1)} all-to-all(bf16[16,72,512]{2,1,0:T(8,128)(2,1)S(1)} %sum_pair.1), channel_id=1, replica_groups=mesh['z'=16,'y'=4,'x'=4,'core'=2] {'y','x'}, dimensions={0} | all-to-all | bytes 2359296 | tf_op jit(solution)/shard_map/all_to_all | solution.py:385
  83.4 0.3 sum_plane.1
  83.7 18.9 %all_to_all.32.arrived_ref.refs_2_ = bf16[16,8,512]{2,1,0:T(8,128)(2,1)S(1)} all-to-all(bf16[16,8,512]{2,1,0:T(8,128)(2,1)S(1)} %sum_plane.1), channel_id=1, replica_groups=mesh['z'=16,'y'=4,'x'=4,'core'=2] {'z'}, dimensions={0} | all-to-all | bytes 262144 | tf_op jit(solution)/shard_map/all_to_all | solution.py:385
  102.6 0.6 sum_weights.1
  103.3 5.3 %all-to-all-start.4 = ((bf16[16,8,128]{2,1,0:T(8,128)(2,1)}), bf16[16,8,128]{2,1,0:T(8,128)(2,1)S(1)}, u32[]{:S(2)}, u32[]{:S(2)}) async-start(bf16[16,8,128]{2,1,0:T(8,128)(2,1)} %get-tuple-element.30.refs_4_), calls=%async_computation.4 | async-start | bytes 65536 | tf_op jit(solution)/shard_map/all_to_all | solution.py:385
  108.6 0.6 return_rows.1
  109.2 2.5 %collective-permute-start.2 = (bf16[192,512]{1,0:T(8,128)(2,1)S(1)}, bf16[192,512]{1,0:T(8,128)(2,1)S(1)}, u32[]{:S(2)}, u32[]{:S(2)}) collective-permute-start(bf16[192,512]{1,0:T(8,128)(2,1)S(1)} %get-tuple-element.32), channel_id=1, source_target_pairs={{0,4},{2,6},{4,0},{6,2},{1,5},{3,7},{5,1},{7,3},{8,12},{10,14},{12... | collective-permute-start | bytes 589832 | tf_op jit(solution)/shard_map/ppermute | solution.py:464
  111.8 2.2 %collective-permute-start.3 = (bf16[192,512]{1,0:T(8,128)(2,1)S(1)}, bf16[192,512]{1,0:T(8,128)(2,1)S(1)}, u32[]{:S(2)}, u32[]{:S(2)}) collective-permute-start(bf16[192,512]{1,0:T(8,128)(2,1)S(1)} %get-tuple-element.33), channel_id=1, source_target_pairs={{0,2},{2,0},{4,6},{6,4},{1,3},{3,1},{5,7},{7,5},{8,10},{10,8},{12,... | collective-permute-start | bytes 589832 | tf_op jit(solution)/shard_map/ppermute | solution.py:464
  114.0 4.2 %collective-permute-start.4 = (bf16[192,512]{1,0:T(8,128)(2,1)S(1)}, bf16[192,512]{1,0:T(8,128)(2,1)S(1)}, u32[]{:S(2)}, u32[]{:S(2)}) collective-permute-start(bf16[192,512]{1,0:T(8,128)(2,1)S(1)} %get-tuple-element.34), channel_id=1, source_target_pairs={{0,6},{2,4},{4,2},{6,0},{1,7},{3,5},{5,3},{7,1},{8,14},{10,12},{12... | collective-permute-start | bytes 589832 | tf_op jit(solution)/shard_map/ppermute | solution.py:464
  118.2 1.9 %all-to-all-done.4.refs_0_ = bf16[16,8,128]{2,1,0:T(8,128)(2,1)S(1)} async-done(((bf16[16,8,128]{2,1,0:T(8,128)(2,1)}), bf16[16,8,128]{2,1,0:T(8,128)(2,1)S(1)}, u32[]{:S(2)}, u32[]{:S(2)}) %all-to-all-start.4) | async-done | bytes 32800 | tf_op jit(solution)/shard_map/all_to_all | solution.py:385
  120.1 0.1 gather_weights.1.whole_ref
  120.2 0.8 spread_weights.1
  121.1 3.7 %all-to-all-start.5 = ((bf16[16,32,512]{2,1,0:T(8,128)(2,1)}), bf16[16,32,512]{2,1,0:T(8,128)(2,1)S(1)}, u32[]{:S(2)}, u32[]{:S(2)}) async-start(bf16[16,32,512]{2,1,0:T(8,128)(2,1)} %spread_weights.1), calls=%async_computation.5 | async-start | bytes 1048576 | tf_op jit(solution)/shard_map/all_to_all | solution.py:385
  124.8 0.0 collective-permute-done.2.refs_0_
  124.8 0.0 collective-permute-done.3.refs_1_
  124.8 0.0 collective-permute-done.4.refs_2_
  124.8 0.1 sum_rows.1
  124.9 8.9 %all-to-all-done.5 = bf16[16,32,512]{2,1,0:T(8,128)(2,1)S(1)} async-done(((bf16[16,32,512]{2,1,0:T(8,128)(2,1)}), bf16[16,32,512]{2,1,0:T(8,128)(2,1)S(1)}, u32[]{:S(2)}, u32[]{:S(2)}) %all-to-all-start.5) | async-done | bytes 524320 | tf_op jit(solution)/shard_map/all_to_all | solution.py:385
  133.8 6.3 %collective-permute-start.5 = (bf16[608,512]{1,0:T(8,128)(2,1)S(1)}, bf16[608,512]{1,0:T(8,128)(2,1)S(1)}, u32[]{:S(2)}, u32[]{:S(2)}) collective-permute-start(bf16[608,512]{1,0:T(8,128)(2,1)S(1)} %join.1), channel_id=1, source_target_pairs={{0,1},{1,0},{2,3},{3,2},{4,5},{5,4},{6,7},{7,6},{8,9},{9,8},{10,11... | collective-permute-start | bytes 1867784 | tf_op jit(solution)/shard_map/ppermute | solution.py:388
  140.2 1.7 %collective-permute-done.5.far_ref = bf16[608,512]{1,0:T(8,128)(2,1)S(1)} collective-permute-done((bf16[608,512]{1,0:T(8,128)(2,1)S(1)}, bf16[608,512]{1,0:T(8,128)(2,1)S(1)}, u32[]{:S(2)}, u32[]{:S(2)}) %collective-permute-start.5) | collective-permute-done | bytes 622624 | tf_op jit(solution)/shard_map/ppermute | solution.py:388
  141.8 1.2 finish.1
  (14 shorter events, 0.1 us)
Async XLA Ops:
  0.6 18.6 %copy-start.12 = (bf16[512]{0:T(512)(128)(2,1)S(1)}, bf16[512]{0:T(512)(128)(2,1)}, u32[]{:S(2)}) copy-start(bf16[512]{0:T(512)(128)(2,1)} %param.20) | copy-start | bytes 3076
  0.6 18.7 %copy-start.9 = (s32[1,14]{1,0:T(1,128)S(1)}, s32[1,14]{1,0:T(1,128)}, u32[]{:S(2)}) copy-start(s32[1,14]{1,0:T(1,128)} %src_ref.3) | copy-start | bytes 172
  0.7 18.7 %copy-start.8 = (s32[1,14]{1,0:T(1,128)S(1)}, s32[1,14]{1,0:T(1,128)}, u32[]{:S(2)}) copy-start(s32[1,14]{1,0:T(1,128)} %dst_ref.3) | copy-start | bytes 172
  0.7 18.7 %copy-start.6 = (bf16[14,128,128]{2,1,0:T(8,128)(2,1)S(1)}, bf16[14,128,128]{2,1,0:T(8,128)(2,1)}, u32[]{:S(2)}) copy-start(bf16[14,128,128]{2,1,0:T(8,128)(2,1)} %tiles_ref.3) | copy-start | bytes 1376260
  0.7 18.7 %copy-start.7 = (s32[512]{0:T(512)S(1)}, s32[512]{0:T(512)}, u32[]{:S(2)}) copy-start(s32[512]{0:T(512)} %param.13) | copy-start | bytes 6148
  2.9 27.8 %all-to-all-start = ((bf16[16,8,512]{2,1,0:T(8,128)(2,1)}), bf16[16,8,512]{2,1,0:T(8,128)(2,1)S(1)}, u32[]{:S(2)}, u32[]{:S(2)}) async-start(bf16[16,8,512]{2,1,0:T(8,128)(2,1)} %bitcast.20), calls=%async_computation | async-start | bytes 262144 | tf_op jit(solution)/shard_map/all_to_all | solution.py:385
  19.3 1.1 copy-start
  20.5 1.0 copy-start.4
  26.2 1.5 %copy-start.10 = (bf16[2560,512]{1,0:T(8,128)(2,1)}, bf16[2560,512]{1,0:T(8,128)(2,1)S(1)}, u32[]{:S(2)}) copy-start(bf16[2560,512]{1,0:T(8,128)(2,1)S(1)} %get-tuple-element.24.mats_ref) | copy-start | bytes 7864324
  30.6 24.5 %copy-start.2 = (bf16[512,512]{1,0:T(8,128)(2,1)S(1)}, bf16[512,512]{1,0:T(8,128)(2,1)}, u32[]{:S(2)}) copy-start(bf16[512,512]{1,0:T(8,128)(2,1)} %w_neigh_ref.1) | copy-start | bytes 1572868
  30.6 24.5 %copy-start.3 = (bf16[512,512]{1,0:T(8,128)(2,1)S(1)}, bf16[512,512]{1,0:T(8,128)(2,1)}, u32[]{:S(2)}) copy-start(bf16[512,512]{1,0:T(8,128)(2,1)} %cot_ref.1) | copy-start | bytes 1572868
  30.6 24.5 %copy-start.11 = (bf16[2560,512]{1,0:T(8,128)(2,1)S(1)}, bf16[2560,512]{1,0:T(8,128)(2,1)}, u32[]{:S(2)}) copy-start(bf16[2560,512]{1,0:T(8,128)(2,1)} %copy-done.10) | copy-start | bytes 7864324
  46.8 8.3 %collective-permute-start = (bf16[512,512]{1,0:T(8,128)(2,1)S(1)}, bf16[512,512]{1,0:T(8,128)(2,1)S(1)}, u32[]{:S(2)}, u32[]{:S(2)}) collective-permute-start(bf16[512,512]{1,0:T(8,128)(2,1)S(1)} %bitcast.13), channel_id=1, source_target_pairs={{0,1},{1,0},{2,3},{3,2},{4,5},{5,4},{6,7},{7,6},{8,9},{9,8},{10,11... | collective-permute-start | bytes 1572872 | tf_op jit(solution)/shard_map/ppermute | solution.py:388
  55.1 5.0 %copy-start.5 = (bf16[512,512]{1,0:T(8,128)(2,1)S(1)}, bf16[512,512]{1,0:T(8,128)(2,1)}, u32[]{:S(2)}) copy-start(bf16[512,512]{1,0:T(8,128)(2,1)} %w_self_ref.3) | copy-start | bytes 1572868
  57.9 4.6 %collective-permute-start.1 = (bf16[1040,512]{1,0:T(8,128)(2,1)S(1)}, bf16[1040,512]{1,0:T(8,128)(2,1)S(1)}, u32[]{:S(2)}, u32[]{:S(2)}) collective-permute-start(bf16[1040,512]{1,0:T(8,128)(2,1)S(1)} %get-tuple-element.27), channel_id=1, source_target_pairs={{0,1},{1,0},{2,3},{3,2},{4,5},{5,4},{6,7},{7,6},{8,9},{9,8},{10,11... | collective-permute-start | bytes 3194888 | tf_op jit(solution)/shard_map/ppermute | solution.py:388
  83.4 25.1 %copy-start.1 = (s32[1,64,8]{1,2,0:T(8,128)S(1)}, s32[1,64,8]{1,2,0:T(8,128)}, u32[]{:S(2)}) copy-start(s32[1,64,8]{1,2,0:T(8,128)} %param.12) | copy-start | bytes 6148
  103.3 16.8 %all-to-all-start.4 = ((bf16[16,8,128]{2,1,0:T(8,128)(2,1)}), bf16[16,8,128]{2,1,0:T(8,128)(2,1)S(1)}, u32[]{:S(2)}, u32[]{:S(2)}) async-start(bf16[16,8,128]{2,1,0:T(8,128)(2,1)} %get-tuple-element.30.refs_4_), calls=%async_computation.4 | async-start | bytes 65536 | tf_op jit(solution)/shard_map/all_to_all | solution.py:385
  109.2 15.6 %collective-permute-start.2 = (bf16[192,512]{1,0:T(8,128)(2,1)S(1)}, bf16[192,512]{1,0:T(8,128)(2,1)S(1)}, u32[]{:S(2)}, u32[]{:S(2)}) collective-permute-start(bf16[192,512]{1,0:T(8,128)(2,1)S(1)} %get-tuple-element.32), channel_id=1, source_target_pairs={{0,4},{2,6},{4,0},{6,2},{1,5},{3,7},{5,1},{7,3},{8,12},{10,14},{12... | collective-permute-start | bytes 589832 | tf_op jit(solution)/shard_map/ppermute | solution.py:464
  111.8 13.0 %collective-permute-start.3 = (bf16[192,512]{1,0:T(8,128)(2,1)S(1)}, bf16[192,512]{1,0:T(8,128)(2,1)S(1)}, u32[]{:S(2)}, u32[]{:S(2)}) collective-permute-start(bf16[192,512]{1,0:T(8,128)(2,1)S(1)} %get-tuple-element.33), channel_id=1, source_target_pairs={{0,2},{2,0},{4,6},{6,4},{1,3},{3,1},{5,7},{7,5},{8,10},{10,8},{12,... | collective-permute-start | bytes 589832 | tf_op jit(solution)/shard_map/ppermute | solution.py:464
  114.0 10.8 %collective-permute-start.4 = (bf16[192,512]{1,0:T(8,128)(2,1)S(1)}, bf16[192,512]{1,0:T(8,128)(2,1)S(1)}, u32[]{:S(2)}, u32[]{:S(2)}) collective-permute-start(bf16[192,512]{1,0:T(8,128)(2,1)S(1)} %get-tuple-element.34), channel_id=1, source_target_pairs={{0,6},{2,4},{4,2},{6,0},{1,7},{3,5},{5,3},{7,1},{8,14},{10,12},{12... | collective-permute-start | bytes 589832 | tf_op jit(solution)/shard_map/ppermute | solution.py:464
  121.1 12.7 %all-to-all-start.5 = ((bf16[16,32,512]{2,1,0:T(8,128)(2,1)}), bf16[16,32,512]{2,1,0:T(8,128)(2,1)S(1)}, u32[]{:S(2)}, u32[]{:S(2)}) async-start(bf16[16,32,512]{2,1,0:T(8,128)(2,1)} %spread_weights.1), calls=%async_computation.5 | async-start | bytes 1048576 | tf_op jit(solution)/shard_map/all_to_all | solution.py:385
  133.8 8.0 %collective-permute-start.5 = (bf16[608,512]{1,0:T(8,128)(2,1)S(1)}, bf16[608,512]{1,0:T(8,128)(2,1)S(1)}, u32[]{:S(2)}, u32[]{:S(2)}) collective-permute-start(bf16[608,512]{1,0:T(8,128)(2,1)S(1)} %join.1), channel_id=1, source_target_pairs={{0,1},{1,0},{2,3},{3,2},{4,5},{5,4},{6,7},{7,6},{8,9},{9,8},{10,11... | collective-permute-start | bytes 1867784 | tf_op jit(solution)/shard_map/ppermute | solution.py:388

commit v8 on v7

--- a/solution.py
+++ b/solution.py
@@ -34,11 +34,6 @@
 
 def iota(shape, dim):
     return lax.broadcasted_iota(jnp.int32, shape, dim)
-
-
-def split(wide):
-    high = wide.astype(BF16)
-    return high, (wide - high.astype(F32)).astype(BF16)
 
 
 def call(kernel, name, outs, scalars, arrays, scratch=(), flops=0, after=(), hbm=(), hbm_outs=(), limit=VMEM_BYTES):
@@ -108,13 +103,6 @@
     return dot(places, order.astype(BF16), 1, 1).astype(BF16)
 
 
-def by_z(parts):
-    shape = (2 * parts, 2 * parts)
-    out, into = iota(shape, 0), iota(shape, 1)
-    y, kind, z = out % Y_SIZE, out // Y_SIZE % 2, out // (2 * Y_SIZE)
-    return into == kind * parts + z * Y_SIZE + y
-
-
 def summed_by_z(parts):
     shape = (2 * parts, 2 * parts)
     out, into = iota(shape, 0), iota(shape, 1)
@@ -126,11 +114,24 @@
 
 def send_kernel(rep_ref, lists_hbm, feats_hbm, send_ref, lists_ref, feats_ref, sems):
     lists_copy, feats_copy = fetch((lists_hbm, feats_hbm), (lists_ref, feats_ref), sems)
+    slots, parts = lists_ref.shape
+    rep = rep_ref[0]
+    shape = (2 * parts, parts)
+    line = iota(shape, 0)
+    part = line // (2 * Y_SIZE) * Y_SIZE + line % Y_SIZE
+    of_part = (part == iota(shape, 1)).astype(BF16)
     lists_copy.wait()
-    parts = lists_ref.shape[1]
-    places = boundary_places(rep_ref[0], lists_ref, feats_ref.shape[0], by_z(parts))
+    lists = lists_ref[...]
+    high, low = (lists // 256).astype(BF16), (lists % 256).astype(BF16)
+    wanted = dot(of_part, high, 1, 1) * 256.0 + dot(of_part, low, 1, 1)
+    shape = (2 * parts, slots)
+    is_hub = iota(shape, 0) // Y_SIZE % 2 == 1
+    wanted = jnp.where(is_hub, rep.astype(F32), wanted)
+    wanted = jnp.sum(jnp.where(iota(shape, 1) == rep, wanted, 0.0), axis=1, keepdims=True)
+    places = iota((2 * parts, feats_ref.shape[0]), 1) == wanted.astype(jnp.int32)
+    places = places.astype(BF16)
     feats_copy.wait()
-    send_ref[...] = dot(places, feats_ref[...], 0, 0).astype(BF16)
+    send_ref[...] = dot(places, feats_ref[...]).astype(BF16)
 
 
 def plane_kernel(arrived_ref, send_ref):
@@ -206,35 +207,30 @@
     send_ref[:width] = jnp.where(is_first, second, first)
     keep_ref[width : width + half] = dot(mats_ref[near_back:far_back, :seeds], d_agg).astype(BF16)
     send_ref[width : width + half] = dot(mats_ref[far_back:chosen_t, :seeds], d_agg).astype(BF16)
-    high, low = split(jnp.sum(d_pre.astype(F32), 0, keepdims=True))
-    row = iota((keep_ref.shape[0] - width - half, width), 0)
-    pair = jnp.where(
-        row == 0, high.astype(F32), jnp.where(row == 1, low.astype(F32), 0.0)
-    ).astype(BF16)
-    keep_ref[width + half :] = pair
-    send_ref[width + half :] = pair
-
-
-def pair_sum_kernel(keep_ref, other_ref, send_ref):
+    bias = two_rows(jnp.sum(d_pre.astype(F32), 0, keepdims=True), keep_ref.shape[0] - width - half)
+    keep_ref[width + half :] = bias
+    send_ref[width + half :] = bias
+
+
+def two_rows(wide, rows):
+    high = wide.astype(BF16).astype(F32)
+    row = iota((rows, wide.shape[1]), 0)
+    return jnp.where(row == 0, high, jnp.where(row == 1, wide - high, 0.0)).astype(BF16)
+
+
+def pair_sum_kernel(keep_ref, other_ref, send_ref, bias_ref):
     chunks, lines, width = send_ref.shape
     total = keep_ref[...].astype(F32) + other_ref[...].astype(F32)
-    weight, table = width // chunks, (lines - 8 - width // chunks)
-    tail = width + chunks * table
-    high, low = split(total[tail : tail + 1] + total[tail + 1 : tail + 2])
-    row = iota((8, width), 0)
-    pair = jnp.where(row == 0, high.astype(F32), jnp.where(row == 1, low.astype(F32), 0.0))
+    weight = width // chunks
+    table = lines - weight
+    bias_ref[...] = jnp.sum(total[width + chunks * table :], 0, keepdims=True)
+    total = total.astype(BF16)
     for chunk in range(chunks):
-        send_ref[chunk] = jnp.concatenate(
-            [
-                total[chunk * weight : (chunk + 1) * weight],
-                total[width + chunk * table : width + (chunk + 1) * table],
-                pair,
-            ],
-            0,
-        ).astype(BF16)
-
-
-def plane_sum_kernel(arrived_ref, send_ref):
+        send_ref[chunk, :weight] = total[chunk * weight : (chunk + 1) * weight]
+        send_ref[chunk, weight:] = total[width + chunk * table : width + (chunk + 1) * table]
+
+
+def plane_sum_kernel(arrived_ref, bias_ref, send_ref):
     chunks, lines, width = arrived_ref.shape
     depth, block, _ = send_ref.shape
     weight = width // chunks
@@ -248,7 +244,7 @@
             some = some + arrived_ref[y * X_SIZE + x].astype(F32)
         rows.append(some[weight : weight + depth])
         rest = some if rest is None else rest + some
-    bias = jnp.zeros((depth, width), F32) + jnp.sum(rest[tail:], 0, keepdims=True)
+    bias = jnp.zeros((depth, width), F32) + bias_ref[...]
     rows += [rest[weight + depth : tail], rest[:weight], bias]
     rows = jnp.concatenate(rows, 0).astype(BF16)
     shape = (depth * block, rows.shape[0])
@@ -311,7 +307,9 @@
     own_ref[...] = dot(seeded, w_self_ref[...], 1, 1) + dot(adj_ref[...], d_agg_ref[...], 0, 0)
 
 
-def scatter_kernel(rep_ref, lists_ref, arrived_ref, own_ref, keep_ref, *send_refs_and_total):
+def scatter_kernel(
+    rep_ref, lists_ref, arrived_ref, own_ref, bias_ref, keep_ref, *send_refs_and_total
+):
     *send_refs, total_ref = send_refs_and_total
     rows, width = own_ref.shape
     rep = rep_ref[0]
@@ -324,16 +322,23 @@
             place = jnp.bitwise_xor(rep, step * CORES + core)
             some = total_ref[pl.ds(pl.multiple_of(place * share, 32), share), :]
             ref[core * share : (core + 1) * share] = some.astype(ref.dtype)
-
-
-def row_sum_kernel(keep_ref, *refs):
-    *arrived_refs, own_ref, send_ref = refs
+    bias = two_rows(bias_ref[...], send_refs[0].shape[0] - CORES * share)
+    for ref in send_refs:
+        ref[CORES * share :] = bias
+
+
+def row_sum_kernel(keep_ref, bias_ref, *refs):
+    *arrived_refs, own_ref, send_ref, bias_sum_ref, bias_send_ref = refs
     share = own_ref.shape[0]
-    total = keep_ref[...]
+    total, bias = keep_ref[...], bias_ref[...]
     for ref in arrived_refs:
-        total = total + ref[...].astype(F32)
+        arrived = ref[...].astype(F32)
+        total = total + arrived[: CORES * share]
+        bias = bias + jnp.sum(arrived[CORES * share :], 0, keepdims=True)
     own_ref[...] = total[:share]
     send_ref[...] = total[share:].astype(BF16)
+    bias_sum_ref[...] = bias
+    bias_send_ref[...] = two_rows(bias, bias_send_ref.shape[0])
 
 
 def join_kernel(weights_ref, rows_ref, send_ref):
@@ -342,13 +347,18 @@
     send_ref[width:] = rows_ref[...]
 
 
-def finish_kernel(core_ref, near_ref, own_ref, far_ref, first_ref, second_ref, rows_ref):
+def finish_kernel(core_ref, near_ref, own_ref, bias_sum_ref, far_ref, *refs):
+    *bias_refs, first_ref, second_ref, rows_ref, bias_ref = refs
     width = near_ref.shape[0]
     near, far = near_ref[...], far_ref[:width]
     is_first = core_ref[0] == 0
     first_ref[...] = jnp.where(is_first, near, far)
     second_ref[...] = jnp.where(is_first, far, near)
     rows_ref[...] = own_ref[...] + far_ref[width:].astype(F32)
+    bias = bias_sum_ref[...]
+    for ref in bias_refs:
+        bias = bias + jnp.sum(ref[...].astype(F32), 0, keepdims=True)
+    bias_ref[...] = bias
 
 
 def body(
@@ -434,19 +444,19 @@
         scratch=[pltpu.VMEM((seeds, rows), BF16)],
         flops=2 * seeds * width * 3 * rows,
     )
-    (plane_send,) = call(
+    plane_send, pair_bias = call(
         pair_sum_kernel, "sum_pair",
-        [((PLANE, width // PLANE + 2 * depth + 8, width), BF16)],
+        [((PLANE, width // PLANE + 2 * depth, width), BF16), ((1, width), F32)],
         [], [keep, pair_arrived], after=[own],
     )
     plane_arrived = swap(plane_send, ("y", "x"))
     (depth_send,) = call(
         plane_sum_kernel, "sum_plane",
         [((depth, 2 * Y_SIZE, width), BF16)],
-        [], [plane_arrived],
+        [], [plane_arrived, pair_bias],
     )
     depth_arrived = swap(depth_send, "z")
-    weight_send, bias_row = call(
+    weight_send, depth_bias = call(
         functools.partial(weight_kernel, scale), "sum_weights",
         [((depth, 2 * Y_SIZE, LANES), BF16), ((1, width), F32)],
         [], [depth_arrived],
@@ -455,8 +465,8 @@
     share = rows // reps
     row_keep, *row_sends = call(
         scatter_kernel, "return_rows",
-        [((CORES * share, width), F32)] + [((CORES * share, width), BF16)] * (X_SIZE - 1),
-        [rep], [lists, depth_arrived, own],
+        [((CORES * share, width), F32)] + [((CORES * share + 16, width), BF16)] * (X_SIZE - 1),
+        [rep], [lists, depth_arrived, own, depth_bias],
         scratch=[pltpu.VMEM((rows, width), F32)],
         flops=4 * parts * rows * width, after=[weight_send],
     )
@@ -468,25 +478,35 @@
         gather_kernel, "gather_weights", [((width // PLANE, width), BF16)],
         [], [weight_depth], flops=window, after=[row_keep],
     )
-    row_own, row_send = call(
-        row_sum_kernel, "sum_rows", [((share, width), F32), ((share, width), BF16)],
-        [], [row_keep, *row_arrived], flops=window,
-    )
+    row_own, row_send, x_bias, bias_send = call(
+        row_sum_kernel, "sum_rows",
+        [((share, width), F32), ((share, width), BF16), ((1, width), F32), ((16, width), BF16)],
+        [], [row_keep, depth_bias, *row_arrived], flops=window,
+    )
+    bias_arrived = [
+        lax.ppermute(bias_send, "y", [(y, y ^ step) for y in range(Y_SIZE)])
+        for step in range(1, Y_SIZE)
+    ]
     (weight_plane,) = call(
         spread_kernel, "spread_weights", [((PLANE, width // PLANE, width), BF16)],
         [], [weight_rows],
     )
     weight_near = swap(weight_plane, ("y", "x")).reshape(width, width)
     (last_send,) = call(
-        join_kernel, "join", [((width + share, width), BF16)], [], [weight_near, row_send]
-    )
-    grad_self, grad_neigh, input_grad = call(
+        join_kernel, "join", [((width + share, width), BF16)], [], [weight_near, row_send],
+        after=bias_arrived,
+    )
+    grad_self, grad_neigh, input_grad, grad_bias = call(
         finish_kernel, "finish",
-        [((width, width), BF16), ((width, width), BF16), ((share, width), F32)],
-        [core], [weight_near, row_own, pair(last_send)],
-    )
-    grad_bias = bias_row.reshape(width)
-    return (out, input_grad, grad_self, grad_neigh, grad_bias)
+        [
+            ((width, width), BF16),
+            ((width, width), BF16),
+            ((share, width), F32),
+            ((1, width), F32),
+        ],
+        [core], [weight_near, row_own, x_bias, pair(last_send), *bias_arrived],
+    )
+    return (out, input_grad, grad_self, grad_neigh, grad_bias.reshape(width))
 
 
 def solution(mesh):

time: 144 us -> 149 us (1.035)
  waiting for transfers between devices: 17 us -> 8 us
  starting transfers between devices: 49.1 us -> 58 us
  local copies, waits for them, and re-layouts: 3.72 us -> 7.4 us
  blocking collectives: 55.6 us -> 57.4 us
    all_to_all x3, waiting for transfers between devices: 13.6 us -> 1.81 us  [swap(): return lax.all_to_all(values, axis, split_axis=0, concat_axis=0, tiled=True)]
    ppermute x0 -> x3, starting transfers between devices: none -> 8.98 us  [body(): lax.ppermute(bias_send, 'y', [(y, y ^ step) for y in range(Y_SIZE)])]
    unnamed x26 -> x32, local copies, waits for them, and re-layouts: 3.72 us -> 6.72 us
    ppermute x0 -> x3, waiting for transfers between devices: none -> 2.84 us  [body(): lax.ppermute(bias_send, 'y', [(y, y ^ step) for y in range(Y_SIZE)])]
    all_to_all x3, blocking collectives: 55.6 us -> 57.4 us  [swap(): return lax.all_to_all(values, axis, split_axis=0, concat_axis=0, tiled=True)]
  transfers between devices with their start and end apart: 9 -> 12, of which waited for: 6 -> 5; matrix products, arithmetic and copies ran while one was open for 0% -> 0% of each run, Pallas kernels for 6% -> 6%
where the time goes in v8:
time: 149 us; the launch traced here: 148 us
  starting transfers between devices  58 us (39%)
  blocking collectives  57.4 us (39%)
  Pallas kernels  16 us (11%)
  waiting for transfers between devices  8 us (5%)
  local copies, waits for them, and re-layouts  7.4 us (5%)
  between operations  1.6 us (1%)
    all_to_all x3, blocking collectives, swap(): return lax.all_to_all(values, axis, split_axis=0, concat_axis=0, tiled=True)  57.4 us
    all_to_all x3, starting transfers between devices, swap(): return lax.all_to_all(values, axis, split_axis=0, concat_axis=0, tiled=True)  24.9 us
    pallas_call x14, Pallas kernels, call(): pl.pallas_call(kernel, out_shape=shapes, in_specs=[pl.BlockSpec(memory_sp...  16 us
    ppermute x3, starting transfers between devices, pair(): return lax.ppermute(values, 'core', [(0, 1), (1, 0)])  15.2 us
    ppermute x3, starting transfers between devices, body(): lax.ppermute(bias_send, 'y', [(y, y ^ step) for y in range(Y_SIZE)])  8.98 us
    ppermute x3, starting transfers between devices, body(): lax.ppermute(row_sends[step - 1], 'x', [(x, x ^ step) for x in range(X_SI...  8.98 us
    unnamed x32, local copies, waits for them, and re-layouts  6.72 us
    ppermute x3, waiting for transfers between devices, pair(): return lax.ppermute(values, 'core', [(0, 1), (1, 0)])  3.34 us
  transfers between devices with their start and end apart: 12, of which 5 were waited for; matrix products, arithmetic and copies ran while one was open for 0% of the time, Pallas kernels for 6%

profile of v8, /device:TPU:1, one launch (start us, length us, event | category | flops | bytes accessed | tf_op | source)
XLA Modules:
  0.0 148.3 jit_solution(6803953829318796112)
XLA Ops:
  0.6 2.1 %pick_boundary.1 = bf16[128,512]{1,0:T(8,128)(2,1)} custom-call(s32[1]{0:T(128)} %bitcast.1.rep_ref.refs_0_, s32[8,64]{1,0:T(8,128)} %bitcast.16, bf16[768,512]{1,0:T(8,128)(2,1)} %feats_ref.1), custom_call_target="tpu_custom_call" | custom-call | flops 100663296 | bytes 919552 | tf_op jit(solution)/shard_map/pick_boundary/pallas_call | solution.py:46
  2.7 15.8 %all-to-all-start = ((bf16[16,8,512]{2,1,0:T(8,128)(2,1)}), bf16[16,8,512]{2,1,0:T(8,128)(2,1)S(1)}, u32[]{:S(2)}, u32[]{:S(2)}) async-start(bf16[16,8,512]{2,1,0:T(8,128)(2,1)} %bitcast.20), calls=%async_computation | async-start | bytes 262144 | tf_op jit(solution)/shard_map/all_to_all | solution.py:395
  19.2 0.7 reshape.42.bias_ref
  19.8 1.1 copy-done
  21.0 1.0 copy-done.4
  22.0 1.0 copy-done.6
  23.0 0.7 copy-done.8
  23.7 0.7 copy-done.10
  24.4 0.7 copy-done.12
  25.0 4.8 %own_rows.1 = (bf16[2560,512]{1,0:T(8,128)(2,1)S(1)}, f32[1024,512]{1,0:T(8,128)S(1)}) custom-call(s32[1]{0:T(128)} %bitcast.core_ref, s32[1,14]{1,0:T(1,128)S(1)} %copy-done.10, s32[1,14]{1,0:T(1,128)S(1)} %copy-done.12, s32[1]{0:T(128)S(6)} %copy.16.count_ref, bf16[14,128,128]{2,1,0:T(8,128)(2,1)S(1)} %copy-done.6, bf16[768,512]{1,0:T(8,128)(2,1)S(1)} %copy-done, ...), custom_call_target="tpu_custom_call" | custom-call | flops 3623878656 | bytes 6491136 | tf_op jit(solution)/shard_map/own_rows/pallas_call | solution.py:46
  29.9 1.5 %copy-done.14 = bf16[2560,512]{1,0:T(8,128)(2,1)} copy-done((bf16[2560,512]{1,0:T(8,128)(2,1)}, bf16[2560,512]{1,0:T(8,128)(2,1)S(1)}, u32[]{:S(2)}) %copy-start.14) | copy-done | bytes 2621464
  31.4 0.0 all-to-all-done
  31.4 0.2 spread_plane.1
  31.6 15.8 %all_to_all.30 = bf16[16,32,512]{2,1,0:T(8,128)(2,1)S(1)} all-to-all(bf16[16,32,512]{2,1,0:T(8,128)(2,1)S(1)} %spread_plane.1), channel_id=1, replica_groups=mesh['z'=16,'y'=4,'x'=4,'core'=2] {'y','x'}, dimensions={0} | all-to-all | bytes 1048576 | tf_op jit(solution)/shard_map/all_to_all | solution.py:395
  47.4 6.1 %collective-permute-start = (bf16[512,512]{1,0:T(8,128)(2,1)S(1)}, bf16[512,512]{1,0:T(8,128)(2,1)S(1)}, u32[]{:S(2)}, u32[]{:S(2)}) collective-permute-start(bf16[512,512]{1,0:T(8,128)(2,1)S(1)} %bitcast.13), channel_id=1, source_target_pairs={{0,1},{1,0},{2,3},{3,2},{4,5},{5,4},{6,7},{7,6},{8,9},{9,8},{10,11... | collective-permute-start | bytes 1572872 | tf_op jit(solution)/shard_map/ppermute | solution.py:398
  53.5 1.5 %collective-permute-done.far_ref = bf16[512,512]{1,0:T(8,128)(2,1)S(1)} collective-permute-done((bf16[512,512]{1,0:T(8,128)(2,1)S(1)}, bf16[512,512]{1,0:T(8,128)(2,1)S(1)}, u32[]{:S(2)}, u32[]{:S(2)}) %collective-permute-start) | collective-permute-done | bytes 524320 | tf_op jit(solution)/shard_map/ppermute | solution.py:398
  55.0 0.0 copy-start.7
  55.0 0.0 copy-start.9
  55.0 0.0 copy-start.11
  55.1 0.0 copy-start.13
  55.1 2.7 %forward_backward.1 = (bf16[512,512]{1,0:T(8,128)(2,1)}, bf16[512,512]{1,0:T(8,128)(2,1)S(1)}, bf16[512,512]{1,0:T(8,128)(2,1)S(1)}, bf16[1040,512]{1,0:T(8,128)(2,1)S(1)}, bf16[1040,512]{1,0:T(8,128)(2,1)S(1)}) custom-call(s32[1]{0:T(128)} %bitcast.core_ref, bf16[512,512]{1,0:T(8,128)(2,1)S(1)} %bitcast.14, ...), custom_call_target="tpu_custom_call" | custom-call | flops 2147483648 | bytes 10518528 | tf_op jit(solution)/shard_map/forward_backward/pallas_call | solution.py:46
  57.8 2.3 %collective-permute-start.1 = (bf16[1040,512]{1,0:T(8,128)(2,1)S(1)}, bf16[1040,512]{1,0:T(8,128)(2,1)S(1)}, u32[]{:S(2)}, u32[]{:S(2)}) collective-permute-start(bf16[1040,512]{1,0:T(8,128)(2,1)S(1)} %get-tuple-element.32), channel_id=1, source_target_pairs={{0,1},{1,0},{2,3},{3,2},{4,5},{5,4},{6,7},{7,6},{8,9},{9,8},{10,11... | collective-permute-start | bytes 3194888 | tf_op jit(solution)/shard_map/ppermute | solution.py:398
  60.1 2.1 %own_rows_back.1.refs_2_.refs_3_ = f32[768,512]{1,0:T(8,128)S(1)} custom-call(s32[1,14]{1,0:T(1,128)S(1)} %copy-done.11, s32[1,14]{1,0:T(1,128)S(1)} %copy-done.13, s32[1]{0:T(128)S(6)} %copy.16.count_ref, bf16[14,128,128]{2,1,0:T(8,128)(2,1)S(1)} %copy-done.7, s32[1,512]{1,0:T(1,128)S(1)} %bitcast.19, bf16[512,512]{1,0:T(8,128)(2,1)S(1)} %get-tuple-element.33.d_pre_ref, ...), custom_call_target="tpu_custom_call" | custom-call | flops 1207959552 | bytes 3606528 | tf_op jit(solution)/shard_map/own_rows_back/pallas_call | solution.py:46
  62.2 0.2 collective-permute-done.1.refs_1_
  62.3 0.2 sum_pair.1
  62.6 0.0 copy-start.1
  62.6 19.0 %all_to_all.31.arrived_ref = bf16[16,64,512]{2,1,0:T(8,128)(2,1)S(1)} all-to-all(bf16[16,64,512]{2,1,0:T(8,128)(2,1)S(1)} %get-tuple-element.35), channel_id=1, replica_groups=mesh['z'=16,'y'=4,'x'=4,'core'=2] {'y','x'}, dimensions={0} | all-to-all | bytes 2097152 | tf_op jit(solution)/shard_map/all_to_all | solution.py:395
  81.6 0.3 sum_plane.1
  81.9 22.5 %all_to_all.32.arrived_ref.refs_2_ = bf16[16,8,512]{2,1,0:T(8,128)(2,1)S(1)} all-to-all(bf16[16,8,512]{2,1,0:T(8,128)(2,1)S(1)} %sum_plane.1), channel_id=1, replica_groups=mesh['z'=16,'y'=4,'x'=4,'core'=2] {'z'}, dimensions={0} | all-to-all | bytes 262144 | tf_op jit(solution)/shard_map/all_to_all | solution.py:395
  104.4 0.6 sum_weights.1
  105.1 5.1 %all-to-all-start.4 = ((bf16[16,8,128]{2,1,0:T(8,128)(2,1)}), bf16[16,8,128]{2,1,0:T(8,128)(2,1)S(1)}, u32[]{:S(2)}, u32[]{:S(2)}) async-start(bf16[16,8,128]{2,1,0:T(8,128)(2,1)} %get-tuple-element.37.refs_5_), calls=%async_computation.4 | async-start | bytes 65536 | tf_op jit(solution)/shard_map/all_to_all | solution.py:395
  110.2 0.6 return_rows.1
  110.8 3.8 %collective-permute-start.2 = (bf16[208,512]{1,0:T(8,128)(2,1)S(1)}, bf16[208,512]{1,0:T(8,128)(2,1)S(1)}, u32[]{:S(2)}, u32[]{:S(2)}) collective-permute-start(bf16[208,512]{1,0:T(8,128)(2,1)S(1)} %get-tuple-element.40), channel_id=1, source_target_pairs={{0,4},{2,6},{4,0},{6,2},{1,5},{3,7},{5,1},{7,3},{8,12},{10,14},{12... | collective-permute-start | bytes 638984 | tf_op jit(solution)/shard_map/ppermute | solution.py:474
  114.7 1.9 %collective-permute-start.3 = (bf16[208,512]{1,0:T(8,128)(2,1)S(1)}, bf16[208,512]{1,0:T(8,128)(2,1)S(1)}, u32[]{:S(2)}, u32[]{:S(2)}) collective-permute-start(bf16[208,512]{1,0:T(8,128)(2,1)S(1)} %get-tuple-element.41), channel_id=1, source_target_pairs={{0,2},{2,0},{4,6},{6,4},{1,3},{3,1},{5,7},{7,5},{8,10},{10,8},{12,... | collective-permute-start | bytes 638984 | tf_op jit(solution)/shard_map/ppermute | solution.py:474
  116.6 3.2 %collective-permute-start.4 = (bf16[208,512]{1,0:T(8,128)(2,1)S(1)}, bf16[208,512]{1,0:T(8,128)(2,1)S(1)}, u32[]{:S(2)}, u32[]{:S(2)}) collective-permute-start(bf16[208,512]{1,0:T(8,128)(2,1)S(1)} %get-tuple-element.42), channel_id=1, source_target_pairs={{0,6},{2,4},{4,2},{6,0},{1,7},{3,5},{5,3},{7,1},{8,14},{10,12},{12... | collective-permute-start | bytes 638984 | tf_op jit(solution)/shard_map/ppermute | solution.py:474
  119.8 1.8 %all-to-all-done.4.refs_0_ = bf16[16,8,128]{2,1,0:T(8,128)(2,1)S(1)} async-done(((bf16[16,8,128]{2,1,0:T(8,128)(2,1)}), bf16[16,8,128]{2,1,0:T(8,128)(2,1)S(1)}, u32[]{:S(2)}, u32[]{:S(2)}) %all-to-all-start.4) | async-done | bytes 32800 | tf_op jit(solution)/shard_map/all_to_all | solution.py:395
  121.6 0.1 gather_weights.1.whole_ref
  121.8 0.8 spread_weights.1
  122.6 4.0 %all-to-all-start.5 = ((bf16[16,32,512]{2,1,0:T(8,128)(2,1)}), bf16[16,32,512]{2,1,0:T(8,128)(2,1)S(1)}, u32[]{:S(2)}, u32[]{:S(2)}) async-start(bf16[16,32,512]{2,1,0:T(8,128)(2,1)} %spread_weights.1), calls=%async_computation.5 | async-start | bytes 1048576 | tf_op jit(solution)/shard_map/all_to_all | solution.py:395
  126.7 0.0 collective-permute-done.3.refs_1_
  126.7 0.1 sum_rows.1
  126.8 4.5 %collective-permute-start.7 = (bf16[16,512]{1,0:T(8,128)(2,1)S(1)}, bf16[16,512]{1,0:T(8,128)(2,1)S(1)}, u32[]{:S(2)}, u32[]{:S(2)}) collective-permute-start(bf16[16,512]{1,0:T(8,128)(2,1)S(1)} %get-tuple-element.46), channel_id=1, source_target_pairs={{0,24},{8,16},{16,8},{24,0},{1,25},{9,17},{17,9},{25,1},{2,26},{10... | collective-permute-start | bytes 49160 | tf_op jit(solution)/shard_map/ppermute | solution.py:487
  131.3 2.5 %collective-permute-start.6 = (bf16[16,512]{1,0:T(8,128)(2,1)S(1)}, bf16[16,512]{1,0:T(8,128)(2,1)S(1)}, u32[]{:S(2)}, u32[]{:S(2)}) collective-permute-start(bf16[16,512]{1,0:T(8,128)(2,1)S(1)} %get-tuple-element.46), channel_id=1, source_target_pairs={{0,16},{8,24},{16,0},{24,8},{1,17},{9,25},{17,1},{25,9},{2,18},{10... | collective-permute-start | bytes 49160 | tf_op jit(solution)/shard_map/ppermute | solution.py:487
  133.8 2.0 %collective-permute-start.5 = (bf16[16,512]{1,0:T(8,128)(2,1)S(1)}, bf16[16,512]{1,0:T(8,128)(2,1)S(1)}, u32[]{:S(2)}, u32[]{:S(2)}) collective-permute-start(bf16[16,512]{1,0:T(8,128)(2,1)S(1)} %get-tuple-element.46), channel_id=1, source_target_pairs={{0,8},{8,0},{16,24},{24,16},{1,9},{9,1},{17,25},{25,17},{2,10},{10... | collective-permute-start | bytes 49160 | tf_op jit(solution)/shard_map/ppermute | solution.py:487
  135.8 2.8 %collective-permute-done.6.refs_3_.refs_1_ = bf16[16,512]{1,0:T(8,128)(2,1)S(1)} collective-permute-done((bf16[16,512]{1,0:T(8,128)(2,1)S(1)}, bf16[16,512]{1,0:T(8,128)(2,1)S(1)}, u32[]{:S(2)}, u32[]{:S(2)}) %collective-permute-start.6) | collective-permute-done | bytes 16416 | tf_op jit(solution)/shard_map/ppermute | solution.py:487
  138.7 6.8 %collective-permute-start.8 = (bf16[608,512]{1,0:T(8,128)(2,1)S(1)}, bf16[608,512]{1,0:T(8,128)(2,1)S(1)}, u32[]{:S(2)}, u32[]{:S(2)}) collective-permute-start(bf16[608,512]{1,0:T(8,128)(2,1)S(1)} %join.1), channel_id=1, source_target_pairs={{0,1},{1,0},{2,3},{3,2},{4,5},{5,4},{6,7},{7,6},{8,9},{9,8},{10,11... | collective-permute-start | bytes 1867784 | tf_op jit(solution)/shard_map/ppermute | solution.py:398
  145.5 1.7 %collective-permute-done.8.far_ref = bf16[608,512]{1,0:T(8,128)(2,1)S(1)} collective-permute-done((bf16[608,512]{1,0:T(8,128)(2,1)S(1)}, bf16[608,512]{1,0:T(8,128)(2,1)S(1)}, u32[]{:S(2)}, u32[]{:S(2)}) %collective-permute-start.8) | collective-permute-done | bytes 622624 | tf_op jit(solution)/shard_map/ppermute | solution.py:398
  147.2 1.1 finish.1
  (26 shorter events, 0.1 us)
Async XLA Ops:
  2.7 28.6 %all-to-all-start = ((bf16[16,8,512]{2,1,0:T(8,128)(2,1)}), bf16[16,8,512]{2,1,0:T(8,128)(2,1)S(1)}, u32[]{:S(2)}, u32[]{:S(2)}) async-start(bf16[16,8,512]{2,1,0:T(8,128)(2,1)} %bitcast.20), calls=%async_computation | async-start | bytes 262144 | tf_op jit(solution)/shard_map/all_to_all | solution.py:395
  19.8 1.1 copy-start
  21.0 1.0 copy-start.4
  22.0 1.0 copy-start.6
  23.0 0.7 copy-start.8
  23.7 0.7 copy-start.10
  24.4 0.7 copy-start.12
  29.9 1.5 %copy-start.14 = (bf16[2560,512]{1,0:T(8,128)(2,1)}, bf16[2560,512]{1,0:T(8,128)(2,1)S(1)}, u32[]{:S(2)}) copy-start(bf16[2560,512]{1,0:T(8,128)(2,1)S(1)} %get-tuple-element.29.mats_ref) | copy-start | bytes 7864324
  31.4 23.6 %copy-start.2 = (bf16[512,512]{1,0:T(8,128)(2,1)S(1)}, bf16[512,512]{1,0:T(8,128)(2,1)}, u32[]{:S(2)}) copy-start(bf16[512,512]{1,0:T(8,128)(2,1)} %w_neigh_ref.1) | copy-start | bytes 1572868
  31.4 23.6 %copy-start.3 = (bf16[512,512]{1,0:T(8,128)(2,1)S(1)}, bf16[512,512]{1,0:T(8,128)(2,1)}, u32[]{:S(2)}) copy-start(bf16[512,512]{1,0:T(8,128)(2,1)} %cot_ref.1) | copy-start | bytes 1572868
  31.4 23.6 %copy-start.15 = (bf16[2560,512]{1,0:T(8,128)(2,1)S(1)}, bf16[2560,512]{1,0:T(8,128)(2,1)}, u32[]{:S(2)}) copy-start(bf16[2560,512]{1,0:T(8,128)(2,1)} %copy-done.14) | copy-start | bytes 7864324
  47.4 7.6 %collective-permute-start = (bf16[512,512]{1,0:T(8,128)(2,1)S(1)}, bf16[512,512]{1,0:T(8,128)(2,1)S(1)}, u32[]{:S(2)}, u32[]{:S(2)}) collective-permute-start(bf16[512,512]{1,0:T(8,128)(2,1)S(1)} %bitcast.13), channel_id=1, source_target_pairs={{0,1},{1,0},{2,3},{3,2},{4,5},{5,4},{6,7},{7,6},{8,9},{9,8},{10,11... | collective-permute-start | bytes 1572872 | tf_op jit(solution)/shard_map/ppermute | solution.py:398
  55.0 5.0 %copy-start.5 = (bf16[512,512]{1,0:T(8,128)(2,1)S(1)}, bf16[512,512]{1,0:T(8,128)(2,1)}, u32[]{:S(2)}) copy-start(bf16[512,512]{1,0:T(8,128)(2,1)} %w_self_ref.3) | copy-start | bytes 1572868
  55.0 5.0 %copy-start.7 = (bf16[14,128,128]{2,1,0:T(8,128)(2,1)S(1)}, bf16[14,128,128]{2,1,0:T(8,128)(2,1)}, u32[]{:S(2)}) copy-start(bf16[14,128,128]{2,1,0:T(8,128)(2,1)} %tiles_ref.3) | copy-start | bytes 1376260
  55.0 5.0 %copy-start.9 = (s32[512]{0:T(512)S(1)}, s32[512]{0:T(512)}, u32[]{:S(2)}) copy-start(s32[512]{0:T(512)} %param.13) | copy-start | bytes 6148
  55.0 5.0 %copy-start.11 = (s32[1,14]{1,0:T(1,128)S(1)}, s32[1,14]{1,0:T(1,128)}, u32[]{:S(2)}) copy-start(s32[1,14]{1,0:T(1,128)} %dst_ref.3) | copy-start | bytes 172
  55.1 5.0 %copy-start.13 = (s32[1,14]{1,0:T(1,128)S(1)}, s32[1,14]{1,0:T(1,128)}, u32[]{:S(2)}) copy-start(s32[1,14]{1,0:T(1,128)} %src_ref.3) | copy-start | bytes 172
  57.8 4.6 %collective-permute-start.1 = (bf16[1040,512]{1,0:T(8,128)(2,1)S(1)}, bf16[1040,512]{1,0:T(8,128)(2,1)S(1)}, u32[]{:S(2)}, u32[]{:S(2)}) collective-permute-start(bf16[1040,512]{1,0:T(8,128)(2,1)S(1)} %get-tuple-element.32), channel_id=1, source_target_pairs={{0,1},{1,0},{2,3},{3,2},{4,5},{5,4},{6,7},{7,6},{8,9},{9,8},{10,11... | collective-permute-start | bytes 3194888 | tf_op jit(solution)/shard_map/ppermute | solution.py:398
  62.6 47.6 %copy-start.1 = (s32[1,64,8]{1,2,0:T(8,128)S(1)}, s32[1,64,8]{1,2,0:T(8,128)}, u32[]{:S(2)}) copy-start(s32[1,64,8]{1,2,0:T(8,128)} %param.12) | copy-start | bytes 6148
  105.1 16.6 %all-to-all-start.4 = ((bf16[16,8,128]{2,1,0:T(8,128)(2,1)}), bf16[16,8,128]{2,1,0:T(8,128)(2,1)S(1)}, u32[]{:S(2)}, u32[]{:S(2)}) async-start(bf16[16,8,128]{2,1,0:T(8,128)(2,1)} %get-tuple-element.37.refs_5_), calls=%async_computation.4 | async-start | bytes 65536 | tf_op jit(solution)/shard_map/all_to_all | solution.py:395
  110.8 15.8 %collective-permute-start.2 = (bf16[208,512]{1,0:T(8,128)(2,1)S(1)}, bf16[208,512]{1,0:T(8,128)(2,1)S(1)}, u32[]{:S(2)}, u32[]{:S(2)}) collective-permute-start(bf16[208,512]{1,0:T(8,128)(2,1)S(1)} %get-tuple-element.40), channel_id=1, source_target_pairs={{0,4},{2,6},{4,0},{6,2},{1,5},{3,7},{5,1},{7,3},{8,12},{10,14},{12... | collective-permute-start | bytes 638984 | tf_op jit(solution)/shard_map/ppermute | solution.py:474
  114.7 12.0 %collective-permute-start.3 = (bf16[208,512]{1,0:T(8,128)(2,1)S(1)}, bf16[208,512]{1,0:T(8,128)(2,1)S(1)}, u32[]{:S(2)}, u32[]{:S(2)}) collective-permute-start(bf16[208,512]{1,0:T(8,128)(2,1)S(1)} %get-tuple-element.41), channel_id=1, source_target_pairs={{0,2},{2,0},{4,6},{6,4},{1,3},{3,1},{5,7},{7,5},{8,10},{10,8},{12,... | collective-permute-start | bytes 638984 | tf_op jit(solution)/shard_map/ppermute | solution.py:474
  116.6 10.1 %collective-permute-start.4 = (bf16[208,512]{1,0:T(8,128)(2,1)S(1)}, bf16[208,512]{1,0:T(8,128)(2,1)S(1)}, u32[]{:S(2)}, u32[]{:S(2)}) collective-permute-start(bf16[208,512]{1,0:T(8,128)(2,1)S(1)} %get-tuple-element.42), channel_id=1, source_target_pairs={{0,6},{2,4},{4,2},{6,0},{1,7},{3,5},{5,3},{7,1},{8,14},{10,12},{12... | collective-permute-start | bytes 638984 | tf_op jit(solution)/shard_map/ppermute | solution.py:474
  122.6 16.0 %all-to-all-start.5 = ((bf16[16,32,512]{2,1,0:T(8,128)(2,1)}), bf16[16,32,512]{2,1,0:T(8,128)(2,1)S(1)}, u32[]{:S(2)}, u32[]{:S(2)}) async-start(bf16[16,32,512]{2,1,0:T(8,128)(2,1)} %spread_weights.1), calls=%async_computation.5 | async-start | bytes 1048576 | tf_op jit(solution)/shard_map/all_to_all | solution.py:395
  126.8 9.0 %collective-permute-start.7 = (bf16[16,512]{1,0:T(8,128)(2,1)S(1)}, bf16[16,512]{1,0:T(8,128)(2,1)S(1)}, u32[]{:S(2)}, u32[]{:S(2)}) collective-permute-start(bf16[16,512]{1,0:T(8,128)(2,1)S(1)} %get-tuple-element.46), channel_id=1, source_target_pairs={{0,24},{8,16},{16,8},{24,0},{1,25},{9,17},{17,9},{25,1},{2,26},{10... | collective-permute-start | bytes 49160 | tf_op jit(solution)/shard_map/ppermute | solution.py:487
  131.3 7.4 %collective-permute-start.6 = (bf16[16,512]{1,0:T(8,128)(2,1)S(1)}, bf16[16,512]{1,0:T(8,128)(2,1)S(1)}, u32[]{:S(2)}, u32[]{:S(2)}) collective-permute-start(bf16[16,512]{1,0:T(8,128)(2,1)S(1)} %get-tuple-element.46), channel_id=1, source_target_pairs={{0,16},{8,24},{16,0},{24,8},{1,17},{9,25},{17,1},{25,9},{2,18},{10... | collective-permute-start | bytes 49160 | tf_op jit(solution)/shard_map/ppermute | solution.py:487
  133.8 4.9 %collective-permute-start.5 = (bf16[16,512]{1,0:T(8,128)(2,1)S(1)}, bf16[16,512]{1,0:T(8,128)(2,1)S(1)}, u32[]{:S(2)}, u32[]{:S(2)}) collective-permute-start(bf16[16,512]{1,0:T(8,128)(2,1)S(1)} %get-tuple-element.46), channel_id=1, source_target_pairs={{0,8},{8,0},{16,24},{24,16},{1,9},{9,1},{17,25},{25,17},{2,10},{10... | collective-permute-start | bytes 49160 | tf_op jit(solution)/shard_map/ppermute | solution.py:487
  138.7 8.5 %collective-permute-start.8 = (bf16[608,512]{1,0:T(8,128)(2,1)S(1)}, bf16[608,512]{1,0:T(8,128)(2,1)S(1)}, u32[]{:S(2)}, u32[]{:S(2)}) collective-permute-start(bf16[608,512]{1,0:T(8,128)(2,1)S(1)} %join.1), channel_id=1, source_target_pairs={{0,1},{1,0},{2,3},{3,2},{4,5},{5,4},{6,7},{7,6},{8,9},{9,8},{10,11... | collective-permute-start | bytes 1867784 | tf_op jit(solution)/shard_map/ppermute | solution.py:398

commit v9 on v7

--- a/solution.py
+++ b/solution.py
@@ -18,6 +18,8 @@
 PLANE = Y_SIZE * X_SIZE
 BF16 = jnp.bfloat16
 F32 = jnp.float32
+ROUND_FLOPS = 0
+SUM_FLOPS = 20_000_000_000
 VMEM_BYTES = 24 * 1024 * 1024
 FULL_VMEM_BYTES = 65 * 1000 * 1024
 
@@ -234,11 +236,10 @@
         ).astype(BF16)
 
 
-def plane_sum_kernel(arrived_ref, send_ref):
+def plane_sum_kernel(arrived_ref, send_ref, round_ref, whole_ref):
     chunks, lines, width = arrived_ref.shape
     depth, block, _ = send_ref.shape
     weight = width // chunks
-    each = weight // depth
     tail = weight + 2 * depth
     rows = []
     rest = None
@@ -248,50 +249,33 @@
             some = some + arrived_ref[y * X_SIZE + x].astype(F32)
         rows.append(some[weight : weight + depth])
         rest = some if rest is None else rest + some
-    bias = jnp.zeros((depth, width), F32) + jnp.sum(rest[tail:], 0, keepdims=True)
-    rows += [rest[weight + depth : tail], rest[:weight], bias]
-    rows = jnp.concatenate(rows, 0).astype(BF16)
+    rows = jnp.concatenate(rows + [rest[weight + depth : tail]], 0).astype(BF16)
     shape = (depth * block, rows.shape[0])
     out, into = iota(shape, 0), iota(shape, 1)
     line, z = out % block, out // block
-    first = (Y_SIZE + 1) * depth
-    of_weight = jnp.logical_and(line > Y_SIZE, line <= Y_SIZE + each)
-    wanted = jnp.where(
-        of_weight,
-        first + z * each + line - Y_SIZE - 1,
-        jnp.where(line <= Y_SIZE, line * depth, first + weight) + z,
-    )
+    wanted = jnp.where(line <= Y_SIZE, line * depth + z, -1)
     send_ref[...] = move(into == wanted, rows).reshape(depth, block, width)
-
-
-def weight_kernel(scale, arrived_ref, send_ref, bias_ref):
-    depth, block, width = arrived_ref.shape
-    total = jnp.sum(arrived_ref[...].astype(F32), 0) * scale
-    each = block - Y_SIZE - 2
-    row = iota((block, LANES), 0)
-    done = jnp.zeros((block, LANES), F32)
-    for group in range(width // LANES):
-        for line in range(each):
-            some = total[Y_SIZE + 1 + line : Y_SIZE + 2 + line, group * LANES : (group + 1) * LANES]
-            done = jnp.where(row == group * each + line, some, done)
-    done = done.astype(BF16)
-    for z in range(depth):
-        send_ref[z] = done
-    bias_ref[...] = total[block - 1 :]
-
-
-def gather_kernel(arrived_ref, whole_ref):
-    weight, width = whole_ref.shape
-    depth, block, _ = arrived_ref.shape
-    groups = width // LANES
-    each = weight // depth
-    arrived = arrived_ref[...].reshape(depth * block, LANES)
-    shape = (weight, depth * block)
-    out, into = iota(shape, 0), iota(shape, 1)
-    z, line = out // each, out % each
-    for group in range(groups):
-        rows = move(into == z * block + group * each + line, arrived)
-        whole_ref[:, group * LANES : (group + 1) * LANES] = rows
+    whole_ref[:weight] = rest[:weight]
+    bias = jnp.sum(rest[tail:], 0, keepdims=True)
+    row = iota((whole_ref.shape[0] - weight, width), 0)
+    whole_ref[weight:] = jnp.where(row == 0, bias, 0.0)
+    round_ref[...] = whole_ref[...].astype(BF16)
+
+
+def sum_four(own_ref, beside_ref, far_ref, farther_ref):
+    pair = own_ref[...].astype(F32) + beside_ref[...].astype(F32)
+    return pair + (far_ref[...].astype(F32) + farther_ref[...].astype(F32))
+
+
+def round_kernel(own_ref, beside_ref, far_ref, farther_ref, send_ref):
+    send_ref[...] = sum_four(own_ref, beside_ref, far_ref, farther_ref).astype(BF16)
+
+
+def weight_kernel(scale, own_ref, beside_ref, far_ref, farther_ref, whole_ref, bias_ref):
+    weight = whole_ref.shape[0]
+    total = sum_four(own_ref, beside_ref, far_ref, farther_ref) * scale
+    whole_ref[...] = total[:weight].astype(BF16)
+    bias_ref[...] = jnp.sum(total[weight:], 0, keepdims=True)
 
 
 def spread_kernel(whole_ref, send_ref):
@@ -440,41 +424,52 @@
         [], [keep, pair_arrived], after=[own],
     )
     plane_arrived = swap(plane_send, ("y", "x"))
-    (depth_send,) = call(
+    weight = width // PLANE
+    depth_send, round_send = call(
         plane_sum_kernel, "sum_plane",
-        [((depth, 2 * Y_SIZE, width), BF16)],
+        [((depth, 2 * Y_SIZE, width), BF16), ((weight + 16, width), BF16)],
         [], [plane_arrived],
+        scratch=[pltpu.VMEM((weight + 16, width), F32)],
     )
     depth_arrived = swap(depth_send, "z")
-    weight_send, bias_row = call(
+
+    def four(values, stride):
+        steps = [stride * step for step in range(1, 4)] if stride < depth else [0, 0, 0]
+        moved = {
+            step: lax.ppermute(values, "z", [(z, z ^ step) for z in range(depth)])
+            for step in sorted(steps, key=lambda step: -min(step, depth - step))
+            if step
+        }
+        return [values] + [moved[step] if step else jnp.zeros_like(values) for step in steps]
+
+    (round_send,) = call(
+        round_kernel, "sum_round", [((weight + 16, width), BF16)], [], four(round_send, 1),
+        flops=ROUND_FLOPS,
+    )
+    weight_rows, bias_row = call(
         functools.partial(weight_kernel, scale), "sum_weights",
-        [((depth, 2 * Y_SIZE, LANES), BF16), ((1, width), F32)],
-        [], [depth_arrived],
-    )
-    weight_depth = swap(weight_send, "z")
+        [((weight, width), BF16), ((1, width), F32)], [], four(round_send, 4),
+        flops=SUM_FLOPS,
+    )
     share = rows // reps
     row_keep, *row_sends = call(
         scatter_kernel, "return_rows",
         [((CORES * share, width), F32)] + [((CORES * share, width), BF16)] * (X_SIZE - 1),
         [rep], [lists, depth_arrived, own],
         scratch=[pltpu.VMEM((rows, width), F32)],
-        flops=4 * parts * rows * width, after=[weight_send],
+        flops=4 * parts * rows * width,
     )
     row_arrived = [
         lax.ppermute(row_sends[step - 1], "x", [(x, x ^ step) for x in range(X_SIZE)])
         for step in (2, 1, 3)
     ]
-    (weight_rows,) = call(
-        gather_kernel, "gather_weights", [((width // PLANE, width), BF16)],
-        [], [weight_depth], flops=window, after=[row_keep],
-    )
     row_own, row_send = call(
         row_sum_kernel, "sum_rows", [((share, width), F32), ((share, width), BF16)],
         [], [row_keep, *row_arrived], flops=window,
     )
     (weight_plane,) = call(
         spread_kernel, "spread_weights", [((PLANE, width // PLANE, width), BF16)],
-        [], [weight_rows],
+        [], [weight_rows], after=[row_keep],
     )
     weight_near = swap(weight_plane, ("y", "x")).reshape(width, width)
     (last_send,) = call(

time: 144 us -> 155 us (1.076)
  starting transfers between devices: 49.1 us -> 76.3 us
  blocking collectives: 55.6 us -> 36.7 us
  waiting for transfers between devices: 17 us -> 19.2 us
    ppermute x0 -> x6, starting transfers between devices: none -> 25.5 us  [four(): lax.ppermute(values, 'z', [(z, z ^ step) for z in range(depth)])]
    all_to_all x3 -> x2, blocking collectives: 55.6 us -> 36.7 us  [swap(): return lax.all_to_all(values, axis, split_axis=0, concat_axis=0, tiled=True)]
    ppermute x0 -> x6, waiting for transfers between devices: none -> 4.25 us  [four(): lax.ppermute(values, 'z', [(z, z ^ step) for z in range(depth)])]
    all_to_all x3, waiting for transfers between devices: 13.6 us -> 11.6 us  [swap(): return lax.all_to_all(values, axis, split_axis=0, concat_axis=0, tiled=True)]
    all_to_all x3, starting transfers between devices: 24.7 us -> 26.3 us  [swap(): return lax.all_to_all(values, axis, split_axis=0, concat_axis=0, tiled=True)]
  transfers between devices with their start and end apart: 9 -> 15, of which waited for: 6 -> 6; matrix products, arithmetic and copies ran while one was open for 0% -> 0% of each run, Pallas kernels for 6% -> 6%
where the time goes in v9:
time: 155 us; the launch traced here: 154 us
  starting transfers between devices  76.3 us (49%)
  blocking collectives  36.7 us (24%)
  waiting for transfers between devices  19.2 us (12%)
  Pallas kernels  16.5 us (11%)
  local copies, waits for them, and re-layouts  3.71 us (2%)
  between operations  1.67 us (1%)
    all_to_all x2, blocking collectives, swap(): return lax.all_to_all(values, axis, split_axis=0, concat_axis=0, tiled=True)  36.7 us
    all_to_all x3, starting transfers between devices, swap(): return lax.all_to_all(values, axis, split_axis=0, concat_axis=0, tiled=True)  26.3 us
    ppermute x6, starting transfers between devices, four(): lax.ppermute(values, 'z', [(z, z ^ step) for z in range(depth)])  25.5 us
    pallas_call x14, Pallas kernels, call(): pl.pallas_call(kernel, out_shape=shapes, in_specs=[pl.BlockSpec(memory_sp...  16.5 us
    ppermute x3, starting transfers between devices, pair(): return lax.ppermute(values, 'core', [(0, 1), (1, 0)])  15.4 us
    all_to_all x3, waiting for transfers between devices, swap(): return lax.all_to_all(values, axis, split_axis=0, concat_axis=0, tiled=True)  11.6 us
    ppermute x3, starting transfers between devices, body(): lax.ppermute(row_sends[step - 1], 'x', [(x, x ^ step) for x in range(X_SI...  8.98 us
    ppermute x6, waiting for transfers between devices, four(): lax.ppermute(values, 'z', [(z, z ^ step) for z in range(depth)])  4.25 us
  transfers between devices with their start and end apart: 15, of which 6 were waited for; matrix products, arithmetic and copies ran while one was open for 0% of the time, Pallas kernels for 6%

profile of v9, /device:TPU:1, one launch (start us, length us, event | category | flops | bytes accessed | tf_op | source)
XLA Modules:
  0.0 154.0 jit_solution(10815655549632622625)
XLA Ops:
  0.7 2.2 %pick_boundary.1 = bf16[128,512]{1,0:T(8,128)(2,1)} custom-call(s32[1]{0:T(128)} %bitcast.1.rep_ref, s32[8,64]{1,0:T(8,128)} %bitcast.16, bf16[768,512]{1,0:T(8,128)(2,1)} %feats_ref.1), custom_call_target="tpu_custom_call" | custom-call | flops 100663296 | bytes 919552 | tf_op jit(solution)/shard_map/pick_boundary/pallas_call | solution.py:53
  2.9 15.8 %all-to-all-start = ((bf16[16,8,512]{2,1,0:T(8,128)(2,1)}), bf16[16,8,512]{2,1,0:T(8,128)(2,1)S(1)}, u32[]{:S(2)}, u32[]{:S(2)}) async-start(bf16[16,8,512]{2,1,0:T(8,128)(2,1)} %bitcast.20), calls=%async_computation | async-start | bytes 262144 | tf_op jit(solution)/shard_map/all_to_all | solution.py:369
  19.3 0.0 copy-start
  19.4 1.1 copy-done
  20.5 1.0 copy-done.4
  21.5 4.9 %own_rows.1 = (bf16[2560,512]{1,0:T(8,128)(2,1)S(1)}, f32[1024,512]{1,0:T(8,128)S(1)}) custom-call(s32[1]{0:T(128)} %bitcast.core_ref, s32[1,14]{1,0:T(1,128)S(1)} %copy-done.8, s32[1,14]{1,0:T(1,128)S(1)} %copy-done.9, s32[1]{0:T(128)S(6)} %copy.16.count_ref, bf16[14,128,128]{2,1,0:T(8,128)(2,1)S(1)} %copy-done.6, bf16[768,512]{1,0:T(8,128)(2,1)S(1)} %copy-done, ...), custom_call_target="tpu_custom_call" | custom-call | flops 3623878656 | bytes 6491136 | tf_op jit(solution)/shard_map/own_rows/pallas_call | solution.py:53
  26.4 1.5 copy-done.10
  27.9 2.7 %all-to-all-done = bf16[16,8,512]{2,1,0:T(8,128)(2,1)S(1)} async-done(((bf16[16,8,512]{2,1,0:T(8,128)(2,1)}), bf16[16,8,512]{2,1,0:T(8,128)(2,1)S(1)}, u32[]{:S(2)}, u32[]{:S(2)}) %all-to-all-start) | async-done | bytes 131104 | tf_op jit(solution)/shard_map/all_to_all | solution.py:369
  30.6 0.2 spread_plane.1
  30.8 16.0 %all_to_all.25 = bf16[16,32,512]{2,1,0:T(8,128)(2,1)S(1)} all-to-all(bf16[16,32,512]{2,1,0:T(8,128)(2,1)S(1)} %spread_plane.1), channel_id=1, replica_groups=mesh['z'=16,'y'=4,'x'=4,'core'=2] {'y','x'}, dimensions={0} | all-to-all | bytes 1048576 | tf_op jit(solution)/shard_map/all_to_all | solution.py:369
  46.8 6.8 %collective-permute-start = (bf16[512,512]{1,0:T(8,128)(2,1)S(1)}, bf16[512,512]{1,0:T(8,128)(2,1)S(1)}, u32[]{:S(2)}, u32[]{:S(2)}) collective-permute-start(bf16[512,512]{1,0:T(8,128)(2,1)S(1)} %bitcast.13), channel_id=1, source_target_pairs={{0,1},{1,0},{2,3},{3,2},{4,5},{5,4},{6,7},{7,6},{8,9},{9,8},{10,11... | collective-permute-start | bytes 1572872 | tf_op jit(solution)/shard_map/ppermute | solution.py:372
  53.6 1.5 collective-permute-done.far_ref
  55.1 2.7 %forward_backward.1 = (bf16[512,512]{1,0:T(8,128)(2,1)}, bf16[512,512]{1,0:T(8,128)(2,1)S(1)}, bf16[512,512]{1,0:T(8,128)(2,1)S(1)}, bf16[1040,512]{1,0:T(8,128)(2,1)S(1)}, bf16[1040,512]{1,0:T(8,128)(2,1)S(1)}) custom-call(s32[1]{0:T(128)} %bitcast.core_ref, bf16[512,512]{1,0:T(8,128)(2,1)S(1)} %bitcast.14, ...), custom_call_target="tpu_custom_call" | custom-call | flops 2147483648 | bytes 10518528 | tf_op jit(solution)/shard_map/forward_backward/pallas_call | solution.py:53
  57.8 2.3 %collective-permute-start.1 = (bf16[1040,512]{1,0:T(8,128)(2,1)S(1)}, bf16[1040,512]{1,0:T(8,128)(2,1)S(1)}, u32[]{:S(2)}, u32[]{:S(2)}) collective-permute-start(bf16[1040,512]{1,0:T(8,128)(2,1)S(1)} %get-tuple-element.29), channel_id=1, source_target_pairs={{0,1},{1,0},{2,3},{3,2},{4,5},{5,4},{6,7},{7,6},{8,9},{9,8},{10,11... | collective-permute-start | bytes 3194888 | tf_op jit(solution)/shard_map/ppermute | solution.py:372
  60.1 2.1 %own_rows_back.1.refs_2_.own_ref = f32[768,512]{1,0:T(8,128)S(1)} custom-call(s32[1,14]{1,0:T(1,128)S(1)} %copy-done.8, s32[1,14]{1,0:T(1,128)S(1)} %copy-done.9, s32[1]{0:T(128)S(6)} %copy.16.count_ref, bf16[14,128,128]{2,1,0:T(8,128)(2,1)S(1)} %copy-done.6, s32[1,512]{1,0:T(1,128)S(1)} %bitcast.19, bf16[512,512]{1,0:T(8,128)(2,1)S(1)} %get-tuple-element.30.d_pre_ref, ...), custom_call_target="tpu_custom_call" | custom-call | flops 1207959552 | bytes 3606528 | tf_op jit(solution)/shard_map/own_rows_back/pallas_call | solution.py:53
  62.2 0.2 collective-permute-done.1.refs_1_
  62.4 0.2 sum_pair.1
  62.7 20.7 %all_to_all.26.arrived_ref = bf16[16,72,512]{2,1,0:T(8,128)(2,1)S(1)} all-to-all(bf16[16,72,512]{2,1,0:T(8,128)(2,1)S(1)} %sum_pair.1), channel_id=1, replica_groups=mesh['z'=16,'y'=4,'x'=4,'core'=2] {'y','x'}, dimensions={0} | all-to-all | bytes 2359296 | tf_op jit(solution)/shard_map/all_to_all | solution.py:369
  83.4 0.9 sum_plane.1
  84.3 7.0 %all-to-all-start.3 = ((bf16[16,8,512]{2,1,0:T(8,128)(2,1)}), bf16[16,8,512]{2,1,0:T(8,128)(2,1)S(1)}, u32[]{:S(2)}, u32[]{:S(2)}) async-start(bf16[16,8,512]{2,1,0:T(8,128)(2,1)} %get-tuple-element.34), calls=%async_computation.3 | async-start | bytes 262144 | tf_op jit(solution)/shard_map/all_to_all | solution.py:369
  91.3 5.1 %collective-permute-start.4 = (bf16[48,512]{1,0:T(8,128)(2,1)S(1)}, bf16[48,512]{1,0:T(8,128)(2,1)S(1)}, u32[]{:S(2)}, u32[]{:S(2)}) collective-permute-start(bf16[48,512]{1,0:T(8,128)(2,1)S(1)} %get-tuple-element.32.own_ref), channel_id=1, source_target_pairs={{0,96},{32,64},{64,32},{96,0},{128,224},{160,192},{192,160},{224,1... | collective-permute-start | bytes 147464 | tf_op jit(solution)/shard_map/ppermute | solution.py:439
  96.3 1.9 %collective-permute-start.3 = (bf16[48,512]{1,0:T(8,128)(2,1)S(1)}, bf16[48,512]{1,0:T(8,128)(2,1)S(1)}, u32[]{:S(2)}, u32[]{:S(2)}) collective-permute-start(bf16[48,512]{1,0:T(8,128)(2,1)S(1)} %get-tuple-element.32.own_ref), channel_id=1, source_target_pairs={{0,64},{32,96},{64,0},{96,32},{128,192},{160,224},{192,128},{224,1... | collective-permute-start | bytes 147464 | tf_op jit(solution)/shard_map/ppermute | solution.py:439
  98.3 2.3 %collective-permute-start.2 = (bf16[48,512]{1,0:T(8,128)(2,1)S(1)}, bf16[48,512]{1,0:T(8,128)(2,1)S(1)}, u32[]{:S(2)}, u32[]{:S(2)}) collective-permute-start(bf16[48,512]{1,0:T(8,128)(2,1)S(1)} %get-tuple-element.32.own_ref), channel_id=1, source_target_pairs={{0,32},{32,0},{64,96},{96,64},{128,160},{160,128},{192,224},{224,1... | collective-permute-start | bytes 147464 | tf_op jit(solution)/shard_map/ppermute | solution.py:439
  100.6 0.0 collective-permute-done.4.farther_ref
  100.6 4.2 %collective-permute-done.3.far_ref = bf16[48,512]{1,0:T(8,128)(2,1)S(1)} collective-permute-done((bf16[48,512]{1,0:T(8,128)(2,1)S(1)}, bf16[48,512]{1,0:T(8,128)(2,1)S(1)}, u32[]{:S(2)}, u32[]{:S(2)}) %collective-permute-start.3) | collective-permute-done | bytes 49184 | tf_op jit(solution)/shard_map/ppermute | solution.py:439
  104.8 0.0 collective-permute-done.2.beside_ref
  104.9 5.2 %collective-permute-start.7 = (bf16[48,512]{1,0:T(8,128)(2,1)S(1)}, bf16[48,512]{1,0:T(8,128)(2,1)S(1)}, u32[]{:S(2)}, u32[]{:S(2)}) collective-permute-start(bf16[48,512]{1,0:T(8,128)(2,1)S(1)} %sum_round.1.own_ref), channel_id=1, source_target_pairs={{0,384},{32,416},{64,448},{96,480},{128,256},{160,288},{192,320},{... | collective-permute-start | bytes 147464 | tf_op jit(solution)/shard_map/ppermute | solution.py:439
  110.0 9.2 %collective-permute-start.6 = (bf16[48,512]{1,0:T(8,128)(2,1)S(1)}, bf16[48,512]{1,0:T(8,128)(2,1)S(1)}, u32[]{:S(2)}, u32[]{:S(2)}) collective-permute-start(bf16[48,512]{1,0:T(8,128)(2,1)S(1)} %sum_round.1.own_ref), channel_id=1, source_target_pairs={{0,256},{32,288},{64,320},{96,352},{128,384},{160,416},{192,448},{... | collective-permute-start | bytes 147464 | tf_op jit(solution)/shard_map/ppermute | solution.py:439
  119.2 1.9 %collective-permute-start.5 = (bf16[48,512]{1,0:T(8,128)(2,1)S(1)}, bf16[48,512]{1,0:T(8,128)(2,1)S(1)}, u32[]{:S(2)}, u32[]{:S(2)}) collective-permute-start(bf16[48,512]{1,0:T(8,128)(2,1)S(1)} %sum_round.1.own_ref), channel_id=1, source_target_pairs={{0,128},{32,160},{64,192},{96,224},{128,0},{160,32},{192,64},{224,... | collective-permute-start | bytes 147464 | tf_op jit(solution)/shard_map/ppermute | solution.py:439
  121.1 0.0 all-to-all-done.3.arrived_ref
  121.2 0.6 return_rows.1
  121.8 2.7 %collective-permute-start.8 = (bf16[192,512]{1,0:T(8,128)(2,1)S(1)}, bf16[192,512]{1,0:T(8,128)(2,1)S(1)}, u32[]{:S(2)}, u32[]{:S(2)}) collective-permute-start(bf16[192,512]{1,0:T(8,128)(2,1)S(1)} %get-tuple-element.36), channel_id=1, source_target_pairs={{0,4},{2,6},{4,0},{6,2},{1,5},{3,7},{5,1},{7,3},{8,12},{10,14},{12... | collective-permute-start | bytes 589832 | tf_op jit(solution)/shard_map/ppermute | solution.py:463
  124.5 2.2 %collective-permute-start.9 = (bf16[192,512]{1,0:T(8,128)(2,1)S(1)}, bf16[192,512]{1,0:T(8,128)(2,1)S(1)}, u32[]{:S(2)}, u32[]{:S(2)}) collective-permute-start(bf16[192,512]{1,0:T(8,128)(2,1)S(1)} %get-tuple-element.37), channel_id=1, source_target_pairs={{0,2},{2,0},{4,6},{6,4},{1,3},{3,1},{5,7},{7,5},{8,10},{10,8},{12,... | collective-permute-start | bytes 589832 | tf_op jit(solution)/shard_map/ppermute | solution.py:463
  126.7 0.0 collective-permute-done.7.farther_ref
  126.7 4.1 %collective-permute-start.10 = (bf16[192,512]{1,0:T(8,128)(2,1)S(1)}, bf16[192,512]{1,0:T(8,128)(2,1)S(1)}, u32[]{:S(2)}, u32[]{:S(2)}) collective-permute-start(bf16[192,512]{1,0:T(8,128)(2,1)S(1)} %get-tuple-element.38), channel_id=1, source_target_pairs={{0,6},{2,4},{4,2},{6,0},{1,7},{3,5},{5,3},{7,1},{8,14},{10,12},{12... | collective-permute-start | bytes 589832 | tf_op jit(solution)/shard_map/ppermute | solution.py:463
  130.8 0.0 collective-permute-done.6.far_ref
  130.8 0.0 collective-permute-done.5.beside_ref
  130.8 0.6 sum_weights.1
  131.4 0.8 spread_weights.1
  132.3 3.6 %all-to-all-start.4 = ((bf16[16,32,512]{2,1,0:T(8,128)(2,1)}), bf16[16,32,512]{2,1,0:T(8,128)(2,1)S(1)}, u32[]{:S(2)}, u32[]{:S(2)}) async-start(bf16[16,32,512]{2,1,0:T(8,128)(2,1)} %spread_weights.1), calls=%async_computation.4 | async-start | bytes 1048576 | tf_op jit(solution)/shard_map/all_to_all | solution.py:369
  135.9 0.0 collective-permute-done.8.refs_0_
  135.9 0.0 collective-permute-done.9.refs_1_
  135.9 0.0 collective-permute-done.10.refs_2_
  135.9 0.1 sum_rows.1
  136.0 8.9 %all-to-all-done.4 = bf16[16,32,512]{2,1,0:T(8,128)(2,1)S(1)} async-done(((bf16[16,32,512]{2,1,0:T(8,128)(2,1)}), bf16[16,32,512]{2,1,0:T(8,128)(2,1)S(1)}, u32[]{:S(2)}, u32[]{:S(2)}) %all-to-all-start.4) | async-done | bytes 524320 | tf_op jit(solution)/shard_map/all_to_all | solution.py:369
  144.9 6.4 %collective-permute-start.11 = (bf16[608,512]{1,0:T(8,128)(2,1)S(1)}, bf16[608,512]{1,0:T(8,128)(2,1)S(1)}, u32[]{:S(2)}, u32[]{:S(2)}) collective-permute-start(bf16[608,512]{1,0:T(8,128)(2,1)S(1)} %join.1), channel_id=1, source_target_pairs={{0,1},{1,0},{2,3},{3,2},{4,5},{5,4},{6,7},{7,6},{8,9},{9,8},{10,11... | collective-permute-start | bytes 1867784 | tf_op jit(solution)/shard_map/ppermute | solution.py:372
  151.3 1.7 %collective-permute-done.11.far_ref = bf16[608,512]{1,0:T(8,128)(2,1)S(1)} collective-permute-done((bf16[608,512]{1,0:T(8,128)(2,1)S(1)}, bf16[608,512]{1,0:T(8,128)(2,1)S(1)}, u32[]{:S(2)}, u32[]{:S(2)}) %collective-permute-start.11) | collective-permute-done | bytes 622624 | tf_op jit(solution)/shard_map/ppermute | solution.py:372
  152.9 1.1 finish.1
  (25 shorter events, 0.1 us)
Async XLA Ops:
  0.6 18.6 %copy-start.12 = (bf16[512]{0:T(512)(128)(2,1)S(1)}, bf16[512]{0:T(512)(128)(2,1)}, u32[]{:S(2)}) copy-start(bf16[512]{0:T(512)(128)(2,1)} %param.20) | copy-start | bytes 3076
  0.6 18.7 %copy-start.9 = (s32[1,14]{1,0:T(1,128)S(1)}, s32[1,14]{1,0:T(1,128)}, u32[]{:S(2)}) copy-start(s32[1,14]{1,0:T(1,128)} %src_ref.3) | copy-start | bytes 172
  0.7 18.7 %copy-start.8 = (s32[1,14]{1,0:T(1,128)S(1)}, s32[1,14]{1,0:T(1,128)}, u32[]{:S(2)}) copy-start(s32[1,14]{1,0:T(1,128)} %dst_ref.3) | copy-start | bytes 172
  0.7 18.7 %copy-start.6 = (bf16[14,128,128]{2,1,0:T(8,128)(2,1)S(1)}, bf16[14,128,128]{2,1,0:T(8,128)(2,1)}, u32[]{:S(2)}) copy-start(bf16[14,128,128]{2,1,0:T(8,128)(2,1)} %tiles_ref.3) | copy-start | bytes 1376260
  0.7 18.7 %copy-start.7 = (s32[512]{0:T(512)S(1)}, s32[512]{0:T(512)}, u32[]{:S(2)}) copy-start(s32[512]{0:T(512)} %param.13) | copy-start | bytes 6148
  2.9 27.8 %all-to-all-start = ((bf16[16,8,512]{2,1,0:T(8,128)(2,1)}), bf16[16,8,512]{2,1,0:T(8,128)(2,1)S(1)}, u32[]{:S(2)}, u32[]{:S(2)}) async-start(bf16[16,8,512]{2,1,0:T(8,128)(2,1)} %bitcast.20), calls=%async_computation | async-start | bytes 262144 | tf_op jit(solution)/shard_map/all_to_all | solution.py:369
  19.3 1.1 copy-start
  20.5 1.0 copy-start.4
  26.4 1.5 copy-start.10
  30.6 24.5 %copy-start.2 = (bf16[512,512]{1,0:T(8,128)(2,1)S(1)}, bf16[512,512]{1,0:T(8,128)(2,1)}, u32[]{:S(2)}) copy-start(bf16[512,512]{1,0:T(8,128)(2,1)} %w_neigh_ref.1) | copy-start | bytes 1572868
  30.6 24.5 %copy-start.3 = (bf16[512,512]{1,0:T(8,128)(2,1)S(1)}, bf16[512,512]{1,0:T(8,128)(2,1)}, u32[]{:S(2)}) copy-start(bf16[512,512]{1,0:T(8,128)(2,1)} %cot_ref.1) | copy-start | bytes 1572868
  30.6 24.5 %copy-start.11 = (bf16[2560,512]{1,0:T(8,128)(2,1)S(1)}, bf16[2560,512]{1,0:T(8,128)(2,1)}, u32[]{:S(2)}) copy-start(bf16[2560,512]{1,0:T(8,128)(2,1)} %copy-done.10) | copy-start | bytes 7864324
  46.8 8.3 %collective-permute-start = (bf16[512,512]{1,0:T(8,128)(2,1)S(1)}, bf16[512,512]{1,0:T(8,128)(2,1)S(1)}, u32[]{:S(2)}, u32[]{:S(2)}) collective-permute-start(bf16[512,512]{1,0:T(8,128)(2,1)S(1)} %bitcast.13), channel_id=1, source_target_pairs={{0,1},{1,0},{2,3},{3,2},{4,5},{5,4},{6,7},{7,6},{8,9},{9,8},{10,11... | collective-permute-start | bytes 1572872 | tf_op jit(solution)/shard_map/ppermute | solution.py:372
  55.1 5.0 %copy-start.5 = (bf16[512,512]{1,0:T(8,128)(2,1)S(1)}, bf16[512,512]{1,0:T(8,128)(2,1)}, u32[]{:S(2)}) copy-start(bf16[512,512]{1,0:T(8,128)(2,1)} %w_self_ref.3) | copy-start | bytes 1572868
  57.8 4.6 %collective-permute-start.1 = (bf16[1040,512]{1,0:T(8,128)(2,1)S(1)}, bf16[1040,512]{1,0:T(8,128)(2,1)S(1)}, u32[]{:S(2)}, u32[]{:S(2)}) collective-permute-start(bf16[1040,512]{1,0:T(8,128)(2,1)S(1)} %get-tuple-element.29), channel_id=1, source_target_pairs={{0,1},{1,0},{2,3},{3,2},{4,5},{5,4},{6,7},{7,6},{8,9},{9,8},{10,11... | collective-permute-start | bytes 3194888 | tf_op jit(solution)/shard_map/ppermute | solution.py:372
  83.4 37.8 %copy-start.1 = (s32[1,64,8]{1,2,0:T(8,128)S(1)}, s32[1,64,8]{1,2,0:T(8,128)}, u32[]{:S(2)}) copy-start(s32[1,64,8]{1,2,0:T(8,128)} %param.12) | copy-start | bytes 6148
  84.3 36.9 %all-to-all-start.3 = ((bf16[16,8,512]{2,1,0:T(8,128)(2,1)}), bf16[16,8,512]{2,1,0:T(8,128)(2,1)S(1)}, u32[]{:S(2)}, u32[]{:S(2)}) async-start(bf16[16,8,512]{2,1,0:T(8,128)(2,1)} %get-tuple-element.34), calls=%async_computation.3 | async-start | bytes 262144 | tf_op jit(solution)/shard_map/all_to_all | solution.py:369
  91.3 9.3 %collective-permute-start.4 = (bf16[48,512]{1,0:T(8,128)(2,1)S(1)}, bf16[48,512]{1,0:T(8,128)(2,1)S(1)}, u32[]{:S(2)}, u32[]{:S(2)}) collective-permute-start(bf16[48,512]{1,0:T(8,128)(2,1)S(1)} %get-tuple-element.32.own_ref), channel_id=1, source_target_pairs={{0,96},{32,64},{64,32},{96,0},{128,224},{160,192},{192,160},{224,1... | collective-permute-start | bytes 147464 | tf_op jit(solution)/shard_map/ppermute | solution.py:439
  96.3 8.5 %collective-permute-start.3 = (bf16[48,512]{1,0:T(8,128)(2,1)S(1)}, bf16[48,512]{1,0:T(8,128)(2,1)S(1)}, u32[]{:S(2)}, u32[]{:S(2)}) collective-permute-start(bf16[48,512]{1,0:T(8,128)(2,1)S(1)} %get-tuple-element.32.own_ref), channel_id=1, source_target_pairs={{0,64},{32,96},{64,0},{96,32},{128,192},{160,224},{192,128},{224,1... | collective-permute-start | bytes 147464 | tf_op jit(solution)/shard_map/ppermute | solution.py:439
  98.3 6.6 %collective-permute-start.2 = (bf16[48,512]{1,0:T(8,128)(2,1)S(1)}, bf16[48,512]{1,0:T(8,128)(2,1)S(1)}, u32[]{:S(2)}, u32[]{:S(2)}) collective-permute-start(bf16[48,512]{1,0:T(8,128)(2,1)S(1)} %get-tuple-element.32.own_ref), channel_id=1, source_target_pairs={{0,32},{32,0},{64,96},{96,64},{128,160},{160,128},{192,224},{224,1... | collective-permute-start | bytes 147464 | tf_op jit(solution)/shard_map/ppermute | solution.py:439
  104.9 21.9 %collective-permute-start.7 = (bf16[48,512]{1,0:T(8,128)(2,1)S(1)}, bf16[48,512]{1,0:T(8,128)(2,1)S(1)}, u32[]{:S(2)}, u32[]{:S(2)}) collective-permute-start(bf16[48,512]{1,0:T(8,128)(2,1)S(1)} %sum_round.1.own_ref), channel_id=1, source_target_pairs={{0,384},{32,416},{64,448},{96,480},{128,256},{160,288},{192,320},{... | collective-permute-start | bytes 147464 | tf_op jit(solution)/shard_map/ppermute | solution.py:439
  110.0 20.8 %collective-permute-start.6 = (bf16[48,512]{1,0:T(8,128)(2,1)S(1)}, bf16[48,512]{1,0:T(8,128)(2,1)S(1)}, u32[]{:S(2)}, u32[]{:S(2)}) collective-permute-start(bf16[48,512]{1,0:T(8,128)(2,1)S(1)} %sum_round.1.own_ref), channel_id=1, source_target_pairs={{0,256},{32,288},{64,320},{96,352},{128,384},{160,416},{192,448},{... | collective-permute-start | bytes 147464 | tf_op jit(solution)/shard_map/ppermute | solution.py:439
  119.2 11.6 %collective-permute-start.5 = (bf16[48,512]{1,0:T(8,128)(2,1)S(1)}, bf16[48,512]{1,0:T(8,128)(2,1)S(1)}, u32[]{:S(2)}, u32[]{:S(2)}) collective-permute-start(bf16[48,512]{1,0:T(8,128)(2,1)S(1)} %sum_round.1.own_ref), channel_id=1, source_target_pairs={{0,128},{32,160},{64,192},{96,224},{128,0},{160,32},{192,64},{224,... | collective-permute-start | bytes 147464 | tf_op jit(solution)/shard_map/ppermute | solution.py:439
  121.8 14.1 %collective-permute-start.8 = (bf16[192,512]{1,0:T(8,128)(2,1)S(1)}, bf16[192,512]{1,0:T(8,128)(2,1)S(1)}, u32[]{:S(2)}, u32[]{:S(2)}) collective-permute-start(bf16[192,512]{1,0:T(8,128)(2,1)S(1)} %get-tuple-element.36), channel_id=1, source_target_pairs={{0,4},{2,6},{4,0},{6,2},{1,5},{3,7},{5,1},{7,3},{8,12},{10,14},{12... | collective-permute-start | bytes 589832 | tf_op jit(solution)/shard_map/ppermute | solution.py:463
  124.5 11.4 %collective-permute-start.9 = (bf16[192,512]{1,0:T(8,128)(2,1)S(1)}, bf16[192,512]{1,0:T(8,128)(2,1)S(1)}, u32[]{:S(2)}, u32[]{:S(2)}) collective-permute-start(bf16[192,512]{1,0:T(8,128)(2,1)S(1)} %get-tuple-element.37), channel_id=1, source_target_pairs={{0,2},{2,0},{4,6},{6,4},{1,3},{3,1},{5,7},{7,5},{8,10},{10,8},{12,... | collective-permute-start | bytes 589832 | tf_op jit(solution)/shard_map/ppermute | solution.py:463
  126.7 9.2 %collective-permute-start.10 = (bf16[192,512]{1,0:T(8,128)(2,1)S(1)}, bf16[192,512]{1,0:T(8,128)(2,1)S(1)}, u32[]{:S(2)}, u32[]{:S(2)}) collective-permute-start(bf16[192,512]{1,0:T(8,128)(2,1)S(1)} %get-tuple-element.38), channel_id=1, source_target_pairs={{0,6},{2,4},{4,2},{6,0},{1,7},{3,5},{5,3},{7,1},{8,14},{10,12},{12... | collective-permute-start | bytes 589832 | tf_op jit(solution)/shard_map/ppermute | solution.py:463
  132.3 12.6 %all-to-all-start.4 = ((bf16[16,32,512]{2,1,0:T(8,128)(2,1)}), bf16[16,32,512]{2,1,0:T(8,128)(2,1)S(1)}, u32[]{:S(2)}, u32[]{:S(2)}) async-start(bf16[16,32,512]{2,1,0:T(8,128)(2,1)} %spread_weights.1), calls=%async_computation.4 | async-start | bytes 1048576 | tf_op jit(solution)/shard_map/all_to_all | solution.py:369
  144.9 8.0 %collective-permute-start.11 = (bf16[608,512]{1,0:T(8,128)(2,1)S(1)}, bf16[608,512]{1,0:T(8,128)(2,1)S(1)}, u32[]{:S(2)}, u32[]{:S(2)}) collective-permute-start(bf16[608,512]{1,0:T(8,128)(2,1)S(1)} %join.1), channel_id=1, source_target_pairs={{0,1},{1,0},{2,3},{3,2},{4,5},{5,4},{6,7},{7,6},{8,9},{9,8},{10,11... | collective-permute-start | bytes 1867784 | tf_op jit(solution)/shard_map/ppermute | solution.py:372

commit v10 on v8

--- a/solution.py
+++ b/solution.py
@@ -34,6 +34,12 @@
 
 def iota(shape, dim):
     return lax.broadcasted_iota(jnp.int32, shape, dim)
+
+
+def two_rows(wide, rows):
+    high = wide.astype(BF16).astype(F32)
+    row = iota((rows, wide.shape[1]), 0)
+    return jnp.where(row == 0, high, jnp.where(row == 1, wide - high, 0.0)).astype(BF16)
 
 
 def call(kernel, name, outs, scalars, arrays, scratch=(), flops=0, after=(), hbm=(), hbm_outs=(), limit=VMEM_BYTES):
@@ -115,36 +121,57 @@
 def send_kernel(rep_ref, lists_hbm, feats_hbm, send_ref, lists_ref, feats_ref, sems):
     lists_copy, feats_copy = fetch((lists_hbm, feats_hbm), (lists_ref, feats_ref), sems)
     slots, parts = lists_ref.shape
+    depth = parts // Y_SIZE
     rep = rep_ref[0]
     shape = (2 * parts, parts)
-    line = iota(shape, 0)
-    part = line // (2 * Y_SIZE) * Y_SIZE + line % Y_SIZE
-    of_part = (part == iota(shape, 1)).astype(BF16)
+    out, into = iota(shape, 0), iota(shape, 1)
+    row, z = out % (2 * Y_SIZE), out // (2 * Y_SIZE)
+    of_part = (into == z * Y_SIZE + row % Y_SIZE).astype(BF16)
     lists_copy.wait()
     lists = lists_ref[...]
     high, low = (lists // 256).astype(BF16), (lists % 256).astype(BF16)
     wanted = dot(of_part, high, 1, 1) * 256.0 + dot(of_part, low, 1, 1)
     shape = (2 * parts, slots)
-    is_hub = iota(shape, 0) // Y_SIZE % 2 == 1
-    wanted = jnp.where(is_hub, rep.astype(F32), wanted)
+    row = iota(shape, 0) % (2 * Y_SIZE)
+    wanted = jnp.where(row < Y_SIZE, wanted, rep.astype(F32))
     wanted = jnp.sum(jnp.where(iota(shape, 1) == rep, wanted, 0.0), axis=1, keepdims=True)
     places = iota((2 * parts, feats_ref.shape[0]), 1) == wanted.astype(jnp.int32)
     places = places.astype(BF16)
     feats_copy.wait()
-    send_ref[...] = dot(places, feats_ref[...]).astype(BF16)
+    rows = dot(places, feats_ref[...]).astype(BF16)
+    lines = send_ref.shape[0] // depth
+    shape = (depth * lines, 2 * parts)
+    out, into = iota(shape, 0), iota(shape, 1)
+    line, z = out % lines, out // lines
+    packed = jnp.zeros(send_ref.shape, F32)
+    for group in range(rows.shape[1] // LANES):
+        first = group * (Y_SIZE + 1)
+        wanted = jnp.where(
+            jnp.logical_and(line >= first, line <= first + Y_SIZE),
+            z * (2 * Y_SIZE) + line - first,
+            -1,
+        )
+        lanes = slice(group * LANES, (group + 1) * LANES)
+        packed += dot((into == wanted).astype(BF16), rows[:, lanes])
+    send_ref[...] = packed.astype(BF16)
 
 
 def plane_kernel(arrived_ref, send_ref):
-    chunk = send_ref.shape[1]
+    _, chunk, width = send_ref.shape
     depth = chunk // 2
     total = arrived_ref.shape[0]
-    shape = (total, total)
+    lines = total // depth
+    shape = (Y_SIZE * chunk, total)
     out, into = iota(shape, 0), iota(shape, 1)
     z, kind, y = out % depth, out // depth % 2, out // chunk
-    moved = move(into == z * (2 * Y_SIZE) + kind * Y_SIZE + y, arrived_ref[...])
-    for y_to in range(Y_SIZE):
-        for x_to in range(X_SIZE):
-            send_ref[y_to * X_SIZE + x_to] = moved[y_to * chunk : (y_to + 1) * chunk]
+    first = z * lines + jnp.where(kind == 0, y, Y_SIZE)
+    arrived = arrived_ref[...]
+    for group in range(width // LANES):
+        moved = move(into == first + group * (Y_SIZE + 1), arrived)
+        lanes = slice(group * LANES, (group + 1) * LANES)
+        for y_to in range(Y_SIZE):
+            for x_to in range(X_SIZE):
+                send_ref[y_to * X_SIZE + x_to, :, lanes] = moved[y_to * chunk : (y_to + 1) * chunk]
 
 
 def own_kernel(
@@ -212,12 +239,6 @@
     send_ref[width + half :] = bias
 
 
-def two_rows(wide, rows):
-    high = wide.astype(BF16).astype(F32)
-    row = iota((rows, wide.shape[1]), 0)
-    return jnp.where(row == 0, high, jnp.where(row == 1, wide - high, 0.0)).astype(BF16)
-
-
 def pair_sum_kernel(keep_ref, other_ref, send_ref, bias_ref):
     chunks, lines, width = send_ref.shape
     total = keep_ref[...].astype(F32) + other_ref[...].astype(F32)
@@ -290,9 +311,12 @@
         whole_ref[:, group * LANES : (group + 1) * LANES] = rows
 
 
-def spread_kernel(whole_ref, send_ref):
-    for chunk in range(send_ref.shape[0]):
-        send_ref[chunk] = whole_ref[...]
+def spread_kernel(whole_ref, bias_ref, send_ref):
+    chunks, lines, _ = send_ref.shape
+    bias = two_rows(bias_ref[...], lines - whole_ref.shape[0]).astype(F32)
+    message = jnp.concatenate([whole_ref[...].astype(F32), bias], 0).astype(BF16)
+    for chunk in range(chunks):
+        send_ref[chunk] = message
 
 
 def own_back_kernel(
@@ -307,9 +331,7 @@
     own_ref[...] = dot(seeded, w_self_ref[...], 1, 1) + dot(adj_ref[...], d_agg_ref[...], 0, 0)
 
 
-def scatter_kernel(
-    rep_ref, lists_ref, arrived_ref, own_ref, bias_ref, keep_ref, *send_refs_and_total
-):
+def scatter_kernel(rep_ref, lists_ref, arrived_ref, own_ref, keep_ref, *send_refs_and_total):
     *send_refs, total_ref = send_refs_and_total
     rows, width = own_ref.shape
     rep = rep_ref[0]
@@ -322,43 +344,37 @@
             place = jnp.bitwise_xor(rep, step * CORES + core)
             some = total_ref[pl.ds(pl.multiple_of(place * share, 32), share), :]
             ref[core * share : (core + 1) * share] = some.astype(ref.dtype)
-    bias = two_rows(bias_ref[...], send_refs[0].shape[0] - CORES * share)
-    for ref in send_refs:
-        ref[CORES * share :] = bias
-
-
-def row_sum_kernel(keep_ref, bias_ref, *refs):
-    *arrived_refs, own_ref, send_ref, bias_sum_ref, bias_send_ref = refs
+
+
+def row_sum_kernel(keep_ref, *refs):
+    *arrived_refs, own_ref, send_ref = refs
     share = own_ref.shape[0]
-    total, bias = keep_ref[...], bias_ref[...]
+    total = keep_ref[...]
     for ref in arrived_refs:
-        arrived = ref[...].astype(F32)
-        total = total + arrived[: CORES * share]
-        bias = bias + jnp.sum(arrived[CORES * share :], 0, keepdims=True)
+        total = total + ref[...].astype(F32)
     own_ref[...] = total[:share]
     send_ref[...] = total[share:].astype(BF16)
-    bias_sum_ref[...] = bias
-    bias_send_ref[...] = two_rows(bias, bias_send_ref.shape[0])
-
-
-def join_kernel(weights_ref, rows_ref, send_ref):
-    width = weights_ref.shape[0]
-    send_ref[:width] = weights_ref[...]
+
+
+def join_kernel(arrived_ref, rows_ref, send_ref, bias_ref):
+    chunks, _, width = arrived_ref.shape
+    weight = width // chunks
+    bias = jnp.zeros(bias_ref.shape, F32)
+    for chunk in range(chunks):
+        arrived = arrived_ref[chunk].astype(F32)
+        send_ref[chunk * weight : (chunk + 1) * weight] = arrived[:weight].astype(BF16)
+        bias = bias + jnp.sum(arrived[weight:], 0, keepdims=True)
     send_ref[width:] = rows_ref[...]
-
-
-def finish_kernel(core_ref, near_ref, own_ref, bias_sum_ref, far_ref, *refs):
-    *bias_refs, first_ref, second_ref, rows_ref, bias_ref = refs
-    width = near_ref.shape[0]
-    near, far = near_ref[...], far_ref[:width]
+    bias_ref[...] = bias
+
+
+def finish_kernel(core_ref, near_ref, own_ref, far_ref, first_ref, second_ref, rows_ref):
+    width = first_ref.shape[0]
+    near, far = near_ref[:width], far_ref[:width]
     is_first = core_ref[0] == 0
     first_ref[...] = jnp.where(is_first, near, far)
     second_ref[...] = jnp.where(is_first, far, near)
     rows_ref[...] = own_ref[...] + far_ref[width:].astype(F32)
-    bias = bias_sum_ref[...]
-    for ref in bias_refs:
-        bias = bias + jnp.sum(ref[...].astype(F32), 0, keepdims=True)
-    bias_ref[...] = bias
 
 
 def body(
@@ -397,11 +413,13 @@
     def pair(values):
         return lax.ppermute(values, "core", [(0, 1), (1, 0)])
 
+    lines = -(-(Y_SIZE + 1) * (width // LANES) // 8) * 8
     (send,) = call(
-        send_kernel, "pick_boundary", [((2 * parts, width), BF16)], [rep], [], hbm=[lists, feats],
-        scratch=fetched([lists, feats]), flops=4 * parts * rows * width, limit=FULL_VMEM_BYTES,
-    )
-    by_depth = swap(send.reshape(depth, 2 * Y_SIZE, width), "z").reshape(2 * parts, width)
+        send_kernel, "pick_boundary", [((depth * lines, LANES), BF16)], [rep], [],
+        hbm=[lists, feats], scratch=fetched([lists, feats]), flops=4 * parts * rows * width,
+        limit=FULL_VMEM_BYTES,
+    )
+    by_depth = swap(send.reshape(depth, lines, LANES), "z").reshape(depth * lines, LANES)
     mats, sums = call(
         own_kernel, "own_rows",
         [
@@ -456,7 +474,7 @@
         [], [plane_arrived, pair_bias],
     )
     depth_arrived = swap(depth_send, "z")
-    weight_send, depth_bias = call(
+    weight_send, plane_bias = call(
         functools.partial(weight_kernel, scale), "sum_weights",
         [((depth, 2 * Y_SIZE, LANES), BF16), ((1, width), F32)],
         [], [depth_arrived],
@@ -465,8 +483,8 @@
     share = rows // reps
     row_keep, *row_sends = call(
         scatter_kernel, "return_rows",
-        [((CORES * share, width), F32)] + [((CORES * share + 16, width), BF16)] * (X_SIZE - 1),
-        [rep], [lists, depth_arrived, own, depth_bias],
+        [((CORES * share, width), F32)] + [((CORES * share, width), BF16)] * (X_SIZE - 1),
+        [rep], [lists, depth_arrived, own],
         scratch=[pltpu.VMEM((rows, width), F32)],
         flops=4 * parts * rows * width, after=[weight_send],
     )
@@ -478,35 +496,26 @@
         gather_kernel, "gather_weights", [((width // PLANE, width), BF16)],
         [], [weight_depth], flops=window, after=[row_keep],
     )
-    row_own, row_send, x_bias, bias_send = call(
-        row_sum_kernel, "sum_rows",
-        [((share, width), F32), ((share, width), BF16), ((1, width), F32), ((16, width), BF16)],
-        [], [row_keep, depth_bias, *row_arrived], flops=window,
-    )
-    bias_arrived = [
-        lax.ppermute(bias_send, "y", [(y, y ^ step) for y in range(Y_SIZE)])
-        for step in range(1, Y_SIZE)
-    ]
+    row_own, row_send = call(
+        row_sum_kernel, "sum_rows", [((share, width), F32), ((share, width), BF16)],
+        [], [row_keep, *row_arrived], flops=window,
+    )
     (weight_plane,) = call(
-        spread_kernel, "spread_weights", [((PLANE, width // PLANE, width), BF16)],
-        [], [weight_rows],
-    )
-    weight_near = swap(weight_plane, ("y", "x")).reshape(width, width)
-    (last_send,) = call(
-        join_kernel, "join", [((width + share, width), BF16)], [], [weight_near, row_send],
-        after=bias_arrived,
-    )
-    grad_self, grad_neigh, input_grad, grad_bias = call(
+        spread_kernel, "spread_weights", [((PLANE, width // PLANE + 8, width), BF16)],
+        [], [weight_rows, plane_bias],
+    )
+    weight_near = swap(weight_plane, ("y", "x"))
+    last_send, grad_bias = call(
+        join_kernel, "join", [((width + share, width), BF16), ((1, width), F32)],
+        [], [weight_near, row_send],
+    )
+    grad_self, grad_neigh, input_grad = call(
         finish_kernel, "finish",
-        [
-            ((width, width), BF16),
-            ((width, width), BF16),
-            ((share, width), F32),
-            ((1, width), F32),
-        ],
-        [core], [weight_near, row_own, x_bias, pair(last_send), *bias_arrived],
-    )
-    return (out, input_grad, grad_self, grad_neigh, grad_bias.reshape(width))
+        [((width, width), BF16), ((width, width), BF16), ((share, width), F32)],
+        [core], [last_send, row_own, pair(last_send)],
+    )
+    grad_bias = grad_bias.reshape(width)
+    return (out, input_grad, grad_self, grad_neigh, grad_bias)
 
 
 def solution(mesh):

time: 149 us -> 147 us (0.987)
  starting transfers between devices: 58 us -> 47.1 us
  waiting for transfers between devices: 8 us -> 14.8 us
  blocking collectives: 57.4 us -> 58.9 us
    all_to_all x3, waiting for transfers between devices: 1.81 us -> 11.4 us  [swap(): return lax.all_to_all(values, axis, split_axis=0, concat_axis=0, tiled=True)]
    ppermute x3 -> x0, starting transfers between devices: 8.98 us -> none  [body(): lax.ppermute(bias_send, 'y', [(y, y ^ step) for y in range(Y_SIZE)])]
    ppermute x3 -> x0, waiting for transfers between devices: 2.84 us -> none  [body(): lax.ppermute(bias_send, 'y', [(y, y ^ step) for y in range(Y_SIZE)])]
    ppermute x3, starting transfers between devices: 15.2 us -> 13.3 us  [pair(): return lax.ppermute(values, 'core', [(0, 1), (1, 0)])]
    all_to_all x3, blocking collectives: 57.4 us -> 58.9 us  [swap(): return lax.all_to_all(values, axis, split_axis=0, concat_axis=0, tiled=True)]
  transfers between devices with their start and end apart: 12 -> 9, of which waited for: 5 -> 5; matrix products, arithmetic and copies ran while one was open for 0% -> 0% of each run, Pallas kernels for 6% -> 6%
where the time goes in v10:
time: 147 us
  blocking collectives  58.9 us (40%)
  starting transfers between devices  47.1 us (32%)
  Pallas kernels  16.9 us (11%)
  waiting for transfers between devices  14.8 us (10%)
  local copies, waits for them, and re-layouts  7.4 us (5%)
  between operations  1.56 us (1%)
    all_to_all x3, blocking collectives, swap(): return lax.all_to_all(values, axis, split_axis=0, concat_axis=0, tiled=True)  58.9 us
    all_to_all x3, starting transfers between devices, swap(): return lax.all_to_all(values, axis, split_axis=0, concat_axis=0, tiled=True)  24.9 us
    pallas_call x14, Pallas kernels, call(): pl.pallas_call(kernel, out_shape=shapes, in_specs=[pl.BlockSpec(memory_sp...  16.9 us
    ppermute x3, starting transfers between devices, pair(): return lax.ppermute(values, 'core', [(0, 1), (1, 0)])  13.3 us
    all_to_all x3, waiting for transfers between devices, swap(): return lax.all_to_all(values, axis, split_axis=0, concat_axis=0, tiled=True)  11.4 us
    ppermute x3, starting transfers between devices, body(): lax.ppermute(row_sends[step - 1], 'x', [(x, x ^ step) for x in range(X_SI...  8.98 us
    unnamed x32, local copies, waits for them, and re-layouts  6.71 us
    ppermute x3, waiting for transfers between devices, pair(): return lax.ppermute(values, 'core', [(0, 1), (1, 0)])  3.38 us
  transfers between devices with their start and end apart: 9, of which 5 were waited for; matrix products, arithmetic and copies ran while one was open for 0% of the time, Pallas kernels for 6%

profile of v10, /device:TPU:1, one launch (start us, length us, event | category | flops | bytes accessed | tf_op | source)
XLA Modules:
  0.0 146.6 jit_solution(14354532916467376236)
XLA Ops:
  0.6 2.4 %pick_boundary.1 = bf16[384,128]{1,0:T(8,128)(2,1)} custom-call(s32[1]{0:T(128)} %bitcast.1.rep_ref.refs_0_, s32[8,64]{1,0:T(8,128)} %bitcast.13, bf16[768,512]{1,0:T(8,128)(2,1)} %feats_ref.1), custom_call_target="tpu_custom_call" | custom-call | flops 100663296 | bytes 886784 | tf_op jit(solution)/shard_map/pick_boundary/pallas_call | solution.py:52
  3.0 15.8 %all-to-all-start = ((bf16[16,24,128]{2,1,0:T(8,128)(2,1)}), bf16[16,24,128]{2,1,0:T(8,128)(2,1)S(1)}, u32[]{:S(2)}, u32[]{:S(2)}) async-start(bf16[16,24,128]{2,1,0:T(8,128)(2,1)} %bitcast.17), calls=%async_computation | async-start | bytes 196608 | tf_op jit(solution)/shard_map/all_to_all | solution.py:411
  19.5 0.7 reshape.39.bias_ref
  20.1 1.1 copy-done
  21.3 1.0 copy-done.4
  22.3 1.0 copy-done.6
  23.3 0.7 copy-done.8
  24.0 0.7 copy-done.10
  24.7 0.7 copy-done.12
  25.3 4.7 %own_rows.1 = (bf16[2560,512]{1,0:T(8,128)(2,1)S(1)}, f32[1024,512]{1,0:T(8,128)S(1)}) custom-call(s32[1]{0:T(128)} %bitcast.core_ref, s32[1,14]{1,0:T(1,128)S(1)} %copy-done.10, s32[1,14]{1,0:T(1,128)S(1)} %copy-done.12, s32[1]{0:T(128)S(6)} %copy.16.count_ref, bf16[14,128,128]{2,1,0:T(8,128)(2,1)S(1)} %copy-done.6, bf16[768,512]{1,0:T(8,128)(2,1)S(1)} %copy-done, ...), custom_call_target="tpu_custom_call" | custom-call | flops 3623878656 | bytes 6491136 | tf_op jit(solution)/shard_map/own_rows/pallas_call | solution.py:52
  30.1 1.5 %copy-done.14 = bf16[2560,512]{1,0:T(8,128)(2,1)} copy-done((bf16[2560,512]{1,0:T(8,128)(2,1)}, bf16[2560,512]{1,0:T(8,128)(2,1)S(1)}, u32[]{:S(2)}) %copy-start.14) | copy-done | bytes 2621464
  31.6 0.0 all-to-all-done
  31.6 0.3 spread_plane.1
  31.9 16.6 %all_to_all.30 = bf16[16,32,512]{2,1,0:T(8,128)(2,1)S(1)} all-to-all(bf16[16,32,512]{2,1,0:T(8,128)(2,1)S(1)} %spread_plane.1), channel_id=1, replica_groups=mesh['z'=16,'y'=4,'x'=4,'core'=2] {'y','x'}, dimensions={0} | all-to-all | bytes 1048576 | tf_op jit(solution)/shard_map/all_to_all | solution.py:411
  48.5 4.7 %collective-permute-start = (bf16[512,512]{1,0:T(8,128)(2,1)S(1)}, bf16[512,512]{1,0:T(8,128)(2,1)S(1)}, u32[]{:S(2)}, u32[]{:S(2)}) collective-permute-start(bf16[512,512]{1,0:T(8,128)(2,1)S(1)} %bitcast.10), channel_id=1, source_target_pairs={{0,1},{1,0},{2,3},{3,2},{4,5},{5,4},{6,7},{7,6},{8,9},{9,8},{10,11... | collective-permute-start | bytes 1572872 | tf_op jit(solution)/shard_map/ppermute | solution.py:414
  53.2 1.5 %collective-permute-done.far_ref = bf16[512,512]{1,0:T(8,128)(2,1)S(1)} collective-permute-done((bf16[512,512]{1,0:T(8,128)(2,1)S(1)}, bf16[512,512]{1,0:T(8,128)(2,1)S(1)}, u32[]{:S(2)}, u32[]{:S(2)}) %collective-permute-start) | collective-permute-done | bytes 524320 | tf_op jit(solution)/shard_map/ppermute | solution.py:414
  54.7 0.0 copy-start.7
  54.8 0.0 copy-start.9
  54.8 0.0 copy-start.11
  54.8 0.0 copy-start.13
  54.8 2.7 %forward_backward.1 = (bf16[512,512]{1,0:T(8,128)(2,1)}, bf16[512,512]{1,0:T(8,128)(2,1)S(1)}, bf16[512,512]{1,0:T(8,128)(2,1)S(1)}, bf16[1040,512]{1,0:T(8,128)(2,1)S(1)}, bf16[1040,512]{1,0:T(8,128)(2,1)S(1)}) custom-call(s32[1]{0:T(128)} %bitcast.core_ref, bf16[512,512]{1,0:T(8,128)(2,1)S(1)} %bitcast.11, ...), custom_call_target="tpu_custom_call" | custom-call | flops 2147483648 | bytes 10518528 | tf_op jit(solution)/shard_map/forward_backward/pallas_call | solution.py:52
  57.5 2.3 %collective-permute-start.1 = (bf16[1040,512]{1,0:T(8,128)(2,1)S(1)}, bf16[1040,512]{1,0:T(8,128)(2,1)S(1)}, u32[]{:S(2)}, u32[]{:S(2)}) collective-permute-start(bf16[1040,512]{1,0:T(8,128)(2,1)S(1)} %get-tuple-element.31), channel_id=1, source_target_pairs={{0,1},{1,0},{2,3},{3,2},{4,5},{5,4},{6,7},{7,6},{8,9},{9,8},{10,11... | collective-permute-start | bytes 3194888 | tf_op jit(solution)/shard_map/ppermute | solution.py:414
  59.8 2.0 %own_rows_back.1.refs_2_.refs_3_ = f32[768,512]{1,0:T(8,128)S(1)} custom-call(s32[1,14]{1,0:T(1,128)S(1)} %copy-done.11, s32[1,14]{1,0:T(1,128)S(1)} %copy-done.13, s32[1]{0:T(128)S(6)} %copy.16.count_ref, bf16[14,128,128]{2,1,0:T(8,128)(2,1)S(1)} %copy-done.7, s32[1,512]{1,0:T(1,128)S(1)} %bitcast.16, bf16[512,512]{1,0:T(8,128)(2,1)S(1)} %get-tuple-element.32.d_pre_ref, ...), custom_call_target="tpu_custom_call" | custom-call | flops 1207959552 | bytes 3606528 | tf_op jit(solution)/shard_map/own_rows_back/pallas_call | solution.py:52
  61.9 0.2 collective-permute-done.1.refs_1_
  62.1 0.2 sum_pair.1
  62.3 0.0 copy-start.1
  62.3 19.0 %all_to_all.31.arrived_ref = bf16[16,64,512]{2,1,0:T(8,128)(2,1)S(1)} all-to-all(bf16[16,64,512]{2,1,0:T(8,128)(2,1)S(1)} %get-tuple-element.34), channel_id=1, replica_groups=mesh['z'=16,'y'=4,'x'=4,'core'=2] {'y','x'}, dimensions={0} | all-to-all | bytes 2097152 | tf_op jit(solution)/shard_map/all_to_all | solution.py:411
  81.3 0.3 sum_plane.1
  81.6 23.3 %all_to_all.32.arrived_ref.refs_2_ = bf16[16,8,512]{2,1,0:T(8,128)(2,1)S(1)} all-to-all(bf16[16,8,512]{2,1,0:T(8,128)(2,1)S(1)} %sum_plane.1), channel_id=1, replica_groups=mesh['z'=16,'y'=4,'x'=4,'core'=2] {'z'}, dimensions={0} | all-to-all | bytes 262144 | tf_op jit(solution)/shard_map/all_to_all | solution.py:411
  104.9 0.6 sum_weights.1
  105.6 5.1 %all-to-all-start.4 = ((bf16[16,8,128]{2,1,0:T(8,128)(2,1)}), bf16[16,8,128]{2,1,0:T(8,128)(2,1)S(1)}, u32[]{:S(2)}, u32[]{:S(2)}) async-start(bf16[16,8,128]{2,1,0:T(8,128)(2,1)} %get-tuple-element.36.refs_4_), calls=%async_computation.4 | async-start | bytes 65536 | tf_op jit(solution)/shard_map/all_to_all | solution.py:411
  110.7 0.6 return_rows.1
  111.3 3.8 %collective-permute-start.2 = (bf16[192,512]{1,0:T(8,128)(2,1)S(1)}, bf16[192,512]{1,0:T(8,128)(2,1)S(1)}, u32[]{:S(2)}, u32[]{:S(2)}) collective-permute-start(bf16[192,512]{1,0:T(8,128)(2,1)S(1)} %get-tuple-element.39), channel_id=1, source_target_pairs={{0,4},{2,6},{4,0},{6,2},{1,5},{3,7},{5,1},{7,3},{8,12},{10,14},{12... | collective-permute-start | bytes 589832 | tf_op jit(solution)/shard_map/ppermute | solution.py:492
  115.1 1.9 %collective-permute-start.3 = (bf16[192,512]{1,0:T(8,128)(2,1)S(1)}, bf16[192,512]{1,0:T(8,128)(2,1)S(1)}, u32[]{:S(2)}, u32[]{:S(2)}) collective-permute-start(bf16[192,512]{1,0:T(8,128)(2,1)S(1)} %get-tuple-element.40), channel_id=1, source_target_pairs={{0,2},{2,0},{4,6},{6,4},{1,3},{3,1},{5,7},{7,5},{8,10},{10,8},{12,... | collective-permute-start | bytes 589832 | tf_op jit(solution)/shard_map/ppermute | solution.py:492
  117.1 3.2 %collective-permute-start.4 = (bf16[192,512]{1,0:T(8,128)(2,1)S(1)}, bf16[192,512]{1,0:T(8,128)(2,1)S(1)}, u32[]{:S(2)}, u32[]{:S(2)}) collective-permute-start(bf16[192,512]{1,0:T(8,128)(2,1)S(1)} %get-tuple-element.41), channel_id=1, source_target_pairs={{0,6},{2,4},{4,2},{6,0},{1,7},{3,5},{5,3},{7,1},{8,14},{10,12},{12... | collective-permute-start | bytes 589832 | tf_op jit(solution)/shard_map/ppermute | solution.py:492
  120.3 1.8 %all-to-all-done.4.refs_0_ = bf16[16,8,128]{2,1,0:T(8,128)(2,1)S(1)} async-done(((bf16[16,8,128]{2,1,0:T(8,128)(2,1)}), bf16[16,8,128]{2,1,0:T(8,128)(2,1)S(1)}, u32[]{:S(2)}, u32[]{:S(2)}) %all-to-all-start.4) | async-done | bytes 32800 | tf_op jit(solution)/shard_map/all_to_all | solution.py:411
  122.1 0.1 gather_weights.1.whole_ref
  122.3 0.9 spread_weights.1
  123.2 4.0 %all-to-all-start.5 = ((bf16[16,40,512]{2,1,0:T(8,128)(2,1)}), bf16[16,40,512]{2,1,0:T(8,128)(2,1)S(1)}, u32[]{:S(2)}, u32[]{:S(2)}) async-start(bf16[16,40,512]{2,1,0:T(8,128)(2,1)} %spread_weights.1), calls=%async_computation.5 | async-start | bytes 1310720 | tf_op jit(solution)/shard_map/all_to_all | solution.py:411
  127.2 0.0 collective-permute-done.2.refs_0_
  127.2 0.0 collective-permute-done.3.refs_1_
  127.2 0.0 collective-permute-done.4.refs_2_
  127.2 0.1 sum_rows.1
  127.3 9.6 %all-to-all-done.5.arrived_ref = bf16[16,40,512]{2,1,0:T(8,128)(2,1)S(1)} async-done(((bf16[16,40,512]{2,1,0:T(8,128)(2,1)}), bf16[16,40,512]{2,1,0:T(8,128)(2,1)S(1)}, u32[]{:S(2)}, u32[]{:S(2)}) %all-to-all-start.5) | async-done | bytes 655392 | tf_op jit(solution)/shard_map/all_to_all | solution.py:411
  136.9 0.7 join.1
  137.6 6.3 %collective-permute-start.5 = (bf16[608,512]{1,0:T(8,128)(2,1)S(1)}, bf16[608,512]{1,0:T(8,128)(2,1)S(1)}, u32[]{:S(2)}, u32[]{:S(2)}) collective-permute-start(bf16[608,512]{1,0:T(8,128)(2,1)S(1)} %get-tuple-element.43.near_ref), channel_id=1, source_target_pairs={{0,1},{1,0},{2,3},{3,2},{4,5},{5,4},{6,7},{7,6},{8,9},{9,8},{10,11... | collective-permute-start | bytes 1867784 | tf_op jit(solution)/shard_map/ppermute | solution.py:414
  143.9 1.7 %collective-permute-done.5.far_ref = bf16[608,512]{1,0:T(8,128)(2,1)S(1)} collective-permute-done((bf16[608,512]{1,0:T(8,128)(2,1)S(1)}, bf16[608,512]{1,0:T(8,128)(2,1)S(1)}, u32[]{:S(2)}, u32[]{:S(2)}) %collective-permute-start.5) | collective-permute-done | bytes 622624 | tf_op jit(solution)/shard_map/ppermute | solution.py:414
  145.5 1.1 finish.1
  (20 shorter events, 0.0 us)
Async XLA Ops:
  3.0 28.5 %all-to-all-start = ((bf16[16,24,128]{2,1,0:T(8,128)(2,1)}), bf16[16,24,128]{2,1,0:T(8,128)(2,1)S(1)}, u32[]{:S(2)}, u32[]{:S(2)}) async-start(bf16[16,24,128]{2,1,0:T(8,128)(2,1)} %bitcast.17), calls=%async_computation | async-start | bytes 196608 | tf_op jit(solution)/shard_map/all_to_all | solution.py:411
  20.1 1.1 copy-start
  21.3 1.0 copy-start.4
  22.3 1.0 copy-start.6
  23.3 0.7 copy-start.8
  24.0 0.7 copy-start.10
  24.7 0.7 copy-start.12
  30.1 1.5 %copy-start.14 = (bf16[2560,512]{1,0:T(8,128)(2,1)}, bf16[2560,512]{1,0:T(8,128)(2,1)S(1)}, u32[]{:S(2)}) copy-start(bf16[2560,512]{1,0:T(8,128)(2,1)S(1)} %get-tuple-element.28.mats_ref) | copy-start | bytes 7864324
  31.6 23.2 %copy-start.2 = (bf16[512,512]{1,0:T(8,128)(2,1)S(1)}, bf16[512,512]{1,0:T(8,128)(2,1)}, u32[]{:S(2)}) copy-start(bf16[512,512]{1,0:T(8,128)(2,1)} %w_neigh_ref.1) | copy-start | bytes 1572868
  31.6 23.2 %copy-start.3 = (bf16[512,512]{1,0:T(8,128)(2,1)S(1)}, bf16[512,512]{1,0:T(8,128)(2,1)}, u32[]{:S(2)}) copy-start(bf16[512,512]{1,0:T(8,128)(2,1)} %cot_ref.1) | copy-start | bytes 1572868
  31.6 23.2 %copy-start.15 = (bf16[2560,512]{1,0:T(8,128)(2,1)S(1)}, bf16[2560,512]{1,0:T(8,128)(2,1)}, u32[]{:S(2)}) copy-start(bf16[2560,512]{1,0:T(8,128)(2,1)} %copy-done.14) | copy-start | bytes 7864324
  48.5 6.2 %collective-permute-start = (bf16[512,512]{1,0:T(8,128)(2,1)S(1)}, bf16[512,512]{1,0:T(8,128)(2,1)S(1)}, u32[]{:S(2)}, u32[]{:S(2)}) collective-permute-start(bf16[512,512]{1,0:T(8,128)(2,1)S(1)} %bitcast.10), channel_id=1, source_target_pairs={{0,1},{1,0},{2,3},{3,2},{4,5},{5,4},{6,7},{7,6},{8,9},{9,8},{10,11... | collective-permute-start | bytes 1572872 | tf_op jit(solution)/shard_map/ppermute | solution.py:414
  54.7 5.0 %copy-start.5 = (bf16[512,512]{1,0:T(8,128)(2,1)S(1)}, bf16[512,512]{1,0:T(8,128)(2,1)}, u32[]{:S(2)}) copy-start(bf16[512,512]{1,0:T(8,128)(2,1)} %w_self_ref.3) | copy-start | bytes 1572868
  54.7 5.0 %copy-start.7 = (bf16[14,128,128]{2,1,0:T(8,128)(2,1)S(1)}, bf16[14,128,128]{2,1,0:T(8,128)(2,1)}, u32[]{:S(2)}) copy-start(bf16[14,128,128]{2,1,0:T(8,128)(2,1)} %tiles_ref.3) | copy-start | bytes 1376260
  54.8 5.0 %copy-start.9 = (s32[512]{0:T(512)S(1)}, s32[512]{0:T(512)}, u32[]{:S(2)}) copy-start(s32[512]{0:T(512)} %param.13) | copy-start | bytes 6148
  54.8 5.0 %copy-start.11 = (s32[1,14]{1,0:T(1,128)S(1)}, s32[1,14]{1,0:T(1,128)}, u32[]{:S(2)}) copy-start(s32[1,14]{1,0:T(1,128)} %dst_ref.3) | copy-start | bytes 172
  54.8 5.0 %copy-start.13 = (s32[1,14]{1,0:T(1,128)S(1)}, s32[1,14]{1,0:T(1,128)}, u32[]{:S(2)}) copy-start(s32[1,14]{1,0:T(1,128)} %src_ref.3) | copy-start | bytes 172
  57.5 4.6 %collective-permute-start.1 = (bf16[1040,512]{1,0:T(8,128)(2,1)S(1)}, bf16[1040,512]{1,0:T(8,128)(2,1)S(1)}, u32[]{:S(2)}, u32[]{:S(2)}) collective-permute-start(bf16[1040,512]{1,0:T(8,128)(2,1)S(1)} %get-tuple-element.31), channel_id=1, source_target_pairs={{0,1},{1,0},{2,3},{3,2},{4,5},{5,4},{6,7},{7,6},{8,9},{9,8},{10,11... | collective-permute-start | bytes 3194888 | tf_op jit(solution)/shard_map/ppermute | solution.py:414
  62.3 48.3 %copy-start.1 = (s32[1,64,8]{1,2,0:T(8,128)S(1)}, s32[1,64,8]{1,2,0:T(8,128)}, u32[]{:S(2)}) copy-start(s32[1,64,8]{1,2,0:T(8,128)} %param.12) | copy-start | bytes 6148
  105.6 16.6 %all-to-all-start.4 = ((bf16[16,8,128]{2,1,0:T(8,128)(2,1)}), bf16[16,8,128]{2,1,0:T(8,128)(2,1)S(1)}, u32[]{:S(2)}, u32[]{:S(2)}) async-start(bf16[16,8,128]{2,1,0:T(8,128)(2,1)} %get-tuple-element.36.refs_4_), calls=%async_computation.4 | async-start | bytes 65536 | tf_op jit(solution)/shard_map/all_to_all | solution.py:411
  111.3 15.9 %collective-permute-start.2 = (bf16[192,512]{1,0:T(8,128)(2,1)S(1)}, bf16[192,512]{1,0:T(8,128)(2,1)S(1)}, u32[]{:S(2)}, u32[]{:S(2)}) collective-permute-start(bf16[192,512]{1,0:T(8,128)(2,1)S(1)} %get-tuple-element.39), channel_id=1, source_target_pairs={{0,4},{2,6},{4,0},{6,2},{1,5},{3,7},{5,1},{7,3},{8,12},{10,14},{12... | collective-permute-start | bytes 589832 | tf_op jit(solution)/shard_map/ppermute | solution.py:492
  115.1 12.1 %collective-permute-start.3 = (bf16[192,512]{1,0:T(8,128)(2,1)S(1)}, bf16[192,512]{1,0:T(8,128)(2,1)S(1)}, u32[]{:S(2)}, u32[]{:S(2)}) collective-permute-start(bf16[192,512]{1,0:T(8,128)(2,1)S(1)} %get-tuple-element.40), channel_id=1, source_target_pairs={{0,2},{2,0},{4,6},{6,4},{1,3},{3,1},{5,7},{7,5},{8,10},{10,8},{12,... | collective-permute-start | bytes 589832 | tf_op jit(solution)/shard_map/ppermute | solution.py:492
  117.1 10.2 %collective-permute-start.4 = (bf16[192,512]{1,0:T(8,128)(2,1)S(1)}, bf16[192,512]{1,0:T(8,128)(2,1)S(1)}, u32[]{:S(2)}, u32[]{:S(2)}) collective-permute-start(bf16[192,512]{1,0:T(8,128)(2,1)S(1)} %get-tuple-element.41), channel_id=1, source_target_pairs={{0,6},{2,4},{4,2},{6,0},{1,7},{3,5},{5,3},{7,1},{8,14},{10,12},{12... | collective-permute-start | bytes 589832 | tf_op jit(solution)/shard_map/ppermute | solution.py:492
  123.2 13.7 %all-to-all-start.5 = ((bf16[16,40,512]{2,1,0:T(8,128)(2,1)}), bf16[16,40,512]{2,1,0:T(8,128)(2,1)S(1)}, u32[]{:S(2)}, u32[]{:S(2)}) async-start(bf16[16,40,512]{2,1,0:T(8,128)(2,1)} %spread_weights.1), calls=%async_computation.5 | async-start | bytes 1310720 | tf_op jit(solution)/shard_map/all_to_all | solution.py:411
  137.6 8.0 %collective-permute-start.5 = (bf16[608,512]{1,0:T(8,128)(2,1)S(1)}, bf16[608,512]{1,0:T(8,128)(2,1)S(1)}, u32[]{:S(2)}, u32[]{:S(2)}) collective-permute-start(bf16[608,512]{1,0:T(8,128)(2,1)S(1)} %get-tuple-element.43.near_ref), channel_id=1, source_target_pairs={{0,1},{1,0},{2,3},{3,2},{4,5},{5,4},{6,7},{7,6},{8,9},{9,8},{10,11... | collective-permute-start | bytes 1867784 | tf_op jit(solution)/shard_map/ppermute | solution.py:414

commit v11 on v10

--- a/solution.py
+++ b/solution.py
@@ -19,7 +19,6 @@
 BF16 = jnp.bfloat16
 F32 = jnp.float32
 VMEM_BYTES = 24 * 1024 * 1024
-FULL_VMEM_BYTES = 65 * 1000 * 1024
 
 
 def dot(a, b, contract_a=1, contract_b=0):
@@ -42,7 +41,7 @@
     return jnp.where(row == 0, high, jnp.where(row == 1, wide - high, 0.0)).astype(BF16)
 
 
-def call(kernel, name, outs, scalars, arrays, scratch=(), flops=0, after=(), hbm=(), hbm_outs=(), limit=VMEM_BYTES):
+def call(kernel, name, outs, scalars, arrays, scratch=(), flops=0, after=(), hbm=(), hbm_outs=()):
     if after:
         inner, at = kernel, len(scalars) + len(arrays) + len(hbm)
         kernel = lambda *refs: inner(*refs[:at], *refs[at + len(after) :])
@@ -59,10 +58,10 @@
         out_specs=tuple([pl.BlockSpec(memory_space=pltpu.VMEM)] * len(outs))
         + tuple([pl.BlockSpec(memory_space=pltpu.HBM)] * len(hbm_outs)),
         scratch_shapes=list(scratch),
-        compiler_params=pltpu.CompilerParams(vmem_limit_bytes=limit),
+        compiler_params=pltpu.CompilerParams(vmem_limit_bytes=VMEM_BYTES),
         cost_estimate=pl.CostEstimate(flops=flops, bytes_accessed=size, transcendentals=0),
         name=name,
-    )(*scalars, *arrays, *hbm, *after)
+    )(*scalars, *arrays, *(pltpu.with_memory_space_constraint(a, pltpu.HBM) for a in hbm), *after)
 
 
 def fetched(arrays):
@@ -175,22 +174,33 @@
 
 
 def own_kernel(
-    core_ref, dst_ref, src_ref, count_ref, tiles_ref, feats_ref, seeds_ref, w_self_ref, bias_ref,
-    mats_ref, sums_ref, own_adj_ref, adj_ref,
+    core_ref, count_ref, dst_hbm, src_hbm, tiles_hbm, feats_hbm, seeds_hbm, w_self_hbm,
+    sums_ref, mats_hbm, dst_ref, src_ref, tiles_ref, feats_ref, seeds_ref, w_self_ref,
+    sems, own_adj_ref, adj_ref, mats_ref, out_sem,
 ):
+    *tile_copies, feats_copy, seeds_copy, w_self_copy = fetch(
+        (dst_hbm, src_hbm, tiles_hbm, feats_hbm, seeds_hbm, w_self_hbm),
+        (dst_ref, src_ref, tiles_ref, feats_ref, seeds_ref, w_self_ref),
+        sems,
+    )
     rows = feats_ref.shape[0]
     seeds = seeds_ref.shape[1]
+    for copy in tile_copies:
+        copy.wait()
     own_blocks = rows // BLK
     table = adj_ref.shape[1]
     place_tiles(dst_ref, src_ref, count_ref, tiles_ref, own_adj_ref, 0, own_blocks)
     place_tiles(
         dst_ref, src_ref, count_ref, tiles_ref, adj_ref, own_blocks, own_blocks + table // BLK
     )
+    seeds_copy.wait()
+    feats_copy.wait()
     picks = (iota((rows, seeds), 0) == seeds_ref[...]).astype(BF16)
     feats = feats_ref[...]
     mats_ref[2 * seeds + adj_ref.shape[1] :, :seeds] = dot(feats, picks, 0, 0).astype(BF16)
     chosen = dot(picks, feats, 0, 0).astype(BF16)
-    sums_ref[:seeds] = dot(chosen, w_self_ref[...]) + bias_ref[...].astype(F32)
+    w_self_copy.wait()
+    sums_ref[:seeds] = dot(chosen, w_self_ref[...])
     sums_ref[seeds:] = dot(own_adj_ref[...], feats)
     adj = adj_ref[...]
     half = table // 2
@@ -205,10 +215,13 @@
         mats_ref[far * seeds : (far + 1) * seeds, :half] = dot(adj, order, 1, 1).astype(BF16)
         first = 2 * seeds + far * half
         mats_ref[first : first + half, :seeds] = dot(order, adj, 1, 1).astype(BF16)
+    back = pltpu.make_async_copy(mats_ref, mats_hbm, out_sem)
+    back.start()
+    back.wait()
 
 
 def middle_kernel(
-    core_ref, near_ref, far_ref, mats_ref, sums_ref, w_neigh_ref, cot_ref,
+    core_ref, near_ref, far_ref, mats_ref, sums_ref, w_neigh_ref, cot_ref, bias_in_ref,
     out_ref, d_pre_ref, d_agg_ref, keep_ref, send_ref,
 ):
     width = w_neigh_ref.shape[0]
@@ -220,7 +233,7 @@
         + dot(mats_ref[:seeds, :half], near_ref[...])
         + dot(mats_ref[seeds : 2 * seeds, :half], far_ref[...])
     ).astype(BF16)
-    preact = sums_ref[:seeds] + dot(aggregate, w_neigh_ref[...])
+    preact = sums_ref[:seeds] + dot(aggregate, w_neigh_ref[...]) + bias_in_ref[...].astype(F32)
     gate = jax.nn.sigmoid(preact)
     out_ref[...] = (preact * gate).astype(BF16)
     d_pre = (cot_ref[...].astype(F32) * gate * (1.0 + preact * (1.0 - gate))).astype(BF16)
@@ -417,21 +430,24 @@
     (send,) = call(
         send_kernel, "pick_boundary", [((depth * lines, LANES), BF16)], [rep], [],
         hbm=[lists, feats], scratch=fetched([lists, feats]), flops=4 * parts * rows * width,
-        limit=FULL_VMEM_BYTES,
     )
     by_depth = swap(send.reshape(depth, lines, LANES), "z").reshape(depth * lines, LANES)
-    mats, sums = call(
-        own_kernel, "own_rows",
-        [
-            ((2 * (seeds + half) + width, max(seeds, half)), BF16),
-            ((2 * seeds, width), F32),
+    mats_shape = (2 * (seeds + half) + width, max(seeds, half))
+    own_args = [tile_dst, tile_src, tiles, feats, seed_row, w_self]
+    sums, mats = call(
+        own_kernel, "own_rows", [((2 * seeds, width), F32)], [core, tile_count], [],
+        hbm=own_args,
+        hbm_outs=[(mats_shape, BF16)],
+        scratch=[pltpu.SMEM(a.shape, a.dtype) for a in (tile_dst, tile_src)]
+        + fetched(own_args)[2:]
+        + [
+            pltpu.VMEM((seeds, rows), BF16),
+            pltpu.VMEM((seeds, 2 * half), BF16),
+            pltpu.VMEM(mats_shape, BF16),
+            pltpu.SemaphoreType.DMA,
         ],
-        [core, *tile_scalars],
-        [tiles, feats, seed_row, w_self, bias.reshape(1, width)],
-        scratch=[pltpu.VMEM((seeds, rows), BF16), pltpu.VMEM((seeds, 2 * half), BF16)],
         flops=2 * seeds * (3 * rows * width + width * width + 8 * half * half),
     )
-
     (plane,) = call(
         plane_kernel, "spread_plane", [((PLANE, 2 * depth, width), BF16)], [], [by_depth],
         flops=8 * parts * parts * width, after=[sums],
@@ -450,7 +466,7 @@
         ],
         [core],
         [
-            near, far, mats, sums, w_neigh, cotangent,
+            near, far, mats, sums, w_neigh, cotangent, bias.reshape(1, width),
         ],
         flops=2 * seeds * width * (4 * half + 4 * width),
     )

time: 147 us -> 142 us (0.966)
  local copies, waits for them, and re-layouts: 7.4 us -> 0.05 us
  blocking collectives: 58.9 us -> 53.2 us
  waiting for transfers between devices: 14.8 us -> 18.8 us
  Pallas kernels: 16.9 us -> 19.3 us
    unnamed x32 -> x20, local copies, waits for them, and re-layouts: 6.71 us -> 0.05 us
    all_to_all x3, blocking collectives: 58.9 us -> 53.2 us  [swap(): return lax.all_to_all(values, axis, split_axis=0, concat_axis=0, tiled=True)]
    all_to_all x3, waiting for transfers between devices: 11.4 us -> 15.5 us  [swap(): return lax.all_to_all(values, axis, split_axis=0, concat_axis=0, tiled=True)]
    pallas_call x14, Pallas kernels: 16.9 us -> 19.3 us  [call(): pl.pallas_call(kernel, out_shape=shapes, in_specs=[pl.BlockSpec(memory_sp...]
  transfers between devices with their start and end apart: 9 -> 9, of which waited for: 5 -> 6; matrix products, arithmetic and copies ran while one was open for 0% -> 0% of each run, Pallas kernels for 6% -> 8%
where the time goes in v11:
time: 142 us; the launch traced here: 141 us
  blocking collectives  53.2 us (37%)
  starting transfers between devices  48.4 us (34%)
  Pallas kernels  19.3 us (14%)
  waiting for transfers between devices  18.8 us (13%)
  between operations  1.56 us (1%)
    all_to_all x3, blocking collectives, swap(): return lax.all_to_all(values, axis, split_axis=0, concat_axis=0, tiled=True)  53.2 us
    all_to_all x3, starting transfers between devices, swap(): return lax.all_to_all(values, axis, split_axis=0, concat_axis=0, tiled=True)  24.9 us
    pallas_call x14, Pallas kernels, call(): pl.pallas_call(kernel, out_shape=shapes, in_specs=[pl.BlockSpec(memory_sp...  19.3 us
    all_to_all x3, waiting for transfers between devices, swap(): return lax.all_to_all(values, axis, split_axis=0, concat_axis=0, tiled=True)  15.5 us
    ppermute x3, starting transfers between devices, pair(): return lax.ppermute(values, 'core', [(0, 1), (1, 0)])  14.6 us
    ppermute x3, starting transfers between devices, body(): lax.ppermute(row_sends[step - 1], 'x', [(x, x ^ step) for x in range(X_SI...  8.98 us
    ppermute x3, waiting for transfers between devices, pair(): return lax.ppermute(values, 'core', [(0, 1), (1, 0)])  3.32 us
  transfers between devices with their start and end apart: 9, of which 6 were waited for; matrix products, arithmetic and copies ran while one was open for 0% of the time, Pallas kernels for 8%

profile of v11, /device:TPU:1, one launch (start us, length us, event | category | flops | bytes accessed | tf_op | source)
XLA Modules:
  0.0 141.4 jit_solution(12280245206794042972)
XLA Ops:
  0.6 2.4 %pick_boundary.1 = bf16[384,128]{1,0:T(8,128)(2,1)} custom-call(s32[1]{0:T(128)} %bitcast.1.rep_ref.refs_0_, s32[8,64]{1,0:T(8,128)} %bitcast.13, bf16[768,512]{1,0:T(8,128)(2,1)} %feats_hbm.3), custom_call_target="tpu_custom_call" | custom-call | flops 100663296 | bytes 886784 | tf_op jit(solution)/shard_map/pick_boundary/pallas_call | solution.py:51
  3.0 15.8 %all-to-all-start = ((bf16[16,24,128]{2,1,0:T(8,128)(2,1)}), bf16[16,24,128]{2,1,0:T(8,128)(2,1)S(1)}, u32[]{:S(2)}, u32[]{:S(2)}) async-start(bf16[16,24,128]{2,1,0:T(8,128)(2,1)} %bitcast.4), calls=%async_computation | async-start | bytes 196608 | tf_op jit(solution)/shard_map/all_to_all | solution.py:424
  19.5 7.1 %own_rows.1 = (f32[1024,512]{1,0:T(8,128)S(1)}, bf16[2560,512]{1,0:T(8,128)(2,1)}) custom-call(s32[1]{0:T(128)} %bitcast.core_ref, s32[1]{0:T(128)S(6)} %copy.16.count_ref, s32[1,14]{1,0:T(1,128)} %dst_ref.1, s32[1,14]{1,0:T(1,128)} %src_ref.1, bf16[14,128,128]{2,1,0:T(8,128)(2,1)} %tiles_ref.1, bf16[768,512]{1,0:T(8,128)(2,1)} %feats_hbm.3, ...), custom_call_target="tpu_custom_call" | custom-call | flops 3623878656 | bytes 6490224 | tf_op jit(solution)/shard_map/own_rows/pallas_call | solution.py:51
  26.5 4.1 %all-to-all-done = bf16[16,24,128]{2,1,0:T(8,128)(2,1)S(1)} async-done(((bf16[16,24,128]{2,1,0:T(8,128)(2,1)}), bf16[16,24,128]{2,1,0:T(8,128)(2,1)S(1)}, u32[]{:S(2)}, u32[]{:S(2)}) %all-to-all-start) | async-done | bytes 98336 | tf_op jit(solution)/shard_map/all_to_all | solution.py:424
  30.7 0.3 spread_plane.1
  31.0 15.8 %all_to_all.30 = bf16[16,32,512]{2,1,0:T(8,128)(2,1)S(1)} all-to-all(bf16[16,32,512]{2,1,0:T(8,128)(2,1)S(1)} %spread_plane.1), channel_id=1, replica_groups=mesh['z'=16,'y'=4,'x'=4,'core'=2] {'y','x'}, dimensions={0} | all-to-all | bytes 1048576 | tf_op jit(solution)/shard_map/all_to_all | solution.py:424
  46.8 6.0 %collective-permute-start = (bf16[512,512]{1,0:T(8,128)(2,1)S(1)}, bf16[512,512]{1,0:T(8,128)(2,1)S(1)}, u32[]{:S(2)}, u32[]{:S(2)}) collective-permute-start(bf16[512,512]{1,0:T(8,128)(2,1)S(1)} %bitcast.10), channel_id=1, source_target_pairs={{0,1},{1,0},{2,3},{3,2},{4,5},{5,4},{6,7},{7,6},{8,9},{9,8},{10,11... | collective-permute-start | bytes 1572872 | tf_op jit(solution)/shard_map/ppermute | solution.py:427
  52.8 0.0 copy-done.9
  52.8 1.5 %collective-permute-done.far_ref = bf16[512,512]{1,0:T(8,128)(2,1)S(1)} collective-permute-done((bf16[512,512]{1,0:T(8,128)(2,1)S(1)}, bf16[512,512]{1,0:T(8,128)(2,1)S(1)}, u32[]{:S(2)}, u32[]{:S(2)}) %collective-permute-start) | collective-permute-done | bytes 524320 | tf_op jit(solution)/shard_map/ppermute | solution.py:427
  54.3 0.0 copy-done.1
  54.3 0.0 copy-done.2
  54.3 0.0 copy-start.4
  54.3 0.0 copy-start.5
  54.3 0.0 copy-start.6
  54.4 0.0 copy-start.7
  54.4 2.7 %forward_backward.1 = (bf16[512,512]{1,0:T(8,128)(2,1)}, bf16[512,512]{1,0:T(8,128)(2,1)S(1)}, bf16[512,512]{1,0:T(8,128)(2,1)S(1)}, bf16[1040,512]{1,0:T(8,128)(2,1)S(1)}, bf16[1040,512]{1,0:T(8,128)(2,1)S(1)}) custom-call(s32[1]{0:T(128)} %bitcast.core_ref, bf16[512,512]{1,0:T(8,128)(2,1)S(1)} %bitcast.11, ...), custom_call_target="tpu_custom_call" | custom-call | flops 2147483648 | bytes 10519552 | tf_op jit(solution)/shard_map/forward_backward/pallas_call | solution.py:51
  57.1 2.3 %collective-permute-start.1 = (bf16[1040,512]{1,0:T(8,128)(2,1)S(1)}, bf16[1040,512]{1,0:T(8,128)(2,1)S(1)}, u32[]{:S(2)}, u32[]{:S(2)}) collective-permute-start(bf16[1040,512]{1,0:T(8,128)(2,1)S(1)} %get-tuple-element.31), channel_id=1, source_target_pairs={{0,1},{1,0},{2,3},{3,2},{4,5},{5,4},{6,7},{7,6},{8,9},{9,8},{10,11... | collective-permute-start | bytes 3194888 | tf_op jit(solution)/shard_map/ppermute | solution.py:427
  59.4 0.0 copy-done.3
  59.4 0.0 copy-done.4
  59.4 0.0 copy-done.5
  59.4 0.0 copy-done.6
  59.5 0.0 copy-done.7
  59.5 2.1 %own_rows_back.1.refs_2_.refs_3_ = f32[768,512]{1,0:T(8,128)S(1)} custom-call(s32[1,14]{1,0:T(1,128)S(1)} %copy-done.6, s32[1,14]{1,0:T(1,128)S(1)} %copy-done.7, s32[1]{0:T(128)S(6)} %copy.16.count_ref, bf16[14,128,128]{2,1,0:T(8,128)(2,1)S(1)} %copy-done.4, s32[1,512]{1,0:T(1,128)S(1)} %bitcast.16, bf16[512,512]{1,0:T(8,128)(2,1)S(1)} %get-tuple-element.32.d_pre_ref, ...), custom_call_target="tpu_custom_call" | custom-call | flops 1207959552 | bytes 3606528 | tf_op jit(solution)/shard_map/own_rows_back/pallas_call | solution.py:51
  61.5 0.2 collective-permute-done.1.refs_1_
  61.7 0.2 sum_pair.1
  62.0 0.0 copy-start
  62.0 19.0 %all_to_all.31.arrived_ref = bf16[16,64,512]{2,1,0:T(8,128)(2,1)S(1)} all-to-all(bf16[16,64,512]{2,1,0:T(8,128)(2,1)S(1)} %get-tuple-element.34), channel_id=1, replica_groups=mesh['z'=16,'y'=4,'x'=4,'core'=2] {'y','x'}, dimensions={0} | all-to-all | bytes 2097152 | tf_op jit(solution)/shard_map/all_to_all | solution.py:424
  81.0 0.3 sum_plane.1
  81.3 18.4 %all_to_all.32.arrived_ref.refs_2_ = bf16[16,8,512]{2,1,0:T(8,128)(2,1)S(1)} all-to-all(bf16[16,8,512]{2,1,0:T(8,128)(2,1)S(1)} %sum_plane.1), channel_id=1, replica_groups=mesh['z'=16,'y'=4,'x'=4,'core'=2] {'z'}, dimensions={0} | all-to-all | bytes 262144 | tf_op jit(solution)/shard_map/all_to_all | solution.py:424
  99.7 0.6 sum_weights.1
  100.3 5.1 %all-to-all-start.4 = ((bf16[16,8,128]{2,1,0:T(8,128)(2,1)}), bf16[16,8,128]{2,1,0:T(8,128)(2,1)S(1)}, u32[]{:S(2)}, u32[]{:S(2)}) async-start(bf16[16,8,128]{2,1,0:T(8,128)(2,1)} %get-tuple-element.36.refs_4_), calls=%async_computation.4 | async-start | bytes 65536 | tf_op jit(solution)/shard_map/all_to_all | solution.py:424
  105.4 0.6 return_rows.1
  106.1 3.8 %collective-permute-start.2 = (bf16[192,512]{1,0:T(8,128)(2,1)S(1)}, bf16[192,512]{1,0:T(8,128)(2,1)S(1)}, u32[]{:S(2)}, u32[]{:S(2)}) collective-permute-start(bf16[192,512]{1,0:T(8,128)(2,1)S(1)} %get-tuple-element.39), channel_id=1, source_target_pairs={{0,4},{2,6},{4,0},{6,2},{1,5},{3,7},{5,1},{7,3},{8,12},{10,14},{12... | collective-permute-start | bytes 589832 | tf_op jit(solution)/shard_map/ppermute | solution.py:508
  109.9 1.9 %collective-permute-start.3 = (bf16[192,512]{1,0:T(8,128)(2,1)S(1)}, bf16[192,512]{1,0:T(8,128)(2,1)S(1)}, u32[]{:S(2)}, u32[]{:S(2)}) collective-permute-start(bf16[192,512]{1,0:T(8,128)(2,1)S(1)} %get-tuple-element.40), channel_id=1, source_target_pairs={{0,2},{2,0},{4,6},{6,4},{1,3},{3,1},{5,7},{7,5},{8,10},{10,8},{12,... | collective-permute-start | bytes 589832 | tf_op jit(solution)/shard_map/ppermute | solution.py:508
  111.8 3.2 %collective-permute-start.4 = (bf16[192,512]{1,0:T(8,128)(2,1)S(1)}, bf16[192,512]{1,0:T(8,128)(2,1)S(1)}, u32[]{:S(2)}, u32[]{:S(2)}) collective-permute-start(bf16[192,512]{1,0:T(8,128)(2,1)S(1)} %get-tuple-element.41), channel_id=1, source_target_pairs={{0,6},{2,4},{4,2},{6,0},{1,7},{3,5},{5,3},{7,1},{8,14},{10,12},{12... | collective-permute-start | bytes 589832 | tf_op jit(solution)/shard_map/ppermute | solution.py:508
  115.1 1.8 %all-to-all-done.4.refs_0_ = bf16[16,8,128]{2,1,0:T(8,128)(2,1)S(1)} async-done(((bf16[16,8,128]{2,1,0:T(8,128)(2,1)}), bf16[16,8,128]{2,1,0:T(8,128)(2,1)S(1)}, u32[]{:S(2)}, u32[]{:S(2)}) %all-to-all-start.4) | async-done | bytes 32800 | tf_op jit(solution)/shard_map/all_to_all | solution.py:424
  116.9 0.1 gather_weights.1.whole_ref
  117.0 0.9 spread_weights.1
  117.9 4.0 %all-to-all-start.5 = ((bf16[16,40,512]{2,1,0:T(8,128)(2,1)}), bf16[16,40,512]{2,1,0:T(8,128)(2,1)S(1)}, u32[]{:S(2)}, u32[]{:S(2)}) async-start(bf16[16,40,512]{2,1,0:T(8,128)(2,1)} %spread_weights.1), calls=%async_computation.5 | async-start | bytes 1310720 | tf_op jit(solution)/shard_map/all_to_all | solution.py:424
  121.9 0.0 collective-permute-done.2.refs_0_
  122.0 0.0 collective-permute-done.3.refs_1_
  122.0 0.0 collective-permute-done.4.refs_2_
  122.0 0.1 sum_rows.1
  122.1 9.6 %all-to-all-done.5.arrived_ref = bf16[16,40,512]{2,1,0:T(8,128)(2,1)S(1)} async-done(((bf16[16,40,512]{2,1,0:T(8,128)(2,1)}), bf16[16,40,512]{2,1,0:T(8,128)(2,1)S(1)}, u32[]{:S(2)}, u32[]{:S(2)}) %all-to-all-start.5) | async-done | bytes 655392 | tf_op jit(solution)/shard_map/all_to_all | solution.py:424
  131.6 0.7 join.1
  132.3 6.3 %collective-permute-start.5 = (bf16[608,512]{1,0:T(8,128)(2,1)S(1)}, bf16[608,512]{1,0:T(8,128)(2,1)S(1)}, u32[]{:S(2)}, u32[]{:S(2)}) collective-permute-start(bf16[608,512]{1,0:T(8,128)(2,1)S(1)} %get-tuple-element.43.near_ref), channel_id=1, source_target_pairs={{0,1},{1,0},{2,3},{3,2},{4,5},{5,4},{6,7},{7,6},{8,9},{9,8},{10,11... | collective-permute-start | bytes 1867784 | tf_op jit(solution)/shard_map/ppermute | solution.py:427
  138.6 1.7 %collective-permute-done.5.far_ref = bf16[608,512]{1,0:T(8,128)(2,1)S(1)} collective-permute-done((bf16[608,512]{1,0:T(8,128)(2,1)S(1)}, bf16[608,512]{1,0:T(8,128)(2,1)S(1)}, u32[]{:S(2)}, u32[]{:S(2)}) %collective-permute-start.5) | collective-permute-done | bytes 622624 | tf_op jit(solution)/shard_map/ppermute | solution.py:427
  140.3 1.1 finish.1
  (8 shorter events, 0.0 us)
Async XLA Ops:
  3.0 27.6 %all-to-all-start = ((bf16[16,24,128]{2,1,0:T(8,128)(2,1)}), bf16[16,24,128]{2,1,0:T(8,128)(2,1)S(1)}, u32[]{:S(2)}, u32[]{:S(2)}) async-start(bf16[16,24,128]{2,1,0:T(8,128)(2,1)} %bitcast.4), calls=%async_computation | async-start | bytes 196608 | tf_op jit(solution)/shard_map/all_to_all | solution.py:424
  30.7 22.1 %copy-start.9 = (bf16[512]{0:T(512)(128)(2,1)S(1)}, bf16[512]{0:T(512)(128)(2,1)}, u32[]{:S(2)}) copy-start(bf16[512]{0:T(512)(128)(2,1)} %param.20) | copy-start | bytes 3076
  30.7 23.6 %copy-start.1 = (bf16[512,512]{1,0:T(8,128)(2,1)S(1)}, bf16[512,512]{1,0:T(8,128)(2,1)}, u32[]{:S(2)}) copy-start(bf16[512,512]{1,0:T(8,128)(2,1)} %w_neigh_ref.1) | copy-start | bytes 1572868
  30.7 23.6 %copy-start.2 = (bf16[512,512]{1,0:T(8,128)(2,1)S(1)}, bf16[512,512]{1,0:T(8,128)(2,1)}, u32[]{:S(2)}) copy-start(bf16[512,512]{1,0:T(8,128)(2,1)} %cot_ref.1) | copy-start | bytes 1572868
  30.7 23.6 %copy-start.8 = (bf16[2560,512]{1,0:T(8,128)(2,1)S(1)}, bf16[2560,512]{1,0:T(8,128)(2,1)}, u32[]{:S(2)}) copy-start(bf16[2560,512]{1,0:T(8,128)(2,1)} %get-tuple-element.28.mats_ref) | copy-start | bytes 7864324
  46.8 7.5 %collective-permute-start = (bf16[512,512]{1,0:T(8,128)(2,1)S(1)}, bf16[512,512]{1,0:T(8,128)(2,1)S(1)}, u32[]{:S(2)}, u32[]{:S(2)}) collective-permute-start(bf16[512,512]{1,0:T(8,128)(2,1)S(1)} %bitcast.10), channel_id=1, source_target_pairs={{0,1},{1,0},{2,3},{3,2},{4,5},{5,4},{6,7},{7,6},{8,9},{9,8},{10,11... | collective-permute-start | bytes 1572872 | tf_op jit(solution)/shard_map/ppermute | solution.py:427
  54.3 5.1 %copy-start.3 = (bf16[512,512]{1,0:T(8,128)(2,1)S(1)}, bf16[512,512]{1,0:T(8,128)(2,1)}, u32[]{:S(2)}) copy-start(bf16[512,512]{1,0:T(8,128)(2,1)} %w_self_ref.1) | copy-start | bytes 1572868
  54.3 5.1 %copy-start.4 = (bf16[14,128,128]{2,1,0:T(8,128)(2,1)S(1)}, bf16[14,128,128]{2,1,0:T(8,128)(2,1)}, u32[]{:S(2)}) copy-start(bf16[14,128,128]{2,1,0:T(8,128)(2,1)} %tiles_ref.1) | copy-start | bytes 1376260
  54.3 5.1 %copy-start.5 = (s32[512]{0:T(512)S(1)}, s32[512]{0:T(512)}, u32[]{:S(2)}) copy-start(s32[512]{0:T(512)} %param.13) | copy-start | bytes 6148
  54.3 5.1 %copy-start.6 = (s32[1,14]{1,0:T(1,128)S(1)}, s32[1,14]{1,0:T(1,128)}, u32[]{:S(2)}) copy-start(s32[1,14]{1,0:T(1,128)} %dst_ref.1) | copy-start | bytes 172
  54.4 5.1 %copy-start.7 = (s32[1,14]{1,0:T(1,128)S(1)}, s32[1,14]{1,0:T(1,128)}, u32[]{:S(2)}) copy-start(s32[1,14]{1,0:T(1,128)} %src_ref.1) | copy-start | bytes 172
  57.1 4.6 %collective-permute-start.1 = (bf16[1040,512]{1,0:T(8,128)(2,1)S(1)}, bf16[1040,512]{1,0:T(8,128)(2,1)S(1)}, u32[]{:S(2)}, u32[]{:S(2)}) collective-permute-start(bf16[1040,512]{1,0:T(8,128)(2,1)S(1)} %get-tuple-element.31), channel_id=1, source_target_pairs={{0,1},{1,0},{2,3},{3,2},{4,5},{5,4},{6,7},{7,6},{8,9},{9,8},{10,11... | collective-permute-start | bytes 3194888 | tf_op jit(solution)/shard_map/ppermute | solution.py:427
  62.0 43.5 %copy-start = (s32[1,64,8]{1,2,0:T(8,128)S(1)}, s32[1,64,8]{1,2,0:T(8,128)}, u32[]{:S(2)}) copy-start(s32[1,64,8]{1,2,0:T(8,128)} %param.12) | copy-start | bytes 6148
  100.3 16.6 %all-to-all-start.4 = ((bf16[16,8,128]{2,1,0:T(8,128)(2,1)}), bf16[16,8,128]{2,1,0:T(8,128)(2,1)S(1)}, u32[]{:S(2)}, u32[]{:S(2)}) async-start(bf16[16,8,128]{2,1,0:T(8,128)(2,1)} %get-tuple-element.36.refs_4_), calls=%async_computation.4 | async-start | bytes 65536 | tf_op jit(solution)/shard_map/all_to_all | solution.py:424
  106.1 15.9 %collective-permute-start.2 = (bf16[192,512]{1,0:T(8,128)(2,1)S(1)}, bf16[192,512]{1,0:T(8,128)(2,1)S(1)}, u32[]{:S(2)}, u32[]{:S(2)}) collective-permute-start(bf16[192,512]{1,0:T(8,128)(2,1)S(1)} %get-tuple-element.39), channel_id=1, source_target_pairs={{0,4},{2,6},{4,0},{6,2},{1,5},{3,7},{5,1},{7,3},{8,12},{10,14},{12... | collective-permute-start | bytes 589832 | tf_op jit(solution)/shard_map/ppermute | solution.py:508
  109.9 12.1 %collective-permute-start.3 = (bf16[192,512]{1,0:T(8,128)(2,1)S(1)}, bf16[192,512]{1,0:T(8,128)(2,1)S(1)}, u32[]{:S(2)}, u32[]{:S(2)}) collective-permute-start(bf16[192,512]{1,0:T(8,128)(2,1)S(1)} %get-tuple-element.40), channel_id=1, source_target_pairs={{0,2},{2,0},{4,6},{6,4},{1,3},{3,1},{5,7},{7,5},{8,10},{10,8},{12,... | collective-permute-start | bytes 589832 | tf_op jit(solution)/shard_map/ppermute | solution.py:508
  111.8 10.1 %collective-permute-start.4 = (bf16[192,512]{1,0:T(8,128)(2,1)S(1)}, bf16[192,512]{1,0:T(8,128)(2,1)S(1)}, u32[]{:S(2)}, u32[]{:S(2)}) collective-permute-start(bf16[192,512]{1,0:T(8,128)(2,1)S(1)} %get-tuple-element.41), channel_id=1, source_target_pairs={{0,6},{2,4},{4,2},{6,0},{1,7},{3,5},{5,3},{7,1},{8,14},{10,12},{12... | collective-permute-start | bytes 589832 | tf_op jit(solution)/shard_map/ppermute | solution.py:508
  117.9 13.7 %all-to-all-start.5 = ((bf16[16,40,512]{2,1,0:T(8,128)(2,1)}), bf16[16,40,512]{2,1,0:T(8,128)(2,1)S(1)}, u32[]{:S(2)}, u32[]{:S(2)}) async-start(bf16[16,40,512]{2,1,0:T(8,128)(2,1)} %spread_weights.1), calls=%async_computation.5 | async-start | bytes 1310720 | tf_op jit(solution)/shard_map/all_to_all | solution.py:424
  132.3 8.0 %collective-permute-start.5 = (bf16[608,512]{1,0:T(8,128)(2,1)S(1)}, bf16[608,512]{1,0:T(8,128)(2,1)S(1)}, u32[]{:S(2)}, u32[]{:S(2)}) collective-permute-start(bf16[608,512]{1,0:T(8,128)(2,1)S(1)} %get-tuple-element.43.near_ref), channel_id=1, source_target_pairs={{0,1},{1,0},{2,3},{3,2},{4,5},{5,4},{6,7},{7,6},{8,9},{9,8},{10,11... | collective-permute-start | bytes 1867784 | tf_op jit(solution)/shard_map/ppermute | solution.py:427

commit v12 on v11

--- a/solution.py
+++ b/solution.py
@@ -118,7 +118,16 @@
 
 
 def send_kernel(rep_ref, lists_hbm, feats_hbm, send_ref, lists_ref, feats_ref, sems):
-    lists_copy, feats_copy = fetch((lists_hbm, feats_hbm), (lists_ref, feats_ref), sems)
+    lists_copy = pltpu.make_async_copy(lists_hbm, lists_ref, sems.at[0])
+    lists_copy.start()
+    count = sems.shape[0] - 1
+    piece = feats_ref.shape[0] // count
+    feats_copies = []
+    for at in range(count):
+        rows = pl.ds(at * piece, piece)
+        copy = pltpu.make_async_copy(feats_hbm.at[rows], feats_ref.at[rows], sems.at[1 + at])
+        copy.start()
+        feats_copies.append(copy)
     slots, parts = lists_ref.shape
     depth = parts // Y_SIZE
     rep = rep_ref[0]
@@ -136,7 +145,8 @@
     wanted = jnp.sum(jnp.where(iota(shape, 1) == rep, wanted, 0.0), axis=1, keepdims=True)
     places = iota((2 * parts, feats_ref.shape[0]), 1) == wanted.astype(jnp.int32)
     places = places.astype(BF16)
-    feats_copy.wait()
+    for copy in feats_copies:
+        copy.wait()
     rows = dot(places, feats_ref[...]).astype(BF16)
     lines = send_ref.shape[0] // depth
     shape = (depth * lines, 2 * parts)
@@ -369,25 +379,47 @@
     send_ref[...] = total[share:].astype(BF16)
 
 
-def join_kernel(arrived_ref, rows_ref, send_ref, bias_ref):
+def join_kernel(arrived_ref, rows_ref, send_ref):
+    chunks, _, width = arrived_ref.shape
+    weight = width // chunks
+    for chunk in range(chunks):
+        send_ref[chunk * weight : (chunk + 1) * weight] = arrived_ref[chunk, :weight]
+    send_ref[width:] = rows_ref[...]
+
+
+def bias_kernel(arrived_ref, bias_ref):
     chunks, _, width = arrived_ref.shape
     weight = width // chunks
     bias = jnp.zeros(bias_ref.shape, F32)
     for chunk in range(chunks):
         arrived = arrived_ref[chunk].astype(F32)
-        send_ref[chunk * weight : (chunk + 1) * weight] = arrived[:weight].astype(BF16)
         bias = bias + jnp.sum(arrived[weight:], 0, keepdims=True)
-    send_ref[width:] = rows_ref[...]
     bias_ref[...] = bias
 
 
-def finish_kernel(core_ref, near_ref, own_ref, far_ref, first_ref, second_ref, rows_ref):
-    width = first_ref.shape[0]
-    near, far = near_ref[:width], far_ref[:width]
-    is_first = core_ref[0] == 0
-    first_ref[...] = jnp.where(is_first, near, far)
-    second_ref[...] = jnp.where(is_first, far, near)
+def finish_kernel(core_ref, near_ref, own_ref, far_ref, rows_ref, first_hbm, second_hbm, sems):
+    width = first_hbm.shape[0]
+    weights = pl.ds(0, width)
+
+    def copies(near_to, far_to):
+        return (
+            pltpu.make_async_copy(near_ref.at[weights], near_to, sems.at[0]),
+            pltpu.make_async_copy(far_ref.at[weights], far_to, sems.at[1]),
+        )
+
+    @pl.when(core_ref[0] == 0)
+    def _():
+        for copy in copies(first_hbm, second_hbm):
+            copy.start()
+
+    @pl.when(core_ref[0] != 0)
+    def _():
+        for copy in copies(second_hbm, first_hbm):
+            copy.start()
+
     rows_ref[...] = own_ref[...] + far_ref[width:].astype(F32)
+    for copy in copies(first_hbm, second_hbm):
+        copy.wait()
 
 
 def body(
@@ -429,7 +461,8 @@
     lines = -(-(Y_SIZE + 1) * (width // LANES) // 8) * 8
     (send,) = call(
         send_kernel, "pick_boundary", [((depth * lines, LANES), BF16)], [rep], [],
-        hbm=[lists, feats], scratch=fetched([lists, feats]), flops=4 * parts * rows * width,
+        hbm=[lists, feats], flops=4 * parts * rows * width,
+        scratch=fetched([lists, feats])[:2] + [pltpu.SemaphoreType.DMA((1 + 4,))],
     )
     by_depth = swap(send.reshape(depth, lines, LANES), "z").reshape(depth * lines, LANES)
     mats_shape = (2 * (seeds + half) + width, max(seeds, half))
@@ -521,14 +554,17 @@
         [], [weight_rows, plane_bias],
     )
     weight_near = swap(weight_plane, ("y", "x"))
-    last_send, grad_bias = call(
-        join_kernel, "join", [((width + share, width), BF16), ((1, width), F32)],
-        [], [weight_near, row_send],
-    )
-    grad_self, grad_neigh, input_grad = call(
-        finish_kernel, "finish",
-        [((width, width), BF16), ((width, width), BF16), ((share, width), F32)],
+    (last_send,) = call(
+        join_kernel, "join", [((width + share, width), BF16)], [], [weight_near, row_send]
+    )
+    (grad_bias,) = call(
+        bias_kernel, "sum_bias", [((1, width), F32)], [], [weight_near], after=[last_send]
+    )
+    input_grad, grad_self, grad_neigh = call(
+        finish_kernel, "finish", [((share, width), F32)],
         [core], [last_send, row_own, pair(last_send)],
+        hbm_outs=[((width, width), BF16), ((width, width), BF16)],
+        scratch=[pltpu.SemaphoreType.DMA((2,))],
     )
     grad_bias = grad_bias.reshape(width)
     return (out, input_grad, grad_self, grad_neigh, grad_bias)

time: 142 us -> 142 us (level)
    pallas_call x14 -> x15, Pallas kernels: 19.3 us -> 20 us  [call(): pl.pallas_call(kernel, out_shape=shapes, in_specs=[pl.BlockSpec(memory_sp...]
where the time goes in v12:
time: 142 us; the launch traced here: 141 us
  blocking collectives  53.2 us (37%)
  starting transfers between devices  48.4 us (34%)
  Pallas kernels  20 us (14%)
  waiting for transfers between devices  18.2 us (13%)
  between operations  1.56 us (1%)
    all_to_all x3, blocking collectives, swap(): return lax.all_to_all(values, axis, split_axis=0, concat_axis=0, tiled=True)  53.2 us
    all_to_all x3, starting transfers between devices, swap(): return lax.all_to_all(values, axis, split_axis=0, concat_axis=0, tiled=True)  24.9 us
    pallas_call x15, Pallas kernels, call(): pl.pallas_call(kernel, out_shape=shapes, in_specs=[pl.BlockSpec(memory_sp...  20 us
    all_to_all x3, waiting for transfers between devices, swap(): return lax.all_to_all(values, axis, split_axis=0, concat_axis=0, tiled=True)  15.5 us
    ppermute x3, starting transfers between devices, pair(): return lax.ppermute(values, 'core', [(0, 1), (1, 0)])  14.6 us
    ppermute x3, starting transfers between devices, body(): lax.ppermute(row_sends[step - 1], 'x', [(x, x ^ step) for x in range(X_SI...  8.98 us
  transfers between devices with their start and end apart: 9, of which 6 were waited for; matrix products, arithmetic and copies ran while one was open for 0% of the time, Pallas kernels for 8%

profile of v12, /device:TPU:1, one launch (start us, length us, event | category | flops | bytes accessed | tf_op | source)
XLA Modules:
  0.0 141.4 jit_solution(2238861591116495935)
XLA Ops:
  0.6 2.5 %pick_boundary.1 = bf16[384,128]{1,0:T(8,128)(2,1)} custom-call(s32[1]{0:T(128)} %bitcast.1.rep_ref.refs_0_, s32[8,64]{1,0:T(8,128)} %bitcast.13, bf16[768,512]{1,0:T(8,128)(2,1)} %feats_hbm.3), custom_call_target="tpu_custom_call" | custom-call | flops 100663296 | bytes 886784 | tf_op jit(solution)/shard_map/pick_boundary/pallas_call | solution.py:51
  3.1 15.8 %all-to-all-start = ((bf16[16,24,128]{2,1,0:T(8,128)(2,1)}), bf16[16,24,128]{2,1,0:T(8,128)(2,1)S(1)}, u32[]{:S(2)}, u32[]{:S(2)}) async-start(bf16[16,24,128]{2,1,0:T(8,128)(2,1)} %bitcast.4), calls=%async_computation | async-start | bytes 196608 | tf_op jit(solution)/shard_map/all_to_all | solution.py:456
  19.6 7.0 %own_rows.1 = (f32[1024,512]{1,0:T(8,128)S(1)}, bf16[2560,512]{1,0:T(8,128)(2,1)}) custom-call(s32[1]{0:T(128)} %bitcast.core_ref, s32[1]{0:T(128)S(6)} %copy.16.count_ref, s32[1,14]{1,0:T(1,128)} %dst_ref.1, s32[1,14]{1,0:T(1,128)} %src_ref.1, bf16[14,128,128]{2,1,0:T(8,128)(2,1)} %tiles_ref.1, bf16[768,512]{1,0:T(8,128)(2,1)} %feats_hbm.3, ...), custom_call_target="tpu_custom_call" | custom-call | flops 3623878656 | bytes 6490224 | tf_op jit(solution)/shard_map/own_rows/pallas_call | solution.py:51
  26.6 4.2 %all-to-all-done = bf16[16,24,128]{2,1,0:T(8,128)(2,1)S(1)} async-done(((bf16[16,24,128]{2,1,0:T(8,128)(2,1)}), bf16[16,24,128]{2,1,0:T(8,128)(2,1)S(1)}, u32[]{:S(2)}, u32[]{:S(2)}) %all-to-all-start) | async-done | bytes 98336 | tf_op jit(solution)/shard_map/all_to_all | solution.py:456
  30.8 0.3 spread_plane.1
  31.1 15.8 %all_to_all.30 = bf16[16,32,512]{2,1,0:T(8,128)(2,1)S(1)} all-to-all(bf16[16,32,512]{2,1,0:T(8,128)(2,1)S(1)} %spread_plane.1), channel_id=1, replica_groups=mesh['z'=16,'y'=4,'x'=4,'core'=2] {'y','x'}, dimensions={0} | all-to-all | bytes 1048576 | tf_op jit(solution)/shard_map/all_to_all | solution.py:456
  46.9 6.0 %collective-permute-start = (bf16[512,512]{1,0:T(8,128)(2,1)S(1)}, bf16[512,512]{1,0:T(8,128)(2,1)S(1)}, u32[]{:S(2)}, u32[]{:S(2)}) collective-permute-start(bf16[512,512]{1,0:T(8,128)(2,1)S(1)} %bitcast.10), channel_id=1, source_target_pairs={{0,1},{1,0},{2,3},{3,2},{4,5},{5,4},{6,7},{7,6},{8,9},{9,8},{10,11... | collective-permute-start | bytes 1572872 | tf_op jit(solution)/shard_map/ppermute | solution.py:459
  52.9 0.0 copy-done.9
  52.9 1.5 %collective-permute-done.far_ref = bf16[512,512]{1,0:T(8,128)(2,1)S(1)} collective-permute-done((bf16[512,512]{1,0:T(8,128)(2,1)S(1)}, bf16[512,512]{1,0:T(8,128)(2,1)S(1)}, u32[]{:S(2)}, u32[]{:S(2)}) %collective-permute-start) | collective-permute-done | bytes 524320 | tf_op jit(solution)/shard_map/ppermute | solution.py:459
  54.4 0.0 copy-done.1
  54.4 0.0 copy-done.2
  54.4 0.0 copy-done.8
  54.4 0.0 copy-start.4
  54.4 0.0 copy-start.5
  54.4 0.0 copy-start.6
  54.5 0.0 copy-start.7
  54.5 2.7 %forward_backward.1 = (bf16[512,512]{1,0:T(8,128)(2,1)}, bf16[512,512]{1,0:T(8,128)(2,1)S(1)}, bf16[512,512]{1,0:T(8,128)(2,1)S(1)}, bf16[1040,512]{1,0:T(8,128)(2,1)S(1)}, bf16[1040,512]{1,0:T(8,128)(2,1)S(1)}) custom-call(s32[1]{0:T(128)} %bitcast.core_ref, bf16[512,512]{1,0:T(8,128)(2,1)S(1)} %bitcast.11, ...), custom_call_target="tpu_custom_call" | custom-call | flops 2147483648 | bytes 10519552 | tf_op jit(solution)/shard_map/forward_backward/pallas_call | solution.py:51
  57.2 2.3 %collective-permute-start.1 = (bf16[1040,512]{1,0:T(8,128)(2,1)S(1)}, bf16[1040,512]{1,0:T(8,128)(2,1)S(1)}, u32[]{:S(2)}, u32[]{:S(2)}) collective-permute-start(bf16[1040,512]{1,0:T(8,128)(2,1)S(1)} %get-tuple-element.29), channel_id=1, source_target_pairs={{0,1},{1,0},{2,3},{3,2},{4,5},{5,4},{6,7},{7,6},{8,9},{9,8},{10,11... | collective-permute-start | bytes 3194888 | tf_op jit(solution)/shard_map/ppermute | solution.py:459
  59.5 0.0 copy-done.3
  59.5 0.0 copy-done.4
  59.5 0.0 copy-done.5
  59.6 2.1 %own_rows_back.1.refs_2_.refs_3_ = f32[768,512]{1,0:T(8,128)S(1)} custom-call(s32[1,14]{1,0:T(1,128)S(1)} %copy-done.6, s32[1,14]{1,0:T(1,128)S(1)} %copy-done.7, s32[1]{0:T(128)S(6)} %copy.16.count_ref, bf16[14,128,128]{2,1,0:T(8,128)(2,1)S(1)} %copy-done.4, s32[1,512]{1,0:T(1,128)S(1)} %bitcast.16, bf16[512,512]{1,0:T(8,128)(2,1)S(1)} %get-tuple-element.30.d_pre_ref, ...), custom_call_target="tpu_custom_call" | custom-call | flops 1207959552 | bytes 3606528 | tf_op jit(solution)/shard_map/own_rows_back/pallas_call | solution.py:51
  61.6 0.2 collective-permute-done.1.refs_1_
  61.8 0.2 sum_pair.1
  62.1 0.0 copy-start
  62.1 19.0 %all_to_all.31.arrived_ref = bf16[16,64,512]{2,1,0:T(8,128)(2,1)S(1)} all-to-all(bf16[16,64,512]{2,1,0:T(8,128)(2,1)S(1)} %get-tuple-element.32), channel_id=1, replica_groups=mesh['z'=16,'y'=4,'x'=4,'core'=2] {'y','x'}, dimensions={0} | all-to-all | bytes 2097152 | tf_op jit(solution)/shard_map/all_to_all | solution.py:456
  81.1 0.3 sum_plane.1
  81.4 18.3 %all_to_all.32.arrived_ref.refs_2_ = bf16[16,8,512]{2,1,0:T(8,128)(2,1)S(1)} all-to-all(bf16[16,8,512]{2,1,0:T(8,128)(2,1)S(1)} %sum_plane.1), channel_id=1, replica_groups=mesh['z'=16,'y'=4,'x'=4,'core'=2] {'z'}, dimensions={0} | all-to-all | bytes 262144 | tf_op jit(solution)/shard_map/all_to_all | solution.py:456
  99.7 0.6 sum_weights.1
  100.4 5.1 %all-to-all-start.4 = ((bf16[16,8,128]{2,1,0:T(8,128)(2,1)}), bf16[16,8,128]{2,1,0:T(8,128)(2,1)S(1)}, u32[]{:S(2)}, u32[]{:S(2)}) async-start(bf16[16,8,128]{2,1,0:T(8,128)(2,1)} %get-tuple-element.34.refs_4_), calls=%async_computation.4 | async-start | bytes 65536 | tf_op jit(solution)/shard_map/all_to_all | solution.py:456
  105.5 0.0 copy-done
  105.5 0.7 return_rows.1
  106.2 3.8 %collective-permute-start.2 = (bf16[192,512]{1,0:T(8,128)(2,1)S(1)}, bf16[192,512]{1,0:T(8,128)(2,1)S(1)}, u32[]{:S(2)}, u32[]{:S(2)}) collective-permute-start(bf16[192,512]{1,0:T(8,128)(2,1)S(1)} %get-tuple-element.37), channel_id=1, source_target_pairs={{0,4},{2,6},{4,0},{6,2},{1,5},{3,7},{5,1},{7,3},{8,12},{10,14},{12... | collective-permute-start | bytes 589832 | tf_op jit(solution)/shard_map/ppermute | solution.py:541
  110.0 1.9 %collective-permute-start.3 = (bf16[192,512]{1,0:T(8,128)(2,1)S(1)}, bf16[192,512]{1,0:T(8,128)(2,1)S(1)}, u32[]{:S(2)}, u32[]{:S(2)}) collective-permute-start(bf16[192,512]{1,0:T(8,128)(2,1)S(1)} %get-tuple-element.38), channel_id=1, source_target_pairs={{0,2},{2,0},{4,6},{6,4},{1,3},{3,1},{5,7},{7,5},{8,10},{10,8},{12,... | collective-permute-start | bytes 589832 | tf_op jit(solution)/shard_map/ppermute | solution.py:541
  111.9 3.3 %collective-permute-start.4 = (bf16[192,512]{1,0:T(8,128)(2,1)S(1)}, bf16[192,512]{1,0:T(8,128)(2,1)S(1)}, u32[]{:S(2)}, u32[]{:S(2)}) collective-permute-start(bf16[192,512]{1,0:T(8,128)(2,1)S(1)} %get-tuple-element.39), channel_id=1, source_target_pairs={{0,6},{2,4},{4,2},{6,0},{1,7},{3,5},{5,3},{7,1},{8,14},{10,12},{12... | collective-permute-start | bytes 589832 | tf_op jit(solution)/shard_map/ppermute | solution.py:541
  115.2 1.8 %all-to-all-done.4.refs_0_ = bf16[16,8,128]{2,1,0:T(8,128)(2,1)S(1)} async-done(((bf16[16,8,128]{2,1,0:T(8,128)(2,1)}), bf16[16,8,128]{2,1,0:T(8,128)(2,1)S(1)}, u32[]{:S(2)}, u32[]{:S(2)}) %all-to-all-start.4) | async-done | bytes 32800 | tf_op jit(solution)/shard_map/all_to_all | solution.py:456
  117.0 0.1 gather_weights.1.whole_ref
  117.1 0.9 spread_weights.1
  118.0 4.0 %all-to-all-start.5 = ((bf16[16,40,512]{2,1,0:T(8,128)(2,1)}), bf16[16,40,512]{2,1,0:T(8,128)(2,1)S(1)}, u32[]{:S(2)}, u32[]{:S(2)}) async-start(bf16[16,40,512]{2,1,0:T(8,128)(2,1)} %spread_weights.1), calls=%async_computation.5 | async-start | bytes 1310720 | tf_op jit(solution)/shard_map/all_to_all | solution.py:456
  122.0 0.0 collective-permute-done.2.refs_0_
  122.0 0.0 collective-permute-done.3.refs_1_
  122.1 0.0 collective-permute-done.4.refs_2_
  122.1 0.1 sum_rows.1
  122.2 9.6 %all-to-all-done.5.arrived_ref.refs_0_ = bf16[16,40,512]{2,1,0:T(8,128)(2,1)S(1)} async-done(((bf16[16,40,512]{2,1,0:T(8,128)(2,1)}), bf16[16,40,512]{2,1,0:T(8,128)(2,1)S(1)}, u32[]{:S(2)}, u32[]{:S(2)}) %all-to-all-start.5) | async-done | bytes 655392 | tf_op jit(solution)/shard_map/all_to_all | solution.py:456
  131.8 6.3 %collective-permute-start.5 = (bf16[608,512]{1,0:T(8,128)(2,1)S(1)}, bf16[608,512]{1,0:T(8,128)(2,1)S(1)}, u32[]{:S(2)}, u32[]{:S(2)}) collective-permute-start(bf16[608,512]{1,0:T(8,128)(2,1)S(1)} %join.1.near_ref.refs_1_), channel_id=1, source_target_pairs={{0,1},{1,0},{2,3},{3,2},{4,5},{5,4},{6,7},{7,6},{8,9},{9,8},{10,11... | collective-permute-start | bytes 1867784 | tf_op jit(solution)/shard_map/ppermute | solution.py:459
  138.1 0.7 sum_bias.1
  138.7 1.0 collective-permute-done.5.far_ref
  139.7 1.7 %finish.1 = (f32[96,512]{1,0:T(8,128)}, bf16[512,512]{1,0:T(8,128)(2,1)}, bf16[512,512]{1,0:T(8,128)(2,1)}) custom-call(s32[1]{0:T(128)} %bitcast.core_ref, bf16[608,512]{1,0:T(8,128)(2,1)S(1)} %join.1.near_ref.refs_1_, f32[96,512]{1,0:T(8,128)S(1)} %get-tuple-element.41.own_ref, bf16[608,512]{1,0:T(8,128)(2,1)S(1)} %collective-permute-done.5.far_ref), custom_call_target="tpu_custom_call" | custom-call | bytes 2686976 | tf_op jit(solution)/shard_map/finish/pallas_call | solution.py:51
  (9 shorter events, 0.1 us)
Async XLA Ops:
  3.1 27.6 %all-to-all-start = ((bf16[16,24,128]{2,1,0:T(8,128)(2,1)}), bf16[16,24,128]{2,1,0:T(8,128)(2,1)S(1)}, u32[]{:S(2)}, u32[]{:S(2)}) async-start(bf16[16,24,128]{2,1,0:T(8,128)(2,1)} %bitcast.4), calls=%async_computation | async-start | bytes 196608 | tf_op jit(solution)/shard_map/all_to_all | solution.py:456
  30.8 22.1 %copy-start.9 = (bf16[512]{0:T(512)(128)(2,1)S(1)}, bf16[512]{0:T(512)(128)(2,1)}, u32[]{:S(2)}) copy-start(bf16[512]{0:T(512)(128)(2,1)} %param.20) | copy-start | bytes 3076
  30.8 23.6 %copy-start.1 = (bf16[512,512]{1,0:T(8,128)(2,1)S(1)}, bf16[512,512]{1,0:T(8,128)(2,1)}, u32[]{:S(2)}) copy-start(bf16[512,512]{1,0:T(8,128)(2,1)} %w_neigh_ref.1) | copy-start | bytes 1572868
  30.8 23.6 %copy-start.2 = (bf16[512,512]{1,0:T(8,128)(2,1)S(1)}, bf16[512,512]{1,0:T(8,128)(2,1)}, u32[]{:S(2)}) copy-start(bf16[512,512]{1,0:T(8,128)(2,1)} %cot_ref.1) | copy-start | bytes 1572868
  30.8 23.6 %copy-start.8 = (bf16[2560,512]{1,0:T(8,128)(2,1)S(1)}, bf16[2560,512]{1,0:T(8,128)(2,1)}, u32[]{:S(2)}) copy-start(bf16[2560,512]{1,0:T(8,128)(2,1)} %get-tuple-element.26.mats_ref) | copy-start | bytes 7864324
  46.9 7.5 %collective-permute-start = (bf16[512,512]{1,0:T(8,128)(2,1)S(1)}, bf16[512,512]{1,0:T(8,128)(2,1)S(1)}, u32[]{:S(2)}, u32[]{:S(2)}) collective-permute-start(bf16[512,512]{1,0:T(8,128)(2,1)S(1)} %bitcast.10), channel_id=1, source_target_pairs={{0,1},{1,0},{2,3},{3,2},{4,5},{5,4},{6,7},{7,6},{8,9},{9,8},{10,11... | collective-permute-start | bytes 1572872 | tf_op jit(solution)/shard_map/ppermute | solution.py:459
  54.4 5.1 %copy-start.3 = (bf16[512,512]{1,0:T(8,128)(2,1)S(1)}, bf16[512,512]{1,0:T(8,128)(2,1)}, u32[]{:S(2)}) copy-start(bf16[512,512]{1,0:T(8,128)(2,1)} %w_self_ref.1) | copy-start | bytes 1572868
  54.4 5.1 %copy-start.4 = (bf16[14,128,128]{2,1,0:T(8,128)(2,1)S(1)}, bf16[14,128,128]{2,1,0:T(8,128)(2,1)}, u32[]{:S(2)}) copy-start(bf16[14,128,128]{2,1,0:T(8,128)(2,1)} %tiles_ref.1) | copy-start | bytes 1376260
  54.4 5.1 %copy-start.5 = (s32[512]{0:T(512)S(1)}, s32[512]{0:T(512)}, u32[]{:S(2)}) copy-start(s32[512]{0:T(512)} %param.13) | copy-start | bytes 6148
  54.4 5.1 %copy-start.6 = (s32[1,14]{1,0:T(1,128)S(1)}, s32[1,14]{1,0:T(1,128)}, u32[]{:S(2)}) copy-start(s32[1,14]{1,0:T(1,128)} %dst_ref.1) | copy-start | bytes 172
  54.5 5.1 %copy-start.7 = (s32[1,14]{1,0:T(1,128)S(1)}, s32[1,14]{1,0:T(1,128)}, u32[]{:S(2)}) copy-start(s32[1,14]{1,0:T(1,128)} %src_ref.1) | copy-start | bytes 172
  57.2 4.6 %collective-permute-start.1 = (bf16[1040,512]{1,0:T(8,128)(2,1)S(1)}, bf16[1040,512]{1,0:T(8,128)(2,1)S(1)}, u32[]{:S(2)}, u32[]{:S(2)}) collective-permute-start(bf16[1040,512]{1,0:T(8,128)(2,1)S(1)} %get-tuple-element.29), channel_id=1, source_target_pairs={{0,1},{1,0},{2,3},{3,2},{4,5},{5,4},{6,7},{7,6},{8,9},{9,8},{10,11... | collective-permute-start | bytes 3194888 | tf_op jit(solution)/shard_map/ppermute | solution.py:459
  62.1 43.4 %copy-start = (s32[1,64,8]{1,2,0:T(8,128)S(1)}, s32[1,64,8]{1,2,0:T(8,128)}, u32[]{:S(2)}) copy-start(s32[1,64,8]{1,2,0:T(8,128)} %param.12) | copy-start | bytes 6148
  100.4 16.6 %all-to-all-start.4 = ((bf16[16,8,128]{2,1,0:T(8,128)(2,1)}), bf16[16,8,128]{2,1,0:T(8,128)(2,1)S(1)}, u32[]{:S(2)}, u32[]{:S(2)}) async-start(bf16[16,8,128]{2,1,0:T(8,128)(2,1)} %get-tuple-element.34.refs_4_), calls=%async_computation.4 | async-start | bytes 65536 | tf_op jit(solution)/shard_map/all_to_all | solution.py:456
  106.2 15.9 %collective-permute-start.2 = (bf16[192,512]{1,0:T(8,128)(2,1)S(1)}, bf16[192,512]{1,0:T(8,128)(2,1)S(1)}, u32[]{:S(2)}, u32[]{:S(2)}) collective-permute-start(bf16[192,512]{1,0:T(8,128)(2,1)S(1)} %get-tuple-element.37), channel_id=1, source_target_pairs={{0,4},{2,6},{4,0},{6,2},{1,5},{3,7},{5,1},{7,3},{8,12},{10,14},{12... | collective-permute-start | bytes 589832 | tf_op jit(solution)/shard_map/ppermute | solution.py:541
  110.0 12.1 %collective-permute-start.3 = (bf16[192,512]{1,0:T(8,128)(2,1)S(1)}, bf16[192,512]{1,0:T(8,128)(2,1)S(1)}, u32[]{:S(2)}, u32[]{:S(2)}) collective-permute-start(bf16[192,512]{1,0:T(8,128)(2,1)S(1)} %get-tuple-element.38), channel_id=1, source_target_pairs={{0,2},{2,0},{4,6},{6,4},{1,3},{3,1},{5,7},{7,5},{8,10},{10,8},{12,... | collective-permute-start | bytes 589832 | tf_op jit(solution)/shard_map/ppermute | solution.py:541
  111.9 10.2 %collective-permute-start.4 = (bf16[192,512]{1,0:T(8,128)(2,1)S(1)}, bf16[192,512]{1,0:T(8,128)(2,1)S(1)}, u32[]{:S(2)}, u32[]{:S(2)}) collective-permute-start(bf16[192,512]{1,0:T(8,128)(2,1)S(1)} %get-tuple-element.39), channel_id=1, source_target_pairs={{0,6},{2,4},{4,2},{6,0},{1,7},{3,5},{5,3},{7,1},{8,14},{10,12},{12... | collective-permute-start | bytes 589832 | tf_op jit(solution)/shard_map/ppermute | solution.py:541
  118.0 13.7 %all-to-all-start.5 = ((bf16[16,40,512]{2,1,0:T(8,128)(2,1)}), bf16[16,40,512]{2,1,0:T(8,128)(2,1)S(1)}, u32[]{:S(2)}, u32[]{:S(2)}) async-start(bf16[16,40,512]{2,1,0:T(8,128)(2,1)} %spread_weights.1), calls=%async_computation.5 | async-start | bytes 1310720 | tf_op jit(solution)/shard_map/all_to_all | solution.py:456
  131.8 8.0 %collective-permute-start.5 = (bf16[608,512]{1,0:T(8,128)(2,1)S(1)}, bf16[608,512]{1,0:T(8,128)(2,1)S(1)}, u32[]{:S(2)}, u32[]{:S(2)}) collective-permute-start(bf16[608,512]{1,0:T(8,128)(2,1)S(1)} %join.1.near_ref.refs_1_), channel_id=1, source_target_pairs={{0,1},{1,0},{2,3},{3,2},{4,5},{5,4},{6,7},{7,6},{8,9},{9,8},{10,11... | collective-permute-start | bytes 1867784 | tf_op jit(solution)/shard_map/ppermute | solution.py:459

commit v13 on v11

--- a/solution.py
+++ b/solution.py
@@ -369,15 +369,21 @@
     send_ref[...] = total[share:].astype(BF16)
 
 
-def join_kernel(arrived_ref, rows_ref, send_ref, bias_ref):
+def join_kernel(arrived_ref, rows_ref, send_ref):
+    chunks, _, width = arrived_ref.shape
+    weight = width // chunks
+    for chunk in range(chunks):
+        send_ref[chunk * weight : (chunk + 1) * weight] = arrived_ref[chunk, :weight]
+    send_ref[width:] = rows_ref[...]
+
+
+def bias_kernel(arrived_ref, bias_ref):
     chunks, _, width = arrived_ref.shape
     weight = width // chunks
     bias = jnp.zeros(bias_ref.shape, F32)
     for chunk in range(chunks):
         arrived = arrived_ref[chunk].astype(F32)
-        send_ref[chunk * weight : (chunk + 1) * weight] = arrived[:weight].astype(BF16)
         bias = bias + jnp.sum(arrived[weight:], 0, keepdims=True)
-    send_ref[width:] = rows_ref[...]
     bias_ref[...] = bias
 
 
@@ -521,9 +527,11 @@
         [], [weight_rows, plane_bias],
     )
     weight_near = swap(weight_plane, ("y", "x"))
-    last_send, grad_bias = call(
-        join_kernel, "join", [((width + share, width), BF16), ((1, width), F32)],
-        [], [weight_near, row_send],
+    (last_send,) = call(
+        join_kernel, "join", [((width + share, width), BF16)], [], [weight_near, row_send]
+    )
+    (grad_bias,) = call(
+        bias_kernel, "sum_bias", [((1, width), F32)], [], [weight_near], after=[last_send]
     )
     grad_self, grad_neigh, input_grad = call(
         finish_kernel, "finish",

time: 142 us -> 141 us (level)
    pallas_call x14 -> x15, Pallas kernels: 19.3 us -> 19.2 us  [call(): pl.pallas_call(kernel, out_shape=shapes, in_specs=[pl.BlockSpec(memory_sp...]
where the time goes in v13:
time: 141 us
  blocking collectives  53.3 us (38%)
  starting transfers between devices  48.4 us (34%)
  Pallas kernels  19.2 us (14%)
  waiting for transfers between devices  18.3 us (13%)
  between operations  1.56 us (1%)
    all_to_all x3, blocking collectives, swap(): return lax.all_to_all(values, axis, split_axis=0, concat_axis=0, tiled=True)  53.3 us
    all_to_all x3, starting transfers between devices, swap(): return lax.all_to_all(values, axis, split_axis=0, concat_axis=0, tiled=True)  24.9 us
    pallas_call x15, Pallas kernels, call(): pl.pallas_call(kernel, out_shape=shapes, in_specs=[pl.BlockSpec(memory_sp...  19.2 us
    all_to_all x3, waiting for transfers between devices, swap(): return lax.all_to_all(values, axis, split_axis=0, concat_axis=0, tiled=True)  15.6 us
    ppermute x3, starting transfers between devices, pair(): return lax.ppermute(values, 'core', [(0, 1), (1, 0)])  14.6 us
    ppermute x3, starting transfers between devices, body(): lax.ppermute(row_sends[step - 1], 'x', [(x, x ^ step) for x in range(X_SI...  8.98 us
  transfers between devices with their start and end apart: 9, of which 6 were waited for; matrix products, arithmetic and copies ran while one was open for 0% of the time, Pallas kernels for 8%

profile of v13, /device:TPU:1, one launch (start us, length us, event | category | flops | bytes accessed | tf_op | source)
XLA Modules:
  0.0 140.8 jit_solution(7499216727027572340)
XLA Ops:
  0.6 2.4 %pick_boundary.1 = bf16[384,128]{1,0:T(8,128)(2,1)} custom-call(s32[1]{0:T(128)} %bitcast.1.rep_ref.refs_0_, s32[8,64]{1,0:T(8,128)} %bitcast.13, bf16[768,512]{1,0:T(8,128)(2,1)} %feats_hbm.3), custom_call_target="tpu_custom_call" | custom-call | flops 100663296 | bytes 886784 | tf_op jit(solution)/shard_map/pick_boundary/pallas_call | solution.py:51
  3.0 15.8 %all-to-all-start = ((bf16[16,24,128]{2,1,0:T(8,128)(2,1)}), bf16[16,24,128]{2,1,0:T(8,128)(2,1)S(1)}, u32[]{:S(2)}, u32[]{:S(2)}) async-start(bf16[16,24,128]{2,1,0:T(8,128)(2,1)} %bitcast.4), calls=%async_computation | async-start | bytes 196608 | tf_op jit(solution)/shard_map/all_to_all | solution.py:430
  19.5 7.0 %own_rows.1 = (f32[1024,512]{1,0:T(8,128)S(1)}, bf16[2560,512]{1,0:T(8,128)(2,1)}) custom-call(s32[1]{0:T(128)} %bitcast.core_ref, s32[1]{0:T(128)S(6)} %copy.16.count_ref, s32[1,14]{1,0:T(1,128)} %dst_ref.1, s32[1,14]{1,0:T(1,128)} %src_ref.1, bf16[14,128,128]{2,1,0:T(8,128)(2,1)} %tiles_ref.1, bf16[768,512]{1,0:T(8,128)(2,1)} %feats_hbm.3, ...), custom_call_target="tpu_custom_call" | custom-call | flops 3623878656 | bytes 6490224 | tf_op jit(solution)/shard_map/own_rows/pallas_call | solution.py:51
  26.5 4.2 %all-to-all-done = bf16[16,24,128]{2,1,0:T(8,128)(2,1)S(1)} async-done(((bf16[16,24,128]{2,1,0:T(8,128)(2,1)}), bf16[16,24,128]{2,1,0:T(8,128)(2,1)S(1)}, u32[]{:S(2)}, u32[]{:S(2)}) %all-to-all-start) | async-done | bytes 98336 | tf_op jit(solution)/shard_map/all_to_all | solution.py:430
  30.7 0.3 spread_plane.1
  31.0 15.8 %all_to_all.30 = bf16[16,32,512]{2,1,0:T(8,128)(2,1)S(1)} all-to-all(bf16[16,32,512]{2,1,0:T(8,128)(2,1)S(1)} %spread_plane.1), channel_id=1, replica_groups=mesh['z'=16,'y'=4,'x'=4,'core'=2] {'y','x'}, dimensions={0} | all-to-all | bytes 1048576 | tf_op jit(solution)/shard_map/all_to_all | solution.py:430
  46.8 6.0 %collective-permute-start = (bf16[512,512]{1,0:T(8,128)(2,1)S(1)}, bf16[512,512]{1,0:T(8,128)(2,1)S(1)}, u32[]{:S(2)}, u32[]{:S(2)}) collective-permute-start(bf16[512,512]{1,0:T(8,128)(2,1)S(1)} %bitcast.10), channel_id=1, source_target_pairs={{0,1},{1,0},{2,3},{3,2},{4,5},{5,4},{6,7},{7,6},{8,9},{9,8},{10,11... | collective-permute-start | bytes 1572872 | tf_op jit(solution)/shard_map/ppermute | solution.py:433
  52.8 0.0 copy-done.9
  52.8 1.5 %collective-permute-done.far_ref = bf16[512,512]{1,0:T(8,128)(2,1)S(1)} collective-permute-done((bf16[512,512]{1,0:T(8,128)(2,1)S(1)}, bf16[512,512]{1,0:T(8,128)(2,1)S(1)}, u32[]{:S(2)}, u32[]{:S(2)}) %collective-permute-start) | collective-permute-done | bytes 524320 | tf_op jit(solution)/shard_map/ppermute | solution.py:433
  54.3 0.0 copy-done.1
  54.3 0.0 copy-done.2
  54.3 0.0 copy-start.4
  54.3 0.0 copy-start.5
  54.3 0.0 copy-start.6
  54.4 0.0 copy-start.7
  54.4 2.7 %forward_backward.1 = (bf16[512,512]{1,0:T(8,128)(2,1)}, bf16[512,512]{1,0:T(8,128)(2,1)S(1)}, bf16[512,512]{1,0:T(8,128)(2,1)S(1)}, bf16[1040,512]{1,0:T(8,128)(2,1)S(1)}, bf16[1040,512]{1,0:T(8,128)(2,1)S(1)}) custom-call(s32[1]{0:T(128)} %bitcast.core_ref, bf16[512,512]{1,0:T(8,128)(2,1)S(1)} %bitcast.11, ...), custom_call_target="tpu_custom_call" | custom-call | flops 2147483648 | bytes 10519552 | tf_op jit(solution)/shard_map/forward_backward/pallas_call | solution.py:51
  57.1 2.3 %collective-permute-start.1 = (bf16[1040,512]{1,0:T(8,128)(2,1)S(1)}, bf16[1040,512]{1,0:T(8,128)(2,1)S(1)}, u32[]{:S(2)}, u32[]{:S(2)}) collective-permute-start(bf16[1040,512]{1,0:T(8,128)(2,1)S(1)} %get-tuple-element.29), channel_id=1, source_target_pairs={{0,1},{1,0},{2,3},{3,2},{4,5},{5,4},{6,7},{7,6},{8,9},{9,8},{10,11... | collective-permute-start | bytes 3194888 | tf_op jit(solution)/shard_map/ppermute | solution.py:433
  59.4 0.0 copy-done.3
  59.4 0.0 copy-done.4
  59.4 0.0 copy-done.5
  59.4 0.0 copy-done.6
  59.5 0.0 copy-done.7
  59.5 2.0 %own_rows_back.1.refs_2_.refs_3_ = f32[768,512]{1,0:T(8,128)S(1)} custom-call(s32[1,14]{1,0:T(1,128)S(1)} %copy-done.6, s32[1,14]{1,0:T(1,128)S(1)} %copy-done.7, s32[1]{0:T(128)S(6)} %copy.16.count_ref, bf16[14,128,128]{2,1,0:T(8,128)(2,1)S(1)} %copy-done.4, s32[1,512]{1,0:T(1,128)S(1)} %bitcast.16, bf16[512,512]{1,0:T(8,128)(2,1)S(1)} %get-tuple-element.30.d_pre_ref, ...), custom_call_target="tpu_custom_call" | custom-call | flops 1207959552 | bytes 3606528 | tf_op jit(solution)/shard_map/own_rows_back/pallas_call | solution.py:51
  61.5 0.2 collective-permute-done.1.refs_1_
  61.7 0.2 sum_pair.1
  62.0 0.0 copy-start
  62.0 19.0 %all_to_all.31.arrived_ref = bf16[16,64,512]{2,1,0:T(8,128)(2,1)S(1)} all-to-all(bf16[16,64,512]{2,1,0:T(8,128)(2,1)S(1)} %get-tuple-element.32), channel_id=1, replica_groups=mesh['z'=16,'y'=4,'x'=4,'core'=2] {'y','x'}, dimensions={0} | all-to-all | bytes 2097152 | tf_op jit(solution)/shard_map/all_to_all | solution.py:430
  81.0 0.3 sum_plane.1
  81.3 18.4 %all_to_all.32.arrived_ref.refs_2_ = bf16[16,8,512]{2,1,0:T(8,128)(2,1)S(1)} all-to-all(bf16[16,8,512]{2,1,0:T(8,128)(2,1)S(1)} %sum_plane.1), channel_id=1, replica_groups=mesh['z'=16,'y'=4,'x'=4,'core'=2] {'z'}, dimensions={0} | all-to-all | bytes 262144 | tf_op jit(solution)/shard_map/all_to_all | solution.py:430
  99.7 0.6 sum_weights.1
  100.4 5.1 %all-to-all-start.4 = ((bf16[16,8,128]{2,1,0:T(8,128)(2,1)}), bf16[16,8,128]{2,1,0:T(8,128)(2,1)S(1)}, u32[]{:S(2)}, u32[]{:S(2)}) async-start(bf16[16,8,128]{2,1,0:T(8,128)(2,1)} %get-tuple-element.34.refs_4_), calls=%async_computation.4 | async-start | bytes 65536 | tf_op jit(solution)/shard_map/all_to_all | solution.py:430
  105.5 0.6 return_rows.1
  106.1 3.8 %collective-permute-start.2 = (bf16[192,512]{1,0:T(8,128)(2,1)S(1)}, bf16[192,512]{1,0:T(8,128)(2,1)S(1)}, u32[]{:S(2)}, u32[]{:S(2)}) collective-permute-start(bf16[192,512]{1,0:T(8,128)(2,1)S(1)} %get-tuple-element.37), channel_id=1, source_target_pairs={{0,4},{2,6},{4,0},{6,2},{1,5},{3,7},{5,1},{7,3},{8,12},{10,14},{12... | collective-permute-start | bytes 589832 | tf_op jit(solution)/shard_map/ppermute | solution.py:514
  109.9 1.9 %collective-permute-start.3 = (bf16[192,512]{1,0:T(8,128)(2,1)S(1)}, bf16[192,512]{1,0:T(8,128)(2,1)S(1)}, u32[]{:S(2)}, u32[]{:S(2)}) collective-permute-start(bf16[192,512]{1,0:T(8,128)(2,1)S(1)} %get-tuple-element.38), channel_id=1, source_target_pairs={{0,2},{2,0},{4,6},{6,4},{1,3},{3,1},{5,7},{7,5},{8,10},{10,8},{12,... | collective-permute-start | bytes 589832 | tf_op jit(solution)/shard_map/ppermute | solution.py:514
  111.9 3.2 %collective-permute-start.4 = (bf16[192,512]{1,0:T(8,128)(2,1)S(1)}, bf16[192,512]{1,0:T(8,128)(2,1)S(1)}, u32[]{:S(2)}, u32[]{:S(2)}) collective-permute-start(bf16[192,512]{1,0:T(8,128)(2,1)S(1)} %get-tuple-element.39), channel_id=1, source_target_pairs={{0,6},{2,4},{4,2},{6,0},{1,7},{3,5},{5,3},{7,1},{8,14},{10,12},{12... | collective-permute-start | bytes 589832 | tf_op jit(solution)/shard_map/ppermute | solution.py:514
  115.1 1.8 %all-to-all-done.4.refs_0_ = bf16[16,8,128]{2,1,0:T(8,128)(2,1)S(1)} async-done(((bf16[16,8,128]{2,1,0:T(8,128)(2,1)}), bf16[16,8,128]{2,1,0:T(8,128)(2,1)S(1)}, u32[]{:S(2)}, u32[]{:S(2)}) %all-to-all-start.4) | async-done | bytes 32800 | tf_op jit(solution)/shard_map/all_to_all | solution.py:430
  116.9 0.1 gather_weights.1.whole_ref
  117.1 0.9 spread_weights.1
  118.0 4.0 %all-to-all-start.5 = ((bf16[16,40,512]{2,1,0:T(8,128)(2,1)}), bf16[16,40,512]{2,1,0:T(8,128)(2,1)S(1)}, u32[]{:S(2)}, u32[]{:S(2)}) async-start(bf16[16,40,512]{2,1,0:T(8,128)(2,1)} %spread_weights.1), calls=%async_computation.5 | async-start | bytes 1310720 | tf_op jit(solution)/shard_map/all_to_all | solution.py:430
  122.0 0.0 collective-permute-done.2.refs_0_
  122.0 0.0 collective-permute-done.3.refs_1_
  122.0 0.0 collective-permute-done.4.refs_2_
  122.0 0.1 sum_rows.1
  122.1 9.6 %all-to-all-done.5.arrived_ref.refs_0_ = bf16[16,40,512]{2,1,0:T(8,128)(2,1)S(1)} async-done(((bf16[16,40,512]{2,1,0:T(8,128)(2,1)}), bf16[16,40,512]{2,1,0:T(8,128)(2,1)S(1)}, u32[]{:S(2)}, u32[]{:S(2)}) %all-to-all-start.5) | async-done | bytes 655392 | tf_op jit(solution)/shard_map/all_to_all | solution.py:430
  131.7 6.3 %collective-permute-start.5 = (bf16[608,512]{1,0:T(8,128)(2,1)S(1)}, bf16[608,512]{1,0:T(8,128)(2,1)S(1)}, u32[]{:S(2)}, u32[]{:S(2)}) collective-permute-start(bf16[608,512]{1,0:T(8,128)(2,1)S(1)} %join.1.near_ref.refs_1_), channel_id=1, source_target_pairs={{0,1},{1,0},{2,3},{3,2},{4,5},{5,4},{6,7},{7,6},{8,9},{9,8},{10,11... | collective-permute-start | bytes 1867784 | tf_op jit(solution)/shard_map/ppermute | solution.py:433
  138.1 0.7 sum_bias.1
  138.7 1.0 collective-permute-done.5.far_ref
  139.7 1.1 finish.1
  (9 shorter events, 0.1 us)
Async XLA Ops:
  3.0 27.6 %all-to-all-start = ((bf16[16,24,128]{2,1,0:T(8,128)(2,1)}), bf16[16,24,128]{2,1,0:T(8,128)(2,1)S(1)}, u32[]{:S(2)}, u32[]{:S(2)}) async-start(bf16[16,24,128]{2,1,0:T(8,128)(2,1)} %bitcast.4), calls=%async_computation | async-start | bytes 196608 | tf_op jit(solution)/shard_map/all_to_all | solution.py:430
  30.7 22.1 %copy-start.9 = (bf16[512]{0:T(512)(128)(2,1)S(1)}, bf16[512]{0:T(512)(128)(2,1)}, u32[]{:S(2)}) copy-start(bf16[512]{0:T(512)(128)(2,1)} %param.20) | copy-start | bytes 3076
  30.7 23.6 %copy-start.1 = (bf16[512,512]{1,0:T(8,128)(2,1)S(1)}, bf16[512,512]{1,0:T(8,128)(2,1)}, u32[]{:S(2)}) copy-start(bf16[512,512]{1,0:T(8,128)(2,1)} %w_neigh_ref.1) | copy-start | bytes 1572868
  30.7 23.6 %copy-start.2 = (bf16[512,512]{1,0:T(8,128)(2,1)S(1)}, bf16[512,512]{1,0:T(8,128)(2,1)}, u32[]{:S(2)}) copy-start(bf16[512,512]{1,0:T(8,128)(2,1)} %cot_ref.1) | copy-start | bytes 1572868
  30.7 23.6 %copy-start.8 = (bf16[2560,512]{1,0:T(8,128)(2,1)S(1)}, bf16[2560,512]{1,0:T(8,128)(2,1)}, u32[]{:S(2)}) copy-start(bf16[2560,512]{1,0:T(8,128)(2,1)} %get-tuple-element.26.mats_ref) | copy-start | bytes 7864324
  46.8 7.5 %collective-permute-start = (bf16[512,512]{1,0:T(8,128)(2,1)S(1)}, bf16[512,512]{1,0:T(8,128)(2,1)S(1)}, u32[]{:S(2)}, u32[]{:S(2)}) collective-permute-start(bf16[512,512]{1,0:T(8,128)(2,1)S(1)} %bitcast.10), channel_id=1, source_target_pairs={{0,1},{1,0},{2,3},{3,2},{4,5},{5,4},{6,7},{7,6},{8,9},{9,8},{10,11... | collective-permute-start | bytes 1572872 | tf_op jit(solution)/shard_map/ppermute | solution.py:433
  54.3 5.1 %copy-start.3 = (bf16[512,512]{1,0:T(8,128)(2,1)S(1)}, bf16[512,512]{1,0:T(8,128)(2,1)}, u32[]{:S(2)}) copy-start(bf16[512,512]{1,0:T(8,128)(2,1)} %w_self_ref.1) | copy-start | bytes 1572868
  54.3 5.1 %copy-start.4 = (bf16[14,128,128]{2,1,0:T(8,128)(2,1)S(1)}, bf16[14,128,128]{2,1,0:T(8,128)(2,1)}, u32[]{:S(2)}) copy-start(bf16[14,128,128]{2,1,0:T(8,128)(2,1)} %tiles_ref.1) | copy-start | bytes 1376260
  54.3 5.1 %copy-start.5 = (s32[512]{0:T(512)S(1)}, s32[512]{0:T(512)}, u32[]{:S(2)}) copy-start(s32[512]{0:T(512)} %param.13) | copy-start | bytes 6148
  54.3 5.1 %copy-start.6 = (s32[1,14]{1,0:T(1,128)S(1)}, s32[1,14]{1,0:T(1,128)}, u32[]{:S(2)}) copy-start(s32[1,14]{1,0:T(1,128)} %dst_ref.1) | copy-start | bytes 172
  54.4 5.1 %copy-start.7 = (s32[1,14]{1,0:T(1,128)S(1)}, s32[1,14]{1,0:T(1,128)}, u32[]{:S(2)}) copy-start(s32[1,14]{1,0:T(1,128)} %src_ref.1) | copy-start | bytes 172
  57.1 4.6 %collective-permute-start.1 = (bf16[1040,512]{1,0:T(8,128)(2,1)S(1)}, bf16[1040,512]{1,0:T(8,128)(2,1)S(1)}, u32[]{:S(2)}, u32[]{:S(2)}) collective-permute-start(bf16[1040,512]{1,0:T(8,128)(2,1)S(1)} %get-tuple-element.29), channel_id=1, source_target_pairs={{0,1},{1,0},{2,3},{3,2},{4,5},{5,4},{6,7},{7,6},{8,9},{9,8},{10,11... | collective-permute-start | bytes 3194888 | tf_op jit(solution)/shard_map/ppermute | solution.py:433
  62.0 43.5 %copy-start = (s32[1,64,8]{1,2,0:T(8,128)S(1)}, s32[1,64,8]{1,2,0:T(8,128)}, u32[]{:S(2)}) copy-start(s32[1,64,8]{1,2,0:T(8,128)} %param.12) | copy-start | bytes 6148
  100.4 16.6 %all-to-all-start.4 = ((bf16[16,8,128]{2,1,0:T(8,128)(2,1)}), bf16[16,8,128]{2,1,0:T(8,128)(2,1)S(1)}, u32[]{:S(2)}, u32[]{:S(2)}) async-start(bf16[16,8,128]{2,1,0:T(8,128)(2,1)} %get-tuple-element.34.refs_4_), calls=%async_computation.4 | async-start | bytes 65536 | tf_op jit(solution)/shard_map/all_to_all | solution.py:430
  106.1 15.9 %collective-permute-start.2 = (bf16[192,512]{1,0:T(8,128)(2,1)S(1)}, bf16[192,512]{1,0:T(8,128)(2,1)S(1)}, u32[]{:S(2)}, u32[]{:S(2)}) collective-permute-start(bf16[192,512]{1,0:T(8,128)(2,1)S(1)} %get-tuple-element.37), channel_id=1, source_target_pairs={{0,4},{2,6},{4,0},{6,2},{1,5},{3,7},{5,1},{7,3},{8,12},{10,14},{12... | collective-permute-start | bytes 589832 | tf_op jit(solution)/shard_map/ppermute | solution.py:514
  109.9 12.1 %collective-permute-start.3 = (bf16[192,512]{1,0:T(8,128)(2,1)S(1)}, bf16[192,512]{1,0:T(8,128)(2,1)S(1)}, u32[]{:S(2)}, u32[]{:S(2)}) collective-permute-start(bf16[192,512]{1,0:T(8,128)(2,1)S(1)} %get-tuple-element.38), channel_id=1, source_target_pairs={{0,2},{2,0},{4,6},{6,4},{1,3},{3,1},{5,7},{7,5},{8,10},{10,8},{12,... | collective-permute-start | bytes 589832 | tf_op jit(solution)/shard_map/ppermute | solution.py:514
  111.9 10.2 %collective-permute-start.4 = (bf16[192,512]{1,0:T(8,128)(2,1)S(1)}, bf16[192,512]{1,0:T(8,128)(2,1)S(1)}, u32[]{:S(2)}, u32[]{:S(2)}) collective-permute-start(bf16[192,512]{1,0:T(8,128)(2,1)S(1)} %get-tuple-element.39), channel_id=1, source_target_pairs={{0,6},{2,4},{4,2},{6,0},{1,7},{3,5},{5,3},{7,1},{8,14},{10,12},{12... | collective-permute-start | bytes 589832 | tf_op jit(solution)/shard_map/ppermute | solution.py:514
  118.0 13.7 %all-to-all-start.5 = ((bf16[16,40,512]{2,1,0:T(8,128)(2,1)}), bf16[16,40,512]{2,1,0:T(8,128)(2,1)S(1)}, u32[]{:S(2)}, u32[]{:S(2)}) async-start(bf16[16,40,512]{2,1,0:T(8,128)(2,1)} %spread_weights.1), calls=%async_computation.5 | async-start | bytes 1310720 | tf_op jit(solution)/shard_map/all_to_all | solution.py:430
  131.7 8.0 %collective-permute-start.5 = (bf16[608,512]{1,0:T(8,128)(2,1)S(1)}, bf16[608,512]{1,0:T(8,128)(2,1)S(1)}, u32[]{:S(2)}, u32[]{:S(2)}) collective-permute-start(bf16[608,512]{1,0:T(8,128)(2,1)S(1)} %join.1.near_ref.refs_1_), channel_id=1, source_target_pairs={{0,1},{1,0},{2,3},{3,2},{4,5},{5,4},{6,7},{7,6},{8,9},{9,8},{10,11... | collective-permute-start | bytes 1867784 | tf_op jit(solution)/shard_map/ppermute | solution.py:433

commit v14 on v13

--- a/solution.py
+++ b/solution.py
@@ -176,7 +176,7 @@
 def own_kernel(
     core_ref, count_ref, dst_hbm, src_hbm, tiles_hbm, feats_hbm, seeds_hbm, w_self_hbm,
     sums_ref, mats_hbm, dst_ref, src_ref, tiles_ref, feats_ref, seeds_ref, w_self_ref,
-    sems, own_adj_ref, adj_ref, mats_ref, out_sem,
+    sems, own_adj_ref, adj_ref, mats_ref, out_sems,
 ):
     *tile_copies, feats_copy, seeds_copy, w_self_copy = fetch(
         (dst_hbm, src_hbm, tiles_hbm, feats_hbm, seeds_hbm, w_self_hbm),
@@ -193,15 +193,6 @@
     place_tiles(
         dst_ref, src_ref, count_ref, tiles_ref, adj_ref, own_blocks, own_blocks + table // BLK
     )
-    seeds_copy.wait()
-    feats_copy.wait()
-    picks = (iota((rows, seeds), 0) == seeds_ref[...]).astype(BF16)
-    feats = feats_ref[...]
-    mats_ref[2 * seeds + adj_ref.shape[1] :, :seeds] = dot(feats, picks, 0, 0).astype(BF16)
-    chosen = dot(picks, feats, 0, 0).astype(BF16)
-    w_self_copy.wait()
-    sums_ref[:seeds] = dot(chosen, w_self_ref[...])
-    sums_ref[seeds:] = dot(own_adj_ref[...], feats)
     adj = adj_ref[...]
     half = table // 2
     depth = half // PLANE // 2
@@ -215,23 +206,40 @@
         mats_ref[far * seeds : (far + 1) * seeds, :half] = dot(adj, order, 1, 1).astype(BF16)
         first = 2 * seeds + far * half
         mats_ref[first : first + half, :seeds] = dot(order, adj, 1, 1).astype(BF16)
-    back = pltpu.make_async_copy(mats_ref, mats_hbm, out_sem)
-    back.start()
-    back.wait()
+    ready = pl.ds(0, 2 * (seeds + half))
+    early = pltpu.make_async_copy(mats_ref.at[ready], mats_hbm.at[ready], out_sems.at[0])
+    early.start()
+    seeds_copy.wait()
+    feats_copy.wait()
+    picks = (iota((rows, seeds), 0) == seeds_ref[...]).astype(BF16)
+    feats = feats_ref[...]
+    mats_ref[2 * (seeds + half) :, :seeds] = dot(feats, picks, 0, 0).astype(BF16)
+    rest = pl.ds(2 * (seeds + half), mats_ref.shape[0] - 2 * (seeds + half))
+    late = pltpu.make_async_copy(mats_ref.at[rest], mats_hbm.at[rest], out_sems.at[1])
+    late.start()
+    chosen = dot(picks, feats, 0, 0).astype(BF16)
+    w_self_copy.wait()
+    sums_ref[:seeds] = dot(chosen, w_self_ref[...])
+    sums_ref[seeds:] = dot(own_adj_ref[...], feats)
+    early.wait()
+    late.wait()
+
+
+def near_kernel(near_ref, mats_ref, sums_ref, part_ref):
+    seeds, half = part_ref.shape[0], near_ref.shape[0]
+    part_ref[...] = sums_ref[seeds:] + dot(mats_ref[:seeds, :half], near_ref[...])
 
 
 def middle_kernel(
-    core_ref, near_ref, far_ref, mats_ref, sums_ref, w_neigh_ref, cot_ref, bias_in_ref,
+    core_ref, part_ref, far_ref, mats_ref, sums_ref, w_neigh_ref, cot_ref, bias_in_ref,
     out_ref, d_pre_ref, d_agg_ref, keep_ref, send_ref,
 ):
     width = w_neigh_ref.shape[0]
-    half = near_ref.shape[0]
+    half = far_ref.shape[0]
     seeds = cot_ref.shape[0]
     near_back, far_back, chosen_t = (2 * seeds + step * half for step in range(3))
     aggregate = (
-        sums_ref[seeds:]
-        + dot(mats_ref[:seeds, :half], near_ref[...])
-        + dot(mats_ref[seeds : 2 * seeds, :half], far_ref[...])
+        part_ref[...] + dot(mats_ref[seeds : 2 * seeds, :half], far_ref[...])
     ).astype(BF16)
     preact = sums_ref[:seeds] + dot(aggregate, w_neigh_ref[...]) + bias_in_ref[...].astype(F32)
     gate = jax.nn.sigmoid(preact)
@@ -450,7 +458,7 @@
             pltpu.VMEM((seeds, rows), BF16),
             pltpu.VMEM((seeds, 2 * half), BF16),
             pltpu.VMEM(mats_shape, BF16),
-            pltpu.SemaphoreType.DMA,
+            pltpu.SemaphoreType.DMA((2,)),
         ],
         flops=2 * seeds * (3 * rows * width + width * width + 8 * half * half),
     )
@@ -461,6 +469,10 @@
     near = swap(plane, ("y", "x")).reshape(half, width)
     far = pair(near)
 
+    (part,) = call(
+        near_kernel, "near_rows", [((seeds, width), F32)], [], [near, mats, sums],
+        flops=2 * seeds * width * half,
+    )
     out, d_pre, d_agg, keep, pair_send = call(
         middle_kernel, "forward_backward",
         [
@@ -472,7 +484,7 @@
         ],
         [core],
         [
-            near, far, mats, sums, w_neigh, cotangent, bias.reshape(1, width),
+            part, far, mats, sums, w_neigh, cotangent, bias.reshape(1, width),
         ],
         flops=2 * seeds * width * (4 * half + 4 * width),
     )

time: 141 us -> 140 us (level)
    pallas_call x15 -> x16, Pallas kernels: 19.2 us -> 18.1 us  [call(): pl.pallas_call(kernel, out_shape=shapes, in_specs=[pl.BlockSpec(memory_sp...]
where the time goes in v14:
time: 140 us; the launch traced here: 139 us
  blocking collectives  52 us (37%)
  starting transfers between devices  48.4 us (35%)
  waiting for transfers between devices  19.1 us (14%)
  Pallas kernels  18.1 us (13%)
  between operations  1.59 us (1%)
    all_to_all x3, blocking collectives, swap(): return lax.all_to_all(values, axis, split_axis=0, concat_axis=0, tiled=True)  52 us
    all_to_all x3, starting transfers between devices, swap(): return lax.all_to_all(values, axis, split_axis=0, concat_axis=0, tiled=True)  24.9 us
    pallas_call x16, Pallas kernels, call(): pl.pallas_call(kernel, out_shape=shapes, in_specs=[pl.BlockSpec(memory_sp...  18.1 us
    all_to_all x3, waiting for transfers between devices, swap(): return lax.all_to_all(values, axis, split_axis=0, concat_axis=0, tiled=True)  16.9 us
    ppermute x3, starting transfers between devices, pair(): return lax.ppermute(values, 'core', [(0, 1), (1, 0)])  14.6 us
    ppermute x3, starting transfers between devices, body(): lax.ppermute(row_sends[step - 1], 'x', [(x, x ^ step) for x in range(X_SI...  8.98 us
  transfers between devices with their start and end apart: 9, of which 6 were waited for; matrix products, arithmetic and copies ran while one was open for 0% of the time, Pallas kernels for 8%

profile of v14, /device:TPU:1, one launch (start us, length us, event | category | flops | bytes accessed | tf_op | source)
XLA Modules:
  0.0 139.2 jit_solution(3551000221052947522)
XLA Ops:
  0.6 2.4 %pick_boundary.1 = bf16[384,128]{1,0:T(8,128)(2,1)} custom-call(s32[1]{0:T(128)} %bitcast.1.rep_ref.refs_0_, s32[8,64]{1,0:T(8,128)} %bitcast.13, bf16[768,512]{1,0:T(8,128)(2,1)} %feats_hbm.3), custom_call_target="tpu_custom_call" | custom-call | flops 100663296 | bytes 886784 | tf_op jit(solution)/shard_map/pick_boundary/pallas_call | solution.py:51
  3.0 15.8 %all-to-all-start = ((bf16[16,24,128]{2,1,0:T(8,128)(2,1)}), bf16[16,24,128]{2,1,0:T(8,128)(2,1)S(1)}, u32[]{:S(2)}, u32[]{:S(2)}) async-start(bf16[16,24,128]{2,1,0:T(8,128)(2,1)} %bitcast.4), calls=%async_computation | async-start | bytes 196608 | tf_op jit(solution)/shard_map/all_to_all | solution.py:438
  19.5 5.7 %own_rows.1 = (f32[1024,512]{1,0:T(8,128)S(1)}, bf16[2560,512]{1,0:T(8,128)(2,1)}) custom-call(s32[1]{0:T(128)} %bitcast.core_ref, s32[1]{0:T(128)S(6)} %copy.16.count_ref, s32[1,14]{1,0:T(1,128)} %dst_ref.1, s32[1,14]{1,0:T(1,128)} %src_ref.1, bf16[14,128,128]{2,1,0:T(8,128)(2,1)} %tiles_ref.1, bf16[768,512]{1,0:T(8,128)(2,1)} %feats_hbm.3, ...), custom_call_target="tpu_custom_call" | custom-call | flops 3623878656 | bytes 6490224 | tf_op jit(solution)/shard_map/own_rows/pallas_call | solution.py:51
  25.2 5.5 %all-to-all-done = bf16[16,24,128]{2,1,0:T(8,128)(2,1)S(1)} async-done(((bf16[16,24,128]{2,1,0:T(8,128)(2,1)}), bf16[16,24,128]{2,1,0:T(8,128)(2,1)S(1)}, u32[]{:S(2)}, u32[]{:S(2)}) %all-to-all-start) | async-done | bytes 98336 | tf_op jit(solution)/shard_map/all_to_all | solution.py:438
  30.7 0.3 spread_plane.1
  31.0 15.7 %all_to_all.30 = bf16[16,32,512]{2,1,0:T(8,128)(2,1)S(1)} all-to-all(bf16[16,32,512]{2,1,0:T(8,128)(2,1)S(1)} %spread_plane.1), channel_id=1, replica_groups=mesh['z'=16,'y'=4,'x'=4,'core'=2] {'y','x'}, dimensions={0} | all-to-all | bytes 1048576 | tf_op jit(solution)/shard_map/all_to_all | solution.py:438
  46.7 6.0 %collective-permute-start = (bf16[512,512]{1,0:T(8,128)(2,1)S(1)}, bf16[512,512]{1,0:T(8,128)(2,1)S(1)}, u32[]{:S(2)}, u32[]{:S(2)}) collective-permute-start(bf16[512,512]{1,0:T(8,128)(2,1)S(1)} %bitcast.10), channel_id=1, source_target_pairs={{0,1},{1,0},{2,3},{3,2},{4,5},{5,4},{6,7},{7,6},{8,9},{9,8},{10,11... | collective-permute-start | bytes 1572872 | tf_op jit(solution)/shard_map/ppermute | solution.py:441
  52.6 0.0 copy-done.9
  52.7 0.0 copy-done
  52.7 0.0 copy-start.2
  52.7 0.0 copy-start.3
  52.7 0.4 near_rows.1.part_ref
  53.1 0.0 copy-start.4
  53.2 0.0 copy-start.5
  53.2 0.0 copy-start.6
  53.2 0.0 copy-start.7
  53.2 0.0 copy-start.8
  53.2 1.0 collective-permute-done.far_ref
  54.2 0.0 copy-done.2
  54.2 2.5 %forward_backward.1 = (bf16[512,512]{1,0:T(8,128)(2,1)}, bf16[512,512]{1,0:T(8,128)(2,1)S(1)}, bf16[512,512]{1,0:T(8,128)(2,1)S(1)}, bf16[1040,512]{1,0:T(8,128)(2,1)S(1)}, bf16[1040,512]{1,0:T(8,128)(2,1)S(1)}) custom-call(s32[1]{0:T(128)} %bitcast.core_ref, f32[512,512]{1,0:T(8,128)S(1)} %near_rows.1.part_ref, ...), custom_call_target="tpu_custom_call" | custom-call | flops 2147483648 | bytes 11043840 | tf_op jit(solution)/shard_map/forward_backward/pallas_call | solution.py:51
  56.6 2.3 %collective-permute-start.1 = (bf16[1040,512]{1,0:T(8,128)(2,1)S(1)}, bf16[1040,512]{1,0:T(8,128)(2,1)S(1)}, u32[]{:S(2)}, u32[]{:S(2)}) collective-permute-start(bf16[1040,512]{1,0:T(8,128)(2,1)S(1)} %get-tuple-element.29), channel_id=1, source_target_pairs={{0,1},{1,0},{2,3},{3,2},{4,5},{5,4},{6,7},{7,6},{8,9},{9,8},{10,11... | collective-permute-start | bytes 3194888 | tf_op jit(solution)/shard_map/ppermute | solution.py:441
  59.0 2.0 %own_rows_back.1.refs_2_.refs_3_ = f32[768,512]{1,0:T(8,128)S(1)} custom-call(s32[1,14]{1,0:T(1,128)S(1)} %copy-done.7, s32[1,14]{1,0:T(1,128)S(1)} %copy-done.8, s32[1]{0:T(128)S(6)} %copy.16.count_ref, bf16[14,128,128]{2,1,0:T(8,128)(2,1)S(1)} %copy-done.5, s32[1,512]{1,0:T(1,128)S(1)} %bitcast.16, bf16[512,512]{1,0:T(8,128)(2,1)S(1)} %get-tuple-element.30.d_pre_ref, ...), custom_call_target="tpu_custom_call" | custom-call | flops 1207959552 | bytes 3606528 | tf_op jit(solution)/shard_map/own_rows_back/pallas_call | solution.py:51
  61.0 0.2 collective-permute-done.1.refs_1_
  61.2 0.2 sum_pair.1
  61.5 0.0 copy-start.1
  61.5 19.0 %all_to_all.31.arrived_ref = bf16[16,64,512]{2,1,0:T(8,128)(2,1)S(1)} all-to-all(bf16[16,64,512]{2,1,0:T(8,128)(2,1)S(1)} %get-tuple-element.32), channel_id=1, replica_groups=mesh['z'=16,'y'=4,'x'=4,'core'=2] {'y','x'}, dimensions={0} | all-to-all | bytes 2097152 | tf_op jit(solution)/shard_map/all_to_all | solution.py:438
  80.5 0.3 sum_plane.1
  80.8 17.3 %all_to_all.32.arrived_ref.refs_2_ = bf16[16,8,512]{2,1,0:T(8,128)(2,1)S(1)} all-to-all(bf16[16,8,512]{2,1,0:T(8,128)(2,1)S(1)} %sum_plane.1), channel_id=1, replica_groups=mesh['z'=16,'y'=4,'x'=4,'core'=2] {'z'}, dimensions={0} | all-to-all | bytes 262144 | tf_op jit(solution)/shard_map/all_to_all | solution.py:438
  98.1 0.6 sum_weights.1
  98.8 5.1 %all-to-all-start.4 = ((bf16[16,8,128]{2,1,0:T(8,128)(2,1)}), bf16[16,8,128]{2,1,0:T(8,128)(2,1)S(1)}, u32[]{:S(2)}, u32[]{:S(2)}) async-start(bf16[16,8,128]{2,1,0:T(8,128)(2,1)} %get-tuple-element.34.refs_4_), calls=%async_computation.4 | async-start | bytes 65536 | tf_op jit(solution)/shard_map/all_to_all | solution.py:438
  103.9 0.0 copy-done.1
  103.9 0.6 return_rows.1
  104.5 3.8 %collective-permute-start.2 = (bf16[192,512]{1,0:T(8,128)(2,1)S(1)}, bf16[192,512]{1,0:T(8,128)(2,1)S(1)}, u32[]{:S(2)}, u32[]{:S(2)}) collective-permute-start(bf16[192,512]{1,0:T(8,128)(2,1)S(1)} %get-tuple-element.37), channel_id=1, source_target_pairs={{0,4},{2,6},{4,0},{6,2},{1,5},{3,7},{5,1},{7,3},{8,12},{10,14},{12... | collective-permute-start | bytes 589832 | tf_op jit(solution)/shard_map/ppermute | solution.py:526
  108.3 1.9 %collective-permute-start.3 = (bf16[192,512]{1,0:T(8,128)(2,1)S(1)}, bf16[192,512]{1,0:T(8,128)(2,1)S(1)}, u32[]{:S(2)}, u32[]{:S(2)}) collective-permute-start(bf16[192,512]{1,0:T(8,128)(2,1)S(1)} %get-tuple-element.38), channel_id=1, source_target_pairs={{0,2},{2,0},{4,6},{6,4},{1,3},{3,1},{5,7},{7,5},{8,10},{10,8},{12,... | collective-permute-start | bytes 589832 | tf_op jit(solution)/shard_map/ppermute | solution.py:526
  110.3 3.2 %collective-permute-start.4 = (bf16[192,512]{1,0:T(8,128)(2,1)S(1)}, bf16[192,512]{1,0:T(8,128)(2,1)S(1)}, u32[]{:S(2)}, u32[]{:S(2)}) collective-permute-start(bf16[192,512]{1,0:T(8,128)(2,1)S(1)} %get-tuple-element.39), channel_id=1, source_target_pairs={{0,6},{2,4},{4,2},{6,0},{1,7},{3,5},{5,3},{7,1},{8,14},{10,12},{12... | collective-permute-start | bytes 589832 | tf_op jit(solution)/shard_map/ppermute | solution.py:526
  113.5 1.8 %all-to-all-done.4.refs_0_ = bf16[16,8,128]{2,1,0:T(8,128)(2,1)S(1)} async-done(((bf16[16,8,128]{2,1,0:T(8,128)(2,1)}), bf16[16,8,128]{2,1,0:T(8,128)(2,1)S(1)}, u32[]{:S(2)}, u32[]{:S(2)}) %all-to-all-start.4) | async-done | bytes 32800 | tf_op jit(solution)/shard_map/all_to_all | solution.py:438
  115.3 0.1 gather_weights.1.whole_ref
  115.5 0.9 spread_weights.1
  116.4 4.0 %all-to-all-start.5 = ((bf16[16,40,512]{2,1,0:T(8,128)(2,1)}), bf16[16,40,512]{2,1,0:T(8,128)(2,1)S(1)}, u32[]{:S(2)}, u32[]{:S(2)}) async-start(bf16[16,40,512]{2,1,0:T(8,128)(2,1)} %spread_weights.1), calls=%async_computation.5 | async-start | bytes 1310720 | tf_op jit(solution)/shard_map/all_to_all | solution.py:438
  120.4 0.0 collective-permute-done.2.refs_0_
  120.4 0.0 collective-permute-done.3.refs_1_
  120.4 0.0 collective-permute-done.4.refs_2_
  120.4 0.1 sum_rows.1
  120.5 9.6 %all-to-all-done.5.arrived_ref.refs_0_ = bf16[16,40,512]{2,1,0:T(8,128)(2,1)S(1)} async-done(((bf16[16,40,512]{2,1,0:T(8,128)(2,1)}), bf16[16,40,512]{2,1,0:T(8,128)(2,1)S(1)}, u32[]{:S(2)}, u32[]{:S(2)}) %all-to-all-start.5) | async-done | bytes 655392 | tf_op jit(solution)/shard_map/all_to_all | solution.py:438
  130.2 6.3 %collective-permute-start.5 = (bf16[608,512]{1,0:T(8,128)(2,1)S(1)}, bf16[608,512]{1,0:T(8,128)(2,1)S(1)}, u32[]{:S(2)}, u32[]{:S(2)}) collective-permute-start(bf16[608,512]{1,0:T(8,128)(2,1)S(1)} %join.1.near_ref.refs_1_), channel_id=1, source_target_pairs={{0,1},{1,0},{2,3},{3,2},{4,5},{5,4},{6,7},{7,6},{8,9},{9,8},{10,11... | collective-permute-start | bytes 1867784 | tf_op jit(solution)/shard_map/ppermute | solution.py:441
  136.5 0.7 sum_bias.1
  137.1 1.0 collective-permute-done.5.far_ref
  138.1 1.1 finish.1
  (10 shorter events, 0.1 us)
Async XLA Ops:
  3.0 27.6 %all-to-all-start = ((bf16[16,24,128]{2,1,0:T(8,128)(2,1)}), bf16[16,24,128]{2,1,0:T(8,128)(2,1)S(1)}, u32[]{:S(2)}, u32[]{:S(2)}) async-start(bf16[16,24,128]{2,1,0:T(8,128)(2,1)} %bitcast.4), calls=%async_computation | async-start | bytes 196608 | tf_op jit(solution)/shard_map/all_to_all | solution.py:438
  30.7 22.0 %copy-start.9 = (bf16[512]{0:T(512)(128)(2,1)S(1)}, bf16[512]{0:T(512)(128)(2,1)}, u32[]{:S(2)}) copy-start(bf16[512]{0:T(512)(128)(2,1)} %param.20) | copy-start | bytes 3076
  30.7 22.0 %copy-start = (bf16[2560,512]{1,0:T(8,128)(2,1)S(1)}, bf16[2560,512]{1,0:T(8,128)(2,1)}, u32[]{:S(2)}) copy-start(bf16[2560,512]{1,0:T(8,128)(2,1)} %get-tuple-element.26.mats_ref) | copy-start | bytes 7864324
  46.7 7.5 %collective-permute-start = (bf16[512,512]{1,0:T(8,128)(2,1)S(1)}, bf16[512,512]{1,0:T(8,128)(2,1)S(1)}, u32[]{:S(2)}, u32[]{:S(2)}) collective-permute-start(bf16[512,512]{1,0:T(8,128)(2,1)S(1)} %bitcast.10), channel_id=1, source_target_pairs={{0,1},{1,0},{2,3},{3,2},{4,5},{5,4},{6,7},{7,6},{8,9},{9,8},{10,11... | collective-permute-start | bytes 1572872 | tf_op jit(solution)/shard_map/ppermute | solution.py:441
  52.7 1.5 %copy-start.2 = (bf16[512,512]{1,0:T(8,128)(2,1)S(1)}, bf16[512,512]{1,0:T(8,128)(2,1)}, u32[]{:S(2)}) copy-start(bf16[512,512]{1,0:T(8,128)(2,1)} %w_neigh_ref.1) | copy-start | bytes 1572868
  52.7 1.5 %copy-start.3 = (bf16[512,512]{1,0:T(8,128)(2,1)S(1)}, bf16[512,512]{1,0:T(8,128)(2,1)}, u32[]{:S(2)}) copy-start(bf16[512,512]{1,0:T(8,128)(2,1)} %cot_ref.1) | copy-start | bytes 1572868
  53.1 5.8 %copy-start.4 = (bf16[512,512]{1,0:T(8,128)(2,1)S(1)}, bf16[512,512]{1,0:T(8,128)(2,1)}, u32[]{:S(2)}) copy-start(bf16[512,512]{1,0:T(8,128)(2,1)} %w_self_ref.1) | copy-start | bytes 1572868
  53.2 5.8 %copy-start.5 = (bf16[14,128,128]{2,1,0:T(8,128)(2,1)S(1)}, bf16[14,128,128]{2,1,0:T(8,128)(2,1)}, u32[]{:S(2)}) copy-start(bf16[14,128,128]{2,1,0:T(8,128)(2,1)} %tiles_ref.1) | copy-start | bytes 1376260
  53.2 5.8 %copy-start.6 = (s32[512]{0:T(512)S(1)}, s32[512]{0:T(512)}, u32[]{:S(2)}) copy-start(s32[512]{0:T(512)} %param.13) | copy-start | bytes 6148
  53.2 5.8 %copy-start.7 = (s32[1,14]{1,0:T(1,128)S(1)}, s32[1,14]{1,0:T(1,128)}, u32[]{:S(2)}) copy-start(s32[1,14]{1,0:T(1,128)} %dst_ref.1) | copy-start | bytes 172
  53.2 5.8 %copy-start.8 = (s32[1,14]{1,0:T(1,128)S(1)}, s32[1,14]{1,0:T(1,128)}, u32[]{:S(2)}) copy-start(s32[1,14]{1,0:T(1,128)} %src_ref.1) | copy-start | bytes 172
  56.6 4.6 %collective-permute-start.1 = (bf16[1040,512]{1,0:T(8,128)(2,1)S(1)}, bf16[1040,512]{1,0:T(8,128)(2,1)S(1)}, u32[]{:S(2)}, u32[]{:S(2)}) collective-permute-start(bf16[1040,512]{1,0:T(8,128)(2,1)S(1)} %get-tuple-element.29), channel_id=1, source_target_pairs={{0,1},{1,0},{2,3},{3,2},{4,5},{5,4},{6,7},{7,6},{8,9},{9,8},{10,11... | collective-permute-start | bytes 3194888 | tf_op jit(solution)/shard_map/ppermute | solution.py:441
  61.5 42.4 %copy-start.1 = (s32[1,64,8]{1,2,0:T(8,128)S(1)}, s32[1,64,8]{1,2,0:T(8,128)}, u32[]{:S(2)}) copy-start(s32[1,64,8]{1,2,0:T(8,128)} %param.12) | copy-start | bytes 6148
  98.8 16.6 %all-to-all-start.4 = ((bf16[16,8,128]{2,1,0:T(8,128)(2,1)}), bf16[16,8,128]{2,1,0:T(8,128)(2,1)S(1)}, u32[]{:S(2)}, u32[]{:S(2)}) async-start(bf16[16,8,128]{2,1,0:T(8,128)(2,1)} %get-tuple-element.34.refs_4_), calls=%async_computation.4 | async-start | bytes 65536 | tf_op jit(solution)/shard_map/all_to_all | solution.py:438
  104.5 15.9 %collective-permute-start.2 = (bf16[192,512]{1,0:T(8,128)(2,1)S(1)}, bf16[192,512]{1,0:T(8,128)(2,1)S(1)}, u32[]{:S(2)}, u32[]{:S(2)}) collective-permute-start(bf16[192,512]{1,0:T(8,128)(2,1)S(1)} %get-tuple-element.37), channel_id=1, source_target_pairs={{0,4},{2,6},{4,0},{6,2},{1,5},{3,7},{5,1},{7,3},{8,12},{10,14},{12... | collective-permute-start | bytes 589832 | tf_op jit(solution)/shard_map/ppermute | solution.py:526
  108.3 12.1 %collective-permute-start.3 = (bf16[192,512]{1,0:T(8,128)(2,1)S(1)}, bf16[192,512]{1,0:T(8,128)(2,1)S(1)}, u32[]{:S(2)}, u32[]{:S(2)}) collective-permute-start(bf16[192,512]{1,0:T(8,128)(2,1)S(1)} %get-tuple-element.38), channel_id=1, source_target_pairs={{0,2},{2,0},{4,6},{6,4},{1,3},{3,1},{5,7},{7,5},{8,10},{10,8},{12,... | collective-permute-start | bytes 589832 | tf_op jit(solution)/shard_map/ppermute | solution.py:526
  110.3 10.2 %collective-permute-start.4 = (bf16[192,512]{1,0:T(8,128)(2,1)S(1)}, bf16[192,512]{1,0:T(8,128)(2,1)S(1)}, u32[]{:S(2)}, u32[]{:S(2)}) collective-permute-start(bf16[192,512]{1,0:T(8,128)(2,1)S(1)} %get-tuple-element.39), channel_id=1, source_target_pairs={{0,6},{2,4},{4,2},{6,0},{1,7},{3,5},{5,3},{7,1},{8,14},{10,12},{12... | collective-permute-start | bytes 589832 | tf_op jit(solution)/shard_map/ppermute | solution.py:526
  116.4 13.7 %all-to-all-start.5 = ((bf16[16,40,512]{2,1,0:T(8,128)(2,1)}), bf16[16,40,512]{2,1,0:T(8,128)(2,1)S(1)}, u32[]{:S(2)}, u32[]{:S(2)}) async-start(bf16[16,40,512]{2,1,0:T(8,128)(2,1)} %spread_weights.1), calls=%async_computation.5 | async-start | bytes 1310720 | tf_op jit(solution)/shard_map/all_to_all | solution.py:438
  130.2 8.0 %collective-permute-start.5 = (bf16[608,512]{1,0:T(8,128)(2,1)S(1)}, bf16[608,512]{1,0:T(8,128)(2,1)S(1)}, u32[]{:S(2)}, u32[]{:S(2)}) collective-permute-start(bf16[608,512]{1,0:T(8,128)(2,1)S(1)} %join.1.near_ref.refs_1_), channel_id=1, source_target_pairs={{0,1},{1,0},{2,3},{3,2},{4,5},{5,4},{6,7},{7,6},{8,9},{9,8},{10,11... | collective-permute-start | bytes 1867784 | tf_op jit(solution)/shard_map/ppermute | solution.py:441

commit v15 on v14

--- a/solution.py
+++ b/solution.py
@@ -377,12 +377,11 @@
     send_ref[...] = total[share:].astype(BF16)
 
 
-def join_kernel(arrived_ref, rows_ref, send_ref):
+def join_kernel(arrived_ref, send_ref):
     chunks, _, width = arrived_ref.shape
     weight = width // chunks
     for chunk in range(chunks):
         send_ref[chunk * weight : (chunk + 1) * weight] = arrived_ref[chunk, :weight]
-    send_ref[width:] = rows_ref[...]
 
 
 def bias_kernel(arrived_ref, bias_ref):
@@ -395,13 +394,13 @@
     bias_ref[...] = bias
 
 
-def finish_kernel(core_ref, near_ref, own_ref, far_ref, first_ref, second_ref, rows_ref):
+def finish_kernel(core_ref, near_ref, own_ref, far_ref, row_far_ref, first_ref, second_ref, rows_ref):
     width = first_ref.shape[0]
     near, far = near_ref[:width], far_ref[:width]
     is_first = core_ref[0] == 0
     first_ref[...] = jnp.where(is_first, near, far)
     second_ref[...] = jnp.where(is_first, far, near)
-    rows_ref[...] = own_ref[...] + far_ref[width:].astype(F32)
+    rows_ref[...] = own_ref[...] + row_far_ref[...].astype(F32)
 
 
 def body(
@@ -539,8 +538,9 @@
         [], [weight_rows, plane_bias],
     )
     weight_near = swap(weight_plane, ("y", "x"))
+    row_far = pair(row_send)
     (last_send,) = call(
-        join_kernel, "join", [((width + share, width), BF16)], [], [weight_near, row_send]
+        join_kernel, "join", [((width, width), BF16)], [], [weight_near], after=[row_far]
     )
     (grad_bias,) = call(
         bias_kernel, "sum_bias", [((1, width), F32)], [], [weight_near], after=[last_send]
@@ -548,7 +548,7 @@
     grad_self, grad_neigh, input_grad = call(
         finish_kernel, "finish",
         [((width, width), BF16), ((width, width), BF16), ((share, width), F32)],
-        [core], [last_send, row_own, pair(last_send)],
+        [core], [last_send, row_own, pair(last_send), row_far],
     )
     grad_bias = grad_bias.reshape(width)
     return (out, input_grad, grad_self, grad_neigh, grad_bias)

time: 140 us -> 140 us (level)
  waiting for transfers between devices: 19.1 us -> 13.5 us
  starting transfers between devices: 48.4 us -> 53.6 us
    all_to_all x3, waiting for transfers between devices: 16.9 us -> 10.6 us  [swap(): return lax.all_to_all(values, axis, split_axis=0, concat_axis=0, tiled=True)]
    ppermute x3 -> x4, starting transfers between devices: 14.6 us -> 19.8 us  [pair(): return lax.ppermute(values, 'core', [(0, 1), (1, 0)])]
    ppermute x3 -> x4, waiting for transfers between devices: 2.18 us -> 2.9 us  [pair(): return lax.ppermute(values, 'core', [(0, 1), (1, 0)])]
  transfers between devices with their start and end apart: 9 -> 10, of which waited for: 6 -> 7; matrix products, arithmetic and copies ran while one was open for 0% -> 0% of each run, Pallas kernels for 8% -> 8%
where the time goes in v15:
time: 140 us; the launch traced here: 139 us
  starting transfers between devices  53.6 us (38%)
  blocking collectives  51.9 us (37%)
  Pallas kernels  18.2 us (13%)
  waiting for transfers between devices  13.5 us (10%)
  between operations  1.6 us (1%)
    all_to_all x3, blocking collectives, swap(): return lax.all_to_all(values, axis, split_axis=0, concat_axis=0, tiled=True)  51.9 us
    all_to_all x3, starting transfers between devices, swap(): return lax.all_to_all(values, axis, split_axis=0, concat_axis=0, tiled=True)  24.9 us
    ppermute x4, starting transfers between devices, pair(): return lax.ppermute(values, 'core', [(0, 1), (1, 0)])  19.8 us
    pallas_call x16, Pallas kernels, call(): pl.pallas_call(kernel, out_shape=shapes, in_specs=[pl.BlockSpec(memory_sp...  18.2 us
    all_to_all x3, waiting for transfers between devices, swap(): return lax.all_to_all(values, axis, split_axis=0, concat_axis=0, tiled=True)  10.6 us
    ppermute x3, starting transfers between devices, body(): lax.ppermute(row_sends[step - 1], 'x', [(x, x ^ step) for x in range(X_SI...  8.98 us
    ppermute x4, waiting for transfers between devices, pair(): return lax.ppermute(values, 'core', [(0, 1), (1, 0)])  2.9 us
  transfers between devices with their start and end apart: 10, of which 7 were waited for; matrix products, arithmetic and copies ran while one was open for 0% of the time, Pallas kernels for 8%

profile of v15, /device:TPU:1, one launch (start us, length us, event | category | flops | bytes accessed | tf_op | source)
XLA Modules:
  0.0 139.0 jit_solution(6290113727493381277)
XLA Ops:
  0.6 2.4 %pick_boundary.1 = bf16[384,128]{1,0:T(8,128)(2,1)} custom-call(s32[1]{0:T(128)} %bitcast.1.rep_ref.refs_0_, s32[8,64]{1,0:T(8,128)} %bitcast.13, bf16[768,512]{1,0:T(8,128)(2,1)} %feats_hbm.3), custom_call_target="tpu_custom_call" | custom-call | flops 100663296 | bytes 886784 | tf_op jit(solution)/shard_map/pick_boundary/pallas_call | solution.py:51
  3.0 15.8 %all-to-all-start = ((bf16[16,24,128]{2,1,0:T(8,128)(2,1)}), bf16[16,24,128]{2,1,0:T(8,128)(2,1)S(1)}, u32[]{:S(2)}, u32[]{:S(2)}) async-start(bf16[16,24,128]{2,1,0:T(8,128)(2,1)} %bitcast.4), calls=%async_computation | async-start | bytes 196608 | tf_op jit(solution)/shard_map/all_to_all | solution.py:437
  19.5 5.8 %own_rows.1 = (f32[1024,512]{1,0:T(8,128)S(1)}, bf16[2560,512]{1,0:T(8,128)(2,1)}) custom-call(s32[1]{0:T(128)} %bitcast.core_ref, s32[1]{0:T(128)S(6)} %copy.16.count_ref, s32[1,14]{1,0:T(1,128)} %dst_ref.1, s32[1,14]{1,0:T(1,128)} %src_ref.1, bf16[14,128,128]{2,1,0:T(8,128)(2,1)} %tiles_ref.1, bf16[768,512]{1,0:T(8,128)(2,1)} %feats_hbm.3, ...), custom_call_target="tpu_custom_call" | custom-call | flops 3623878656 | bytes 6490224 | tf_op jit(solution)/shard_map/own_rows/pallas_call | solution.py:51
  25.3 5.4 %all-to-all-done = bf16[16,24,128]{2,1,0:T(8,128)(2,1)S(1)} async-done(((bf16[16,24,128]{2,1,0:T(8,128)(2,1)}), bf16[16,24,128]{2,1,0:T(8,128)(2,1)S(1)}, u32[]{:S(2)}, u32[]{:S(2)}) %all-to-all-start) | async-done | bytes 98336 | tf_op jit(solution)/shard_map/all_to_all | solution.py:437
  30.7 0.3 spread_plane.1
  31.0 15.7 %all_to_all.30 = bf16[16,32,512]{2,1,0:T(8,128)(2,1)S(1)} all-to-all(bf16[16,32,512]{2,1,0:T(8,128)(2,1)S(1)} %spread_plane.1), channel_id=1, replica_groups=mesh['z'=16,'y'=4,'x'=4,'core'=2] {'y','x'}, dimensions={0} | all-to-all | bytes 1048576 | tf_op jit(solution)/shard_map/all_to_all | solution.py:437
  46.7 6.0 %collective-permute-start = (bf16[512,512]{1,0:T(8,128)(2,1)S(1)}, bf16[512,512]{1,0:T(8,128)(2,1)S(1)}, u32[]{:S(2)}, u32[]{:S(2)}) collective-permute-start(bf16[512,512]{1,0:T(8,128)(2,1)S(1)} %bitcast.10), channel_id=1, source_target_pairs={{0,1},{1,0},{2,3},{3,2},{4,5},{5,4},{6,7},{7,6},{8,9},{9,8},{10,11... | collective-permute-start | bytes 1572872 | tf_op jit(solution)/shard_map/ppermute | solution.py:440
  52.6 0.0 copy-done.9
  52.7 0.0 copy-done
  52.7 0.0 copy-start.2
  52.7 0.0 copy-start.3
  52.7 0.4 near_rows.1.part_ref
  53.1 0.0 copy-start.4
  53.2 0.0 copy-start.5
  53.2 0.0 copy-start.6
  53.2 0.0 copy-start.7
  53.2 0.0 copy-start.8
  53.2 1.0 collective-permute-done.far_ref
  54.2 2.5 %forward_backward.1 = (bf16[512,512]{1,0:T(8,128)(2,1)}, bf16[512,512]{1,0:T(8,128)(2,1)S(1)}, bf16[512,512]{1,0:T(8,128)(2,1)S(1)}, bf16[1040,512]{1,0:T(8,128)(2,1)S(1)}, bf16[1040,512]{1,0:T(8,128)(2,1)S(1)}) custom-call(s32[1]{0:T(128)} %bitcast.core_ref, f32[512,512]{1,0:T(8,128)S(1)} %near_rows.1.part_ref, ...), custom_call_target="tpu_custom_call" | custom-call | flops 2147483648 | bytes 11043840 | tf_op jit(solution)/shard_map/forward_backward/pallas_call | solution.py:51
  56.6 2.3 %collective-permute-start.1 = (bf16[1040,512]{1,0:T(8,128)(2,1)S(1)}, bf16[1040,512]{1,0:T(8,128)(2,1)S(1)}, u32[]{:S(2)}, u32[]{:S(2)}) collective-permute-start(bf16[1040,512]{1,0:T(8,128)(2,1)S(1)} %get-tuple-element.29), channel_id=1, source_target_pairs={{0,1},{1,0},{2,3},{3,2},{4,5},{5,4},{6,7},{7,6},{8,9},{9,8},{10,11... | collective-permute-start | bytes 3194888 | tf_op jit(solution)/shard_map/ppermute | solution.py:440
  59.0 2.1 %own_rows_back.1.refs_2_.refs_3_ = f32[768,512]{1,0:T(8,128)S(1)} custom-call(s32[1,14]{1,0:T(1,128)S(1)} %copy-done.7, s32[1,14]{1,0:T(1,128)S(1)} %copy-done.8, s32[1]{0:T(128)S(6)} %copy.16.count_ref, bf16[14,128,128]{2,1,0:T(8,128)(2,1)S(1)} %copy-done.5, s32[1,512]{1,0:T(1,128)S(1)} %bitcast.16, bf16[512,512]{1,0:T(8,128)(2,1)S(1)} %get-tuple-element.30.d_pre_ref, ...), custom_call_target="tpu_custom_call" | custom-call | flops 1207959552 | bytes 3606528 | tf_op jit(solution)/shard_map/own_rows_back/pallas_call | solution.py:51
  61.0 0.2 collective-permute-done.1.refs_1_
  61.2 0.2 sum_pair.1
  61.5 0.0 copy-start.1
  61.5 19.0 %all_to_all.31.arrived_ref = bf16[16,64,512]{2,1,0:T(8,128)(2,1)S(1)} all-to-all(bf16[16,64,512]{2,1,0:T(8,128)(2,1)S(1)} %get-tuple-element.32), channel_id=1, replica_groups=mesh['z'=16,'y'=4,'x'=4,'core'=2] {'y','x'}, dimensions={0} | all-to-all | bytes 2097152 | tf_op jit(solution)/shard_map/all_to_all | solution.py:437
  80.5 0.3 sum_plane.1
  80.8 17.2 %all_to_all.32.arrived_ref.refs_2_ = bf16[16,8,512]{2,1,0:T(8,128)(2,1)S(1)} all-to-all(bf16[16,8,512]{2,1,0:T(8,128)(2,1)S(1)} %sum_plane.1), channel_id=1, replica_groups=mesh['z'=16,'y'=4,'x'=4,'core'=2] {'z'}, dimensions={0} | all-to-all | bytes 262144 | tf_op jit(solution)/shard_map/all_to_all | solution.py:437
  98.0 0.6 sum_weights.1
  98.7 5.1 %all-to-all-start.4 = ((bf16[16,8,128]{2,1,0:T(8,128)(2,1)}), bf16[16,8,128]{2,1,0:T(8,128)(2,1)S(1)}, u32[]{:S(2)}, u32[]{:S(2)}) async-start(bf16[16,8,128]{2,1,0:T(8,128)(2,1)} %get-tuple-element.34.refs_4_), calls=%async_computation.4 | async-start | bytes 65536 | tf_op jit(solution)/shard_map/all_to_all | solution.py:437
  103.8 0.6 return_rows.1
  104.4 3.8 %collective-permute-start.2 = (bf16[192,512]{1,0:T(8,128)(2,1)S(1)}, bf16[192,512]{1,0:T(8,128)(2,1)S(1)}, u32[]{:S(2)}, u32[]{:S(2)}) collective-permute-start(bf16[192,512]{1,0:T(8,128)(2,1)S(1)} %get-tuple-element.37), channel_id=1, source_target_pairs={{0,4},{2,6},{4,0},{6,2},{1,5},{3,7},{5,1},{7,3},{8,12},{10,14},{12... | collective-permute-start | bytes 589832 | tf_op jit(solution)/shard_map/ppermute | solution.py:525
  108.2 1.9 %collective-permute-start.3 = (bf16[192,512]{1,0:T(8,128)(2,1)S(1)}, bf16[192,512]{1,0:T(8,128)(2,1)S(1)}, u32[]{:S(2)}, u32[]{:S(2)}) collective-permute-start(bf16[192,512]{1,0:T(8,128)(2,1)S(1)} %get-tuple-element.38), channel_id=1, source_target_pairs={{0,2},{2,0},{4,6},{6,4},{1,3},{3,1},{5,7},{7,5},{8,10},{10,8},{12,... | collective-permute-start | bytes 589832 | tf_op jit(solution)/shard_map/ppermute | solution.py:525
  110.2 3.2 %collective-permute-start.4 = (bf16[192,512]{1,0:T(8,128)(2,1)S(1)}, bf16[192,512]{1,0:T(8,128)(2,1)S(1)}, u32[]{:S(2)}, u32[]{:S(2)}) collective-permute-start(bf16[192,512]{1,0:T(8,128)(2,1)S(1)} %get-tuple-element.39), channel_id=1, source_target_pairs={{0,6},{2,4},{4,2},{6,0},{1,7},{3,5},{5,3},{7,1},{8,14},{10,12},{12... | collective-permute-start | bytes 589832 | tf_op jit(solution)/shard_map/ppermute | solution.py:525
  113.4 1.8 %all-to-all-done.4.refs_0_ = bf16[16,8,128]{2,1,0:T(8,128)(2,1)S(1)} async-done(((bf16[16,8,128]{2,1,0:T(8,128)(2,1)}), bf16[16,8,128]{2,1,0:T(8,128)(2,1)S(1)}, u32[]{:S(2)}, u32[]{:S(2)}) %all-to-all-start.4) | async-done | bytes 32800 | tf_op jit(solution)/shard_map/all_to_all | solution.py:437
  115.2 0.1 gather_weights.1.whole_ref
  115.4 0.9 spread_weights.1
  116.3 4.0 %all-to-all-start.5 = ((bf16[16,40,512]{2,1,0:T(8,128)(2,1)}), bf16[16,40,512]{2,1,0:T(8,128)(2,1)S(1)}, u32[]{:S(2)}, u32[]{:S(2)}) async-start(bf16[16,40,512]{2,1,0:T(8,128)(2,1)} %spread_weights.1), calls=%async_computation.5 | async-start | bytes 1310720 | tf_op jit(solution)/shard_map/all_to_all | solution.py:437
  120.3 0.0 collective-permute-done.2.refs_0_
  120.3 0.0 collective-permute-done.3.refs_1_
  120.3 0.0 collective-permute-done.4.refs_2_
  120.3 0.1 sum_rows.1
  120.4 5.2 %collective-permute-start.5 = (bf16[96,512]{1,0:T(8,128)(2,1)S(1)}, bf16[96,512]{1,0:T(8,128)(2,1)S(1)}, u32[]{:S(2)}, u32[]{:S(2)}) collective-permute-start(bf16[96,512]{1,0:T(8,128)(2,1)S(1)} %get-tuple-element.40), channel_id=1, source_target_pairs={{0,1},{1,0},{2,3},{3,2},{4,5},{5,4},{6,7},{7,6},{8,9},{9,8},{10,11... | collective-permute-start | bytes 294920 | tf_op jit(solution)/shard_map/ppermute | solution.py:440
  125.6 0.9 collective-permute-done.5.refs_1_.row_far_ref
  126.6 3.4 %all-to-all-done.5.refs_0_ = bf16[16,40,512]{2,1,0:T(8,128)(2,1)S(1)} async-done(((bf16[16,40,512]{2,1,0:T(8,128)(2,1)}), bf16[16,40,512]{2,1,0:T(8,128)(2,1)S(1)}, u32[]{:S(2)}, u32[]{:S(2)}) %all-to-all-start.5) | async-done | bytes 655392 | tf_op jit(solution)/shard_map/all_to_all | solution.py:437
  130.0 6.3 %collective-permute-start.6 = (bf16[512,512]{1,0:T(8,128)(2,1)S(1)}, bf16[512,512]{1,0:T(8,128)(2,1)S(1)}, u32[]{:S(2)}, u32[]{:S(2)}) collective-permute-start(bf16[512,512]{1,0:T(8,128)(2,1)S(1)} %join.1.near_ref.refs_1_), channel_id=1, source_target_pairs={{0,1},{1,0},{2,3},{3,2},{4,5},{5,4},{6,7},{7,6},{8,9},{9,8},{10,11... | collective-permute-start | bytes 1572872 | tf_op jit(solution)/shard_map/ppermute | solution.py:440
  136.3 0.7 sum_bias.1
  137.0 0.9 collective-permute-done.6.far_ref
  137.9 1.1 finish.1
  (12 shorter events, 0.1 us)
Async XLA Ops:
  3.0 27.6 %all-to-all-start = ((bf16[16,24,128]{2,1,0:T(8,128)(2,1)}), bf16[16,24,128]{2,1,0:T(8,128)(2,1)S(1)}, u32[]{:S(2)}, u32[]{:S(2)}) async-start(bf16[16,24,128]{2,1,0:T(8,128)(2,1)} %bitcast.4), calls=%async_computation | async-start | bytes 196608 | tf_op jit(solution)/shard_map/all_to_all | solution.py:437
  30.7 22.0 %copy-start.9 = (bf16[512]{0:T(512)(128)(2,1)S(1)}, bf16[512]{0:T(512)(128)(2,1)}, u32[]{:S(2)}) copy-start(bf16[512]{0:T(512)(128)(2,1)} %param.20) | copy-start | bytes 3076
  30.7 22.0 %copy-start = (bf16[2560,512]{1,0:T(8,128)(2,1)S(1)}, bf16[2560,512]{1,0:T(8,128)(2,1)}, u32[]{:S(2)}) copy-start(bf16[2560,512]{1,0:T(8,128)(2,1)} %get-tuple-element.26.mats_ref) | copy-start | bytes 7864324
  46.7 7.5 %collective-permute-start = (bf16[512,512]{1,0:T(8,128)(2,1)S(1)}, bf16[512,512]{1,0:T(8,128)(2,1)S(1)}, u32[]{:S(2)}, u32[]{:S(2)}) collective-permute-start(bf16[512,512]{1,0:T(8,128)(2,1)S(1)} %bitcast.10), channel_id=1, source_target_pairs={{0,1},{1,0},{2,3},{3,2},{4,5},{5,4},{6,7},{7,6},{8,9},{9,8},{10,11... | collective-permute-start | bytes 1572872 | tf_op jit(solution)/shard_map/ppermute | solution.py:440
  52.7 1.5 %copy-start.2 = (bf16[512,512]{1,0:T(8,128)(2,1)S(1)}, bf16[512,512]{1,0:T(8,128)(2,1)}, u32[]{:S(2)}) copy-start(bf16[512,512]{1,0:T(8,128)(2,1)} %w_neigh_ref.1) | copy-start | bytes 1572868
  52.7 1.5 %copy-start.3 = (bf16[512,512]{1,0:T(8,128)(2,1)S(1)}, bf16[512,512]{1,0:T(8,128)(2,1)}, u32[]{:S(2)}) copy-start(bf16[512,512]{1,0:T(8,128)(2,1)} %cot_ref.1) | copy-start | bytes 1572868
  53.1 5.8 %copy-start.4 = (bf16[512,512]{1,0:T(8,128)(2,1)S(1)}, bf16[512,512]{1,0:T(8,128)(2,1)}, u32[]{:S(2)}) copy-start(bf16[512,512]{1,0:T(8,128)(2,1)} %w_self_ref.1) | copy-start | bytes 1572868
  53.2 5.8 %copy-start.5 = (bf16[14,128,128]{2,1,0:T(8,128)(2,1)S(1)}, bf16[14,128,128]{2,1,0:T(8,128)(2,1)}, u32[]{:S(2)}) copy-start(bf16[14,128,128]{2,1,0:T(8,128)(2,1)} %tiles_ref.1) | copy-start | bytes 1376260
  53.2 5.8 %copy-start.6 = (s32[512]{0:T(512)S(1)}, s32[512]{0:T(512)}, u32[]{:S(2)}) copy-start(s32[512]{0:T(512)} %param.13) | copy-start | bytes 6148
  53.2 5.8 %copy-start.7 = (s32[1,14]{1,0:T(1,128)S(1)}, s32[1,14]{1,0:T(1,128)}, u32[]{:S(2)}) copy-start(s32[1,14]{1,0:T(1,128)} %dst_ref.1) | copy-start | bytes 172
  53.2 5.8 %copy-start.8 = (s32[1,14]{1,0:T(1,128)S(1)}, s32[1,14]{1,0:T(1,128)}, u32[]{:S(2)}) copy-start(s32[1,14]{1,0:T(1,128)} %src_ref.1) | copy-start | bytes 172
  56.6 4.6 %collective-permute-start.1 = (bf16[1040,512]{1,0:T(8,128)(2,1)S(1)}, bf16[1040,512]{1,0:T(8,128)(2,1)S(1)}, u32[]{:S(2)}, u32[]{:S(2)}) collective-permute-start(bf16[1040,512]{1,0:T(8,128)(2,1)S(1)} %get-tuple-element.29), channel_id=1, source_target_pairs={{0,1},{1,0},{2,3},{3,2},{4,5},{5,4},{6,7},{7,6},{8,9},{9,8},{10,11... | collective-permute-start | bytes 3194888 | tf_op jit(solution)/shard_map/ppermute | solution.py:440
  61.5 42.3 %copy-start.1 = (s32[1,64,8]{1,2,0:T(8,128)S(1)}, s32[1,64,8]{1,2,0:T(8,128)}, u32[]{:S(2)}) copy-start(s32[1,64,8]{1,2,0:T(8,128)} %param.12) | copy-start | bytes 6148
  98.7 16.6 %all-to-all-start.4 = ((bf16[16,8,128]{2,1,0:T(8,128)(2,1)}), bf16[16,8,128]{2,1,0:T(8,128)(2,1)S(1)}, u32[]{:S(2)}, u32[]{:S(2)}) async-start(bf16[16,8,128]{2,1,0:T(8,128)(2,1)} %get-tuple-element.34.refs_4_), calls=%async_computation.4 | async-start | bytes 65536 | tf_op jit(solution)/shard_map/all_to_all | solution.py:437
  104.4 15.9 %collective-permute-start.2 = (bf16[192,512]{1,0:T(8,128)(2,1)S(1)}, bf16[192,512]{1,0:T(8,128)(2,1)S(1)}, u32[]{:S(2)}, u32[]{:S(2)}) collective-permute-start(bf16[192,512]{1,0:T(8,128)(2,1)S(1)} %get-tuple-element.37), channel_id=1, source_target_pairs={{0,4},{2,6},{4,0},{6,2},{1,5},{3,7},{5,1},{7,3},{8,12},{10,14},{12... | collective-permute-start | bytes 589832 | tf_op jit(solution)/shard_map/ppermute | solution.py:525
  108.2 12.1 %collective-permute-start.3 = (bf16[192,512]{1,0:T(8,128)(2,1)S(1)}, bf16[192,512]{1,0:T(8,128)(2,1)S(1)}, u32[]{:S(2)}, u32[]{:S(2)}) collective-permute-start(bf16[192,512]{1,0:T(8,128)(2,1)S(1)} %get-tuple-element.38), channel_id=1, source_target_pairs={{0,2},{2,0},{4,6},{6,4},{1,3},{3,1},{5,7},{7,5},{8,10},{10,8},{12,... | collective-permute-start | bytes 589832 | tf_op jit(solution)/shard_map/ppermute | solution.py:525
  110.2 10.2 %collective-permute-start.4 = (bf16[192,512]{1,0:T(8,128)(2,1)S(1)}, bf16[192,512]{1,0:T(8,128)(2,1)S(1)}, u32[]{:S(2)}, u32[]{:S(2)}) collective-permute-start(bf16[192,512]{1,0:T(8,128)(2,1)S(1)} %get-tuple-element.39), channel_id=1, source_target_pairs={{0,6},{2,4},{4,2},{6,0},{1,7},{3,5},{5,3},{7,1},{8,14},{10,12},{12... | collective-permute-start | bytes 589832 | tf_op jit(solution)/shard_map/ppermute | solution.py:525
  116.3 13.7 %all-to-all-start.5 = ((bf16[16,40,512]{2,1,0:T(8,128)(2,1)}), bf16[16,40,512]{2,1,0:T(8,128)(2,1)S(1)}, u32[]{:S(2)}, u32[]{:S(2)}) async-start(bf16[16,40,512]{2,1,0:T(8,128)(2,1)} %spread_weights.1), calls=%async_computation.5 | async-start | bytes 1310720 | tf_op jit(solution)/shard_map/all_to_all | solution.py:437
  120.4 6.1 %collective-permute-start.5 = (bf16[96,512]{1,0:T(8,128)(2,1)S(1)}, bf16[96,512]{1,0:T(8,128)(2,1)S(1)}, u32[]{:S(2)}, u32[]{:S(2)}) collective-permute-start(bf16[96,512]{1,0:T(8,128)(2,1)S(1)} %get-tuple-element.40), channel_id=1, source_target_pairs={{0,1},{1,0},{2,3},{3,2},{4,5},{5,4},{6,7},{7,6},{8,9},{9,8},{10,11... | collective-permute-start | bytes 294920 | tf_op jit(solution)/shard_map/ppermute | solution.py:440
  130.0 7.8 %collective-permute-start.6 = (bf16[512,512]{1,0:T(8,128)(2,1)S(1)}, bf16[512,512]{1,0:T(8,128)(2,1)S(1)}, u32[]{:S(2)}, u32[]{:S(2)}) collective-permute-start(bf16[512,512]{1,0:T(8,128)(2,1)S(1)} %join.1.near_ref.refs_1_), channel_id=1, source_target_pairs={{0,1},{1,0},{2,3},{3,2},{4,5},{5,4},{6,7},{7,6},{8,9},{9,8},{10,11... | collective-permute-start | bytes 1572872 | tf_op jit(solution)/shard_map/ppermute | solution.py:440
